TPU v7x, 32 devices: a whole 2x2x4 slice. The times are simulated.
32 devices in a mesh: dp: 8 (over y, x, core), shard: 4 (over z).
Axes of the slice: x: 2, y: 2, z: 4, core: 2. Of those that a mesh axis runs over, the one named last changes fastest.
Arguments:
- tokens: bfloat16 [64, 64, 768], P(('dp', 'shard')), may hold values from -6 to 6
- cotangent: bfloat16 [64, 64, 768], P(('dp', 'shard')), may hold values from -6 to 6
- doc_lengths: int32 [64, 3], P(('dp', 'shard')), may hold values from 0 to 64, as said below
- qkv_w: float32 [3, 768, 768], P(None, 'dp', 'shard'), may hold values from -0.21875 to 0.21875
- out_w: float32 [768, 768], P('dp', 'shard'), may hold values from -0.625 to 0.625
- ffn_w: float32 [2, 768, 3072], P(None, 'dp', 'shard'), may hold values from -0.21875 to 0.21875
- vecs: float32 [12, 768], P(None, ('dp', 'shard')), may hold values from -0.6 to 1.5
- qkv_mom: float32 [3, 768, 768], P(None, 'dp', 'shard'), may hold values from -112 to 112
- out_mom: float32 [768, 768], P('dp', 'shard'), may hold values from -112 to 112
- ffn_mom: float32 [2, 768, 3072], P(None, 'dp', 'shard'), may hold values from -112 to 112
- vec_mom: float32 [12, 768], P(None, ('dp', 'shard')), may hold values from -160 to 160
Outputs:
- layer_out: bfloat16 [64, 64, 768], P(('dp', 'shard'))
- tokens_grad: float32 [64, 64, 768], P(('dp', 'shard'))
- qkv_grad: float32 [3, 768, 768], P(None, 'dp', 'shard')
- out_grad: float32 [768, 768], P('dp', 'shard')
- ffn_grad: float32 [2, 768, 3072], P(None, 'dp', 'shard')
- vec_grad: float32 [12, 768], P(None, ('dp', 'shard'))
- qkv_mom_new: float32 [3, 768, 768], P(None, 'dp', 'shard')
- out_mom_new: float32 [768, 768], P('dp', 'shard')
- ffn_mom_new: float32 [2, 768, 3072], P(None, 'dp', 'shard')
- vec_mom_new: float32 [12, 768], P(None, ('dp', 'shard'))
- qkv_new: float32 [3, 768, 768], P(None, 'dp', 'shard')
- out_new: float32 [768, 768], P('dp', 'shard')
- ffn_new: float32 [2, 768, 3072], P(None, 'dp', 'shard')
- vec_new: float32 [12, 768], P(None, ('dp', 'shard'))
Inputs may be any that keep to these rules, and one draw needn't show every extreme that they name: `doc_lengths`: row s lists the lengths of the documents packed from the start of slot s; a length may be 0; the lengths of a row sum to at most 64 and the rest of the slot is padding; in every draw some slot holds a single document of 64 tokens.
All inputs are finite; a program needn't handle non-finite values.
Results may differ from a plain program's by a relative error of at most 0.018.
Values may be sent and summed in bfloat16 or wider, within the bound.
No kernel may reach another device: no remote copies, remote signals or barrier semaphores. Data moves between devices by JAX's collectives and lax.ppermute only.
A program may use at most 128 MiB of HBM per device.

v0:
```python
import jax
import jax.numpy as jnp
from jax import lax
from jax.sharding import PartitionSpec as P

D = 768
HEADS = 12
HEAD = 64
FF = 3072
NS_STEPS = 3


masked_score = -1e30
norm_eps = 1e-12
momentum_decay = 0.9
muon_rate = 0.8
vec_rate = 0.5
coef_first = 3.4445
coef_second = -4.775
coef_third = 2.0315
ortho_eps = 1e-07


def spread_2(block, axis, owner):
    block = jnp.where(lax.axis_index(axis) == owner, block, jnp.zeros_like(block))
    return lax.psum(block, axis)


def segments(lengths, rows):
    position = jnp.arange(rows, dtype=jnp.int32)
    ends = jnp.cumsum(lengths)
    segment = jnp.sum((position[:, None] >= ends[None, :]).astype(jnp.int32), axis=1)
    valid = position < ends[-1]
    same = segment[:, None] == segment[None, :]
    allowed = same & valid[:, None] | (position[:, None] == position[None, :])
    return (valid, allowed)


def layer_norm(inputs, gain, bias):
    center = inputs - jnp.mean(inputs, axis=-1, keepdims=True)
    spread = jnp.mean(center * center, axis=-1, keepdims=True)
    return center * lax.rsqrt(spread + norm_eps) * gain + bias


def gelu_exact(inputs):
    return jax.nn.gelu(inputs, approximate=False)


def split_heads(matrix):
    return matrix.reshape(matrix.shape[0], HEADS, HEAD)


def gather_weights(qkv_w, out_w, ffn_w, vecs):
    pieces = (
        qkv_w.astype(jnp.bfloat16),
        out_w.astype(jnp.bfloat16),
        ffn_w.astype(jnp.bfloat16),
        vecs.astype(jnp.bfloat16),
    )
    across = (
        lax.all_gather(pieces[0], "shard", axis=2, tiled=True),
        lax.all_gather(pieces[1], "shard", axis=1, tiled=True),
        lax.all_gather(pieces[2], "shard", axis=2, tiled=True),
        lax.all_gather(pieces[3], "shard", axis=1, tiled=True),
    )
    return (
        lax.all_gather(across[0], "dp", axis=1, tiled=True),
        lax.all_gather(across[1], "dp", axis=0, tiled=True),
        lax.all_gather(across[2], "dp", axis=1, tiled=True),
        lax.all_gather(across[3], "dp", axis=1, tiled=True),
    )


def attention_scores(queries_b, keys_b, allowed):
    scores = jnp.einsum(
        "qhd,khd->hqk",
        split_heads(queries_b),
        split_heads(keys_b),
        preferred_element_type=jnp.float32,
    )
    return jnp.where(allowed[None], scores * HEAD ** (-0.5), masked_score)


def forward_pass(tokens_b, lengths, weights):
    qkv_b, out_b, ffn_b, vec_b = weights
    vec = vec_b.astype(jnp.float32)
    rows = tokens_b.shape[0]
    valid, allowed = segments(lengths, rows)
    projected = jnp.einsum("rd,kde->kre", tokens_b, qkv_b, preferred_element_type=jnp.float32)
    queries_b = (projected[0] + vec[0]).astype(jnp.bfloat16)
    keys_b = projected[1].astype(jnp.bfloat16)
    values_b = (projected[2] + vec[1]).astype(jnp.bfloat16)
    scores = attention_scores(queries_b, keys_b, allowed)
    largest = jnp.max(scores, axis=-1, keepdims=True)
    exponent = jnp.exp(scores - largest)
    totals = jnp.sum(exponent, axis=-1, keepdims=True)
    logsum = largest + jnp.log(totals)
    probs_b = (exponent / totals).astype(jnp.bfloat16)
    mixed = jnp.einsum(
        "hqk,khd->qhd", probs_b, split_heads(values_b), preferred_element_type=jnp.float32
    )
    mixed_b = mixed.reshape(rows, -1).astype(jnp.bfloat16)
    attended = jnp.dot(mixed_b, out_b, preferred_element_type=jnp.float32) + vec[2]
    first_in = tokens_b.astype(jnp.float32) + attended
    first = layer_norm(first_in, vec[3], vec[4])
    first_b = first.astype(jnp.bfloat16)
    inner = jnp.dot(first_b, ffn_b[0], preferred_element_type=jnp.float32) + vec[8:].reshape(-1)
    activ_b = gelu_exact(inner).astype(jnp.bfloat16)
    branch = jnp.einsum("rf,df->rd", activ_b, ffn_b[1], preferred_element_type=jnp.float32) + vec[5]
    second_in = first + branch
    result = layer_norm(second_in, vec[6], vec[7]) * valid[:, None].astype(jnp.float32)
    kept = (
        queries_b,
        keys_b,
        values_b,
        logsum,
        mixed_b,
        first_in,
        first_b,
        inner,
        activ_b,
        second_in,
    )
    return (result.astype(jnp.bfloat16), kept)


def backward_pass(cot_b, tokens_b, lengths, weights, kept):
    qkv_b, out_b, ffn_b, vec_b = weights
    vec = vec_b.astype(jnp.float32)
    queries_b, keys_b, values_b, logsum, mixed_b, first_in, first_b, inner, activ_b, second_in = (
        kept
    )
    rows = tokens_b.shape[0]
    valid, allowed = segments(lengths, rows)
    grad_out = cot_b.astype(jnp.float32) * valid[:, None].astype(jnp.float32)
    unused, pull_two = jax.vjp(layer_norm, second_in, vec[6], vec[7])
    d_second, d_gain_two, d_shift_two = pull_two(grad_out)
    d_branch_b = d_second.astype(jnp.bfloat16)
    d_bias_down = jnp.sum(d_branch_b.astype(jnp.float32), axis=0)
    d_activ = jnp.dot(d_branch_b, ffn_b[1], preferred_element_type=jnp.float32)
    unused, pull_gelu = jax.vjp(gelu_exact, inner)
    (d_inner,) = pull_gelu(d_activ)
    d_inner_b = d_inner.astype(jnp.bfloat16)
    d_bias_up = jnp.sum(d_inner_b.astype(jnp.float32), axis=0)
    d_first = d_second + jnp.einsum(
        "rf,df->rd", d_inner_b, ffn_b[0], preferred_element_type=jnp.float32
    )
    unused, pull_one = jax.vjp(layer_norm, first_in, vec[3], vec[4])
    d_first_in, d_gain_one, d_shift_one = pull_one(d_first)
    d_attended_b = d_first_in.astype(jnp.bfloat16)
    d_bias_out = jnp.sum(d_attended_b.astype(jnp.float32), axis=0)
    d_mixed_b = jnp.einsum(
        "re,de->rd", d_attended_b, out_b, preferred_element_type=jnp.float32
    ).astype(jnp.bfloat16)
    scores = attention_scores(queries_b, keys_b, allowed)
    probs = jnp.exp(scores - logsum)
    mixed_heads = split_heads(d_mixed_b)
    d_probs = jnp.einsum(
        "qhd,khd->hqk", mixed_heads, split_heads(values_b), preferred_element_type=jnp.float32
    )
    d_values = jnp.einsum(
        "hqk,qhd->khd", probs.astype(jnp.bfloat16), mixed_heads, preferred_element_type=jnp.float32
    )
    d_scores_b = (probs * (d_probs - jnp.sum(probs * d_probs, axis=-1, keepdims=True))).astype(
        jnp.bfloat16
    )
    d_queries = jnp.einsum(
        "hqk,khd->qhd", d_scores_b, split_heads(keys_b), preferred_element_type=jnp.float32
    ) * HEAD ** (-0.5)
    d_keys = jnp.einsum(
        "hqk,qhd->khd", d_scores_b, split_heads(queries_b), preferred_element_type=jnp.float32
    ) * HEAD ** (-0.5)
    d_proj_b = jnp.stack([d_queries, d_keys, d_values]).reshape(3, rows, -1).astype(jnp.bfloat16)
    d_tokens = d_first_in + jnp.einsum(
        "kre,kde->rd", d_proj_b, qkv_b, preferred_element_type=jnp.float32
    )
    proj_sums = jnp.sum(d_proj_b.astype(jnp.float32), axis=1)
    grad_vec = jnp.concatenate(
        [
            jnp.stack(
                [
                    proj_sums[0],
                    proj_sums[2],
                    d_bias_out,
                    d_gain_one,
                    d_shift_one,
                    d_bias_down,
                    d_gain_two,
                    d_shift_two,
                ]
            ),
            d_bias_up.reshape(-1, vec.shape[1]),
        ],
        axis=0,
    )
    factors = (d_branch_b, activ_b, first_b, d_inner_b, mixed_b, d_attended_b, d_proj_b)
    return (d_tokens, factors, grad_vec)


def orthogonalize_pair(square, wide):
    matrices = (square, wide)
    present = tuple((matrix.astype(jnp.bfloat16) for matrix in matrices))
    states = matrices
    for step in range(NS_STEPS):
        partial_value = tuple(
            (
                jnp.einsum("iw,jw->ij", block, block, preferred_element_type=jnp.float32)
                for block in present
            )
        )
        gram_part = (
            lax.psum_scatter(
                partial_value[0].astype(jnp.bfloat16), "shard", scatter_dimension=0, tiled=True
            ).astype(jnp.float32),
            lax.psum_scatter(
                partial_value[1].astype(jnp.bfloat16), "shard", scatter_dimension=0, tiled=True
            ).astype(jnp.float32),
        )
        grams = (
            lax.all_gather(gram_part[0].astype(jnp.bfloat16), "shard", axis=0, tiled=True).astype(
                jnp.float32
            ),
            lax.all_gather(gram_part[1].astype(jnp.bfloat16), "shard", axis=0, tiled=True).astype(
                jnp.float32
            ),
        )
        if step == 0:
            scales = tuple((jnp.sqrt(jnp.trace(gram)) + ortho_eps for gram in grams))
            grams = tuple((gram / (scale * scale) for gram, scale in zip(grams, scales)))
            present = tuple(
                ((matrix / scale).astype(jnp.bfloat16) for matrix, scale in zip(matrices, scales))
            )
        renewed = []
        for gram, current in zip(grams, present):
            gram_b = gram.astype(jnp.bfloat16)
            once = jnp.dot(gram_b, current, preferred_element_type=jnp.float32)
            twice = jnp.dot(gram_b, once.astype(jnp.bfloat16), preferred_element_type=jnp.float32)
            renewed.append(
                coef_first * current.astype(jnp.float32) + coef_second * once + coef_third * twice
            )
        states = tuple(renewed)
        present = tuple((state.astype(jnp.bfloat16) for state in states))
    return states


def per_device(
    tokens, cotangent, doc_lengths, qkv_w, out_w, ffn_w, vecs, qkv_mom, out_mom, ffn_mom, vec_mom
):
    micro = tokens.shape[0]
    shared = gather_weights(qkv_w, out_w, ffn_w, vecs)
    outputs = []
    stored = []
    for index in range(micro):
        weights = shared
        result_b, kept = forward_pass(tokens[index], doc_lengths[index], weights)
        outputs.append(result_b)
        stored.append(kept)
    grad_rows = [None] * micro
    factor_list = [None] * micro
    vec_total = None
    for index in reversed(range(micro)):
        weights = shared
        d_tokens, factors, vec_part = backward_pass(
            cotangent[index], tokens[index], doc_lengths[index], weights, stored[index]
        )
        grad_rows[index] = d_tokens
        factor_list[index] = factors
        vec_total = vec_part if vec_total is None else vec_total + vec_part
    (
        branch_gradient_rows,
        activation_rows,
        first_norm_rows,
        inner_gradient_rows,
        mixed_all,
        d_attended_all,
        d_proj_all,
    ) = [jnp.stack([factors[place] for factors in factor_list]) for place in range(7)]
    grad_down = jnp.einsum(
        "hzo,hzx->ox", branch_gradient_rows, activation_rows, preferred_element_type=jnp.float32
    )
    up_weight_gradient = jnp.einsum(
        "hzo,hzx->ox", first_norm_rows, inner_gradient_rows, preferred_element_type=jnp.float32
    )
    grad_wout_sum = jnp.einsum(
        "mrd,mre->de", mixed_all, d_attended_all, preferred_element_type=jnp.float32
    )
    grad_qkv_sum = jnp.einsum(
        "mrd,mkre->kde", tokens, d_proj_all, preferred_element_type=jnp.float32
    )
    summed = (grad_qkv_sum, grad_wout_sum, jnp.stack([up_weight_gradient, grad_down]), vec_total)
    reduced = (
        lax.psum_scatter(
            summed[0].astype(jnp.bfloat16), "dp", scatter_dimension=1, tiled=True
        ).astype(jnp.float32),
        lax.psum_scatter(
            summed[1].astype(jnp.bfloat16), "dp", scatter_dimension=0, tiled=True
        ).astype(jnp.float32),
        lax.psum_scatter(
            summed[2].astype(jnp.bfloat16), "dp", scatter_dimension=1, tiled=True
        ).astype(jnp.float32),
        lax.psum_scatter(
            summed[3].astype(jnp.bfloat16), "dp", scatter_dimension=1, tiled=True
        ).astype(jnp.float32),
    )
    grad_qkv, grad_wout, grad_ffn, grad_vec = (
        lax.psum_scatter(
            reduced[0].astype(jnp.bfloat16), "shard", scatter_dimension=2, tiled=True
        ).astype(jnp.float32),
        lax.psum_scatter(
            reduced[1].astype(jnp.bfloat16), "shard", scatter_dimension=1, tiled=True
        ).astype(jnp.float32),
        lax.psum_scatter(
            reduced[2].astype(jnp.bfloat16), "shard", scatter_dimension=2, tiled=True
        ).astype(jnp.float32),
        lax.psum_scatter(
            reduced[3].astype(jnp.bfloat16), "shard", scatter_dimension=1, tiled=True
        ).astype(jnp.float32),
    )
    new_qkv_mom = momentum_decay * qkv_mom + grad_qkv
    new_out_mom = momentum_decay * out_mom + grad_wout
    new_ffn_mom = momentum_decay * ffn_mom + grad_ffn
    square_local = jnp.concatenate([new_qkv_mom, new_out_mom[None]], axis=0)
    square_cols, wide_cols = (
        lax.all_gather(square_local.astype(jnp.bfloat16), "dp", axis=1, tiled=True).astype(
            square_local.dtype
        ),
        lax.all_gather(new_ffn_mom.astype(jnp.bfloat16), "dp", axis=1, tiled=True).astype(
            new_ffn_mom.dtype
        ),
    )
    row = lax.axis_index("dp")
    rows_count = lax.axis_size("dp")
    owners = [place * rows_count // 6 for place in range(6)]
    square_pick = sum(((row == owners[place]).astype(jnp.int32) * place for place in range(4)))
    wide_pick = (row == owners[5]).astype(jnp.int32)
    square_state, wide_state = orthogonalize_pair(
        lax.dynamic_index_in_dim(square_cols, square_pick, 0, keepdims=False),
        lax.dynamic_index_in_dim(wide_cols, wide_pick, 0, keepdims=False),
    )
    depth = qkv_w.shape[1]
    square_rows = []
    for place in range(4):
        whole = spread_2(square_state.astype(jnp.bfloat16), "dp", owners[place]).astype(
            square_state.dtype
        )
        square_rows.append(lax.dynamic_slice_in_dim(whole, row * depth, depth, 0))
    wide_rows = []
    for place in range(4, 6):
        whole = spread_2(wide_state.astype(jnp.bfloat16), "dp", owners[place]).astype(
            wide_state.dtype
        )
        wide_rows.append(lax.dynamic_slice_in_dim(whole, row * depth, depth, 0))
    qkv_new = qkv_w - muon_rate * jnp.stack(square_rows[:3])
    out_new = out_w - muon_rate * square_rows[3]
    ffn_new = ffn_w - muon_rate * (FF / D) ** 0.5 * jnp.stack(wide_rows)
    token_count = tokens.shape[0] * tokens.shape[1] * lax.axis_size("dp") * lax.axis_size("shard")
    new_vec_mom = momentum_decay * vec_mom + grad_vec
    vec_new = vecs - vec_rate * token_count ** (-0.5) * new_vec_mom
    return (
        jnp.stack(outputs),
        jnp.stack(grad_rows),
        grad_qkv,
        grad_wout,
        grad_ffn,
        grad_vec,
        new_qkv_mom,
        new_out_mom,
        new_ffn_mom,
        new_vec_mom,
        qkv_new,
        out_new,
        ffn_new,
        vec_new,
    )


def solution(mesh):
    in_specs = (
        P(("dp", "shard"), None, None),
        P(("dp", "shard"), None, None),
        P(("dp", "shard"), None),
        P(None, "dp", "shard"),
        P("dp", "shard"),
        P(None, "dp", "shard"),
        P(None, ("dp", "shard")),
        P(None, "dp", "shard"),
        P("dp", "shard"),
        P(None, "dp", "shard"),
        P(None, ("dp", "shard")),
    )
    out_specs = (
        P(("dp", "shard"), None, None),
        P(("dp", "shard"), None, None),
        P(None, "dp", "shard"),
        P("dp", "shard"),
        P(None, "dp", "shard"),
        P(None, ("dp", "shard")),
        P(None, "dp", "shard"),
        P("dp", "shard"),
        P(None, "dp", "shard"),
        P(None, ("dp", "shard")),
        P(None, "dp", "shard"),
        P("dp", "shard"),
        P(None, "dp", "shard"),
        P(None, ("dp", "shard")),
    )
    return jax.shard_map(
        per_device, mesh=mesh, in_specs=in_specs, out_specs=out_specs, check_vma=False
    )
```

profile of v0, /device:TPU:0, one launch (start us, length us, event | category | flops | bytes accessed | tf_op | source)
XLA Modules:
  0.0 1022.0 jit_solution(14801140950338418476)
XLA Ops:
  10.3 27.2 %all_gather.48 = bf16[3,96,768]{1,0,2:T(4,128)(2,1)S(1)} all-gather(bf16[3,96,192]{1,0,2:T(4,128)(2,1)S(1)} %copy.384), channel_id=1, replica_groups=mesh['dp'=8,'shard'=4] {'shard'}, dimensions={2}, use_global_device_ids=true | all-gather | bytes 552960 | tf_op jit(solution)/shard_map/all_gather | solution.py:61
  38.9 15.4 %all_gather.52 = bf16[96,768]{0,1:T(8,128)(2,1)S(1)} all-gather(bf16[96,192]{0,1:T(8,128)(2,1)S(1)} %convert_element_type.443), channel_id=1, replica_groups=mesh['dp'=8,'shard'=4] {'shard'}, dimensions={1}, use_global_device_ids=true | all-gather | bytes 184320 | tf_op jit(solution)/shard_map/all_gather | solution.py:62
  55.8 13.1 %all-gather = bf16[4,24,12]{1,2,0:T(8,128)(2,1)S(1)} all-gather(bf16[1,24,12]{1,2,0:T(8,128)(2,1)S(1)} %convert_bitcast_fusion.3), channel_id=1, replica_groups=mesh['dp'=8,'shard'=4] {'shard'}, dimensions={0}, use_global_device_ids=true | all-gather | bytes 2880 | tf_op jit(solution)/shard_map/all_gather | solution.py:64
  69.0 8.9 all-gather.1
  87.5 2.9 convolution_bitcast_fusion.1
  129.9 44.8 %all-gather.21.cloned.1.call-done = bf16[2,768,3072]{2,1,0:T(8,128)(2,1)} async-done(((bf16[2,96,3072]{2,1,0:T(8,128)(2,1)}), bf16[2,768,3072]{2,1,0:T(8,128)(2,1)}) %all-gather.21.cloned.1.call-update) | async-done | bytes 9437200 | tf_op jit(solution)/shard_map/all_gather | solution.py:69
  174.7 5.3 multiply_convert_fusion
  182.1 2.5 multiply_convert_fusion.1
  190.0 3.3 convert_reduce_fusion.1
  194.8 3.3 convert_reduce_fusion
  216.9 2.6 bitcast_convert_fusion.3
  238.6 4.1 fusion.2
  242.7 8.2 copy.463
  250.9 5.0 copy.476
  256.0 5.0 fusion.1
  261.0 3.5 fusion
  264.5 9.1 pad_maximum_fusion
  275.6 32.7 %reduce-scatter.41.cloned.1.call-done = bf16[96,2304]{1,0:T(8,128)(2,1)} async-done(((bf16[768,2304]{1,0:T(8,128)(2,1)}), bf16[96,2304]{1,0:T(8,128)(2,1)}) %reduce-scatter.41.cloned.1.call-update) | async-done | bytes 442384
  312.8 75.8 %reduce-scatter.25.cloned.1.call-done = bf16[2,96,3072]{2,1,0:T(8,128)(2,1)} async-done(((bf16[2,768,3072]{2,1,0:T(8,128)(2,1)}), bf16[2,96,3072]{2,1,0:T(8,128)(2,1)}) %reduce-scatter.25.cloned.1.call-update) | async-done | bytes 1179664 | tf_op jit(solution)/shard_map/reduce_scatter | solution.py:298
  392.2 18.8 %reduce-scatter.23.cloned.1.call-done = bf16[96,192]{0,1:T(8,128)(2,1)} async-done(((bf16[96,768]{0,1:T(8,128)(2,1)}), bf16[96,192]{0,1:T(8,128)(2,1)}) %reduce-scatter.23.cloned.1.call-update) | async-done | bytes 36880 | tf_op jit(solution)/shard_map/reduce_scatter | solution.py:309
  412.6 21.5 %reduce-scatter.21.cloned.1.call-done = bf16[3,96,192]{1,2,0:T(8,128)(2,1)} async-done(((bf16[3,96,768]{1,2,0:T(8,128)(2,1)}), bf16[3,96,192]{1,2,0:T(8,128)(2,1)}) %reduce-scatter.21.cloned.1.call-update) | async-done | bytes 110608 | tf_op jit(solution)/shard_map/reduce_scatter | solution.py:306
  439.2 24.6 %reduce-scatter.27.cloned.1.call-done = bf16[2,96,768]{2,1,0:T(8,128)(2,1)} async-done(((bf16[2,96,3072]{2,1,0:T(8,128)(2,1)}), bf16[2,96,768]{2,1,0:T(8,128)(2,1)}) %reduce-scatter.27.cloned.1.call-update) | async-done | bytes 294928 | tf_op jit(solution)/shard_map/reduce_scatter | solution.py:312
  466.2 24.5 %all-gather.23.cloned.1.call-done = bf16[4,768,192]{2,0,1:T(4,128)(2,1)} async-done(((bf16[4,96,192]{2,0,1:T(4,128)(2,1)}), bf16[4,768,192]{2,0,1:T(4,128)(2,1)}) %all-gather.23.cloned.1.call-update) | async-done | bytes 1179664 | tf_op jit(solution)/shard_map/all_gather | solution.py:324
  490.7 3.1 constant_dynamic-slice_fusion
  493.8 2.8 copy.475
  496.6 2.6 convolution_convert_fusion.5
  499.3 22.8 %all-gather.31.cloned.1.call-done = bf16[2,768,768]{2,1,0:T(8,128)(2,1)} async-done(((bf16[2,96,768]{2,1,0:T(8,128)(2,1)}), bf16[2,768,768]{2,1,0:T(8,128)(2,1)}) %all-gather.31.cloned.1.call-update) | async-done | bytes 2359312 | tf_op jit(solution)/shard_map/all_gather | solution.py:327
  522.0 3.8 convolution_convert_fusion.2
  525.9 27.7 %reduce-scatter.29.cloned.1.call-done = bf16[192,768]{1,0:T(8,128)(2,1)} async-done(((bf16[768,768]{1,0:T(8,128)(2,1)}), bf16[192,768]{1,0:T(8,128)(2,1)}) %reduce-scatter.29.cloned.1.call-update) | async-done | bytes 294928 | tf_op jit(solution)/shard_map/reduce_scatter | solution.py:212
  553.6 30.0 %reduce-scatter.35.cloned.1.call-done = bf16[192,768]{1,0:T(8,128)(2,1)} async-done(((bf16[768,768]{1,0:T(8,128)(2,1)}), bf16[192,768]{1,0:T(8,128)(2,1)}) %reduce-scatter.35.cloned.1.call-update) | async-done | bytes 294928 | tf_op jit(solution)/shard_map/reduce_scatter | solution.py:215
  583.7 30.5 %all-gather.25.cloned.1.call-done = bf16[768,768]{1,0:T(8,128)(2,1)} async-done(((bf16[192,768]{1,0:T(8,128)(2,1)}), bf16[768,768]{1,0:T(8,128)(2,1)}) %all-gather.25.cloned.1.call-update) | async-done | bytes 1179664 | tf_op jit(solution)/shard_map/all_gather | solution.py:220
  621.9 23.4 %all-gather.33.cloned.1.call-done = bf16[768,768]{1,0:T(8,128)(2,1)} async-done(((bf16[192,768]{1,0:T(8,128)(2,1)}), bf16[768,768]{1,0:T(8,128)(2,1)}) %all-gather.33.cloned.1.call-update) | async-done | bytes 1179664 | tf_op jit(solution)/shard_map/all_gather | solution.py:223
  648.0 2.9 fusion.162
  655.4 20.3 %reduce-scatter.31.cloned.1.call-done = bf16[192,768]{1,0:T(8,128)(2,1)} async-done(((bf16[768,768]{1,0:T(8,128)(2,1)}), bf16[192,768]{1,0:T(8,128)(2,1)}) %reduce-scatter.31.cloned.1.call-update) | async-done | bytes 294928 | tf_op jit(solution)/shard_map/reduce_scatter | solution.py:212
  675.8 30.0 %reduce-scatter.37.cloned.1.call-done = bf16[192,768]{1,0:T(8,128)(2,1)} async-done(((bf16[768,768]{1,0:T(8,128)(2,1)}), bf16[192,768]{1,0:T(8,128)(2,1)}) %reduce-scatter.37.cloned.1.call-update) | async-done | bytes 294928 | tf_op jit(solution)/shard_map/reduce_scatter | solution.py:215
  705.9 30.7 %all-gather.27.cloned.1.call-done = bf16[768,768]{1,0:T(8,128)(2,1)} async-done(((bf16[192,768]{1,0:T(8,128)(2,1)}), bf16[768,768]{1,0:T(8,128)(2,1)}) %all-gather.27.cloned.1.call-update) | async-done | bytes 1179664 | tf_op jit(solution)/shard_map/all_gather | solution.py:220
  743.0 24.6 %all-gather.35.cloned.1.call-done = bf16[768,768]{1,0:T(8,128)(2,1)} async-done(((bf16[192,768]{1,0:T(8,128)(2,1)}), bf16[768,768]{1,0:T(8,128)(2,1)}) %all-gather.35.cloned.1.call-update) | async-done | bytes 1179664 | tf_op jit(solution)/shard_map/all_gather | solution.py:223
  767.6 2.9 fusion.185
  775.0 23.3 %reduce-scatter.33.cloned.1.call-done = bf16[192,768]{1,0:T(8,128)(2,1)} async-done(((bf16[768,768]{1,0:T(8,128)(2,1)}), bf16[192,768]{1,0:T(8,128)(2,1)}) %reduce-scatter.33.cloned.1.call-update) | async-done | bytes 294928 | tf_op jit(solution)/shard_map/reduce_scatter | solution.py:212
  798.3 30.2 %reduce-scatter.39.cloned.1.call-done = bf16[192,768]{1,0:T(8,128)(2,1)} async-done(((bf16[768,768]{1,0:T(8,128)(2,1)}), bf16[192,768]{1,0:T(8,128)(2,1)}) %reduce-scatter.39.cloned.1.call-update) | async-done | bytes 294928 | tf_op jit(solution)/shard_map/reduce_scatter | solution.py:215
  858.2 2.7 concatenate.31
  865.9 3.0 broadcast_select_fusion.2
  868.9 21.4 %all-gather.37.cloned.1.call-done = bf16[768,768]{1,0:T(8,128)(2,1)} async-done(((bf16[192,768]{1,0:T(8,128)(2,1)}), bf16[768,768]{1,0:T(8,128)(2,1)}) %all-gather.37.cloned.1.call-update) | async-done | bytes 1179664 | tf_op jit(solution)/shard_map/all_gather | solution.py:223
  890.3 2.9 fusion.186
  893.2 2.8 broadcast_select_fusion.1
  904.6 22.0 %reduce-scatter.45.cloned.1.call-done = bf16[96,12]{1,0:T(8,128)(2,1)} async-done(((bf16[768,12]{1,0:T(8,128)(2,1)}), bf16[96,12]{1,0:T(8,128)(2,1)}) %reduce-scatter.45.cloned.1.call-update) | async-done | bytes 2320
  927.4 11.7 %all-reduce = bf16[12,96]{1,0:T(8,128)(2,1)S(1)} all-reduce(bf16[12,96]{1,0:T(8,128)(2,1)S(1)} %copy.468), channel_id=9, replica_groups=mesh['dp'=8,'shard'=4] {'shard'}, use_global_device_ids=true, to_apply=%region_49.50.clone | all-reduce | flops 1152 | bytes 4608
  946.6 60.0 %all-reduce.4.cloned.1.call-done = (bf16[768,192]{0,1:T(8,128)(2,1)}, bf16[768,192]{0,1:T(8,128)(2,1)}, bf16[768,192]{0,1:T(8,128)(2,1)}, bf16[768,192]{0,1:T(8,...) async-done(((bf16[768,192]{0,1:T(8,128)(2,1)}, bf16[768,192]{0,1:T(8,128)(2,1)}, bf16[768,192]{0,1:T(8,128)(2,1)}, bf16[768,192]{0,1:T(8,128)(2,1)}, ...) | async-done | bytes 3538960 | tf_op jit(solution)/shard_map/psum | solution.py:26
  (417 shorter events, 204.1 us)
Async XLA Ops:
  7.2 31.6 %copy-start.32 = (f32[96,192]{1,0:T(8,128)S(1)}, f32[96,192]{1,0:T(8,128)}, u32[]{:S(2)}) copy-start(f32[96,192]{1,0:T(8,128)} %param.15) | copy-start | bytes 221188
  7.2 48.0 %all-gather.19.cloned.1.call-start = ((), (), s32[]{:S(2)}) async-start(), calls=%async_computation.15 | async-start | bytes 1474560 | tf_op jit(solution)/shard_map/all_gather | solution.py:63
  9.1 78.4 %all-gather.15.cloned.1.call-start = ((), (), s32[]{:S(2)}) async-start(), calls=%async_computation.13 | async-start | bytes 3981312 | tf_op jit(solution)/shard_map/all_gather | solution.py:67
  10.3 45.5 %copy-start.44 = (f32[12,24]{1,0:T(8,128)S(1)}, f32[12,24]{1,0:T(8,128)}, u32[]{:S(2)}) copy-start(f32[12,24]{1,0:T(8,128)} %param.17) | copy-start | bytes 3460
  37.5 41.8 %copy-start.65 = (s32[2,3]{1,0:T(2,128)S(1)}, s32[2,3]{1,0:T(2,128)}, u32[]{:S(2)}) copy-start(s32[2,3]{1,0:T(2,128)} %param.13) | copy-start | bytes 76
  38.7 84.5 %all-gather.17.cloned.1.call-start = ((), (), s32[]{:S(2)}) async-start(), calls=%async_computation.14 | async-start | bytes 1327104 | tf_op jit(solution)/shard_map/all_gather | solution.py:68
  38.9 47.9 %copy-start.23 = (f32[96,192]{0,1:T(8,128)}, f32[96,192]{0,1:T(8,128)S(1)}, u32[]{:S(2)}) copy-start(f32[96,192]{0,1:T(8,128)S(1)} %copy.392) | copy-start | bytes 221188
  55.1 119.5 %all-gather.21.cloned.1.call-start = ((), (), s32[]{:S(2)}) async-start(), calls=%async_computation.16 | async-start | bytes 10616832 | tf_op jit(solution)/shard_map/all_gather | solution.py:69
  55.7 218.0 %reduce-scatter.43.cloned.1.call-start = ((), (), s32[]{:S(2)}) async-start(), calls=%async_computation.36 | async-start | bytes 1327104
  87.5 6.2 copy-start
  123.2 6.6 copy-start.41
  123.2 6.6 copy-start.38
  123.2 6.7 copy-start.43
  198.2 6.0 copy-start.1
  207.0 5.7 copy-start.72
  207.0 5.8 copy-start.9
  207.0 7.1 copy-start.2
  219.5 88.8 %reduce-scatter.41.cloned.1.call-start = ((), (), s32[]{:S(2)}) async-start(), calls=%async_computation.35 | async-start | bytes 3981312
  219.5 5.7 copy-start.4
  255.9 132.7 %reduce-scatter.25.cloned.1.call-start = ((), (), s32[]{:S(2)}) async-start(), calls=%async_computation.19 | async-start | bytes 10616832 | tf_op jit(solution)/shard_map/reduce_scatter | solution.py:298
  273.7 137.3 %reduce-scatter.23.cloned.1.call-start = ((), (), s32[]{:S(2)}) async-start(), calls=%async_computation.18 | async-start | bytes 245760 | tf_op jit(solution)/shard_map/reduce_scatter | solution.py:309
  275.5 158.5 %reduce-scatter.21.cloned.1.call-start = ((), (), s32[]{:S(2)}) async-start(), calls=%async_computation.17 | async-start | bytes 737280 | tf_op jit(solution)/shard_map/reduce_scatter | solution.py:306
  312.8 151.0 %reduce-scatter.27.cloned.1.call-start = ((), (), s32[]{:S(2)}) async-start(), calls=%async_computation.20 | async-start | bytes 1474560 | tf_op jit(solution)/shard_map/reduce_scatter | solution.py:312
  388.7 102.0 %all-gather.23.cloned.1.call-start = ((), (), s32[]{:S(2)}) async-start(), calls=%async_computation.21 | async-start | bytes 1769472 | tf_op jit(solution)/shard_map/all_gather | solution.py:324
  439.2 82.9 %all-gather.31.cloned.1.call-start = ((), (), s32[]{:S(2)}) async-start(), calls=%async_computation.28 | async-start | bytes 2654208 | tf_op jit(solution)/shard_map/all_gather | solution.py:327
  466.1 87.4 %reduce-scatter.29.cloned.1.call-start = ((), (), s32[]{:S(2)}) async-start(), calls=%async_computation.22 | async-start | bytes 1474560 | tf_op jit(solution)/shard_map/reduce_scatter | solution.py:212
  499.2 84.4 %reduce-scatter.35.cloned.1.call-start = ((), (), s32[]{:S(2)}) async-start(), calls=%async_computation.29 | async-start | bytes 1474560 | tf_op jit(solution)/shard_map/reduce_scatter | solution.py:215
  525.8 88.4 %all-gather.25.cloned.1.call-start = ((), (), s32[]{:S(2)}) async-start(), calls=%async_computation.23 | async-start | bytes 1474560 | tf_op jit(solution)/shard_map/all_gather | solution.py:220
  553.6 91.7 %all-gather.33.cloned.1.call-start = ((), (), s32[]{:S(2)}) async-start(), calls=%async_computation.30 | async-start | bytes 1474560 | tf_op jit(solution)/shard_map/all_gather | solution.py:223
  583.7 92.1 %reduce-scatter.31.cloned.1.call-start = ((), (), s32[]{:S(2)}) async-start(), calls=%async_computation.24 | async-start | bytes 1474560 | tf_op jit(solution)/shard_map/reduce_scatter | solution.py:212
  621.8 84.0 %reduce-scatter.37.cloned.1.call-start = ((), (), s32[]{:S(2)}) async-start(), calls=%async_computation.31 | async-start | bytes 1474560 | tf_op jit(solution)/shard_map/reduce_scatter | solution.py:215
  655.4 81.3 %all-gather.27.cloned.1.call-start = ((), (), s32[]{:S(2)}) async-start(), calls=%async_computation.25 | async-start | bytes 1474560 | tf_op jit(solution)/shard_map/all_gather | solution.py:220
  675.8 91.8 %all-gather.35.cloned.1.call-start = ((), (), s32[]{:S(2)}) async-start(), calls=%async_computation.32 | async-start | bytes 1474560 | tf_op jit(solution)/shard_map/all_gather | solution.py:223
  705.9 92.4 %reduce-scatter.33.cloned.1.call-start = ((), (), s32[]{:S(2)}) async-start(), calls=%async_computation.26 | async-start | bytes 1474560 | tf_op jit(solution)/shard_map/reduce_scatter | solution.py:212
  742.7 85.8 %reduce-scatter.39.cloned.1.call-start = ((), (), s32[]{:S(2)}) async-start(), calls=%async_computation.33 | async-start | bytes 1474560 | tf_op jit(solution)/shard_map/reduce_scatter | solution.py:215
  774.9 67.8 %copy-start.52 = (f32[768]{0:T(1024)S(1)}, f32[768]{0:T(1024)}, u32[]{:S(2)}) copy-start(f32[768]{0:T(1024)} %get-tuple-element.154) | copy-start | bytes 9220
  774.9 68.4 %copy-start.51 = (f32[768]{0:T(1024)S(1)}, f32[768]{0:T(1024)}, u32[]{:S(2)}) copy-start(f32[768]{0:T(1024)} %get-tuple-element.114) | copy-start | bytes 9220
  774.9 69.0 %copy-start.50 = (f32[768]{0:T(1024)S(1)}, f32[768]{0:T(1024)}, u32[]{:S(2)}) copy-start(f32[768]{0:T(1024)} %get-tuple-element.123) | copy-start | bytes 9220
  774.9 76.7 %copy-start.49 = (f32[768]{0:T(1024)S(1)}, f32[768]{0:T(1024)}, u32[]{:S(2)}) copy-start(f32[768]{0:T(1024)} %get-tuple-element.122) | copy-start | bytes 9220
  774.9 89.1 %all-gather.29.cloned.1.call-start = ((), (), s32[]{:S(2)}) async-start(), calls=%async_computation.27 | async-start | bytes 1474560 | tf_op jit(solution)/shard_map/all_gather | solution.py:220
  798.3 92.0 %all-gather.37.cloned.1.call-start = ((), (), s32[]{:S(2)}) async-start(), calls=%async_computation.34 | async-start | bytes 1474560 | tf_op jit(solution)/shard_map/all_gather | solution.py:223
  828.5 98.1 %reduce-scatter.45.cloned.1.call-start = ((), (), s32[]{:S(2)}) async-start(), calls=%async_computation.37 | async-start | bytes 221184
  863.9 142.6 %all-reduce.4.cloned.1.call-start = ((), (), s32[]{:S(2)}) async-start(), calls=%async_computation.38 | async-start | bytes 7077888 | tf_op jit(solution)/shard_map/psum | solution.py:26
  901.9 37.1 %copy-start.45 = (f32[12,24]{1,0:T(8,128)S(1)}, f32[12,24]{1,0:T(8,128)}, u32[]{:S(2)}) copy-start(f32[12,24]{1,0:T(8,128)} %param.17) | copy-start | bytes 3460
  901.9 37.1 %copy-start.54 = (f32[12,24]{1,0:T(8,128)S(1)}, f32[12,24]{1,0:T(8,128)}, u32[]{:S(2)}) copy-start(f32[12,24]{1,0:T(8,128)} %param.21) | copy-start | bytes 3460
  903.8 106.0 %copy-start.24 = (f32[96,192]{0,1:T(8,128)S(1)}, f32[96,192]{0,1:T(8,128)}, u32[]{:S(2)}) copy-start(f32[96,192]{0,1:T(8,128)} %copy-done.23) | copy-start | bytes 221188
  903.8 109.6 %copy-start.8 = (f32[2,96,768]{2,1,0:T(8,128)S(1)}, f32[2,96,768]{2,1,0:T(8,128)}, u32[]{:S(2)}) copy-start(f32[2,96,768]{2,1,0:T(8,128)} %param.16) | copy-start | bytes 1769476
  944.8 69.5 %copy-start.19 = (f32[3,96,192]{2,1,0:T(8,128)S(1)}, f32[3,96,192]{2,1,0:T(8,128)}, u32[]{:S(2)}) copy-start(f32[3,96,192]{2,1,0:T(8,128)} %param.14) | copy-start | bytes 663556
  (66 other events, 181.5 us)
Sparse Core Ops, SparseCore 0:
  10.2 40.8 all-gather.18
  53.5 33.9 all-gather.14
  89.9 24.1 all-gather.16
  115.8 58.8 all-gather.20
  219.6 36.7 reduce-scatter.42
  260.1 48.0 reduce-scatter.40
  312.1 76.4 reduce-scatter.24
  391.6 19.3 reduce-scatter.22
  413.8 20.1 reduce-scatter.20
  436.2 27.4 reduce-scatter.26
  466.2 24.3 all-gather.22
  493.0 29.0 all-gather.30
  524.3 29.1 reduce-scatter.28
  555.7 27.8 reduce-scatter.34
  585.1 29.1 all-gather.24
  615.7 29.5 all-gather.32
  647.4 28.2 reduce-scatter.30
  677.9 27.8 reduce-scatter.36
  707.4 29.1 all-gather.26
  738.0 29.5 all-gather.34
  769.9 28.2 reduce-scatter.32
  800.6 27.8 reduce-scatter.38
  830.1 29.1 all-gather.28
  860.7 29.5 all-gather.36
  893.9 32.6 reduce-scatter.44
  931.6 74.9 all-reduce.3
where the time goes:
time: 1030 us; the launch traced here: 1020 us
  waiting for transfers between devices  641 us (62%)
  local copies, waits for them, and re-layouts  123 us (12%)
  matrix products  104 us (10%)
  blocking collectives  76.4 us (7%)
  other arithmetic  57.5 us (6%)
  between operations  17.9 us (2%)
    reduce_scatter x3, waiting for transfers between devices, orthogonalize_pair(): lax.psum_scatter(partial_value[1].astype(jnp.bfloat16), 'shard', scatter_...  90.2 us
    reduce_scatter x1, waiting for transfers between devices, per_device(): lax.psum_scatter(summed[2].astype(jnp.bfloat16), 'dp', scatter_dimension=...  75.8 us
    reduce_scatter x3, waiting for transfers between devices, orthogonalize_pair(): lax.psum_scatter(partial_value[0].astype(jnp.bfloat16), 'shard', scatter_...  71.3 us
    all_gather x3, waiting for transfers between devices, orthogonalize_pair(): lax.all_gather(gram_part[1].astype(jnp.bfloat16), 'shard', axis=0, tiled=...  69.4 us
    all_gather x3, waiting for transfers between devices, orthogonalize_pair(): lax.all_gather(gram_part[0].astype(jnp.bfloat16), 'shard', axis=0, tiled=...  61.2 us
    psum x1, waiting for transfers between devices, spread_2(): return lax.psum(block, axis)  60 us
    unnamed x29, waiting for transfers between devices  55.6 us
    all_gather x1, waiting for transfers between devices, gather_weights(): lax.all_gather(across[2], 'dp', axis=1, tiled=True)  44.8 us
  transfers between devices with their start and end apart: 26, of which 22 were waited for; matrix products, arithmetic and copies ran while one was open for 22% of the time, Pallas kernels for 0%

commit v1 on v0

--- a/solution.py
+++ b/solution.py
@@ -1,6 +1,9 @@
+import math
 import jax
 import jax.numpy as jnp
 from jax import lax
+from jax.experimental import pallas as pl
+from jax.experimental.pallas import tpu as pltpu
 from jax.sharding import PartitionSpec as P
 
 D = 768
@@ -374,7 +377,638 @@
     )
 
 
+def gather_direct(block, axis):
+    count = lax.axis_size(axis)
+    me = lax.axis_index(axis)
+    whole = jnp.zeros((count,) + block.shape, block.dtype)
+    whole = lax.dynamic_update_index_in_dim(whole, block, me, 0)
+    for step in range(1, count):
+        got = lax.ppermute(block, axis, [(i, (i + step) % count) for i in range(count)])
+        whole = lax.dynamic_update_index_in_dim(whole, got, lax.rem(me - step + count, count), 0)
+    return whole
+
+
+def pieces_of(block, axis):
+    count = lax.axis_size(axis)
+    return [block] + [
+        lax.ppermute(block, axis, [(i, (i + step) % count) for i in range(count)])
+        for step in range(1, count)
+    ]
+
+
+def send_parts(parts, axis):
+    count = lax.axis_size(axis)
+    return [parts[0]] + [
+        lax.ppermute(parts[step], axis, [(i, (i + step) % count) for i in range(count)])
+        for step in range(1, count)
+    ]
+
+
+def swap(block, axis, bit):
+    return lax.ppermute(block, axis, [(i, i ^ bit) for i in range(lax.axis_size(axis))])
+
+
+def gather_double(block, axis):
+    me = lax.axis_index(axis)
+    bit = 1
+    whole = block[None]
+    while bit < lax.axis_size(axis):
+        other = swap(whole, axis, bit)
+        high = (me & bit) != 0
+        whole = jnp.concatenate(
+            [jnp.where(high, other, whole), jnp.where(high, whole, other)], axis=0
+        )
+        bit *= 2
+    return whole
+
+
+def dot(left, right, dims):
+    return lax.dot_general(left, right, (dims, ((), ())), preferred_element_type=jnp.float32)
+
+
+def norm_parts(inputs):
+    center = inputs - jnp.mean(inputs, axis=-1, keepdims=True)
+    spread = jnp.mean(center * center, axis=-1, keepdims=True)
+    scale = lax.rsqrt(spread + norm_eps)
+    return center * scale, scale
+
+
+def norm_back(grad, unit, scale, gain):
+    scaled = grad * gain
+    mean_grad = jnp.mean(scaled, axis=-1, keepdims=True)
+    mean_unit = jnp.mean(scaled * unit, axis=-1, keepdims=True)
+    return scale * (scaled - mean_grad - unit * mean_unit)
+
+
+BLOCK = 256
+SPLIT = 4
+
+
+def source_of(column, step):
+    return lax.rem(column - step + SPLIT, SPLIT)
+
+
+def put_pieces(pieces, column, whole):
+    count = pieces[0].shape[0]
+    for step, piece in enumerate(pieces):
+        at = pl.multiple_of(source_of(column, step) * count, count)
+        whole[pl.ds(at, count), :] = piece[...]
+
+
+def take_parts(whole, column, parts):
+    count = parts[0].shape[0]
+    for step, part in enumerate(parts):
+        at = pl.multiple_of(lax.rem(column + step, SPLIT) * count, count)
+        part[...] = whole[pl.ds(at, count), :].astype(part.dtype)
+
+
+def sum_pieces(pieces):
+    total = pieces[0][...]
+    for piece in pieces[1:]:
+        total = total + piece[...].astype(jnp.float32)
+    return total
+
+
+def row_sums(values):
+    return jnp.sum(values, axis=0, keepdims=True)
+
+
+def layer_middle(place, *refs):
+    pieces, refs = refs[:SPLIT], refs[SPLIT:]
+    out_weight, tokens, vec, weights, bias_up, first_b, activ_b, slope, first_in, *refs = refs
+    parts, (moving,) = refs[:SPLIT], refs[SPLIT:]
+    column = place[0]
+    own = pieces[0].shape[1]
+    attended = vec[2:3, :] + tokens[...].astype(jnp.float32)
+    for step, piece in enumerate(pieces):
+        at = pl.multiple_of(source_of(column, step) * own, own)
+        attended = attended + dot(piece[...], out_weight[pl.ds(at, own), :], ((1,), (0,)))
+    moving[...] = attended
+    take_parts(moving, column, [first_in])
+    unit, scale = norm_parts(attended)
+    first_b[...] = (unit * vec[3:4, :] + vec[4:5, :]).astype(jnp.bfloat16)
+    hidden = slope.shape[1]
+    inner = dot(first_b[...], weights[:, :hidden], ((1,), (0,))) + bias_up[...]
+    cdf = 0.5 * (1.0 + lax.erf(inner * 2.0 ** (-0.5)))
+    activ_b[...] = (inner * cdf).astype(jnp.bfloat16)
+    slope[...] = cdf + inner * jnp.exp(-0.5 * inner * inner) * (2.0 * math.pi) ** (-0.5)
+    moving[...] = dot(activ_b[...], weights[:, hidden : 2 * hidden], ((1,), (1,)))
+    take_parts(moving, column, parts)
+
+
+def second_norm(*refs):
+    pieces, refs = refs[:SPLIT], refs[SPLIT:]
+    first_in, vec, cotangent, valid, layer_out, d_branch, d_second, sums = refs
+    unit, scale = norm_parts(first_in[...])
+    first = unit * vec[3:4, :] + vec[4:5, :]
+    unit, scale = norm_parts(first + (sum_pieces(pieces) + vec[5:6, :]))
+    layer_out[...] = ((unit * vec[6:7, :] + vec[7:8, :]) * valid[...]).astype(jnp.bfloat16)
+    grad = cotangent[...].astype(jnp.float32) * valid[...]
+    d_rows = norm_back(grad, unit, scale, vec[6:7, :])
+    d_second[...] = d_rows
+    d_branch[...] = d_rows.astype(jnp.bfloat16)
+    sums[0:1, :] = row_sums(d_branch[...].astype(jnp.float32))
+    sums[1:2, :] = row_sums(grad * unit)
+    sums[2:3, :] = row_sums(grad)
+
+
+def inner_backward(place, *refs):
+    pieces, refs = refs[:SPLIT], refs[SPLIT:]
+    slope, weights, d_branch, d_inner, sums, *refs = refs
+    parts, (moving,) = refs[:SPLIT], refs[SPLIT:]
+    column = place[0]
+    put_pieces(pieces, column, d_branch)
+    hidden = slope.shape[1]
+    d_activ = dot(d_branch[...], weights[:, hidden : 2 * hidden], ((1,), (0,)))
+    d_inner[...] = (d_activ * slope[...]).astype(jnp.bfloat16)
+    sums[...] = row_sums(d_inner[...].astype(jnp.float32))
+    moving[...] = dot(d_inner[...], weights[:, :hidden], ((1,), (1,)))
+    take_parts(moving, column, parts)
+
+
+def inner_gradients(first_b, activ_b, d_inner, d_branch, grads):
+    grads[0] = dot(first_b[...], d_inner[...], ((0,), (0,))).astype(jnp.bfloat16)
+    grads[1] = dot(d_branch[...], activ_b[...], ((0,), (0,))).astype(jnp.bfloat16)
+
+
+def wide_momenta(place, summed, moments, grads, moments_new, mine, far):
+    low = place[0] < SPLIT // 2
+    for part in range(2):
+        grads[part] = summed[part].astype(jnp.float32)
+        moments_new[part] = momentum_decay * moments[part] + grads[part]
+    first, second = moments_new[0].astype(jnp.bfloat16), moments_new[1].astype(jnp.bfloat16)
+    mine[...] = jnp.where(low, first, second)
+    far[...] = jnp.where(low, second, first)
+
+
+def wide_gram(rows, wide, gram):
+    gram[...] = dot(rows[...], wide[...], ((1,), (1,))).astype(jnp.bfloat16)
+
+
+def first_norm(*refs):
+    pieces, refs = refs[:SPLIT], refs[SPLIT:]
+    d_second, first_in, vec, d_first_in, d_attended, sums = refs
+    unit, scale = norm_parts(first_in[...])
+    grad = sum_pieces(pieces) + d_second[...]
+    d_rows = norm_back(grad, unit, scale, vec[3:4, :])
+    d_first_in[...] = d_rows
+    d_attended[...] = d_rows.astype(jnp.bfloat16)
+    sums[0:1, :] = row_sums(d_attended[...].astype(jnp.float32))
+    sums[1:2, :] = row_sums(grad * unit)
+    sums[2:3, :] = row_sums(grad)
+
+
+def split_state(place, kept, other, *refs):
+    blocks, (mine, far) = refs[:SPLIT], refs[SPLIT:]
+    column, even = place[0], place[1] == 0
+    own, hidden = blocks[0].shape[1], mine.shape[1]
+    for step, block in enumerate(blocks):
+        there = lax.rem(column + step, SPLIT)
+        for at in range(SPLIT):
+            lanes = slice(at * own, (at + 1) * own)
+
+            @pl.when(there == at)
+            def _():
+                block[...] = jnp.where(even, kept[:, lanes], other[:, lanes])
+
+    mine[...] = jnp.where(even, other[:, :hidden], kept[:, :hidden])
+    far[...] = jnp.where(even, other[:, hidden:], kept[:, hidden:])
+
+
+def new_weights(place, *refs):
+    pieces, refs = refs[:SPLIT], refs[SPLIT:]
+    mine, far, qkv_w, out_w, ffn_w, qkv_new, out_new, ffn_new, state = refs
+    low = place[0] < SPLIT // 2
+    for step, piece in enumerate(pieces):
+        state[source_of(place[0], step)] = piece[...].astype(jnp.float32)
+    for at in range(SPLIT - 1):
+        qkv_new[at] = qkv_w[at] - muon_rate * state[at]
+    out_new[...] = out_w[...] - muon_rate * state[SPLIT - 1]
+    rate = muon_rate * (FF / D) ** 0.5
+    ffn_new[0] = ffn_w[0] - rate * jnp.where(low, mine[...], far[...]).astype(jnp.float32)
+    ffn_new[1] = ffn_w[1] - rate * jnp.where(low, far[...], mine[...]).astype(jnp.float32)
+
+
+def probabilities(qkv, rows_at, head, own, id_column, id_row):
+    queries = qkv[rows_at, head * HEAD : (head + 1) * HEAD]
+    keys = qkv[rows_at, own + head * HEAD : own + (head + 1) * HEAD]
+    values = qkv[rows_at, 2 * own + head * HEAD : 2 * own + (head + 1) * HEAD]
+    scores = dot(queries, keys, ((1,), (1,))) * HEAD ** (-0.5)
+    scores = jnp.where(id_column[rows_at, :] == id_row[:, rows_at], scores, masked_score)
+    exponent = jnp.exp(scores - jnp.max(scores, axis=-1, keepdims=True))
+    probs = exponent / jnp.sum(exponent, axis=-1, keepdims=True)
+    return queries, keys, values, probs
+
+
+def attention_forward(tokens, weight, bias, id_column, id_row, qkv, mixed):
+    own = mixed.shape[1]
+    proj = weight[:, weight.shape[1] - 3 * own :]
+    qkv[...] = (dot(tokens[...], proj, ((1,), (0,))) + bias[...]).astype(jnp.bfloat16)
+    for start in range(0, tokens.shape[0], BLOCK):
+        rows_at = slice(start, start + BLOCK)
+        for head in range(own // HEAD):
+            queries, keys, values, probs = probabilities(qkv, rows_at, head, own, id_column, id_row)
+            part = dot(probs.astype(jnp.bfloat16), values, ((1,), (0,)))
+            mixed[rows_at, head * HEAD : (head + 1) * HEAD] = part.astype(jnp.bfloat16)
+
+
+def attention_backward(
+    place, *refs
+):
+    pieces, mixed, refs = refs[:SPLIT], refs[SPLIT : 2 * SPLIT], refs[2 * SPLIT :]
+    out_weight, qkv, id_column, id_row, tokens, sums_one, sums_two, sums_up, *refs = refs
+    kept, sent, d_proj, d_attended, sums = refs
+    rows, width = tokens.shape
+    own = qkv.shape[1] // 3
+    column, core = place[0], place[1]
+    put_pieces(pieces, column, d_attended)
+    out_rows = out_weight[pl.ds(pl.multiple_of(column * own, own), own), :]
+    d_mixed = dot(d_attended[...], out_rows, ((1,), (1,))).astype(jnp.bfloat16)
+    for start in range(0, rows, BLOCK):
+        rows_at = slice(start, start + BLOCK)
+        for head in range(own // HEAD):
+            queries, keys, values, probs = probabilities(qkv, rows_at, head, own, id_column, id_row)
+            d_out = d_mixed[rows_at, head * HEAD : (head + 1) * HEAD]
+            d_probs = dot(d_out, values, ((1,), (1,)))
+            d_scores = probs * (d_probs - jnp.sum(probs * d_probs, axis=-1, keepdims=True))
+            d_scores = d_scores.astype(jnp.bfloat16)
+            d_values = dot(probs.astype(jnp.bfloat16), d_out, ((0,), (0,)))
+            d_queries = dot(d_scores, keys, ((1,), (0,))) * HEAD ** (-0.5)
+            d_keys = dot(d_scores, queries, ((0,), (0,))) * HEAD ** (-0.5)
+            for part, value in enumerate((d_queries, d_keys, d_values)):
+                at = part * own + head * HEAD
+                d_proj[rows_at, at : at + HEAD] = value.astype(jnp.bfloat16)
+    d_proj_all = d_proj[...]
+    d_columns = d_attended[:, :own]
+    for place_at in range(1, width // own):
+        other = d_attended[:, place_at * own : (place_at + 1) * own]
+        d_columns = jnp.where(column == place_at, other, d_columns)
+    grad_proj = dot(tokens[...], d_proj_all, ((0,), (0,)))
+    proj_sums = row_sums(d_proj_all.astype(jnp.float32))
+    sums[...] = jnp.zeros_like(sums)
+    for at in range(SPLIT):
+        lanes = slice(at * own, (at + 1) * own)
+        mine = (column == at).astype(jnp.float32)
+        sums[0:1, lanes] = proj_sums[:, :own] * mine
+        sums[1:2, lanes] = proj_sums[:, 2 * own :] * mine
+        sums[8 + at : 9 + at, :] = sums_up[...] * mine
+    sums[2:5, :] = sums_one[0:3, :]
+    sums[5:8, :] = sums_two[0:3, :]
+    depth = kept.shape[1] - sums.shape[0]
+    for group in range(width // depth):
+        at = slice(group * depth, (group + 1) * depth)
+
+        def put(target, kind):
+            target[group // 2, :depth, : 3 * own] = grad_proj[at].astype(kind)
+            target[group // 2, depth:, :] = jnp.zeros((sums.shape[0], width), kind)
+            target[group // 2, depth:, :depth] = sums[:, at].astype(kind)
+
+        pl.when(core == group % 2)(lambda: put(kept, jnp.float32))
+        pl.when(core != group % 2)(lambda: put(sent, jnp.bfloat16))
+    for step, piece in enumerate(mixed):
+        grad_out = dot(piece[...], d_columns, ((0,), (0,)))
+        source = source_of(column, step)
+        for half in range(2):
+            block = grad_out[half * depth : (half + 1) * depth]
+
+            def put_out(target, kind):
+                target[source, :depth, 3 * own :] = block.astype(kind)
+
+            pl.when(core == half)(lambda: put_out(kept, jnp.float32))
+            pl.when(core != half)(lambda: put_out(sent, jnp.bfloat16))
+
+
+def token_parts(place, d_proj, weight, *refs):
+    parts, (moving,) = refs[:SPLIT], refs[SPLIT:]
+    proj = weight[:, weight.shape[1] - d_proj.shape[1] :]
+    moving[...] = dot(d_proj[...], proj, ((1,), (1,)))
+    take_parts(moving, place[0], parts)
+
+
+def pair_sum(place, kept, other, total, *blocks):
+    chip = place[2]
+    total[...] = kept[chip] + other[chip].astype(jnp.float32)
+    for step, block in enumerate(blocks):
+        at = chip ^ (step + 1)
+        block[...] = (kept[at] + other[at].astype(jnp.float32)).astype(jnp.bfloat16)
+
+
+def square_momenta(place, total, *refs):
+    pieces, refs = refs[: SPLIT - 1], refs[SPLIT - 1 :]
+    qkv_mom, out_mom, qkv_grad, out_grad, qkv_new, out_new, *refs = refs
+    blocks, state = refs[:SPLIT], refs[SPLIT]
+    depth, own = out_mom.shape
+    whole = sum_pieces([total, *pieces])
+    vec_own = depth // SPLIT
+    for at in range(SPLIT):
+        grad = whole[:depth, at * own : (at + 1) * own]
+        if at < SPLIT - 1:
+            qkv_grad[at] = grad
+            moment = momentum_decay * qkv_mom[at] + grad
+            qkv_new[at] = moment
+        else:
+            out_grad[...] = grad
+            moment = momentum_decay * out_mom[...] + grad
+            out_new[...] = moment
+        state[at, :depth, :] = moment
+        state[at, depth:, :] = jnp.zeros((whole.shape[0] - depth, own), jnp.float32)
+        state[at, depth:, :vec_own] = whole[depth:, at * vec_own : (at + 1) * vec_own]
+    for step, block in enumerate(blocks):
+        block[...] = state[lax.rem(place[0] + step, SPLIT)].astype(jnp.bfloat16)
+
+
+def join_squares(place, *refs):
+    pieces, (gram, gram_other, mine, other, sums, rows) = refs[:SPLIT], refs[SPLIT:]
+    depth, own = mine.shape[0], pieces[0].shape[1]
+    total = jnp.zeros(sums.shape, jnp.float32)
+    for step, piece in enumerate(pieces):
+        total = total + piece[depth:, :].astype(jnp.float32)
+        for at in range(SPLIT):
+
+            @pl.when(source_of(place[0], step) == at)
+            def _():
+                rows[:, at * own : (at + 1) * own] = piece[:depth, :]
+
+    sums[...] = total
+    even = place[1] == 0
+    gram_sum = (gram[...].astype(jnp.float32) + gram_other[...].astype(jnp.float32)).astype(jnp.bfloat16)
+    mine[...] = jnp.where(even, rows[...], gram_sum)
+    other[...] = jnp.where(even, gram_sum, rows[...])
+
+
+def run_kernel(body, outputs, scalars=0, scratch=(), ties=()):
+    def call(*operands):
+        count = len(operands)
+
+        def whole(*refs):
+            body(*refs[:count], *refs[count + len(ties) :])
+
+        spaces = [pltpu.SMEM] * scalars + [pltpu.VMEM] * (count - scalars) + [pl.ANY] * len(ties)
+        return pl.pallas_call(
+            whole,
+            out_shape=outputs,
+            in_specs=[pl.BlockSpec(memory_space=space) for space in spaces],
+            out_specs=[pl.BlockSpec(memory_space=pltpu.VMEM)] * len(outputs),
+            scratch_shapes=scratch,
+            compiler_params=pltpu.CompilerParams(vmem_limit_bytes=16 * 2**20),
+        )(*operands, *ties)
+
+    return call
+
+
+def newton_schulz(place, *refs):
+    pieces, refs = refs[:SPLIT], refs[SPLIT:]
+    wide, kept, sent, heard, gram, *factors = refs
+    chip, core = place[2], place[1]
+    width = heard.shape[0]
+    for step, piece in enumerate(pieces):
+        at = pl.multiple_of((chip ^ step) * piece.shape[0], piece.shape[0])
+        heard[pl.ds(at, piece.shape[0]), :] = piece[...]
+    depth = kept.shape[0]
+    even = core == 0
+
+    @pl.when(even)
+    def _():
+        gram[...] = dot(heard[...], heard[...], ((1,), (1,)))
+
+    @pl.when(jnp.logical_not(even))
+    def _():
+        gram[...] = heard[...].astype(jnp.float32)
+
+    at_row = lax.broadcasted_iota(jnp.int32, (width, width), 0)
+    at_lane = lax.broadcasted_iota(jnp.int32, (width, width), 1)
+    trace = jnp.sum(jnp.where(at_row == at_lane, gram[...], 0.0), keepdims=True)
+    scale = jnp.sqrt(trace) + ortho_eps
+    gram[...] = gram[...] / (scale * scale)
+    for step, factor in enumerate(factors):
+        gram_b = gram[...].astype(jnp.bfloat16)
+        square = dot(gram_b, gram_b, ((1,), (0,)))
+        factor[...] = (coef_second * gram[...] + coef_third * square).astype(jnp.bfloat16)
+        if step < NS_STEPS - 1:
+            moved = dot(factor[...], gram_b, ((1,), (0,)))
+            twice = dot(factor[...], moved.astype(jnp.bfloat16), ((1,), (0,)))
+            gram[...] = coef_first * coef_first * gram[...] + 2.0 * coef_first * moved + twice
+    count = 2 * depth
+    start = pl.multiple_of(chip * count, count)
+    eye = lax.broadcasted_iota(jnp.int32, (count, width), 0) + start
+    eye = (eye == lax.broadcasted_iota(jnp.int32, (count, width), 1)).astype(jnp.float32)
+    rows = coef_first * eye + factors[-1][pl.ds(start, count), :].astype(jnp.float32)
+    for factor in factors[-2::-1]:
+        rows = coef_first * rows + dot(rows.astype(jnp.bfloat16), factor[...], ((1,), (0,)))
+    rows = (rows / scale).astype(jnp.bfloat16)
+
+    @pl.when(even)
+    def _():
+        state = dot(rows, heard[...], ((1,), (0,))).astype(jnp.bfloat16)
+        kept[:, :width] = state[:depth]
+        sent[:, :width] = state[depth:]
+        kept[:, width:] = jnp.zeros_like(kept[:, width:])
+        sent[:, width:] = jnp.zeros_like(sent[:, width:])
+
+    @pl.when(jnp.logical_not(even))
+    def _():
+        state = dot(rows, wide[...], ((1,), (0,))).astype(jnp.bfloat16)
+        kept[...] = state[depth:]
+        sent[...] = state[:depth]
+
+
+def split_device(
+    tokens, cotangent, doc_lengths, qkv_w, out_w, ffn_w, vecs, qkv_mom, out_mom, ffn_mom, vec_mom
+):
+    micro, rows, width = tokens.shape
+    shards = lax.axis_size("shard")
+    groups = lax.axis_size("dp")
+    column = lax.axis_index("shard")
+    row = lax.axis_index("dp")
+    slots = micro * shards
+    own = qkv_w.shape[2]
+    hidden = ffn_w.shape[2]
+    bf16 = jnp.bfloat16
+
+    packed = jnp.concatenate(
+        [ffn_w[0], ffn_w[1], qkv_w[0], qkv_w[1], qkv_w[2]], axis=1
+    ).astype(bf16)
+    weights = lax.all_gather(packed, "dp", axis=0, tiled=True)
+
+    flat = tokens.reshape(micro * rows, width)
+    vec_rows, vec_own = vecs.shape
+    small = jnp.concatenate(
+        [vecs.astype(bf16).reshape(-1), doc_lengths.astype(bf16).reshape(-1)]
+    )
+    small = jnp.pad(small, (0, 8 * width - small.shape[0])).reshape(8, width)
+    out_flat = out_w.astype(bf16).reshape(-1, width)
+    out_count = out_flat.shape[0]
+    heard = gather_direct(jnp.concatenate([flat, out_flat, small], axis=0), "shard")
+    tokens_b = heard[:, : micro * rows].reshape(slots * rows, width)
+    out_part = heard[:, micro * rows : micro * rows + out_count].reshape(shards, -1, own)
+    out_part = out_part.transpose(1, 0, 2).reshape(-1, width)
+    small = heard[:, micro * rows + out_count :].reshape(shards, -1)
+    lengths = small[:, vecs.size : vecs.size + doc_lengths.size].astype(jnp.int32).reshape(slots, -1)
+    small = small[:, : vecs.size].reshape(shards, vec_rows, vec_own).transpose(1, 0, 2).reshape(vec_rows, -1)
+    vec = gather_double(small, "dp").transpose(1, 0, 2).reshape(vec_rows, -1).astype(jnp.float32)
+    out_b = lax.all_gather(out_part, "dp", axis=0, tiled=True)
+    position = jnp.arange(rows, dtype=jnp.int32)[None]
+    ends = jnp.cumsum(lengths, axis=1)
+    segment = jnp.sum((position[:, :, None] >= ends[:, None, :]).astype(jnp.int32), axis=2)
+    valid = position < ends[:, -1:]
+    slot = jnp.arange(slots, dtype=jnp.int32)[:, None]
+    marks = jnp.where(valid, segment, ends.shape[1] + position) + slot * (ends.shape[1] + rows)
+    id_column, id_row = marks.reshape(-1, 1), marks.reshape(1, -1)
+    valid_own = lax.dynamic_slice_in_dim(valid, column * micro, micro, 0)
+    valid_own = valid_own.reshape(-1, 1).astype(jnp.float32)
+    bias_q = lax.dynamic_slice_in_dim(vec[0], column * own, own, 0)
+    bias_v = lax.dynamic_slice_in_dim(vec[1], column * own, own, 0)
+    bias_proj = jnp.concatenate([bias_q, jnp.zeros_like(bias_q), bias_v])[None]
+    bias_up = lax.dynamic_slice_in_dim(vec[8:].reshape(-1), column * hidden, hidden, 0)
+
+    qkv, mixed_own = run_kernel(
+        attention_forward,
+        [
+            jax.ShapeDtypeStruct((slots * rows, 3 * own), bf16),
+            jax.ShapeDtypeStruct((slots * rows, own), bf16),
+        ],
+    )(tokens_b, weights, bias_proj, id_column, id_row)
+
+    depth = width // groups
+    count = micro * rows
+    whole_b = jax.ShapeDtypeStruct((slots * rows, width), bf16)
+    own_f = jax.ShapeDtypeStruct((count, width), jnp.float32)
+    own_b = jax.ShapeDtypeStruct((count, width), bf16)
+    part_kinds = [own_f] + [own_b] * (shards - 1)
+    sums_kind = jax.ShapeDtypeStruct((8, width), jnp.float32)
+    moving = pltpu.VMEM((slots * rows, width), jnp.float32)
+    place = jnp.stack([column, lax.rem(row, 2), row // 2]).astype(jnp.int32)
+
+    mixed_pieces = pieces_of(mixed_own, "shard")
+    first_b, activ_b, slope, first_in, *parts = run_kernel(
+        layer_middle,
+        [whole_b, whole_b, jax.ShapeDtypeStruct((slots * rows, hidden), jnp.float32), own_f] + part_kinds,
+        scalars=1,
+        scratch=[moving],
+    )(place, *mixed_pieces, out_b, tokens_b, vec, weights, bias_up[None])
+    layer_out, d_branch_own, d_second, sums_two = run_kernel(
+        second_norm, [own_b, own_b, own_f, sums_kind]
+    )(*send_parts(parts, "shard"), first_in, vec, cotangent.reshape(count, width), valid_own)
+    layer_out = layer_out.reshape(tokens.shape)
+    d_branch_b, d_inner_b, d_bias_up, *parts = run_kernel(
+        inner_backward,
+        [whole_b, whole_b, jax.ShapeDtypeStruct((1, hidden), jnp.float32)] + part_kinds,
+        scalars=1,
+        scratch=[moving],
+    )(place, *pieces_of(d_branch_own, "shard"), slope, weights)
+    (grads,) = run_kernel(inner_gradients, [jax.ShapeDtypeStruct((2, width, hidden), bf16)], ties=parts)(
+        first_b, activ_b, d_inner_b, d_branch_b
+    )
+    summed = lax.psum_scatter(grads, "dp", scatter_dimension=1, tiled=True)
+    d_first_in, d_attended_own, sums_one = run_kernel(
+        first_norm, [own_f, own_b, sums_kind]
+    )(*send_parts(parts, "shard"), d_second, first_in, vec)
+    d_attended_pieces = pieces_of(d_attended_own, "shard")
+    moment_kind = jax.ShapeDtypeStruct(ffn_mom.shape, ffn_mom.dtype)
+    wide_kind = jax.ShapeDtypeStruct((depth, hidden), bf16)
+    grad_ffn, new_ffn_mom, mine, far = run_kernel(
+        wide_momenta,
+        [moment_kind, moment_kind, wide_kind, wide_kind],
+        scalars=1,
+        ties=d_attended_pieces,
+    )(place, summed, ffn_mom)
+    even = lax.rem(row, 2) == 0
+    far_rows = swap(far, "shard", shards // 2)
+    wide_rows = jnp.concatenate([mine, far_rows], axis=1)
+    wide = lax.all_gather(wide_rows, "dp", axis=0, tiled=True)
+
+    packed_rows = depth + 16
+    kept, sent, d_proj = run_kernel(
+        attention_backward,
+        [
+            jax.ShapeDtypeStruct((groups // 2, packed_rows, width), jnp.float32),
+            jax.ShapeDtypeStruct((groups // 2, packed_rows, width), bf16),
+            jax.ShapeDtypeStruct((slots * rows, 3 * own), bf16),
+        ],
+        scalars=1,
+        scratch=[pltpu.VMEM((slots * rows, width), bf16), pltpu.VMEM((16, width), jnp.float32)],
+        ties=[far_rows],
+    )(
+        place, *d_attended_pieces, *mixed_pieces, out_b, qkv, id_column, id_row, tokens_b,
+        sums_one, sums_two, d_bias_up,
+    )
+    block_kind = jax.ShapeDtypeStruct((packed_rows, width), bf16)
+    total, *blocks = run_kernel(
+        pair_sum, [jax.ShapeDtypeStruct((packed_rows, width), jnp.float32)] + [block_kind] * 3, scalars=1
+    )(place, kept, swap(sent, "dp", 1))
+    parts = run_kernel(token_parts, part_kinds, scalars=1, scratch=[moving], ties=[total])(
+        place, d_proj, weights
+    )
+    d_tokens = d_first_in + sum(part.astype(jnp.float32) for part in send_parts(parts, "shard"))
+    block_kind = jax.ShapeDtypeStruct((packed_rows, own), bf16)
+    like = [jax.ShapeDtypeStruct(each.shape, each.dtype) for each in (qkv_mom, out_mom)]
+    grad_qkv, grad_wout, new_qkv_mom, new_out_mom, *blocks = run_kernel(
+        square_momenta,
+        like + like + [block_kind] * shards,
+        scalars=1,
+        scratch=[pltpu.VMEM((shards, packed_rows, own), jnp.float32)],
+    )(place, total, *[swap(block, "dp", 2 * at + 2) for at, block in enumerate(blocks)], qkv_mom, out_mom)
+    (gram_rows,) = run_kernel(wide_gram, [jax.ShapeDtypeStruct((depth, width), bf16)], ties=blocks)(
+        wide_rows, wide
+    )
+    row_kind = jax.ShapeDtypeStruct((depth, width), bf16)
+    mine, other, grad_vec = run_kernel(
+        join_squares,
+        [row_kind, row_kind, jax.ShapeDtypeStruct((packed_rows - depth, own), jnp.float32)],
+        scalars=1,
+        scratch=[pltpu.VMEM((depth, width), bf16)],
+        ties=[d_tokens],
+    )(place, *send_parts(blocks, "shard"), gram_rows, swap(gram_rows, "shard", 1))
+    grad_vec = grad_vec[:vec_rows, :vec_own]
+    d_tokens = d_tokens.reshape(tokens.shape)
+    other = swap(other, "dp", 1)
+    pair_rows = jnp.concatenate([jnp.where(even, mine, other), jnp.where(even, other, mine)], axis=0)
+    pair_pieces = [pair_rows] + [swap(pair_rows, "dp", bit) for bit in (2, 4, 6)]
+    state_kind = jax.ShapeDtypeStruct((depth, 2 * hidden), bf16)
+    kept, sent = run_kernel(
+        newton_schulz,
+        [state_kind, state_kind],
+        scalars=1,
+        scratch=[pltpu.VMEM((width, width), bf16), pltpu.VMEM((width, width), jnp.float32)]
+        + [pltpu.VMEM((width, width), bf16)] * NS_STEPS,
+    )(place, *pair_pieces, wide)
+    block_kind = jax.ShapeDtypeStruct((depth, own), bf16)
+    wide_kind = jax.ShapeDtypeStruct((depth, hidden), bf16)
+    *blocks, mine, far = run_kernel(
+        split_state, [block_kind] * shards + [wide_kind, wide_kind], scalars=1
+    )(place, kept, swap(sent, "dp", 1))
+    qkv_new, out_new, ffn_new = run_kernel(
+        new_weights,
+        [jax.ShapeDtypeStruct(each.shape, each.dtype) for each in (qkv_w, out_w, ffn_w)],
+        scalars=1,
+        scratch=[pltpu.VMEM((shards, depth, own), jnp.float32)],
+    )(
+        place, *send_parts(blocks, "shard"), mine, swap(far, "shard", shards // 2), qkv_w, out_w, ffn_w
+    )
+
+    token_count = micro * rows * groups * shards
+    new_vec_mom = momentum_decay * vec_mom + grad_vec
+    vec_new = vecs - vec_rate * token_count ** (-0.5) * new_vec_mom
+    return (
+        layer_out,
+        d_tokens,
+        grad_qkv,
+        grad_wout,
+        grad_ffn,
+        grad_vec,
+        new_qkv_mom,
+        new_out_mom,
+        new_ffn_mom,
+        new_vec_mom,
+        qkv_new,
+        out_new,
+        ffn_new,
+        vec_new,
+    )
+
+
 def solution(mesh):
+    fits = (mesh.shape["dp"], mesh.shape["shard"]) == (8, 4)
     in_specs = (
         P(("dp", "shard"), None, None),
         P(("dp", "shard"), None, None),
@@ -405,5 +1039,5 @@
         P(None, ("dp", "shard")),
     )
     return jax.shard_map(
-        per_device, mesh=mesh, in_specs=in_specs, out_specs=out_specs, check_vma=False
-    )
+        split_device if fits else per_device, mesh=mesh, in_specs=in_specs, out_specs=out_specs, check_vma=False
+    )

time: 1030 us -> 321 us (0.31)
  waiting for transfers between devices: 641 us -> 135 us
  matrix products: 104 us -> 0 us
  blocking collectives: 76.4 us -> 0 us
  local copies, waits for them, and re-layouts: 123 us -> 52.8 us
  starting transfers between devices: 1.3 us -> 65.7 us
  other arithmetic: 57.5 us -> 4.84 us
  Pallas kernels: 0 us -> 46.4 us
    reduce_scatter x10 -> x1, waiting for transfers between devices: 302 us -> 0.01 us  [split_device(): summed = lax.psum_scatter(grads, 'dp', scatter_dimension=1, tiled=True)]
    all_gather x12 -> x3, waiting for transfers between devices: 223 us -> 14 us  [the longest x1 11.9 us: split_device(): out_b = lax.all_gather(out_part, 'dp', axis=0, tiled=True)]
    ppermute x0 -> x42, waiting for transfers between devices: none -> 121 us  [the longest x15 41.9 us: swap(): lax.ppermute(block, axis, [(i, i ^ bit) for i in range(lax.axis_size(axis...]
    dot_general x50 -> x0, matrix products: 104 us -> none  [the longest x6 14.3 us: orthogonalize_pair(): once = jnp.dot(gram_b, current, preferred_element_type=jnp.float32)]
    ppermute x0 -> x42, starting transfers between devices: none -> 65.6 us  [the longest x15 24.4 us: send_parts(): lax.ppermute(parts[step], axis, [(i, (i + step) % count) for i in range(c...]
    all_gather x4 -> x0, blocking collectives: 64.7 us -> none  [the longest x1 27.2 us: gather_weights(): lax.all_gather(pieces[0], 'shard', axis=2, tiled=True)]
    psum x1 -> x0, waiting for transfers between devices: 60 us -> none  [spread_2(): return lax.psum(block, axis)]
    unnamed x29 -> x4, waiting for transfers between devices: 55.6 us -> 0.07 us
  transfers between devices with their start and end apart: 26 -> 46, of which waited for: 22 -> 28; matrix products, arithmetic and copies ran while one was open for 22% -> 3% of each run, Pallas kernels for 0% -> 6%
where the time goes in v1:
time: 321 us; the launch traced here: 319 us
  waiting for transfers between devices  135 us (42%)
  starting transfers between devices  65.7 us (20%)
  local copies, waits for them, and re-layouts  52.8 us (16%)
  Pallas kernels  46.4 us (14%)
  between operations  14.5 us (5%)
  other arithmetic  4.84 us (2%)
    unnamed x147, local copies, waits for them, and re-layouts  46.5 us
    pallas_call x16, Pallas kernels, call(): pl.pallas_call(whole, out_shape=outputs, in_specs=[pl.BlockSpec(memory_sp...  46.4 us
    ppermute x15, waiting for transfers between devices, swap(): lax.ppermute(block, axis, [(i, i ^ bit) for i in range(lax.axis_size(axis...  41.9 us
    ppermute x9, waiting for transfers between devices, pieces_of(): lax.ppermute(block, axis, [(i, (i + step) % count) for i in range(count)])  38 us
    ppermute x15, waiting for transfers between devices, send_parts(): lax.ppermute(parts[step], axis, [(i, (i + step) % count) for i in range(c...  27.1 us
    ppermute x15, starting transfers between devices, send_parts(): lax.ppermute(parts[step], axis, [(i, (i + step) % count) for i in range(c...  24.4 us
    ppermute x9, starting transfers between devices, pieces_of(): lax.ppermute(block, axis, [(i, (i + step) % count) for i in range(count)])  20 us
    ppermute x3, waiting for transfers between devices, gather_direct(): lax.ppermute(block, axis, [(i, (i + step) % count) for i in range(count)])  14.1 us
  transfers between devices with their start and end apart: 46, of which 28 were waited for; matrix products, arithmetic and copies ran while one was open for 3% of the time, Pallas kernels for 6%

profile of v1, /device:TPU:0, one launch (start us, length us, event | category | flops | bytes accessed | tf_op | source)
XLA Modules:
  0.0 319.3 jit_solution(7352042479461100022)
XLA Ops:
  10.9 4.1 %collective-permute-start.1 = (bf16[160,768]{1,0:T(8,128)(2,1)S(1)}, bf16[160,768]{1,0:T(8,128)(2,1)S(1)}, u32[]{:S(2)}, u32[]{:S(2)}) collective-permute-start(bf16[160,768]{1,0:T(8,128)(2,1)S(1)} %pad_maximum_fusion.1), channel_id=1, source_target_pairs={{0,2},{1,3},{2,0},{3,1},{4,6},{5,7},{6,4},{7,5},{8,10},{9,11},{10,... | collective-permute-start | bytes 737288 | tf_op jit(solution)/shard_map/ppermute | solution.py:386
  16.6 2.2 collective-permute-start.2
  19.0 9.6 %collective-permute-done = bf16[160,768]{1,0:T(8,128)(2,1)S(1)} collective-permute-done((bf16[160,768]{1,0:T(8,128)(2,1)S(1)}, bf16[160,768]{1,0:T(8,128)(2,1)S(1)}, u32[]{:S(2)}, u32[]{:S(2)}) %collective-permute-start) | collective-permute-done | bytes 245792 | tf_op jit(solution)/shard_map/ppermute | solution.py:386
  28.6 3.8 %collective-permute-done.1 = bf16[160,768]{1,0:T(8,128)(2,1)S(1)} collective-permute-done((bf16[160,768]{1,0:T(8,128)(2,1)S(1)}, bf16[160,768]{1,0:T(8,128)(2,1)S(1)}, u32[]{:S(2)}, u32[]{:S(2)}) %collective-permute-start.1) | collective-permute-done | bytes 245792 | tf_op jit(solution)/shard_map/ppermute | solution.py:386
  38.1 2.1 collective-permute-done.4
  44.7 2.1 all-gather.4.cloned.1.call-done.refs_1_.refs_8_.refs_6_.refs_2_
  46.7 1.9 copy-done
  50.8 3.4 %shard_map.218 = (bf16[512,576]{1,0:T(8,128)(2,1)S(1)}, bf16[512,192]{1,0:T(8,128)(2,1)}) custom-call(bf16[512,768]{1,0:T(8,128)(2,1)S(1)} %bitcast.37, bf16[768,2112]{1,0:T(8,128)(2,1)S(1)} %copy-done, f32[1,576]{1,0:T(1,128)S(1)} %broadcast_in_dim.42.refs_2_, s32[512,1]{1,0:T(8,128)S(1)} %copy-done.11, s32[1,512]{1,0:T(1,128)S(1)} %add.113.refs_4_.refs_12_), custom_call_target="tpu_custom_call" | custom-call | tf_op jit(solution)/shard_map/pallas_call | solution.py:747
  55.0 3.3 %collective-permute-start.8 = (bf16[512,192]{1,0:T(8,128)(2,1)}, bf16[512,192]{1,0:T(8,128)(2,1)}, u32[]{:S(2)}, u32[]{:S(2)}) collective-permute-start(bf16[512,192]{1,0:T(8,128)(2,1)} %get-tuple-element.75.refs_1_.refs_5_), channel_id=1, source_target_pairs={{0,3},{1,0},{2,1},{3,2},{4,7},{5,4},{6,5},{7,6},{8,11},{9,8},{10,9... | collective-permute-start | bytes 589832 | tf_op jit(solution)/shard_map/ppermute | solution.py:394
  59.0 2.0 collective-permute-start.6
  61.4 11.9 %all-gather.6.cloned.1.call-done.refs_5_.refs_9_ = bf16[768,768]{1,0:T(8,128)(2,1)} async-done(((bf16[96,768]{1,0:T(8,128)(2,1)}), bf16[768,768]{1,0:T(8,128)(2,1)}) %all-gather.6.cloned.1.call-update) | async-done | bytes 1179664 | tf_op jit(solution)/shard_map/all_gather | solution.py:849
  73.3 8.3 %collective-permute-done.7.refs_3_.refs_7_ = bf16[512,192]{1,0:T(8,128)(2,1)} collective-permute-done((bf16[512,192]{1,0:T(8,128)(2,1)}, bf16[512,192]{1,0:T(8,128)(2,1)}, u32[]{:S(2)}, u32[]{:S(2)}) %collective-permute-start.7) | collective-permute-done | bytes 196640 | tf_op jit(solution)/shard_map/ppermute | solution.py:394
  84.0 5.9 %shard_map.219 = (bf16[512,768]{1,0:T(8,128)(2,1)S(1)}, bf16[512,768]{1,0:T(8,128)(2,1)S(1)}, f32[512,768]{1,0:T(8,128)S(1)}, f32[128,768]{1,0:T(8,128)S(1)}, f3...) custom-call(s32[3]{0:T(128)S(1)} %pad_add_fusion.refs_0_, ...), custom_call_target="tpu_custom_call" | custom-call | tf_op jit(solution)/shard_map/pallas_call | solution.py:747
  95.3 1.9 collective-permute-start.10
  97.2 2.9 collective-permute-start.11
  100.4 3.6 %collective-permute-done.9.refs_1_ = bf16[128,768]{1,0:T(8,128)(2,1)} collective-permute-done((bf16[128,768]{1,0:T(8,128)(2,1)}, bf16[128,768]{1,0:T(8,128)(2,1)}, u32[]{:S(2)}, u32[]{:S(2)}) %collective-permute-start.9) | collective-permute-done | bytes 196640 | tf_op jit(solution)/shard_map/ppermute | solution.py:402
  103.9 6.7 %collective-permute-done.10.refs_2_ = bf16[128,768]{1,0:T(8,128)(2,1)} collective-permute-done((bf16[128,768]{1,0:T(8,128)(2,1)}, bf16[128,768]{1,0:T(8,128)(2,1)}, u32[]{:S(2)}, u32[]{:S(2)}) %collective-permute-start.10) | collective-permute-done | bytes 196640 | tf_op jit(solution)/shard_map/ppermute | solution.py:402
  113.6 2.6 shard_map.220
  116.1 6.8 %collective-permute-start.14 = (bf16[128,768]{1,0:T(8,128)(2,1)S(1)}, bf16[128,768]{1,0:T(8,128)(2,1)S(1)}, u32[]{:S(2)}, u32[]{:S(2)}) collective-permute-start(bf16[128,768]{1,0:T(8,128)(2,1)S(1)} %get-tuple-element.82.refs_1_), channel_id=1, source_target_pairs={{0,3},{1,0},{2,1},{3,2},{4,7},{5,4},{6,5},{7,6},{8,11},{9,8},{10,9... | collective-permute-start | bytes 589832 | tf_op jit(solution)/shard_map/ppermute | solution.py:394
  123.6 4.8 %collective-permute-done.14.refs_4_ = bf16[128,768]{1,0:T(8,128)(2,1)S(1)} collective-permute-done((bf16[128,768]{1,0:T(8,128)(2,1)S(1)}, bf16[128,768]{1,0:T(8,128)(2,1)S(1)}, u32[]{:S(2)}, u32[]{:S(2)}) %collective-permute-start.14) | collective-permute-done | bytes 196640 | tf_op jit(solution)/shard_map/ppermute | solution.py:394
  128.4 10.0 %collective-permute-done.13.refs_3_ = bf16[128,768]{1,0:T(8,128)(2,1)S(1)} collective-permute-done((bf16[128,768]{1,0:T(8,128)(2,1)S(1)}, bf16[128,768]{1,0:T(8,128)(2,1)S(1)}, u32[]{:S(2)}, u32[]{:S(2)}) %collective-permute-start.13) | collective-permute-done | bytes 196640 | tf_op jit(solution)/shard_map/ppermute | solution.py:394
  138.4 2.2 shard_map.221
  147.3 2.0 collective-permute-start.16
  149.3 2.8 collective-permute-start.17
  152.1 4.2 %collective-permute-done.15.refs_1_ = bf16[128,768]{1,0:T(8,128)(2,1)S(1)} collective-permute-done((bf16[128,768]{1,0:T(8,128)(2,1)}, bf16[128,768]{1,0:T(8,128)(2,1)S(1)}, u32[]{:S(2)}, u32[]{:S(2)}) %collective-permute-start.15) | collective-permute-done | bytes 196640 | tf_op jit(solution)/shard_map/ppermute | solution.py:402
  156.4 6.7 %collective-permute-done.16.refs_2_ = bf16[128,768]{1,0:T(8,128)(2,1)S(1)} collective-permute-done((bf16[128,768]{1,0:T(8,128)(2,1)}, bf16[128,768]{1,0:T(8,128)(2,1)S(1)}, u32[]{:S(2)}, u32[]{:S(2)}) %collective-permute-start.16) | collective-permute-done | bytes 196640 | tf_op jit(solution)/shard_map/ppermute | solution.py:402
  167.8 5.9 %collective-permute-start.20 = (bf16[128,768]{1,0:T(8,128)(2,1)S(1)}, bf16[128,768]{1,0:T(8,128)(2,1)S(1)}, u32[]{:S(2)}, u32[]{:S(2)}) collective-permute-start(bf16[128,768]{1,0:T(8,128)(2,1)S(1)} %get-tuple-element.90.refs_3_.refs_1_), channel_id=1, source_target_pairs={{0,3},{1,0},{2,1},{3,2},{4,7},{5,4},{6,5},{7,6},{8,11},{9,8},{10,9... | collective-permute-start | bytes 589832 | tf_op jit(solution)/shard_map/ppermute | solution.py:394
  174.9 4.2 %collective-permute-done.20.refs_6_.refs_4_ = bf16[128,768]{1,0:T(8,128)(2,1)S(1)} collective-permute-done((bf16[128,768]{1,0:T(8,128)(2,1)S(1)}, bf16[128,768]{1,0:T(8,128)(2,1)S(1)}, u32[]{:S(2)}, u32[]{:S(2)}) %collective-permute-start.20) | collective-permute-done | bytes 196640 | tf_op jit(solution)/shard_map/ppermute | solution.py:394
  179.8 10.8 %collective-permute-done.19.refs_5_.refs_3_ = bf16[128,768]{1,0:T(8,128)(2,1)S(1)} collective-permute-done((bf16[128,768]{1,0:T(8,128)(2,1)S(1)}, bf16[128,768]{1,0:T(8,128)(2,1)S(1)}, u32[]{:S(2)}, u32[]{:S(2)}) %collective-permute-start.19) | collective-permute-done | bytes 196640 | tf_op jit(solution)/shard_map/ppermute | solution.py:394
  200.4 7.1 %collective-permute-done.21.refs_17_ = bf16[96,768]{1,0:T(8,128)(2,1)S(1)} collective-permute-done((bf16[96,768]{1,0:T(8,128)(2,1)S(1)}, bf16[96,768]{1,0:T(8,128)(2,1)S(1)}, u32[]{:S(2)}, u32[]{:S(2)}) %collective-permute-start.21) | collective-permute-done | bytes 147488 | tf_op jit(solution)/shard_map/ppermute | solution.py:408
  218.6 8.6 %shard_map.225 = (f32[4,112,768]{2,1,0:T(8,128)S(1)}, bf16[4,112,768]{2,1,0:T(8,128)(2,1)S(1)}, bf16[512,576]{1,0:T(8,128)(2,1)S(1)}) custom-call(s32[3]{0:T(128)S(1)} %pad_add_fusion.refs_0_, bf16[128,768]{1,0:T(8,128)(2,1)S(1)} %copy-done.24, bf16[128,768]{1,0:T(8,128)(2,1)S(1)} %copy-done.33, bf16[128,768]{1,0:T(8,128)(2,1)S(1)} %copy-done.30, ...), custom_call_target="tpu_custom_call" | custom-call | tf_op jit(solution)/shard_map/pallas_call | solution.py:747
  227.4 1.9 collective-permute-done.22.refs_2_
  230.1 1.8 collective-permute-start.26
  231.8 2.2 shard_map.227
  234.8 2.7 collective-permute-start.24
  240.7 7.4 %collective-permute-done.27.refs_3_ = bf16[112,768]{1,0:T(8,128)(2,1)S(1)} collective-permute-done((bf16[112,768]{1,0:T(8,128)(2,1)S(1)}, bf16[112,768]{1,0:T(8,128)(2,1)S(1)}, u32[]{:S(2)}, u32[]{:S(2)}) %collective-permute-start.27) | collective-permute-done | bytes 172064 | tf_op jit(solution)/shard_map/ppermute | solution.py:408
  251.8 1.7 copy-done.6
  253.5 1.8 shard_map.229.refs_5_
  255.9 2.6 collective-permute-start.31
  261.3 2.4 collective-permute-done.32.refs_6_
  269.2 1.7 collective-permute-start.34
  270.9 7.3 %collective-permute-done.36.refs_4_ = bf16[192,768]{1,0:T(8,128)(2,1)S(1)} collective-permute-done((bf16[192,768]{1,0:T(8,128)(2,1)S(1)}, bf16[192,768]{1,0:T(8,128)(2,1)S(1)}, u32[]{:S(2)}, u32[]{:S(2)}) %collective-permute-start.36) | collective-permute-done | bytes 294944 | tf_op jit(solution)/shard_map/ppermute | solution.py:408
  278.2 5.4 %collective-permute-done.35.refs_3_ = bf16[192,768]{1,0:T(8,128)(2,1)S(1)} collective-permute-done((bf16[192,768]{1,0:T(8,128)(2,1)S(1)}, bf16[192,768]{1,0:T(8,128)(2,1)S(1)}, u32[]{:S(2)}, u32[]{:S(2)}) %collective-permute-start.35) | collective-permute-done | bytes 294944 | tf_op jit(solution)/shard_map/ppermute | solution.py:408
  283.6 10.4 %shard_map.231 = (bf16[96,1536]{1,0:T(8,128)(2,1)S(1)}, bf16[96,1536]{1,0:T(8,128)(2,1)S(1)}) custom-call(s32[3]{0:T(128)S(1)} %pad_add_fusion.refs_0_, bf16[192,768]{1,0:T(8,128)(2,1)S(1)} %pad_maximum_fusion.refs_1_, bf16[192,768]{1,0:T(8,128)(2,1)S(1)} %collective-permute-done.34.refs_2_, bf16[192,768]{1,0:T(8,128)(2,1)S(1)} %collective-permute-done.35.refs_3_, ...), custom_call_target="tpu_custom_call" | custom-call | tf_op jit(solution)/shard_map/pallas_call | solution.py:747
  298.3 2.3 collective-permute-start.40
  300.6 1.7 collective-permute-start.41
  303.0 4.5 %collective-permute-done.39.refs_3_ = bf16[96,192]{1,0:T(8,128)(2,1)S(1)} collective-permute-done((bf16[96,192]{1,0:T(8,128)(2,1)S(1)}, bf16[96,192]{1,0:T(8,128)(2,1)S(1)}, u32[]{:S(2)}, u32[]{:S(2)}) %collective-permute-start.39) | collective-permute-done | bytes 36896 | tf_op jit(solution)/shard_map/ppermute | solution.py:402
  307.5 3.7 %collective-permute-done.41.refs_6_ = bf16[96,768]{1,0:T(8,128)(2,1)S(1)} collective-permute-done((bf16[96,768]{1,0:T(8,128)(2,1)S(1)}, bf16[96,768]{1,0:T(8,128)(2,1)S(1)}, u32[]{:S(2)}, u32[]{:S(2)}) %collective-permute-start.41) | collective-permute-done | bytes 147488 | tf_op jit(solution)/shard_map/ppermute | solution.py:408
  (279 shorter events, 88.9 us)
Async XLA Ops:
  7.2 39.5 %all-gather.4.cloned.1.call-start = ((), (), s32[]{:S(2)}) async-start(), calls=%async_computation.1 | async-start | bytes 3760128 | tf_op jit(solution)/shard_map/all_gather | solution.py:831
  10.4 62.9 %all-gather.6.cloned.1.call-start = ((), (), s32[]{:S(2)}) async-start(), calls=%async_computation.2 | async-start | bytes 1327104 | tf_op jit(solution)/shard_map/all_gather | solution.py:849
  10.9 21.5 %collective-permute-start.1 = (bf16[160,768]{1,0:T(8,128)(2,1)S(1)}, bf16[160,768]{1,0:T(8,128)(2,1)S(1)}, u32[]{:S(2)}, u32[]{:S(2)}) collective-permute-start(bf16[160,768]{1,0:T(8,128)(2,1)S(1)} %pad_maximum_fusion.1), channel_id=1, source_target_pairs={{0,2},{1,3},{2,0},{3,1},{4,6},{5,7},{6,4},{7,5},{8,10},{9,11},{10,... | collective-permute-start | bytes 737288 | tf_op jit(solution)/shard_map/ppermute | solution.py:386
  15.0 13.5 %collective-permute-start = (bf16[160,768]{1,0:T(8,128)(2,1)S(1)}, bf16[160,768]{1,0:T(8,128)(2,1)S(1)}, u32[]{:S(2)}, u32[]{:S(2)}) collective-permute-start(bf16[160,768]{1,0:T(8,128)(2,1)S(1)} %pad_maximum_fusion.1), channel_id=1, source_target_pairs={{0,1},{1,2},{2,3},{3,0},{4,5},{5,6},{6,7},{7,4},{8,9},{9,10},{10,1... | collective-permute-start | bytes 737288 | tf_op jit(solution)/shard_map/ppermute | solution.py:386
  16.6 16.5 %collective-permute-start.2 = (bf16[160,768]{1,0:T(8,128)(2,1)S(1)}, bf16[160,768]{1,0:T(8,128)(2,1)S(1)}, u32[]{:S(2)}, u32[]{:S(2)}) collective-permute-start(bf16[160,768]{1,0:T(8,128)(2,1)S(1)} %pad_maximum_fusion.1), channel_id=1, source_target_pairs={{0,3},{1,0},{2,1},{3,2},{4,7},{5,4},{6,5},{7,6},{8,11},{9,8},{10,9... | collective-permute-start | bytes 737288 | tf_op jit(solution)/shard_map/ppermute | solution.py:386
  34.4 157.5 %reduce-scatter.2.cloned.1.call-start = ((), (), s32[]{:S(2)}) async-start(), calls=%async_computation.3 | async-start | bytes 2654208 | tf_op jit(solution)/shard_map/reduce_scatter | solution.py:902
  35.1 1.2 collective-permute-start.3
  36.3 3.9 %collective-permute-start.4 = (bf16[2,12,96]{2,1,0:T(8,128)(2,1)S(1)}, bf16[2,12,96]{2,1,0:T(8,128)(2,1)S(1)}, u32[]{:S(2)}, u32[]{:S(2)}) collective-permute-start(bf16[2,12,96]{2,1,0:T(8,128)(2,1)S(1)} %pad_maximum_fusion.3), channel_id=1, source_target_pairs={{0,8},{4,12},{8,0},{12,4},{16,24},{20,28},{24,16},{28,20},{1,9},{5... | collective-permute-start | bytes 13832 | tf_op jit(solution)/shard_map/ppermute | solution.py:408
  40.2 4.1 %collective-permute-start.5 = (bf16[4,12,96]{2,1,0:T(8,128)(2,1)S(1)}, bf16[4,12,96]{2,1,0:T(8,128)(2,1)S(1)}, u32[]{:S(2)}, u32[]{:S(2)}) collective-permute-start(bf16[4,12,96]{2,1,0:T(8,128)(2,1)S(1)} %pad_maximum_fusion.2), channel_id=1, source_target_pairs={{0,16},{4,20},{8,24},{12,28},{16,0},{20,4},{24,8},{28,12},{1,17},{... | collective-permute-start | bytes 27656 | tf_op jit(solution)/shard_map/ppermute | solution.py:408
  55.0 18.3 %collective-permute-start.8 = (bf16[512,192]{1,0:T(8,128)(2,1)}, bf16[512,192]{1,0:T(8,128)(2,1)}, u32[]{:S(2)}, u32[]{:S(2)}) collective-permute-start(bf16[512,192]{1,0:T(8,128)(2,1)} %get-tuple-element.75.refs_1_.refs_5_), channel_id=1, source_target_pairs={{0,3},{1,0},{2,1},{3,2},{4,7},{5,4},{6,5},{7,6},{8,11},{9,8},{10,9... | collective-permute-start | bytes 589832 | tf_op jit(solution)/shard_map/ppermute | solution.py:394
  58.3 23.2 %collective-permute-start.7 = (bf16[512,192]{1,0:T(8,128)(2,1)}, bf16[512,192]{1,0:T(8,128)(2,1)}, u32[]{:S(2)}, u32[]{:S(2)}) collective-permute-start(bf16[512,192]{1,0:T(8,128)(2,1)} %get-tuple-element.75.refs_1_.refs_5_), channel_id=1, source_target_pairs={{0,2},{1,3},{2,0},{3,1},{4,6},{5,7},{6,4},{7,5},{8,10},{9,11},{10,... | collective-permute-start | bytes 589832 | tf_op jit(solution)/shard_map/ppermute | solution.py:394
  59.0 22.6 %collective-permute-start.6 = (bf16[512,192]{1,0:T(8,128)(2,1)}, bf16[512,192]{1,0:T(8,128)(2,1)}, u32[]{:S(2)}, u32[]{:S(2)}) collective-permute-start(bf16[512,192]{1,0:T(8,128)(2,1)} %get-tuple-element.75.refs_1_.refs_5_), channel_id=1, source_target_pairs={{0,1},{1,2},{2,3},{3,0},{4,5},{5,6},{6,7},{7,4},{8,9},{9,10},{10,1... | collective-permute-start | bytes 589832 | tf_op jit(solution)/shard_map/ppermute | solution.py:394
  94.3 9.7 %collective-permute-start.9 = (bf16[128,768]{1,0:T(8,128)(2,1)}, bf16[128,768]{1,0:T(8,128)(2,1)}, u32[]{:S(2)}, u32[]{:S(2)}) collective-permute-start(bf16[128,768]{1,0:T(8,128)(2,1)} %get-tuple-element.77), channel_id=1, source_target_pairs={{0,1},{1,2},{2,3},{3,0},{4,5},{5,6},{6,7},{7,4},{8,9},{9,10},{10,1... | collective-permute-start | bytes 589832 | tf_op jit(solution)/shard_map/ppermute | solution.py:402
  95.3 15.3 %collective-permute-start.10 = (bf16[128,768]{1,0:T(8,128)(2,1)}, bf16[128,768]{1,0:T(8,128)(2,1)}, u32[]{:S(2)}, u32[]{:S(2)}) collective-permute-start(bf16[128,768]{1,0:T(8,128)(2,1)} %get-tuple-element.78), channel_id=1, source_target_pairs={{0,2},{1,3},{2,0},{3,1},{4,6},{5,7},{6,4},{7,5},{8,10},{9,11},{10,... | collective-permute-start | bytes 589832 | tf_op jit(solution)/shard_map/ppermute | solution.py:402
  97.2 13.4 %collective-permute-start.11 = (bf16[128,768]{1,0:T(8,128)(2,1)}, bf16[128,768]{1,0:T(8,128)(2,1)}, u32[]{:S(2)}, u32[]{:S(2)}) collective-permute-start(bf16[128,768]{1,0:T(8,128)(2,1)} %get-tuple-element.79), channel_id=1, source_target_pairs={{0,3},{1,0},{2,1},{3,2},{4,7},{5,4},{6,5},{7,6},{8,11},{9,8},{10,9... | collective-permute-start | bytes 589832 | tf_op jit(solution)/shard_map/ppermute | solution.py:402
  116.1 12.2 %collective-permute-start.14 = (bf16[128,768]{1,0:T(8,128)(2,1)S(1)}, bf16[128,768]{1,0:T(8,128)(2,1)S(1)}, u32[]{:S(2)}, u32[]{:S(2)}) collective-permute-start(bf16[128,768]{1,0:T(8,128)(2,1)S(1)} %get-tuple-element.82.refs_1_), channel_id=1, source_target_pairs={{0,3},{1,0},{2,1},{3,2},{4,7},{5,4},{6,5},{7,6},{8,11},{9,8},{10,9... | collective-permute-start | bytes 589832 | tf_op jit(solution)/shard_map/ppermute | solution.py:394
  123.0 15.4 %collective-permute-start.13 = (bf16[128,768]{1,0:T(8,128)(2,1)S(1)}, bf16[128,768]{1,0:T(8,128)(2,1)S(1)}, u32[]{:S(2)}, u32[]{:S(2)}) collective-permute-start(bf16[128,768]{1,0:T(8,128)(2,1)S(1)} %get-tuple-element.82.refs_1_), channel_id=1, source_target_pairs={{0,2},{1,3},{2,0},{3,1},{4,6},{5,7},{6,4},{7,5},{8,10},{9,11},{10,... | collective-permute-start | bytes 589832 | tf_op jit(solution)/shard_map/ppermute | solution.py:394
  123.0 15.4 %collective-permute-start.12 = (bf16[128,768]{1,0:T(8,128)(2,1)S(1)}, bf16[128,768]{1,0:T(8,128)(2,1)S(1)}, u32[]{:S(2)}, u32[]{:S(2)}) collective-permute-start(bf16[128,768]{1,0:T(8,128)(2,1)S(1)} %get-tuple-element.82.refs_1_), channel_id=1, source_target_pairs={{0,1},{1,2},{2,3},{3,0},{4,5},{5,6},{6,7},{7,4},{8,9},{9,10},{10,1... | collective-permute-start | bytes 589832 | tf_op jit(solution)/shard_map/ppermute | solution.py:394
  146.3 105.5 %all-gather.8.cloned.1.call-start = ((), (), s32[]{:S(2)}) async-start(), calls=%async_computation.4 | async-start | bytes 2654208 | tf_op jit(solution)/shard_map/all_gather | solution.py:918
  146.4 10.0 %collective-permute-start.15 = (bf16[128,768]{1,0:T(8,128)(2,1)}, bf16[128,768]{1,0:T(8,128)(2,1)S(1)}, u32[]{:S(2)}, u32[]{:S(2)}) collective-permute-start(bf16[128,768]{1,0:T(8,128)(2,1)} %copy-done.59), channel_id=1, source_target_pairs={{0,1},{1,2},{2,3},{3,0},{4,5},{5,6},{6,7},{7,4},{8,9},{9,10},{10,1... | collective-permute-start | bytes 589832 | tf_op jit(solution)/shard_map/ppermute | solution.py:402
  147.3 15.7 %collective-permute-start.16 = (bf16[128,768]{1,0:T(8,128)(2,1)}, bf16[128,768]{1,0:T(8,128)(2,1)S(1)}, u32[]{:S(2)}, u32[]{:S(2)}) collective-permute-start(bf16[128,768]{1,0:T(8,128)(2,1)} %copy-done.58), channel_id=1, source_target_pairs={{0,2},{1,3},{2,0},{3,1},{4,6},{5,7},{6,4},{7,5},{8,10},{9,11},{10,... | collective-permute-start | bytes 589832 | tf_op jit(solution)/shard_map/ppermute | solution.py:402
  149.3 13.7 %collective-permute-start.17 = (bf16[128,768]{1,0:T(8,128)(2,1)}, bf16[128,768]{1,0:T(8,128)(2,1)S(1)}, u32[]{:S(2)}, u32[]{:S(2)}) collective-permute-start(bf16[128,768]{1,0:T(8,128)(2,1)} %copy-done.57), channel_id=1, source_target_pairs={{0,3},{1,0},{2,1},{3,2},{4,7},{5,4},{6,5},{7,6},{8,11},{9,8},{10,9... | collective-permute-start | bytes 589832 | tf_op jit(solution)/shard_map/ppermute | solution.py:402
  167.8 11.3 %collective-permute-start.20 = (bf16[128,768]{1,0:T(8,128)(2,1)S(1)}, bf16[128,768]{1,0:T(8,128)(2,1)S(1)}, u32[]{:S(2)}, u32[]{:S(2)}) collective-permute-start(bf16[128,768]{1,0:T(8,128)(2,1)S(1)} %get-tuple-element.90.refs_3_.refs_1_), channel_id=1, source_target_pairs={{0,3},{1,0},{2,1},{3,2},{4,7},{5,4},{6,5},{7,6},{8,11},{9,8},{10,9... | collective-permute-start | bytes 589832 | tf_op jit(solution)/shard_map/ppermute | solution.py:394
  173.7 16.9 %collective-permute-start.19 = (bf16[128,768]{1,0:T(8,128)(2,1)S(1)}, bf16[128,768]{1,0:T(8,128)(2,1)S(1)}, u32[]{:S(2)}, u32[]{:S(2)}) collective-permute-start(bf16[128,768]{1,0:T(8,128)(2,1)S(1)} %get-tuple-element.90.refs_3_.refs_1_), channel_id=1, source_target_pairs={{0,2},{1,3},{2,0},{3,1},{4,6},{5,7},{6,4},{7,5},{8,10},{9,11},{10,... | collective-permute-start | bytes 589832 | tf_op jit(solution)/shard_map/ppermute | solution.py:394
  173.7 17.6 %collective-permute-start.18 = (bf16[128,768]{1,0:T(8,128)(2,1)S(1)}, bf16[128,768]{1,0:T(8,128)(2,1)S(1)}, u32[]{:S(2)}, u32[]{:S(2)}) collective-permute-start(bf16[128,768]{1,0:T(8,128)(2,1)S(1)} %get-tuple-element.90.refs_3_.refs_1_), channel_id=1, source_target_pairs={{0,1},{1,2},{2,3},{3,0},{4,5},{5,6},{6,7},{7,4},{8,9},{9,10},{10,1... | collective-permute-start | bytes 589832 | tf_op jit(solution)/shard_map/ppermute | solution.py:394
  199.3 8.2 %collective-permute-start.21 = (bf16[96,768]{1,0:T(8,128)(2,1)S(1)}, bf16[96,768]{1,0:T(8,128)(2,1)S(1)}, u32[]{:S(2)}, u32[]{:S(2)}) collective-permute-start(bf16[96,768]{1,0:T(8,128)(2,1)S(1)} %get-tuple-element.99), channel_id=1, source_target_pairs={{0,2},{1,3},{2,0},{3,1},{4,6},{5,7},{6,4},{7,5},{8,10},{9,11},{10,... | collective-permute-start | bytes 442376 | tf_op jit(solution)/shard_map/ppermute | solution.py:408
  227.1 2.2 collective-permute-start.22
  230.1 9.5 %collective-permute-start.26 = (bf16[112,768]{1,0:T(8,128)(2,1)S(1)}, bf16[112,768]{1,0:T(8,128)(2,1)S(1)}, u32[]{:S(2)}, u32[]{:S(2)}) collective-permute-start(bf16[112,768]{1,0:T(8,128)(2,1)S(1)} %get-tuple-element.108), channel_id=1, source_target_pairs={{0,8},{4,12},{8,0},{12,4},{16,24},{20,28},{24,16},{28,20},{1,9},{5... | collective-permute-start | bytes 516104 | tf_op jit(solution)/shard_map/ppermute | solution.py:408
  234.8 21.1 %collective-permute-start.23 = (bf16[128,768]{1,0:T(8,128)(2,1)}, bf16[128,768]{1,0:T(8,128)(2,1)S(1)}, u32[]{:S(2)}, u32[]{:S(2)}) collective-permute-start(bf16[128,768]{1,0:T(8,128)(2,1)} %get-tuple-element.105), channel_id=1, source_target_pairs={{0,1},{1,2},{2,3},{3,0},{4,5},{5,6},{6,7},{7,4},{8,9},{9,10},{10,1... | collective-permute-start | bytes 589832 | tf_op jit(solution)/shard_map/ppermute | solution.py:402
  234.8 23.8 %collective-permute-start.24 = (bf16[128,768]{1,0:T(8,128)(2,1)}, bf16[128,768]{1,0:T(8,128)(2,1)}, u32[]{:S(2)}, u32[]{:S(2)}) collective-permute-start(bf16[128,768]{1,0:T(8,128)(2,1)} %get-tuple-element.106), channel_id=1, source_target_pairs={{0,2},{1,3},{2,0},{3,1},{4,6},{5,7},{6,4},{7,5},{8,10},{9,11},{10,... | collective-permute-start | bytes 589832 | tf_op jit(solution)/shard_map/ppermute | solution.py:402
  237.5 21.1 %collective-permute-start.25 = (bf16[128,768]{1,0:T(8,128)(2,1)S(1)}, bf16[128,768]{1,0:T(8,128)(2,1)}, u32[]{:S(2)}, u32[]{:S(2)}) collective-permute-start(bf16[128,768]{1,0:T(8,128)(2,1)S(1)} %get-tuple-element.107), channel_id=1, source_target_pairs={{0,3},{1,0},{2,1},{3,2},{4,7},{5,4},{6,5},{7,6},{8,11},{9,8},{10,9... | collective-permute-start | bytes 589832 | tf_op jit(solution)/shard_map/ppermute | solution.py:402
  238.6 9.5 %collective-permute-start.27 = (bf16[112,768]{1,0:T(8,128)(2,1)S(1)}, bf16[112,768]{1,0:T(8,128)(2,1)S(1)}, u32[]{:S(2)}, u32[]{:S(2)}) collective-permute-start(bf16[112,768]{1,0:T(8,128)(2,1)S(1)} %get-tuple-element.109), channel_id=1, source_target_pairs={{0,16},{4,20},{8,24},{12,28},{16,0},{20,4},{24,8},{28,12},{1,17},{... | collective-permute-start | bytes 516104 | tf_op jit(solution)/shard_map/ppermute | solution.py:408
  239.5 8.6 %collective-permute-start.28 = (bf16[112,768]{1,0:T(8,128)(2,1)S(1)}, bf16[112,768]{1,0:T(8,128)(2,1)S(1)}, u32[]{:S(2)}, u32[]{:S(2)}) collective-permute-start(bf16[112,768]{1,0:T(8,128)(2,1)S(1)} %get-tuple-element.110), channel_id=1, source_target_pairs={{0,24},{4,28},{8,16},{12,20},{16,8},{20,12},{24,0},{28,4},{1,25},{... | collective-permute-start | bytes 516104 | tf_op jit(solution)/shard_map/ppermute | solution.py:408
  249.7 10.1 %collective-permute-start.29 = (bf16[112,192]{1,0:T(8,128)(2,1)}, bf16[112,192]{1,0:T(8,128)(2,1)}, u32[]{:S(2)}, u32[]{:S(2)}) collective-permute-start(bf16[112,192]{1,0:T(8,128)(2,1)} %get-tuple-element.115.refs_3_), channel_id=1, source_target_pairs={{0,1},{1,2},{2,3},{3,0},{4,5},{5,6},{6,7},{7,4},{8,9},{9,10},{10,1... | collective-permute-start | bytes 129032 | tf_op jit(solution)/shard_map/ppermute | solution.py:402
  250.3 9.6 %collective-permute-start.30 = (bf16[112,192]{1,0:T(8,128)(2,1)}, bf16[112,192]{1,0:T(8,128)(2,1)}, u32[]{:S(2)}, u32[]{:S(2)}) collective-permute-start(bf16[112,192]{1,0:T(8,128)(2,1)} %get-tuple-element.116.refs_4_), channel_id=1, source_target_pairs={{0,2},{1,3},{2,0},{3,1},{4,6},{5,7},{6,4},{7,5},{8,10},{9,11},{10,... | collective-permute-start | bytes 129032 | tf_op jit(solution)/shard_map/ppermute | solution.py:402
  255.9 5.4 %collective-permute-start.31 = (bf16[112,192]{1,0:T(8,128)(2,1)}, bf16[112,192]{1,0:T(8,128)(2,1)S(1)}, u32[]{:S(2)}, u32[]{:S(2)}) collective-permute-start(bf16[112,192]{1,0:T(8,128)(2,1)} %get-tuple-element.117.refs_5_), channel_id=1, source_target_pairs={{0,3},{1,0},{2,1},{3,2},{4,7},{5,4},{6,5},{7,6},{8,11},{9,8},{10,9... | collective-permute-start | bytes 129032 | tf_op jit(solution)/shard_map/ppermute | solution.py:402
  258.6 5.1 %collective-permute-start.32 = (bf16[96,768]{1,0:T(8,128)(2,1)S(1)}, bf16[96,768]{1,0:T(8,128)(2,1)S(1)}, u32[]{:S(2)}, u32[]{:S(2)}) collective-permute-start(bf16[96,768]{1,0:T(8,128)(2,1)S(1)} %shard_map.229.refs_5_), channel_id=1, source_target_pairs={{0,1},{1,0},{2,3},{3,2},{4,5},{5,4},{6,7},{7,6},{8,9},{9,8},{10,11... | collective-permute-start | bytes 442376 | tf_op jit(solution)/shard_map/ppermute | solution.py:408
  265.8 1.4 collective-permute-start.33
  267.3 44.0 %copy-start.10 = (f32[2,96,768]{2,1,0:T(8,128)S(1)}, f32[2,96,768]{2,1,0:T(8,128)}, u32[]{:S(2)}) copy-start(f32[2,96,768]{2,1,0:T(8,128)} %refs_9_.1) | copy-start | bytes 1769476
  267.3 44.0 %copy-start.21 = (f32[3,96,192]{2,1,0:T(8,128)S(1)}, f32[3,96,192]{2,1,0:T(8,128)}, u32[]{:S(2)}) copy-start(f32[3,96,192]{2,1,0:T(8,128)} %refs_7_.1) | copy-start | bytes 663556
  267.3 10.9 %collective-permute-start.36 = (bf16[192,768]{1,0:T(8,128)(2,1)S(1)}, bf16[192,768]{1,0:T(8,128)(2,1)S(1)}, u32[]{:S(2)}, u32[]{:S(2)}) collective-permute-start(bf16[192,768]{1,0:T(8,128)(2,1)S(1)} %pad_maximum_fusion.refs_1_), channel_id=1, source_target_pairs={{0,24},{4,28},{8,16},{12,20},{16,8},{20,12},{24,0},{28,4},{1,25},{... | collective-permute-start | bytes 884744 | tf_op jit(solution)/shard_map/ppermute | solution.py:408
  268.5 15.1 %collective-permute-start.35 = (bf16[192,768]{1,0:T(8,128)(2,1)S(1)}, bf16[192,768]{1,0:T(8,128)(2,1)S(1)}, u32[]{:S(2)}, u32[]{:S(2)}) collective-permute-start(bf16[192,768]{1,0:T(8,128)(2,1)S(1)} %pad_maximum_fusion.refs_1_), channel_id=1, source_target_pairs={{0,16},{4,20},{8,24},{12,28},{16,0},{20,4},{24,8},{28,12},{1,17},{... | collective-permute-start | bytes 884744 | tf_op jit(solution)/shard_map/ppermute | solution.py:408
  269.2 14.4 %collective-permute-start.34 = (bf16[192,768]{1,0:T(8,128)(2,1)S(1)}, bf16[192,768]{1,0:T(8,128)(2,1)S(1)}, u32[]{:S(2)}, u32[]{:S(2)}) collective-permute-start(bf16[192,768]{1,0:T(8,128)(2,1)S(1)} %pad_maximum_fusion.refs_1_), channel_id=1, source_target_pairs={{0,8},{4,12},{8,0},{12,4},{16,24},{20,28},{24,16},{28,20},{1,9},{5... | collective-permute-start | bytes 884744 | tf_op jit(solution)/shard_map/ppermute | solution.py:408
  294.0 1.6 collective-permute-start.37
  296.5 6.5 %collective-permute-start.38 = (bf16[96,192]{1,0:T(8,128)(2,1)S(1)}, bf16[96,192]{1,0:T(8,128)(2,1)S(1)}, u32[]{:S(2)}, u32[]{:S(2)}) collective-permute-start(bf16[96,192]{1,0:T(8,128)(2,1)S(1)} %get-tuple-element.128), channel_id=1, source_target_pairs={{0,1},{1,2},{2,3},{3,0},{4,5},{5,6},{6,7},{7,4},{8,9},{9,10},{10,1... | collective-permute-start | bytes 110600 | tf_op jit(solution)/shard_map/ppermute | solution.py:402
  297.4 10.1 %collective-permute-start.39 = (bf16[96,192]{1,0:T(8,128)(2,1)S(1)}, bf16[96,192]{1,0:T(8,128)(2,1)S(1)}, u32[]{:S(2)}, u32[]{:S(2)}) collective-permute-start(bf16[96,192]{1,0:T(8,128)(2,1)S(1)} %get-tuple-element.129), channel_id=1, source_target_pairs={{0,2},{1,3},{2,0},{3,1},{4,6},{5,7},{6,4},{7,5},{8,10},{9,11},{10,... | collective-permute-start | bytes 110600 | tf_op jit(solution)/shard_map/ppermute | solution.py:402
  298.3 9.2 %collective-permute-start.40 = (bf16[96,192]{1,0:T(8,128)(2,1)S(1)}, bf16[96,192]{1,0:T(8,128)(2,1)S(1)}, u32[]{:S(2)}, u32[]{:S(2)}) collective-permute-start(bf16[96,192]{1,0:T(8,128)(2,1)S(1)} %get-tuple-element.130), channel_id=1, source_target_pairs={{0,3},{1,0},{2,1},{3,2},{4,7},{5,4},{6,5},{7,6},{8,11},{9,8},{10,9... | collective-permute-start | bytes 110600 | tf_op jit(solution)/shard_map/ppermute | solution.py:402
  300.6 10.6 %collective-permute-start.41 = (bf16[96,768]{1,0:T(8,128)(2,1)S(1)}, bf16[96,768]{1,0:T(8,128)(2,1)S(1)}, u32[]{:S(2)}, u32[]{:S(2)}) collective-permute-start(bf16[96,768]{1,0:T(8,128)(2,1)S(1)} %get-tuple-element.132), channel_id=1, source_target_pairs={{0,2},{1,3},{2,0},{3,1},{4,6},{5,7},{6,4},{7,5},{8,10},{9,11},{10,... | collective-permute-start | bytes 442376 | tf_op jit(solution)/shard_map/ppermute | solution.py:408
  (70 other events, 442.6 us)
Sparse Core Ops, SparseCore 0:
  10.5 36.1 all-gather.3
  49.2 24.0 all-gather.5
  146.4 43.1 reduce-scatter.1
  209.0 30.9 all-gather.7

commit v2 on v1

--- a/solution.py
+++ b/solution.py
@@ -473,16 +473,23 @@
     return jnp.sum(values, axis=0, keepdims=True)
 
 
+def unpack_rows(piece, rows):
+    count = rows // piece.shape[0]
+    own = piece.shape[1] // count
+    return jnp.concatenate([piece[:, at * own : (at + 1) * own] for at in range(count)], axis=0)
+
+
 def layer_middle(place, *refs):
     pieces, refs = refs[:SPLIT], refs[SPLIT:]
     out_weight, tokens, vec, weights, bias_up, first_b, activ_b, slope, first_in, *refs = refs
     parts, (moving,) = refs[:SPLIT], refs[SPLIT:]
     column = place[0]
-    own = pieces[0].shape[1]
     attended = vec[2:3, :] + tokens[...].astype(jnp.float32)
     for step, piece in enumerate(pieces):
+        rows = unpack_rows(piece, tokens.shape[0])
+        own = rows.shape[1]
         at = pl.multiple_of(source_of(column, step) * own, own)
-        attended = attended + dot(piece[...], out_weight[pl.ds(at, own), :], ((1,), (0,)))
+        attended = attended + dot(rows, out_weight[pl.ds(at, own), :], ((1,), (0,)))
     moving[...] = attended
     take_parts(moving, column, [first_in])
     unit, scale = norm_parts(attended)
@@ -496,14 +503,17 @@
     take_parts(moving, column, parts)
 
 
-def second_norm(*refs):
+def second_norm(place, *refs):
     pieces, refs = refs[:SPLIT], refs[SPLIT:]
-    first_in, vec, cotangent, valid, layer_out, d_branch, d_second, sums = refs
+    first_in, vec, cotangent, ids, layer_out, d_branch, d_second, sums = refs
+    count = first_in.shape[0]
+    at = pl.multiple_of(place[0] * count, count)
+    valid = (ids[pl.ds(at, count), :] >= 0).astype(jnp.float32)
     unit, scale = norm_parts(first_in[...])
     first = unit * vec[3:4, :] + vec[4:5, :]
     unit, scale = norm_parts(first + (sum_pieces(pieces) + vec[5:6, :]))
-    layer_out[...] = ((unit * vec[6:7, :] + vec[7:8, :]) * valid[...]).astype(jnp.bfloat16)
-    grad = cotangent[...].astype(jnp.float32) * valid[...]
+    layer_out[...] = ((unit * vec[6:7, :] + vec[7:8, :]) * valid).astype(jnp.bfloat16)
+    grad = cotangent[...].astype(jnp.float32) * valid
     d_rows = norm_back(grad, unit, scale, vec[6:7, :])
     d_second[...] = d_rows
     d_branch[...] = d_rows.astype(jnp.bfloat16)
@@ -600,8 +610,8 @@
     return queries, keys, values, probs
 
 
-def attention_forward(tokens, weight, bias, id_column, id_row, qkv, mixed):
-    own = mixed.shape[1]
+def attention_forward(place, tokens, weight, bias, id_column, id_row, qkv, mixed):
+    own = qkv.shape[1] // 3
     proj = weight[:, weight.shape[1] - 3 * own :]
     qkv[...] = (dot(tokens[...], proj, ((1,), (0,))) + bias[...]).astype(jnp.bfloat16)
     for start in range(0, tokens.shape[0], BLOCK):
@@ -609,7 +619,8 @@
         for head in range(own // HEAD):
             queries, keys, values, probs = probabilities(qkv, rows_at, head, own, id_column, id_row)
             part = dot(probs.astype(jnp.bfloat16), values, ((1,), (0,)))
-            mixed[rows_at, head * HEAD : (head + 1) * HEAD] = part.astype(jnp.bfloat16)
+            at = start // BLOCK * own + head * HEAD
+            mixed[:, at : at + HEAD] = part.astype(jnp.bfloat16)
 
 
 def attention_backward(
@@ -666,7 +677,7 @@
         pl.when(core == group % 2)(lambda: put(kept, jnp.float32))
         pl.when(core != group % 2)(lambda: put(sent, jnp.bfloat16))
     for step, piece in enumerate(mixed):
-        grad_out = dot(piece[...], d_columns, ((0,), (0,)))
+        grad_out = dot(unpack_rows(piece, rows), d_columns, ((0,), (0,)))
         source = source_of(column, step)
         for half in range(2):
             block = grad_out[half * depth : (half + 1) * depth]
@@ -736,21 +747,62 @@
     other[...] = jnp.where(even, gram_sum, rows[...])
 
 
-def run_kernel(body, outputs, scalars=0, scratch=(), ties=()):
+def join_pair(place, mine, other, rows):
+    depth = mine.shape[0]
+    even = place[1] == 0
+    rows[:depth, :] = jnp.where(even, mine[...], other[...])
+    rows[depth:, :] = jnp.where(even, other[...], mine[...])
+
+
+def run_kernel(body, outputs, scalars=0, scratch=(), ties=(), far=(), far_out=()):
     def call(*operands):
-        count = len(operands)
+        count, made = len(operands), len(outputs)
 
         def whole(*refs):
-            body(*refs[:count], *refs[count + len(ties) :])
-
+            inputs, refs = list(refs[:count]), refs[count + len(ties) :]
+            results, refs = list(refs[:made]), refs[made:]
+            mine, refs = refs[: len(scratch)], refs[len(scratch) :]
+            rooms, refs = refs[: len(far)], refs[len(far) :]
+            rooms_out, refs = refs[: len(far_out)], refs[len(far_out) :]
+            copies = []
+            for at, room in zip(far, rooms):
+                copies.append(pltpu.make_async_copy(inputs[at], room, refs[len(copies)]))
+                copies[-1].start()
+                inputs[at] = room
+            for copy in copies:
+                copy.wait()
+            targets = [results[at] for at in far_out]
+            for at, room in zip(far_out, rooms_out):
+                results[at] = room
+            body(*inputs, *results, *mine)
+            copies_out = []
+            for room, target in zip(rooms_out, targets):
+                at = len(far) + len(copies_out)
+                copies_out.append(pltpu.make_async_copy(room, target, refs[at]))
+                copies_out[-1].start()
+            for copy in copies_out:
+                copy.wait()
+
+        operands = list(operands)
+        for at in far:
+            operands[at] = pltpu.with_memory_space_constraint(operands[at], pltpu.HBM)
+        kinds = list(outputs)
+        for at in far_out:
+            kinds[at] = pltpu.HBM(kinds[at].shape, kinds[at].dtype)
         spaces = [pltpu.SMEM] * scalars + [pltpu.VMEM] * (count - scalars) + [pl.ANY] * len(ties)
+        for at in far:
+            spaces[at] = pltpu.HBM
+        spaces_out = [pltpu.HBM if at in far_out else pltpu.VMEM for at in range(made)]
+        rooms = [pltpu.VMEM(operands[at].shape, operands[at].dtype) for at in far]
+        rooms_out = [pltpu.VMEM(outputs[at].shape, outputs[at].dtype) for at in far_out]
+        signals = [pltpu.SemaphoreType.DMA] * (len(far) + len(far_out))
         return pl.pallas_call(
             whole,
-            out_shape=outputs,
+            out_shape=kinds,
             in_specs=[pl.BlockSpec(memory_space=space) for space in spaces],
-            out_specs=[pl.BlockSpec(memory_space=pltpu.VMEM)] * len(outputs),
-            scratch_shapes=scratch,
-            compiler_params=pltpu.CompilerParams(vmem_limit_bytes=16 * 2**20),
+            out_specs=[pl.BlockSpec(memory_space=space) for space in spaces_out],
+            scratch_shapes=[*scratch, *rooms, *rooms_out, *signals],
+            compiler_params=pltpu.CompilerParams(vmem_limit_bytes=24 * 2**20),
         )(*operands, *ties)
 
     return call
@@ -820,6 +872,7 @@
     groups = lax.axis_size("dp")
     column = lax.axis_index("shard")
     row = lax.axis_index("dp")
+    place = jnp.stack([column, row & 1, row >> 1]).astype(jnp.int32)
     slots = micro * shards
     own = qkv_w.shape[2]
     hidden = ffn_w.shape[2]
@@ -852,22 +905,24 @@
     segment = jnp.sum((position[:, :, None] >= ends[:, None, :]).astype(jnp.int32), axis=2)
     valid = position < ends[:, -1:]
     slot = jnp.arange(slots, dtype=jnp.int32)[:, None]
-    marks = jnp.where(valid, segment, ends.shape[1] + position) + slot * (ends.shape[1] + rows)
+    marks = jnp.where(valid, segment + slot * ends.shape[1], -1 - position - slot * rows)
     id_column, id_row = marks.reshape(-1, 1), marks.reshape(1, -1)
-    valid_own = lax.dynamic_slice_in_dim(valid, column * micro, micro, 0)
-    valid_own = valid_own.reshape(-1, 1).astype(jnp.float32)
     bias_q = lax.dynamic_slice_in_dim(vec[0], column * own, own, 0)
     bias_v = lax.dynamic_slice_in_dim(vec[1], column * own, own, 0)
     bias_proj = jnp.concatenate([bias_q, jnp.zeros_like(bias_q), bias_v])[None]
-    bias_up = lax.dynamic_slice_in_dim(vec[8:].reshape(-1), column * hidden, hidden, 0)
+    bias_up = lax.dynamic_slice_in_dim(vec[8:].reshape(-1), column * hidden, hidden, 0)[None]
 
     qkv, mixed_own = run_kernel(
         attention_forward,
         [
             jax.ShapeDtypeStruct((slots * rows, 3 * own), bf16),
-            jax.ShapeDtypeStruct((slots * rows, own), bf16),
+            jax.ShapeDtypeStruct((BLOCK, slots * rows // BLOCK * own), bf16),
         ],
-    )(tokens_b, weights, bias_proj, id_column, id_row)
+        scalars=1,
+        ties=[vec, bias_up],
+        far=(1, 2, 4),
+        far_out=(0,),
+    )(place, tokens_b, weights, bias_proj, id_column, id_row)
 
     depth = width // groups
     count = micro * rows
@@ -877,7 +932,6 @@
     part_kinds = [own_f] + [own_b] * (shards - 1)
     sums_kind = jax.ShapeDtypeStruct((8, width), jnp.float32)
     moving = pltpu.VMEM((slots * rows, width), jnp.float32)
-    place = jnp.stack([column, lax.rem(row, 2), row // 2]).astype(jnp.int32)
 
     mixed_pieces = pieces_of(mixed_own, "shard")
     first_b, activ_b, slope, first_in, *parts = run_kernel(
@@ -885,38 +939,28 @@
         [whole_b, whole_b, jax.ShapeDtypeStruct((slots * rows, hidden), jnp.float32), own_f] + part_kinds,
         scalars=1,
         scratch=[moving],
-    )(place, *mixed_pieces, out_b, tokens_b, vec, weights, bias_up[None])
+        far=(5, 6, 8),
+    )(place, *mixed_pieces, out_b, tokens_b, vec, weights, bias_up)
     layer_out, d_branch_own, d_second, sums_two = run_kernel(
-        second_norm, [own_b, own_b, own_f, sums_kind]
-    )(*send_parts(parts, "shard"), first_in, vec, cotangent.reshape(count, width), valid_own)
+        second_norm, [own_b, own_b, own_f, sums_kind], scalars=1, far=(7, 8), far_out=(0, 2, 3)
+    )(place, *send_parts(parts, "shard"), first_in, vec, cotangent.reshape(count, width), id_column)
     layer_out = layer_out.reshape(tokens.shape)
     d_branch_b, d_inner_b, d_bias_up, *parts = run_kernel(
         inner_backward,
         [whole_b, whole_b, jax.ShapeDtypeStruct((1, hidden), jnp.float32)] + part_kinds,
         scalars=1,
         scratch=[moving],
+        far=(6,),
+        far_out=(2, 3, 4, 5, 6),
     )(place, *pieces_of(d_branch_own, "shard"), slope, weights)
-    (grads,) = run_kernel(inner_gradients, [jax.ShapeDtypeStruct((2, width, hidden), bf16)], ties=parts)(
+    (grads,) = run_kernel(inner_gradients, [jax.ShapeDtypeStruct((2, width, hidden), bf16)], far_out=(0,))(
         first_b, activ_b, d_inner_b, d_branch_b
     )
     summed = lax.psum_scatter(grads, "dp", scatter_dimension=1, tiled=True)
     d_first_in, d_attended_own, sums_one = run_kernel(
-        first_norm, [own_f, own_b, sums_kind]
+        first_norm, [own_f, own_b, sums_kind], far=(0, 4, 5), far_out=(0, 2)
     )(*send_parts(parts, "shard"), d_second, first_in, vec)
     d_attended_pieces = pieces_of(d_attended_own, "shard")
-    moment_kind = jax.ShapeDtypeStruct(ffn_mom.shape, ffn_mom.dtype)
-    wide_kind = jax.ShapeDtypeStruct((depth, hidden), bf16)
-    grad_ffn, new_ffn_mom, mine, far = run_kernel(
-        wide_momenta,
-        [moment_kind, moment_kind, wide_kind, wide_kind],
-        scalars=1,
-        ties=d_attended_pieces,
-    )(place, summed, ffn_mom)
-    even = lax.rem(row, 2) == 0
-    far_rows = swap(far, "shard", shards // 2)
-    wide_rows = jnp.concatenate([mine, far_rows], axis=1)
-    wide = lax.all_gather(wide_rows, "dp", axis=0, tiled=True)
-
     packed_rows = depth + 16
     kept, sent, d_proj = run_kernel(
         attention_backward,
@@ -927,16 +971,31 @@
         ],
         scalars=1,
         scratch=[pltpu.VMEM((slots * rows, width), bf16), pltpu.VMEM((16, width), jnp.float32)],
-        ties=[far_rows],
+        far=(5, 6, 7, 8, 9, 10, 11, 13, 14, 15),
+        far_out=(0, 2),
     )(
         place, *d_attended_pieces, *mixed_pieces, out_b, qkv, id_column, id_row, tokens_b,
         sums_one, sums_two, d_bias_up,
     )
+    moment_kind = jax.ShapeDtypeStruct(ffn_mom.shape, ffn_mom.dtype)
+    wide_kind = jax.ShapeDtypeStruct((depth, hidden), bf16)
+    grad_ffn, new_ffn_mom, mine, far = run_kernel(
+        wide_momenta,
+        [moment_kind, moment_kind, wide_kind, wide_kind],
+        scalars=1,
+        ties=[kept],
+        far=(1, 2),
+        far_out=(0, 1),
+    )(place, summed, ffn_mom)
+    far_rows = swap(far, "shard", shards // 2)
+    wide_rows = jnp.concatenate([mine, far_rows], axis=1)
+    wide = lax.all_gather(wide_rows, "dp", axis=0, tiled=True)
+
     block_kind = jax.ShapeDtypeStruct((packed_rows, width), bf16)
     total, *blocks = run_kernel(
-        pair_sum, [jax.ShapeDtypeStruct((packed_rows, width), jnp.float32)] + [block_kind] * 3, scalars=1
+        pair_sum, [jax.ShapeDtypeStruct((packed_rows, width), jnp.float32)] + [block_kind] * 3, scalars=1, far=(1,)
     )(place, kept, swap(sent, "dp", 1))
-    parts = run_kernel(token_parts, part_kinds, scalars=1, scratch=[moving], ties=[total])(
+    parts = run_kernel(token_parts, part_kinds, scalars=1, scratch=[moving], ties=[total], far=(1, 2))(
         place, d_proj, weights
     )
     d_tokens = d_first_in + sum(part.astype(jnp.float32) for part in send_parts(parts, "shard"))
@@ -947,8 +1006,10 @@
         like + like + [block_kind] * shards,
         scalars=1,
         scratch=[pltpu.VMEM((shards, packed_rows, own), jnp.float32)],
+        far=(5, 6),
+        far_out=(0, 1, 2, 3),
     )(place, total, *[swap(block, "dp", 2 * at + 2) for at, block in enumerate(blocks)], qkv_mom, out_mom)
-    (gram_rows,) = run_kernel(wide_gram, [jax.ShapeDtypeStruct((depth, width), bf16)], ties=blocks)(
+    (gram_rows,) = run_kernel(wide_gram, [jax.ShapeDtypeStruct((depth, width), bf16)], ties=blocks, far=(0, 1))(
         wide_rows, wide
     )
     row_kind = jax.ShapeDtypeStruct((depth, width), bf16)
@@ -961,8 +1022,9 @@
     )(place, *send_parts(blocks, "shard"), gram_rows, swap(gram_rows, "shard", 1))
     grad_vec = grad_vec[:vec_rows, :vec_own]
     d_tokens = d_tokens.reshape(tokens.shape)
-    other = swap(other, "dp", 1)
-    pair_rows = jnp.concatenate([jnp.where(even, mine, other), jnp.where(even, other, mine)], axis=0)
+    (pair_rows,) = run_kernel(
+        join_pair, [jax.ShapeDtypeStruct((2 * depth, width), bf16)], scalars=1
+    )(place, mine, swap(other, "dp", 1))
     pair_pieces = [pair_rows] + [swap(pair_rows, "dp", bit) for bit in (2, 4, 6)]
     state_kind = jax.ShapeDtypeStruct((depth, 2 * hidden), bf16)
     kept, sent = run_kernel(
@@ -971,6 +1033,7 @@
         scalars=1,
         scratch=[pltpu.VMEM((width, width), bf16), pltpu.VMEM((width, width), jnp.float32)]
         + [pltpu.VMEM((width, width), bf16)] * NS_STEPS,
+        far=(5,),
     )(place, *pair_pieces, wide)
     block_kind = jax.ShapeDtypeStruct((depth, own), bf16)
     wide_kind = jax.ShapeDtypeStruct((depth, hidden), bf16)
@@ -982,6 +1045,8 @@
         [jax.ShapeDtypeStruct(each.shape, each.dtype) for each in (qkv_w, out_w, ffn_w)],
         scalars=1,
         scratch=[pltpu.VMEM((shards, depth, own), jnp.float32)],
+        far=(7, 8, 9),
+        far_out=(0, 1, 2),
     )(
         place, *send_parts(blocks, "shard"), mine, swap(far, "shard", shards // 2), qkv_w, out_w, ffn_w
     )

time: 321 us -> 299 us (0.931)
  local copies, waits for them, and re-layouts: 52.8 us -> 8.58 us
  Pallas kernels: 46.4 us -> 69 us
  waiting for transfers between devices: 135 us -> 141 us
  starting transfers between devices: 65.7 us -> 61.4 us
    unnamed x147 -> x39, local copies, waits for them, and re-layouts: 46.5 us -> 3.05 us
    pallas_call x16 -> x17, Pallas kernels: 46.4 us -> 69 us  [call(): pl.pallas_call(whole, out_shape=kinds, in_specs=[pl.BlockSpec(memory_spac...]
    ppermute x15, waiting for transfers between devices: 41.9 us -> 48.2 us  [swap(): lax.ppermute(block, axis, [(i, i ^ bit) for i in range(lax.axis_size(axis...]
    ppermute x9, waiting for transfers between devices: 38 us -> 34.1 us  [pieces_of(): lax.ppermute(block, axis, [(i, (i + step) % count) for i in range(count)])]
  transfers between devices with their start and end apart: 46 -> 46, of which waited for: 28 -> 27; matrix products, arithmetic and copies ran while one was open for 3% -> 2% of each run, Pallas kernels for 6% -> 10%
where the time goes in v2:
time: 299 us; the launch traced here: 298 us
  waiting for transfers between devices  141 us (47%)
  Pallas kernels  69 us (23%)
  starting transfers between devices  61.4 us (21%)
  between operations  14.5 us (5%)
  local copies, waits for them, and re-layouts  8.58 us (3%)
  other arithmetic  3.62 us (1%)
    pallas_call x17, Pallas kernels, call(): pl.pallas_call(whole, out_shape=kinds, in_specs=[pl.BlockSpec(memory_spac...  69 us
    ppermute x15, waiting for transfers between devices, swap(): lax.ppermute(block, axis, [(i, i ^ bit) for i in range(lax.axis_size(axis...  48.2 us
    ppermute x9, waiting for transfers between devices, pieces_of(): lax.ppermute(block, axis, [(i, (i + step) % count) for i in range(count)])  34.1 us
    ppermute x15, waiting for transfers between devices, send_parts(): lax.ppermute(parts[step], axis, [(i, (i + step) % count) for i in range(c...  28.3 us
    ppermute x15, starting transfers between devices, send_parts(): lax.ppermute(parts[step], axis, [(i, (i + step) % count) for i in range(c...  22.4 us
    ppermute x9, starting transfers between devices, pieces_of(): lax.ppermute(block, axis, [(i, (i + step) % count) for i in range(count)])  18.1 us
    all_gather x1, waiting for transfers between devices, split_device(): out_b = lax.all_gather(out_part, 'dp', axis=0, tiled=True)  14.6 us
    ppermute x3, waiting for transfers between devices, gather_direct(): lax.ppermute(block, axis, [(i, (i + step) % count) for i in range(count)])  14 us
  transfers between devices with their start and end apart: 46, of which 27 were waited for; matrix products, arithmetic and copies ran while one was open for 2% of the time, Pallas kernels for 10%

profile of v2, /device:TPU:0, one launch (start us, length us, event | category | flops | bytes accessed | tf_op | source)
XLA Modules:
  0.0 298.3 jit_solution(15821400767377692145)
XLA Ops:
  10.9 4.1 %collective-permute-start.1 = (bf16[160,768]{1,0:T(8,128)(2,1)S(1)}, bf16[160,768]{1,0:T(8,128)(2,1)S(1)}, u32[]{:S(2)}, u32[]{:S(2)}) collective-permute-start(bf16[160,768]{1,0:T(8,128)(2,1)S(1)} %pad_maximum_fusion), channel_id=1, source_target_pairs={{0,2},{1,3},{2,0},{3,1},{4,6},{5,7},{6,4},{7,5},{8,10},{9,11},{10,... | collective-permute-start | bytes 737288 | tf_op jit(solution)/shard_map/ppermute | solution.py:386
  16.6 2.2 collective-permute-start.2
  19.0 9.5 %collective-permute-done = bf16[160,768]{1,0:T(8,128)(2,1)S(1)} collective-permute-done((bf16[160,768]{1,0:T(8,128)(2,1)S(1)}, bf16[160,768]{1,0:T(8,128)(2,1)S(1)}, u32[]{:S(2)}, u32[]{:S(2)}) %collective-permute-start) | collective-permute-done | bytes 245792 | tf_op jit(solution)/shard_map/ppermute | solution.py:386
  28.6 3.8 %collective-permute-done.1 = bf16[160,768]{1,0:T(8,128)(2,1)S(1)} collective-permute-done((bf16[160,768]{1,0:T(8,128)(2,1)S(1)}, bf16[160,768]{1,0:T(8,128)(2,1)S(1)}, u32[]{:S(2)}, u32[]{:S(2)}) %collective-permute-start.1) | collective-permute-done | bytes 245792 | tf_op jit(solution)/shard_map/ppermute | solution.py:386
  38.1 2.1 collective-permute-done.4
  45.0 1.8 all-gather.4.cloned.1.call-done.refs_2_.refs_8_.refs_6_
  46.7 5.5 %shard_map.218 = (bf16[512,576]{1,0:T(8,128)(2,1)}, bf16[256,384]{1,0:T(8,128)(2,1)S(1)}) custom-call(s32[3]{0:T(128)S(1)} %pad_add_fusion.refs_0_, bf16[512,768]{1,0:T(8,128)(2,1)} %bitcast.38, bf16[768,2112]{1,0:T(8,128)(2,1)} %all-gather.4.cloned.1.call-done.refs_2_.refs_8_.refs_6_, f32[1,576]{1,0:T(1,128)S(1)} %broadcast_in_dim.34.refs_3_, ...), custom_call_target="tpu_custom_call" | custom-call | tf_op jit(solution)/shard_map/pallas_call | solution.py:799
  52.3 3.4 %collective-permute-start.8 = (bf16[256,384]{1,0:T(8,128)(2,1)S(1)}, bf16[256,384]{1,0:T(8,128)(2,1)S(1)}, u32[]{:S(2)}, u32[]{:S(2)}) collective-permute-start(bf16[256,384]{1,0:T(8,128)(2,1)S(1)} %get-tuple-element.75.refs_1_.refs_5_), channel_id=1, source_target_pairs={{0,3},{1,0},{2,1},{3,2},{4,7},{5,4},{6,5},{7,6},{8,11},{9,8},{10,9... | collective-permute-start | bytes 589832 | tf_op jit(solution)/shard_map/ppermute | solution.py:394
  56.7 1.9 collective-permute-start.6
  58.7 14.6 %all-gather.6.cloned.1.call-done.refs_5_.refs_9_ = bf16[768,768]{1,0:T(8,128)(2,1)} async-done(((bf16[96,768]{1,0:T(8,128)(2,1)}), bf16[768,768]{1,0:T(8,128)(2,1)}) %all-gather.6.cloned.1.call-update) | async-done | bytes 1179664 | tf_op jit(solution)/shard_map/all_gather | solution.py:902
  73.3 7.0 %shard_map.219 = (bf16[512,768]{1,0:T(8,128)(2,1)S(1)}, bf16[512,768]{1,0:T(8,128)(2,1)S(1)}, f32[512,768]{1,0:T(8,128)S(1)}, f32[128,768]{1,0:T(8,128)S(1)}, f3...) custom-call(s32[3]{0:T(128)S(1)} %pad_add_fusion.refs_0_, ...), custom_call_target="tpu_custom_call" | custom-call | tf_op jit(solution)/shard_map/pallas_call | solution.py:799
  81.9 2.4 collective-permute-start.10
  84.3 1.9 collective-permute-start.11
  86.2 3.9 %collective-permute-done.9.refs_2_ = bf16[128,768]{1,0:T(8,128)(2,1)S(1)} collective-permute-done((bf16[128,768]{1,0:T(8,128)(2,1)S(1)}, bf16[128,768]{1,0:T(8,128)(2,1)S(1)}, u32[]{:S(2)}, u32[]{:S(2)}) %collective-permute-start.9) | collective-permute-done | bytes 196640 | tf_op jit(solution)/shard_map/ppermute | solution.py:402
  90.1 7.8 %collective-permute-done.10.refs_3_ = bf16[128,768]{1,0:T(8,128)(2,1)S(1)} collective-permute-done((bf16[128,768]{1,0:T(8,128)(2,1)S(1)}, bf16[128,768]{1,0:T(8,128)(2,1)S(1)}, u32[]{:S(2)}, u32[]{:S(2)}) %collective-permute-start.10) | collective-permute-done | bytes 196640 | tf_op jit(solution)/shard_map/ppermute | solution.py:402
  97.9 3.1 %shard_map.220 = (bf16[128,768]{1,0:T(8,128)(2,1)}, bf16[128,768]{1,0:T(8,128)(2,1)S(1)}, f32[128,768]{1,0:T(8,128)}, f32[8,768]{1,0:T(8,128)}) custom-call(s32[3]{0:T(128)S(1)} %pad_add_fusion.refs_0_, f32[128,768]{1,0:T(8,128)S(1)} %get-tuple-element.76.refs_1_, bf16[128,768]{1,0:T(8,128)(2,1)S(1)} %collective-permute-done.9.refs_2_, ...), custom_call_target="tpu_custom_call" | custom-call | tf_op jit(solution)/shard_map/pallas_call | solution.py:799
  100.9 5.7 %collective-permute-start.14 = (bf16[128,768]{1,0:T(8,128)(2,1)S(1)}, bf16[128,768]{1,0:T(8,128)(2,1)S(1)}, u32[]{:S(2)}, u32[]{:S(2)}) collective-permute-start(bf16[128,768]{1,0:T(8,128)(2,1)S(1)} %get-tuple-element.82.refs_1_), channel_id=1, source_target_pairs={{0,3},{1,0},{2,1},{3,2},{4,7},{5,4},{6,5},{7,6},{8,11},{9,8},{10,9... | collective-permute-start | bytes 589832 | tf_op jit(solution)/shard_map/ppermute | solution.py:394
  107.3 4.8 %collective-permute-done.14.refs_4_ = bf16[128,768]{1,0:T(8,128)(2,1)S(1)} collective-permute-done((bf16[128,768]{1,0:T(8,128)(2,1)S(1)}, bf16[128,768]{1,0:T(8,128)(2,1)S(1)}, u32[]{:S(2)}, u32[]{:S(2)}) %collective-permute-start.14) | collective-permute-done | bytes 196640 | tf_op jit(solution)/shard_map/ppermute | solution.py:394
  112.1 12.5 %collective-permute-done.13.refs_3_ = bf16[128,768]{1,0:T(8,128)(2,1)S(1)} collective-permute-done((bf16[128,768]{1,0:T(8,128)(2,1)S(1)}, bf16[128,768]{1,0:T(8,128)(2,1)S(1)}, u32[]{:S(2)}, u32[]{:S(2)}) %collective-permute-start.13) | collective-permute-done | bytes 196640 | tf_op jit(solution)/shard_map/ppermute | solution.py:394
  124.6 5.2 %shard_map.221 = (bf16[512,768]{1,0:T(8,128)(2,1)S(1)}, bf16[512,768]{1,0:T(8,128)(2,1)S(1)}, f32[1,768]{1,0:T(1,128)}, f32[128,768]{1,0:T(8,128)}, bf16[128,768...) custom-call(s32[3]{0:T(128)S(1)} %pad_add_fusion.refs_0_, ...), custom_call_target="tpu_custom_call" | custom-call | tf_op jit(solution)/shard_map/pallas_call | solution.py:799
  129.8 2.9 shard_map.227
  134.5 3.0 %collective-permute-start.17 = (bf16[128,768]{1,0:T(8,128)(2,1)S(1)}, bf16[128,768]{1,0:T(8,128)(2,1)S(1)}, u32[]{:S(2)}, u32[]{:S(2)}) collective-permute-start(bf16[128,768]{1,0:T(8,128)(2,1)S(1)} %copy-done.14), channel_id=1, source_target_pairs={{0,3},{1,0},{2,1},{3,2},{4,7},{5,4},{6,5},{7,6},{8,11},{9,8},{10,9... | collective-permute-start | bytes 589832 | tf_op jit(solution)/shard_map/ppermute | solution.py:402
  137.5 5.8 %collective-permute-done.15.refs_1_ = bf16[128,768]{1,0:T(8,128)(2,1)S(1)} collective-permute-done((bf16[128,768]{1,0:T(8,128)(2,1)S(1)}, bf16[128,768]{1,0:T(8,128)(2,1)S(1)}, u32[]{:S(2)}, u32[]{:S(2)}) %collective-permute-start.15) | collective-permute-done | bytes 196640 | tf_op jit(solution)/shard_map/ppermute | solution.py:402
  143.4 6.7 %collective-permute-done.16.refs_2_ = bf16[128,768]{1,0:T(8,128)(2,1)S(1)} collective-permute-done((bf16[128,768]{1,0:T(8,128)(2,1)S(1)}, bf16[128,768]{1,0:T(8,128)(2,1)S(1)}, u32[]{:S(2)}, u32[]{:S(2)}) %collective-permute-start.16) | collective-permute-done | bytes 196640 | tf_op jit(solution)/shard_map/ppermute | solution.py:402
  150.0 2.4 shard_map.222
  152.5 4.0 %collective-permute-start.20 = (bf16[128,768]{1,0:T(8,128)(2,1)S(1)}, bf16[128,768]{1,0:T(8,128)(2,1)S(1)}, u32[]{:S(2)}, u32[]{:S(2)}) collective-permute-start(bf16[128,768]{1,0:T(8,128)(2,1)S(1)} %get-tuple-element.90.refs_1_), channel_id=1, source_target_pairs={{0,3},{1,0},{2,1},{3,2},{4,7},{5,4},{6,5},{7,6},{8,11},{9,8},{10,9... | collective-permute-start | bytes 589832 | tf_op jit(solution)/shard_map/ppermute | solution.py:394
  157.8 4.0 %collective-permute-done.20.refs_4_ = bf16[128,768]{1,0:T(8,128)(2,1)S(1)} collective-permute-done((bf16[128,768]{1,0:T(8,128)(2,1)S(1)}, bf16[128,768]{1,0:T(8,128)(2,1)S(1)}, u32[]{:S(2)}, u32[]{:S(2)}) %collective-permute-start.20) | collective-permute-done | bytes 196640 | tf_op jit(solution)/shard_map/ppermute | solution.py:394
  161.8 12.8 %collective-permute-done.19.refs_3_ = bf16[128,768]{1,0:T(8,128)(2,1)S(1)} collective-permute-done((bf16[128,768]{1,0:T(8,128)(2,1)S(1)}, bf16[128,768]{1,0:T(8,128)(2,1)S(1)}, u32[]{:S(2)}, u32[]{:S(2)}) %collective-permute-start.19) | collective-permute-done | bytes 196640 | tf_op jit(solution)/shard_map/ppermute | solution.py:394
  174.6 11.7 %shard_map.223 = (f32[4,112,768]{2,1,0:T(8,128)}, bf16[4,112,768]{2,1,0:T(8,128)(2,1)S(1)}, bf16[512,576]{1,0:T(8,128)(2,1)}) custom-call(s32[3]{0:T(128)S(1)} %pad_add_fusion.refs_0_, bf16[128,768]{1,0:T(8,128)(2,1)S(1)} %get-tuple-element.90.refs_1_, bf16[128,768]{1,0:T(8,128)(2,1)S(1)} %collective-permute-done.18.refs_2_, ...), custom_call_target="tpu_custom_call" | custom-call | tf_op jit(solution)/shard_map/pallas_call | solution.py:799
  187.7 2.8 shard_map.228
  191.1 7.2 %collective-permute-done.31 = bf16[96,768]{1,0:T(8,128)(2,1)S(1)} collective-permute-done((bf16[96,768]{1,0:T(8,128)(2,1)S(1)}, bf16[96,768]{1,0:T(8,128)(2,1)S(1)}, u32[]{:S(2)}, u32[]{:S(2)}) %collective-permute-start.31) | collective-permute-done | bytes 147488 | tf_op jit(solution)/shard_map/ppermute | solution.py:408
  199.1 2.1 collective-permute-done.21.refs_2_
  201.3 2.1 shard_map.224
  204.9 3.6 %shard_map.225 = (f32[128,768]{1,0:T(8,128)S(1)}, bf16[128,768]{1,0:T(8,128)(2,1)S(1)}, bf16[128,768]{1,0:T(8,128)(2,1)S(1)}, bf16[128,768]{1,0:T(8,128)(2,1)S(1)}) custom-call(s32[3]{0:T(128)S(1)} %pad_add_fusion.refs_0_, bf16[512,576]{1,0:T(8,128)(2,1)} %get-tuple-element.95.refs_1_, ...), custom_call_target="tpu_custom_call" | custom-call | tf_op jit(solution)/shard_map/pallas_call | solution.py:799
  208.7 3.7 %collective-permute-start.24 = (bf16[128,768]{1,0:T(8,128)(2,1)S(1)}, bf16[128,768]{1,0:T(8,128)(2,1)S(1)}, u32[]{:S(2)}, u32[]{:S(2)}) collective-permute-start(bf16[128,768]{1,0:T(8,128)(2,1)S(1)} %get-tuple-element.102), channel_id=1, source_target_pairs={{0,3},{1,0},{2,1},{3,2},{4,7},{5,4},{6,5},{7,6},{8,11},{9,8},{10,9... | collective-permute-start | bytes 589832 | tf_op jit(solution)/shard_map/ppermute | solution.py:402
  214.5 10.7 %collective-permute-done.26.refs_3_ = bf16[112,768]{1,0:T(8,128)(2,1)S(1)} collective-permute-done((bf16[112,768]{1,0:T(8,128)(2,1)S(1)}, bf16[112,768]{1,0:T(8,128)(2,1)S(1)}, u32[]{:S(2)}, u32[]{:S(2)}) %collective-permute-start.26) | collective-permute-done | bytes 172064 | tf_op jit(solution)/shard_map/ppermute | solution.py:408
  225.2 2.6 shard_map.226
  229.6 2.6 shard_map.229.refs_5_
  232.3 2.9 collective-permute-start.30
  235.3 2.4 collective-permute-done.30.refs_4_
  237.7 2.6 collective-permute-done.32.refs_6_
  244.8 2.0 collective-permute-start.34
  246.8 7.3 %collective-permute-done.36.refs_4_ = bf16[192,768]{1,0:T(8,128)(2,1)S(1)} collective-permute-done((bf16[192,768]{1,0:T(8,128)(2,1)S(1)}, bf16[192,768]{1,0:T(8,128)(2,1)S(1)}, u32[]{:S(2)}, u32[]{:S(2)}) %collective-permute-start.36) | collective-permute-done | bytes 294944 | tf_op jit(solution)/shard_map/ppermute | solution.py:408
  254.1 5.5 %collective-permute-done.35.refs_3_ = bf16[192,768]{1,0:T(8,128)(2,1)S(1)} collective-permute-done((bf16[192,768]{1,0:T(8,128)(2,1)S(1)}, bf16[192,768]{1,0:T(8,128)(2,1)S(1)}, u32[]{:S(2)}, u32[]{:S(2)}) %collective-permute-start.35) | collective-permute-done | bytes 294944 | tf_op jit(solution)/shard_map/ppermute | solution.py:408
  259.6 12.3 %shard_map.232 = (bf16[96,1536]{1,0:T(8,128)(2,1)S(1)}, bf16[96,1536]{1,0:T(8,128)(2,1)S(1)}) custom-call(s32[3]{0:T(128)S(1)} %pad_add_fusion.refs_0_, bf16[192,768]{1,0:T(8,128)(2,1)S(1)} %shard_map.231.refs_1_, bf16[192,768]{1,0:T(8,128)(2,1)S(1)} %collective-permute-done.34.refs_2_, bf16[192,768]{1,0:T(8,128)(2,1)S(1)} %collective-permute-done.35.refs_3_, ...), custom_call_target="tpu_custom_call" | custom-call | tf_op jit(solution)/shard_map/pallas_call | solution.py:799
  276.7 1.9 collective-permute-start.40
  282.7 6.3 %collective-permute-done.41.refs_6_ = bf16[96,768]{1,0:T(8,128)(2,1)S(1)} collective-permute-done((bf16[96,768]{1,0:T(8,128)(2,1)S(1)}, bf16[96,768]{1,0:T(8,128)(2,1)S(1)}, u32[]{:S(2)}, u32[]{:S(2)}) %collective-permute-start.41) | collective-permute-done | bytes 147488 | tf_op jit(solution)/shard_map/ppermute | solution.py:408
  288.9 2.8 shard_map.234
  (167 shorter events, 43.9 us)
Async XLA Ops:
  7.2 39.5 %all-gather.4.cloned.1.call-start = ((), (), s32[]{:S(2)}) async-start(), calls=%async_computation.1 | async-start | bytes 3760128 | tf_op jit(solution)/shard_map/all_gather | solution.py:884
  10.4 62.9 %all-gather.6.cloned.1.call-start = ((), (), s32[]{:S(2)}) async-start(), calls=%async_computation.2 | async-start | bytes 1327104 | tf_op jit(solution)/shard_map/all_gather | solution.py:902
  10.9 21.5 %collective-permute-start.1 = (bf16[160,768]{1,0:T(8,128)(2,1)S(1)}, bf16[160,768]{1,0:T(8,128)(2,1)S(1)}, u32[]{:S(2)}, u32[]{:S(2)}) collective-permute-start(bf16[160,768]{1,0:T(8,128)(2,1)S(1)} %pad_maximum_fusion), channel_id=1, source_target_pairs={{0,2},{1,3},{2,0},{3,1},{4,6},{5,7},{6,4},{7,5},{8,10},{9,11},{10,... | collective-permute-start | bytes 737288 | tf_op jit(solution)/shard_map/ppermute | solution.py:386
  15.0 13.5 %collective-permute-start = (bf16[160,768]{1,0:T(8,128)(2,1)S(1)}, bf16[160,768]{1,0:T(8,128)(2,1)S(1)}, u32[]{:S(2)}, u32[]{:S(2)}) collective-permute-start(bf16[160,768]{1,0:T(8,128)(2,1)S(1)} %pad_maximum_fusion), channel_id=1, source_target_pairs={{0,1},{1,2},{2,3},{3,0},{4,5},{5,6},{6,7},{7,4},{8,9},{9,10},{10,1... | collective-permute-start | bytes 737288 | tf_op jit(solution)/shard_map/ppermute | solution.py:386
  16.6 16.5 %collective-permute-start.2 = (bf16[160,768]{1,0:T(8,128)(2,1)S(1)}, bf16[160,768]{1,0:T(8,128)(2,1)S(1)}, u32[]{:S(2)}, u32[]{:S(2)}) collective-permute-start(bf16[160,768]{1,0:T(8,128)(2,1)S(1)} %pad_maximum_fusion), channel_id=1, source_target_pairs={{0,3},{1,0},{2,1},{3,2},{4,7},{5,4},{6,5},{7,6},{8,11},{9,8},{10,9... | collective-permute-start | bytes 737288 | tf_op jit(solution)/shard_map/ppermute | solution.py:386
  34.4 151.9 %reduce-scatter.2.cloned.1.call-start = ((), (), s32[]{:S(2)}) async-start(), calls=%async_computation.3 | async-start | bytes 2654208 | tf_op jit(solution)/shard_map/reduce_scatter | solution.py:959
  35.1 1.2 collective-permute-start.3
  36.3 3.9 %collective-permute-start.4 = (bf16[2,12,96]{2,1,0:T(8,128)(2,1)S(1)}, bf16[2,12,96]{2,1,0:T(8,128)(2,1)S(1)}, u32[]{:S(2)}, u32[]{:S(2)}) collective-permute-start(bf16[2,12,96]{2,1,0:T(8,128)(2,1)S(1)} %pad_maximum_fusion.2), channel_id=1, source_target_pairs={{0,8},{4,12},{8,0},{12,4},{16,24},{20,28},{24,16},{28,20},{1,9},{5... | collective-permute-start | bytes 13832 | tf_op jit(solution)/shard_map/ppermute | solution.py:408
  40.2 4.1 %collective-permute-start.5 = (bf16[4,12,96]{2,1,0:T(8,128)(2,1)S(1)}, bf16[4,12,96]{2,1,0:T(8,128)(2,1)S(1)}, u32[]{:S(2)}, u32[]{:S(2)}) collective-permute-start(bf16[4,12,96]{2,1,0:T(8,128)(2,1)S(1)} %pad_maximum_fusion.1), channel_id=1, source_target_pairs={{0,16},{4,20},{8,24},{12,28},{16,0},{20,4},{24,8},{28,12},{1,17},{... | collective-permute-start | bytes 27656 | tf_op jit(solution)/shard_map/ppermute | solution.py:408
  52.3 21.0 %collective-permute-start.8 = (bf16[256,384]{1,0:T(8,128)(2,1)S(1)}, bf16[256,384]{1,0:T(8,128)(2,1)S(1)}, u32[]{:S(2)}, u32[]{:S(2)}) collective-permute-start(bf16[256,384]{1,0:T(8,128)(2,1)S(1)} %get-tuple-element.75.refs_1_.refs_5_), channel_id=1, source_target_pairs={{0,3},{1,0},{2,1},{3,2},{4,7},{5,4},{6,5},{7,6},{8,11},{9,8},{10,9... | collective-permute-start | bytes 589832 | tf_op jit(solution)/shard_map/ppermute | solution.py:394
  55.7 17.6 %collective-permute-start.7 = (bf16[256,384]{1,0:T(8,128)(2,1)S(1)}, bf16[256,384]{1,0:T(8,128)(2,1)S(1)}, u32[]{:S(2)}, u32[]{:S(2)}) collective-permute-start(bf16[256,384]{1,0:T(8,128)(2,1)S(1)} %get-tuple-element.75.refs_1_.refs_5_), channel_id=1, source_target_pairs={{0,2},{1,3},{2,0},{3,1},{4,6},{5,7},{6,4},{7,5},{8,10},{9,11},{10,... | collective-permute-start | bytes 589832 | tf_op jit(solution)/shard_map/ppermute | solution.py:394
  56.7 16.6 %collective-permute-start.6 = (bf16[256,384]{1,0:T(8,128)(2,1)S(1)}, bf16[256,384]{1,0:T(8,128)(2,1)S(1)}, u32[]{:S(2)}, u32[]{:S(2)}) collective-permute-start(bf16[256,384]{1,0:T(8,128)(2,1)S(1)} %get-tuple-element.75.refs_1_.refs_5_), channel_id=1, source_target_pairs={{0,1},{1,2},{2,3},{3,0},{4,5},{5,6},{6,7},{7,4},{8,9},{9,10},{10,1... | collective-permute-start | bytes 589832 | tf_op jit(solution)/shard_map/ppermute | solution.py:394
  80.4 49.4 %copy-start.2 = (f32[128,768]{1,0:T(8,128)}, f32[128,768]{1,0:T(8,128)S(1)}, u32[]{:S(2)}) copy-start(f32[128,768]{1,0:T(8,128)S(1)} %get-tuple-element.80.refs_5_) | copy-start | bytes 1179652
  80.4 9.7 %collective-permute-start.9 = (bf16[128,768]{1,0:T(8,128)(2,1)S(1)}, bf16[128,768]{1,0:T(8,128)(2,1)S(1)}, u32[]{:S(2)}, u32[]{:S(2)}) collective-permute-start(bf16[128,768]{1,0:T(8,128)(2,1)S(1)} %get-tuple-element.77), channel_id=1, source_target_pairs={{0,1},{1,2},{2,3},{3,0},{4,5},{5,6},{6,7},{7,4},{8,9},{9,10},{10,1... | collective-permute-start | bytes 589832 | tf_op jit(solution)/shard_map/ppermute | solution.py:402
  81.9 16.0 %collective-permute-start.10 = (bf16[128,768]{1,0:T(8,128)(2,1)S(1)}, bf16[128,768]{1,0:T(8,128)(2,1)S(1)}, u32[]{:S(2)}, u32[]{:S(2)}) collective-permute-start(bf16[128,768]{1,0:T(8,128)(2,1)S(1)} %get-tuple-element.78), channel_id=1, source_target_pairs={{0,2},{1,3},{2,0},{3,1},{4,6},{5,7},{6,4},{7,5},{8,10},{9,11},{10,... | collective-permute-start | bytes 589832 | tf_op jit(solution)/shard_map/ppermute | solution.py:402
  84.3 13.5 %collective-permute-start.11 = (bf16[128,768]{1,0:T(8,128)(2,1)S(1)}, bf16[128,768]{1,0:T(8,128)(2,1)S(1)}, u32[]{:S(2)}, u32[]{:S(2)}) collective-permute-start(bf16[128,768]{1,0:T(8,128)(2,1)S(1)} %get-tuple-element.79), channel_id=1, source_target_pairs={{0,3},{1,0},{2,1},{3,2},{4,7},{5,4},{6,5},{7,6},{8,11},{9,8},{10,9... | collective-permute-start | bytes 589832 | tf_op jit(solution)/shard_map/ppermute | solution.py:402
  100.9 11.1 %collective-permute-start.14 = (bf16[128,768]{1,0:T(8,128)(2,1)S(1)}, bf16[128,768]{1,0:T(8,128)(2,1)S(1)}, u32[]{:S(2)}, u32[]{:S(2)}) collective-permute-start(bf16[128,768]{1,0:T(8,128)(2,1)S(1)} %get-tuple-element.82.refs_1_), channel_id=1, source_target_pairs={{0,3},{1,0},{2,1},{3,2},{4,7},{5,4},{6,5},{7,6},{8,11},{9,8},{10,9... | collective-permute-start | bytes 589832 | tf_op jit(solution)/shard_map/ppermute | solution.py:394
  106.7 17.9 %collective-permute-start.13 = (bf16[128,768]{1,0:T(8,128)(2,1)S(1)}, bf16[128,768]{1,0:T(8,128)(2,1)S(1)}, u32[]{:S(2)}, u32[]{:S(2)}) collective-permute-start(bf16[128,768]{1,0:T(8,128)(2,1)S(1)} %get-tuple-element.82.refs_1_), channel_id=1, source_target_pairs={{0,2},{1,3},{2,0},{3,1},{4,6},{5,7},{6,4},{7,5},{8,10},{9,11},{10,... | collective-permute-start | bytes 589832 | tf_op jit(solution)/shard_map/ppermute | solution.py:394
  107.1 17.4 %collective-permute-start.12 = (bf16[128,768]{1,0:T(8,128)(2,1)S(1)}, bf16[128,768]{1,0:T(8,128)(2,1)S(1)}, u32[]{:S(2)}, u32[]{:S(2)}) collective-permute-start(bf16[128,768]{1,0:T(8,128)(2,1)S(1)} %get-tuple-element.82.refs_1_), channel_id=1, source_target_pairs={{0,1},{1,2},{2,3},{3,0},{4,5},{5,6},{6,7},{7,4},{8,9},{9,10},{10,1... | collective-permute-start | bytes 589832 | tf_op jit(solution)/shard_map/ppermute | solution.py:394
  132.7 41.9 %copy-start.7 = (f32[1,768]{1,0:T(1,128)S(1)}, f32[1,768]{1,0:T(1,128)}, u32[]{:S(2)}) copy-start(f32[1,768]{1,0:T(1,128)} %get-tuple-element.94.refs_16_) | copy-start | bytes 9220
  132.8 96.8 %all-gather.8.cloned.1.call-start = ((), (), s32[]{:S(2)}) async-start(), calls=%async_computation.4 | async-start | bytes 2654208 | tf_op jit(solution)/shard_map/all_gather | solution.py:992
  133.6 9.7 %collective-permute-start.15 = (bf16[128,768]{1,0:T(8,128)(2,1)S(1)}, bf16[128,768]{1,0:T(8,128)(2,1)S(1)}, u32[]{:S(2)}, u32[]{:S(2)}) collective-permute-start(bf16[128,768]{1,0:T(8,128)(2,1)S(1)} %copy-done.16), channel_id=1, source_target_pairs={{0,1},{1,2},{2,3},{3,0},{4,5},{5,6},{6,7},{7,4},{8,9},{9,10},{10,1... | collective-permute-start | bytes 589832 | tf_op jit(solution)/shard_map/ppermute | solution.py:402
  133.7 16.3 %collective-permute-start.16 = (bf16[128,768]{1,0:T(8,128)(2,1)S(1)}, bf16[128,768]{1,0:T(8,128)(2,1)S(1)}, u32[]{:S(2)}, u32[]{:S(2)}) collective-permute-start(bf16[128,768]{1,0:T(8,128)(2,1)S(1)} %copy-done.15), channel_id=1, source_target_pairs={{0,2},{1,3},{2,0},{3,1},{4,6},{5,7},{6,4},{7,5},{8,10},{9,11},{10,... | collective-permute-start | bytes 589832 | tf_op jit(solution)/shard_map/ppermute | solution.py:402
  134.5 15.5 %collective-permute-start.17 = (bf16[128,768]{1,0:T(8,128)(2,1)S(1)}, bf16[128,768]{1,0:T(8,128)(2,1)S(1)}, u32[]{:S(2)}, u32[]{:S(2)}) collective-permute-start(bf16[128,768]{1,0:T(8,128)(2,1)S(1)} %copy-done.14), channel_id=1, source_target_pairs={{0,3},{1,0},{2,1},{3,2},{4,7},{5,4},{6,5},{7,6},{8,11},{9,8},{10,9... | collective-permute-start | bytes 589832 | tf_op jit(solution)/shard_map/ppermute | solution.py:402
  152.5 9.3 %collective-permute-start.20 = (bf16[128,768]{1,0:T(8,128)(2,1)S(1)}, bf16[128,768]{1,0:T(8,128)(2,1)S(1)}, u32[]{:S(2)}, u32[]{:S(2)}) collective-permute-start(bf16[128,768]{1,0:T(8,128)(2,1)S(1)} %get-tuple-element.90.refs_1_), channel_id=1, source_target_pairs={{0,3},{1,0},{2,1},{3,2},{4,7},{5,4},{6,5},{7,6},{8,11},{9,8},{10,9... | collective-permute-start | bytes 589832 | tf_op jit(solution)/shard_map/ppermute | solution.py:394
  156.4 18.2 %collective-permute-start.19 = (bf16[128,768]{1,0:T(8,128)(2,1)S(1)}, bf16[128,768]{1,0:T(8,128)(2,1)S(1)}, u32[]{:S(2)}, u32[]{:S(2)}) collective-permute-start(bf16[128,768]{1,0:T(8,128)(2,1)S(1)} %get-tuple-element.90.refs_1_), channel_id=1, source_target_pairs={{0,2},{1,3},{2,0},{3,1},{4,6},{5,7},{6,4},{7,5},{8,10},{9,11},{10,... | collective-permute-start | bytes 589832 | tf_op jit(solution)/shard_map/ppermute | solution.py:394
  157.8 16.8 %collective-permute-start.18 = (bf16[128,768]{1,0:T(8,128)(2,1)S(1)}, bf16[128,768]{1,0:T(8,128)(2,1)S(1)}, u32[]{:S(2)}, u32[]{:S(2)}) collective-permute-start(bf16[128,768]{1,0:T(8,128)(2,1)S(1)} %get-tuple-element.90.refs_1_), channel_id=1, source_target_pairs={{0,1},{1,2},{2,3},{3,0},{4,5},{5,6},{6,7},{7,4},{8,9},{9,10},{10,1... | collective-permute-start | bytes 589832 | tf_op jit(solution)/shard_map/ppermute | solution.py:394
  190.6 7.7 %collective-permute-start.31 = (bf16[96,768]{1,0:T(8,128)(2,1)S(1)}, bf16[96,768]{1,0:T(8,128)(2,1)S(1)}, u32[]{:S(2)}, u32[]{:S(2)}) collective-permute-start(bf16[96,768]{1,0:T(8,128)(2,1)S(1)} %get-tuple-element.118), channel_id=1, source_target_pairs={{0,2},{1,3},{2,0},{3,1},{4,6},{5,7},{6,4},{7,5},{8,10},{9,11},{10,... | collective-permute-start | bytes 442376 | tf_op jit(solution)/shard_map/ppermute | solution.py:408
  199.1 2.2 collective-permute-start.21
  203.4 9.6 %collective-permute-start.25 = (bf16[112,768]{1,0:T(8,128)(2,1)S(1)}, bf16[112,768]{1,0:T(8,128)(2,1)S(1)}, u32[]{:S(2)}, u32[]{:S(2)}) collective-permute-start(bf16[112,768]{1,0:T(8,128)(2,1)S(1)} %get-tuple-element.103), channel_id=1, source_target_pairs={{0,8},{4,12},{8,0},{12,4},{16,24},{20,28},{24,16},{28,20},{1,9},{5... | collective-permute-start | bytes 516104 | tf_op jit(solution)/shard_map/ppermute | solution.py:408
  208.5 23.7 %collective-permute-start.22 = (bf16[128,768]{1,0:T(8,128)(2,1)S(1)}, bf16[128,768]{1,0:T(8,128)(2,1)S(1)}, u32[]{:S(2)}, u32[]{:S(2)}) collective-permute-start(bf16[128,768]{1,0:T(8,128)(2,1)S(1)} %get-tuple-element.100), channel_id=1, source_target_pairs={{0,1},{1,2},{2,3},{3,0},{4,5},{5,6},{6,7},{7,4},{8,9},{9,10},{10,1... | collective-permute-start | bytes 589832 | tf_op jit(solution)/shard_map/ppermute | solution.py:402
  208.6 26.6 %collective-permute-start.23 = (bf16[128,768]{1,0:T(8,128)(2,1)S(1)}, bf16[128,768]{1,0:T(8,128)(2,1)S(1)}, u32[]{:S(2)}, u32[]{:S(2)}) collective-permute-start(bf16[128,768]{1,0:T(8,128)(2,1)S(1)} %get-tuple-element.101), channel_id=1, source_target_pairs={{0,2},{1,3},{2,0},{3,1},{4,6},{5,7},{6,4},{7,5},{8,10},{9,11},{10,... | collective-permute-start | bytes 589832 | tf_op jit(solution)/shard_map/ppermute | solution.py:402
  208.7 26.5 %collective-permute-start.24 = (bf16[128,768]{1,0:T(8,128)(2,1)S(1)}, bf16[128,768]{1,0:T(8,128)(2,1)S(1)}, u32[]{:S(2)}, u32[]{:S(2)}) collective-permute-start(bf16[128,768]{1,0:T(8,128)(2,1)S(1)} %get-tuple-element.102), channel_id=1, source_target_pairs={{0,3},{1,0},{2,1},{3,2},{4,7},{5,4},{6,5},{7,6},{8,11},{9,8},{10,9... | collective-permute-start | bytes 589832 | tf_op jit(solution)/shard_map/ppermute | solution.py:402
  212.4 12.8 %collective-permute-start.26 = (bf16[112,768]{1,0:T(8,128)(2,1)S(1)}, bf16[112,768]{1,0:T(8,128)(2,1)S(1)}, u32[]{:S(2)}, u32[]{:S(2)}) collective-permute-start(bf16[112,768]{1,0:T(8,128)(2,1)S(1)} %get-tuple-element.104), channel_id=1, source_target_pairs={{0,16},{4,20},{8,24},{12,28},{16,0},{20,4},{24,8},{28,12},{1,17},{... | collective-permute-start | bytes 516104 | tf_op jit(solution)/shard_map/ppermute | solution.py:408
  213.0 12.2 %collective-permute-start.27 = (bf16[112,768]{1,0:T(8,128)(2,1)S(1)}, bf16[112,768]{1,0:T(8,128)(2,1)S(1)}, u32[]{:S(2)}, u32[]{:S(2)}) collective-permute-start(bf16[112,768]{1,0:T(8,128)(2,1)S(1)} %get-tuple-element.105), channel_id=1, source_target_pairs={{0,24},{4,28},{8,16},{12,20},{16,8},{20,12},{24,0},{28,4},{1,25},{... | collective-permute-start | bytes 516104 | tf_op jit(solution)/shard_map/ppermute | solution.py:408
  227.8 7.5 %collective-permute-start.28 = (bf16[112,192]{1,0:T(8,128)(2,1)S(1)}, bf16[112,192]{1,0:T(8,128)(2,1)S(1)}, u32[]{:S(2)}, u32[]{:S(2)}) collective-permute-start(bf16[112,192]{1,0:T(8,128)(2,1)S(1)} %get-tuple-element.114.refs_3_), channel_id=1, source_target_pairs={{0,1},{1,2},{2,3},{3,0},{4,5},{5,6},{6,7},{7,4},{8,9},{9,10},{10,1... | collective-permute-start | bytes 129032 | tf_op jit(solution)/shard_map/ppermute | solution.py:402
  228.5 6.8 %collective-permute-start.29 = (bf16[112,192]{1,0:T(8,128)(2,1)S(1)}, bf16[112,192]{1,0:T(8,128)(2,1)S(1)}, u32[]{:S(2)}, u32[]{:S(2)}) collective-permute-start(bf16[112,192]{1,0:T(8,128)(2,1)S(1)} %get-tuple-element.115.refs_4_), channel_id=1, source_target_pairs={{0,2},{1,3},{2,0},{3,1},{4,6},{5,7},{6,4},{7,5},{8,10},{9,11},{10,... | collective-permute-start | bytes 129032 | tf_op jit(solution)/shard_map/ppermute | solution.py:402
  232.3 5.4 %collective-permute-start.30 = (bf16[112,192]{1,0:T(8,128)(2,1)S(1)}, bf16[112,192]{1,0:T(8,128)(2,1)S(1)}, u32[]{:S(2)}, u32[]{:S(2)}) collective-permute-start(bf16[112,192]{1,0:T(8,128)(2,1)S(1)} %get-tuple-element.116.refs_5_), channel_id=1, source_target_pairs={{0,3},{1,0},{2,1},{3,2},{4,7},{5,4},{6,5},{7,6},{8,11},{9,8},{10,9... | collective-permute-start | bytes 129032 | tf_op jit(solution)/shard_map/ppermute | solution.py:402
  235.2 5.1 %collective-permute-start.32 = (bf16[96,768]{1,0:T(8,128)(2,1)S(1)}, bf16[96,768]{1,0:T(8,128)(2,1)S(1)}, u32[]{:S(2)}, u32[]{:S(2)}) collective-permute-start(bf16[96,768]{1,0:T(8,128)(2,1)S(1)} %shard_map.229.refs_5_), channel_id=1, source_target_pairs={{0,1},{1,0},{2,3},{3,2},{4,5},{5,4},{6,7},{7,6},{8,9},{9,8},{10,11... | collective-permute-start | bytes 442376 | tf_op jit(solution)/shard_map/ppermute | solution.py:408
  241.2 1.4 collective-permute-start.33
  243.2 10.9 %collective-permute-start.36 = (bf16[192,768]{1,0:T(8,128)(2,1)S(1)}, bf16[192,768]{1,0:T(8,128)(2,1)S(1)}, u32[]{:S(2)}, u32[]{:S(2)}) collective-permute-start(bf16[192,768]{1,0:T(8,128)(2,1)S(1)} %shard_map.231.refs_1_), channel_id=1, source_target_pairs={{0,24},{4,28},{8,16},{12,20},{16,8},{20,12},{24,0},{28,4},{1,25},{... | collective-permute-start | bytes 884744 | tf_op jit(solution)/shard_map/ppermute | solution.py:408
  244.8 14.8 %collective-permute-start.35 = (bf16[192,768]{1,0:T(8,128)(2,1)S(1)}, bf16[192,768]{1,0:T(8,128)(2,1)S(1)}, u32[]{:S(2)}, u32[]{:S(2)}) collective-permute-start(bf16[192,768]{1,0:T(8,128)(2,1)S(1)} %shard_map.231.refs_1_), channel_id=1, source_target_pairs={{0,16},{4,20},{8,24},{12,28},{16,0},{20,4},{24,8},{28,12},{1,17},{... | collective-permute-start | bytes 884744 | tf_op jit(solution)/shard_map/ppermute | solution.py:408
  244.8 14.8 %collective-permute-start.34 = (bf16[192,768]{1,0:T(8,128)(2,1)S(1)}, bf16[192,768]{1,0:T(8,128)(2,1)S(1)}, u32[]{:S(2)}, u32[]{:S(2)}) collective-permute-start(bf16[192,768]{1,0:T(8,128)(2,1)S(1)} %shard_map.231.refs_1_), channel_id=1, source_target_pairs={{0,8},{4,12},{8,0},{12,4},{16,24},{20,28},{24,16},{28,20},{1,9},{5... | collective-permute-start | bytes 884744 | tf_op jit(solution)/shard_map/ppermute | solution.py:408
  271.9 1.6 collective-permute-start.37
  274.4 6.5 %collective-permute-start.38 = (bf16[96,192]{1,0:T(8,128)(2,1)S(1)}, bf16[96,192]{1,0:T(8,128)(2,1)S(1)}, u32[]{:S(2)}, u32[]{:S(2)}) collective-permute-start(bf16[96,192]{1,0:T(8,128)(2,1)S(1)} %get-tuple-element.128), channel_id=1, source_target_pairs={{0,1},{1,2},{2,3},{3,0},{4,5},{5,6},{6,7},{7,4},{8,9},{9,10},{10,1... | collective-permute-start | bytes 110600 | tf_op jit(solution)/shard_map/ppermute | solution.py:402
  275.0 7.6 %collective-permute-start.39 = (bf16[96,192]{1,0:T(8,128)(2,1)S(1)}, bf16[96,192]{1,0:T(8,128)(2,1)S(1)}, u32[]{:S(2)}, u32[]{:S(2)}) collective-permute-start(bf16[96,192]{1,0:T(8,128)(2,1)S(1)} %get-tuple-element.129), channel_id=1, source_target_pairs={{0,2},{1,3},{2,0},{3,1},{4,6},{5,7},{6,4},{7,5},{8,10},{9,11},{10,... | collective-permute-start | bytes 110600 | tf_op jit(solution)/shard_map/ppermute | solution.py:402
  276.7 6.0 %collective-permute-start.40 = (bf16[96,192]{1,0:T(8,128)(2,1)S(1)}, bf16[96,192]{1,0:T(8,128)(2,1)S(1)}, u32[]{:S(2)}, u32[]{:S(2)}) collective-permute-start(bf16[96,192]{1,0:T(8,128)(2,1)S(1)} %get-tuple-element.130), channel_id=1, source_target_pairs={{0,3},{1,0},{2,1},{3,2},{4,7},{5,4},{6,5},{7,6},{8,11},{9,8},{10,9... | collective-permute-start | bytes 110600 | tf_op jit(solution)/shard_map/ppermute | solution.py:402
  278.6 10.4 %collective-permute-start.41 = (bf16[96,768]{1,0:T(8,128)(2,1)S(1)}, bf16[96,768]{1,0:T(8,128)(2,1)S(1)}, u32[]{:S(2)}, u32[]{:S(2)}) collective-permute-start(bf16[96,768]{1,0:T(8,128)(2,1)S(1)} %get-tuple-element.132), channel_id=1, source_target_pairs={{0,2},{1,3},{2,0},{3,1},{4,6},{5,7},{6,4},{7,5},{8,10},{9,11},{10,... | collective-permute-start | bytes 442376 | tf_op jit(solution)/shard_map/ppermute | solution.py:408
  (16 other events, 169.6 us)
Sparse Core Ops, SparseCore 0:
  10.5 36.1 all-gather.3
  49.2 24.0 all-gather.5
  132.9 40.2 reduce-scatter.1
  199.2 30.3 all-gather.7

commit v3 on v2

--- a/solution.py
+++ b/solution.py
@@ -441,6 +441,7 @@
 
 
 BLOCK = 256
+PAD = 64
 SPLIT = 4
 
 
@@ -479,7 +480,7 @@
     return jnp.concatenate([piece[:, at * own : (at + 1) * own] for at in range(count)], axis=0)
 
 
-def layer_middle(place, *refs):
+def layer_middle(waits, place, *refs):
     pieces, refs = refs[:SPLIT], refs[SPLIT:]
     out_weight, tokens, vec, weights, bias_up, first_b, activ_b, slope, first_in, *refs = refs
     parts, (moving,) = refs[:SPLIT], refs[SPLIT:]
@@ -495,6 +496,7 @@
     unit, scale = norm_parts(attended)
     first_b[...] = (unit * vec[3:4, :] + vec[4:5, :]).astype(jnp.bfloat16)
     hidden = slope.shape[1]
+    waits[0]()
     inner = dot(first_b[...], weights[:, :hidden], ((1,), (0,))) + bias_up[...]
     cdf = 0.5 * (1.0 + lax.erf(inner * 2.0 ** (-0.5)))
     activ_b[...] = (inner * cdf).astype(jnp.bfloat16)
@@ -551,6 +553,12 @@
     far[...] = jnp.where(low, second, first)
 
 
+def join_wide(mine, far, rows):
+    hidden = mine.shape[1]
+    rows[:, :hidden] = mine[...]
+    rows[:, hidden:] = far[...]
+
+
 def wide_gram(rows, wide, gram):
     gram[...] = dot(rows[...], wide[...], ((1,), (1,))).astype(jnp.bfloat16)
 
@@ -569,9 +577,10 @@
 
 
 def split_state(place, kept, other, *refs):
-    blocks, (mine, far) = refs[:SPLIT], refs[SPLIT:]
+    blocks, (mine,) = refs[:SPLIT], refs[SPLIT:]
     column, even = place[0], place[1] == 0
     own, hidden = blocks[0].shape[1], mine.shape[1]
+    far = blocks[SPLIT // 2]
     for step, block in enumerate(blocks):
         there = lax.rem(column + step, SPLIT)
         for at in range(SPLIT):
@@ -579,24 +588,26 @@
 
             @pl.when(there == at)
             def _():
-                block[...] = jnp.where(even, kept[:, lanes], other[:, lanes])
+                block[:, block.shape[1] - own :] = jnp.where(even, kept[:, lanes], other[:, lanes])
 
     mine[...] = jnp.where(even, other[:, :hidden], kept[:, :hidden])
-    far[...] = jnp.where(even, other[:, hidden:], kept[:, hidden:])
+    far[:, :hidden] = jnp.where(even, other[:, hidden:], kept[:, hidden:])
 
 
 def new_weights(place, *refs):
     pieces, refs = refs[:SPLIT], refs[SPLIT:]
-    mine, far, qkv_w, out_w, ffn_w, qkv_new, out_new, ffn_new, state = refs
+    mine, qkv_w, out_w, ffn_w, qkv_new, out_new, ffn_new, state = refs
     low = place[0] < SPLIT // 2
+    own, hidden = out_w.shape[1], mine.shape[1]
+    far = pieces[SPLIT // 2][:, :hidden]
     for step, piece in enumerate(pieces):
-        state[source_of(place[0], step)] = piece[...].astype(jnp.float32)
+        state[source_of(place[0], step)] = piece[:, piece.shape[1] - own :].astype(jnp.float32)
     for at in range(SPLIT - 1):
         qkv_new[at] = qkv_w[at] - muon_rate * state[at]
     out_new[...] = out_w[...] - muon_rate * state[SPLIT - 1]
     rate = muon_rate * (FF / D) ** 0.5
-    ffn_new[0] = ffn_w[0] - rate * jnp.where(low, mine[...], far[...]).astype(jnp.float32)
-    ffn_new[1] = ffn_w[1] - rate * jnp.where(low, far[...], mine[...]).astype(jnp.float32)
+    ffn_new[0] = ffn_w[0] - rate * jnp.where(low, mine[...], far).astype(jnp.float32)
+    ffn_new[1] = ffn_w[1] - rate * jnp.where(low, far, mine[...]).astype(jnp.float32)
 
 
 def probabilities(qkv, rows_at, head, own, id_column, id_row):
@@ -612,7 +623,7 @@
 
 def attention_forward(place, tokens, weight, bias, id_column, id_row, qkv, mixed):
     own = qkv.shape[1] // 3
-    proj = weight[:, weight.shape[1] - 3 * own :]
+    proj = weight[:, : 3 * own]
     qkv[...] = (dot(tokens[...], proj, ((1,), (0,))) + bias[...]).astype(jnp.bfloat16)
     for start in range(0, tokens.shape[0], BLOCK):
         rows_at = slice(start, start + BLOCK)
@@ -623,9 +634,7 @@
             mixed[:, at : at + HEAD] = part.astype(jnp.bfloat16)
 
 
-def attention_backward(
-    place, *refs
-):
+def attention_backward(waits, place, *refs):
     pieces, mixed, refs = refs[:SPLIT], refs[SPLIT : 2 * SPLIT], refs[2 * SPLIT :]
     out_weight, qkv, id_column, id_row, tokens, sums_one, sums_two, sums_up, *refs = refs
     kept, sent, d_proj, d_attended, sums = refs
@@ -654,6 +663,8 @@
     for place_at in range(1, width // own):
         other = d_attended[:, place_at * own : (place_at + 1) * own]
         d_columns = jnp.where(column == place_at, other, d_columns)
+    for wait in waits:
+        wait()
     grad_proj = dot(tokens[...], d_proj_all, ((0,), (0,)))
     proj_sums = row_sums(d_proj_all.astype(jnp.float32))
     sums[...] = jnp.zeros_like(sums)
@@ -689,11 +700,9 @@
             pl.when(core != half)(lambda: put_out(sent, jnp.bfloat16))
 
 
-def token_parts(place, d_proj, weight, *refs):
-    parts, (moving,) = refs[:SPLIT], refs[SPLIT:]
-    proj = weight[:, weight.shape[1] - d_proj.shape[1] :]
-    moving[...] = dot(d_proj[...], proj, ((1,), (1,)))
-    take_parts(moving, place[0], parts)
+def token_part(d_proj, weight, part):
+    proj = weight[:, : d_proj.shape[1]]
+    part[...] = dot(d_proj[...], proj, ((1,), (1,))).astype(jnp.bfloat16)
 
 
 def pair_sum(place, kept, other, total, *blocks):
@@ -754,8 +763,9 @@
     rows[depth:, :] = jnp.where(even, other[...], mine[...])
 
 
-def run_kernel(body, outputs, scalars=0, scratch=(), ties=(), far=(), far_out=()):
+def run_kernel(body, outputs, scalars=0, scratch=(), ties=(), far=(), far_out=(), late=(), lanes={}):
     def call(*operands):
+        operands = list(operands)
         count, made = len(operands), len(outputs)
 
         def whole(*refs):
@@ -763,28 +773,37 @@
             results, refs = list(refs[:made]), refs[made:]
             mine, refs = refs[: len(scratch)], refs[len(scratch) :]
             rooms, refs = refs[: len(far)], refs[len(far) :]
-            rooms_out, refs = refs[: len(far_out)], refs[len(far_out) :]
+            rooms_out, signals = refs[: len(far_out)], refs[len(far_out) :]
             copies = []
-            for at, room in zip(far, rooms):
-                copies.append(pltpu.make_async_copy(inputs[at], room, refs[len(copies)]))
+            for at, room, signal in zip(far, rooms, signals):
+                source = inputs[at].at[:, lanes[at]] if at in lanes else inputs[at]
+                copies.append(pltpu.make_async_copy(source, room, signal))
                 copies[-1].start()
                 inputs[at] = room
-            for copy in copies:
-                copy.wait()
+            waits = [copy.wait for at, copy in zip(far, copies) if at in late]
+            for at, copy in zip(far, copies):
+                if at not in late:
+                    copy.wait()
             targets = [results[at] for at in far_out]
             for at, room in zip(far_out, rooms_out):
                 results[at] = room
-            body(*inputs, *results, *mine)
+            if late:
+                body(waits, *inputs, *results, *mine)
+            else:
+                body(*inputs, *results, *mine)
             copies_out = []
-            for room, target in zip(rooms_out, targets):
-                at = len(far) + len(copies_out)
-                copies_out.append(pltpu.make_async_copy(room, target, refs[at]))
+            for room, target, signal in zip(rooms_out, targets, signals[len(far) :]):
+                copies_out.append(pltpu.make_async_copy(room, target, signal))
                 copies_out[-1].start()
             for copy in copies_out:
                 copy.wait()
 
-        operands = list(operands)
+        rooms = []
         for at in far:
+            shape = operands[at].shape
+            if at in lanes:
+                shape = (shape[0], lanes[at].size)
+            rooms.append(pltpu.VMEM(shape, operands[at].dtype))
             operands[at] = pltpu.with_memory_space_constraint(operands[at], pltpu.HBM)
         kinds = list(outputs)
         for at in far_out:
@@ -793,7 +812,6 @@
         for at in far:
             spaces[at] = pltpu.HBM
         spaces_out = [pltpu.HBM if at in far_out else pltpu.VMEM for at in range(made)]
-        rooms = [pltpu.VMEM(operands[at].shape, operands[at].dtype) for at in far]
         rooms_out = [pltpu.VMEM(outputs[at].shape, outputs[at].dtype) for at in far_out]
         signals = [pltpu.SemaphoreType.DMA] * (len(far) + len(far_out))
         return pl.pallas_call(
@@ -808,7 +826,7 @@
     return call
 
 
-def newton_schulz(place, *refs):
+def newton_schulz(waits, place, *refs):
     pieces, refs = refs[:SPLIT], refs[SPLIT:]
     wide, kept, sent, heard, gram, *factors = refs
     chip, core = place[2], place[1]
@@ -832,21 +850,23 @@
     trace = jnp.sum(jnp.where(at_row == at_lane, gram[...], 0.0), keepdims=True)
     scale = jnp.sqrt(trace) + ortho_eps
     gram[...] = gram[...] / (scale * scale)
-    for step, factor in enumerate(factors):
+    count = 2 * depth
+    start = pl.multiple_of(chip * count, count)
+    for factor in factors:
         gram_b = gram[...].astype(jnp.bfloat16)
         square = dot(gram_b, gram_b, ((1,), (0,)))
         factor[...] = (coef_second * gram[...] + coef_third * square).astype(jnp.bfloat16)
-        if step < NS_STEPS - 1:
-            moved = dot(factor[...], gram_b, ((1,), (0,)))
-            twice = dot(factor[...], moved.astype(jnp.bfloat16), ((1,), (0,)))
-            gram[...] = coef_first * coef_first * gram[...] + 2.0 * coef_first * moved + twice
-    count = 2 * depth
-    start = pl.multiple_of(chip * count, count)
+        moved = dot(factor[...], gram_b, ((1,), (0,)))
+        twice = dot(factor[...], moved.astype(jnp.bfloat16), ((1,), (0,)))
+        gram[...] = coef_first * coef_first * gram[...] + 2.0 * coef_first * moved + twice
     eye = lax.broadcasted_iota(jnp.int32, (count, width), 0) + start
     eye = (eye == lax.broadcasted_iota(jnp.int32, (count, width), 1)).astype(jnp.float32)
-    rows = coef_first * eye + factors[-1][pl.ds(start, count), :].astype(jnp.float32)
-    for factor in factors[-2::-1]:
+    rows = gram[pl.ds(start, count), :]
+    square = dot(rows.astype(jnp.bfloat16), gram[...].astype(jnp.bfloat16), ((1,), (0,)))
+    rows = coef_first * eye + (coef_second * rows + coef_third * square)
+    for factor in factors[::-1]:
         rows = coef_first * rows + dot(rows.astype(jnp.bfloat16), factor[...], ((1,), (0,)))
+    waits[0]()
     rows = (rows / scale).astype(jnp.bfloat16)
 
     @pl.when(even)
@@ -879,7 +899,7 @@
     bf16 = jnp.bfloat16
 
     packed = jnp.concatenate(
-        [ffn_w[0], ffn_w[1], qkv_w[0], qkv_w[1], qkv_w[2]], axis=1
+        [ffn_w[0], ffn_w[1], qkv_w[0], qkv_w[1], qkv_w[2], jnp.zeros((ffn_w.shape[1], PAD))], axis=1
     ).astype(bf16)
     weights = lax.all_gather(packed, "dp", axis=0, tiled=True)
 
@@ -912,6 +932,8 @@
     bias_proj = jnp.concatenate([bias_q, jnp.zeros_like(bias_q), bias_v])[None]
     bias_up = lax.dynamic_slice_in_dim(vec[8:].reshape(-1), column * hidden, hidden, 0)[None]
 
+    proj_lanes = pl.ds(2 * hidden, weights.shape[1] - 2 * hidden)
+    ffn_lanes = pl.ds(0, 2 * hidden)
     qkv, mixed_own = run_kernel(
         attention_forward,
         [
@@ -922,6 +944,7 @@
         ties=[vec, bias_up],
         far=(1, 2, 4),
         far_out=(0,),
+        lanes={2: proj_lanes},
     )(place, tokens_b, weights, bias_proj, id_column, id_row)
 
     depth = width // groups
@@ -940,6 +963,8 @@
         scalars=1,
         scratch=[moving],
         far=(5, 6, 8),
+        late=(8,),
+        lanes={8: ffn_lanes},
     )(place, *mixed_pieces, out_b, tokens_b, vec, weights, bias_up)
     layer_out, d_branch_own, d_second, sums_two = run_kernel(
         second_norm, [own_b, own_b, own_f, sums_kind], scalars=1, far=(7, 8), far_out=(0, 2, 3)
@@ -952,15 +977,28 @@
         scratch=[moving],
         far=(6,),
         far_out=(2, 3, 4, 5, 6),
+        lanes={6: ffn_lanes},
     )(place, *pieces_of(d_branch_own, "shard"), slope, weights)
     (grads,) = run_kernel(inner_gradients, [jax.ShapeDtypeStruct((2, width, hidden), bf16)], far_out=(0,))(
         first_b, activ_b, d_inner_b, d_branch_b
     )
     summed = lax.psum_scatter(grads, "dp", scatter_dimension=1, tiled=True)
     d_first_in, d_attended_own, sums_one = run_kernel(
-        first_norm, [own_f, own_b, sums_kind], far=(0, 4, 5), far_out=(0, 2)
+        first_norm, [own_f, own_b, sums_kind], far=(0, 4, 5), far_out=(0, 1, 2)
     )(*send_parts(parts, "shard"), d_second, first_in, vec)
     d_attended_pieces = pieces_of(d_attended_own, "shard")
+    moment_kind = jax.ShapeDtypeStruct(ffn_mom.shape, ffn_mom.dtype)
+    wide_kind = jax.ShapeDtypeStruct((depth, hidden), bf16)
+    grad_ffn, new_ffn_mom, mine, far_send = run_kernel(
+        wide_momenta,
+        [moment_kind, moment_kind, wide_kind, wide_kind],
+        scalars=1,
+        ties=d_attended_pieces[1:],
+        far=(1, 2),
+        far_out=(0, 1),
+    )(place, summed, ffn_mom)
+    far_rows = swap(far_send, "shard", shards // 2)
+
     packed_rows = depth + 16
     kept, sent, d_proj = run_kernel(
         attention_backward,
@@ -971,34 +1009,27 @@
         ],
         scalars=1,
         scratch=[pltpu.VMEM((slots * rows, width), bf16), pltpu.VMEM((16, width), jnp.float32)],
-        far=(5, 6, 7, 8, 9, 10, 11, 13, 14, 15),
+        far=(1, 2, 3, 4, 9, 10, 11, 5, 6, 7, 8, 13, 14, 15),
         far_out=(0, 2),
+        late=(5, 6, 7, 8, 13, 14, 15),
+        ties=[far_send],
     )(
         place, *d_attended_pieces, *mixed_pieces, out_b, qkv, id_column, id_row, tokens_b,
         sums_one, sums_two, d_bias_up,
     )
-    moment_kind = jax.ShapeDtypeStruct(ffn_mom.shape, ffn_mom.dtype)
-    wide_kind = jax.ShapeDtypeStruct((depth, hidden), bf16)
-    grad_ffn, new_ffn_mom, mine, far = run_kernel(
-        wide_momenta,
-        [moment_kind, moment_kind, wide_kind, wide_kind],
-        scalars=1,
-        ties=[kept],
-        far=(1, 2),
-        far_out=(0, 1),
-    )(place, summed, ffn_mom)
-    far_rows = swap(far, "shard", shards // 2)
-    wide_rows = jnp.concatenate([mine, far_rows], axis=1)
+    (wide_rows,) = run_kernel(
+        join_wide, [jax.ShapeDtypeStruct((depth, 2 * hidden), bf16)], ties=[kept], far_out=(0,)
+    )(mine, far_rows)
     wide = lax.all_gather(wide_rows, "dp", axis=0, tiled=True)
-
     block_kind = jax.ShapeDtypeStruct((packed_rows, width), bf16)
     total, *blocks = run_kernel(
         pair_sum, [jax.ShapeDtypeStruct((packed_rows, width), jnp.float32)] + [block_kind] * 3, scalars=1, far=(1,)
     )(place, kept, swap(sent, "dp", 1))
-    parts = run_kernel(token_parts, part_kinds, scalars=1, scratch=[moving], ties=[total], far=(1, 2))(
-        place, d_proj, weights
-    )
-    d_tokens = d_first_in + sum(part.astype(jnp.float32) for part in send_parts(parts, "shard"))
+    (part,) = run_kernel(
+        token_part, [whole_b], ties=[total], far=(0, 1), far_out=(0,), lanes={1: proj_lanes}
+    )(d_proj, weights)
+    d_tokens = lax.psum_scatter(part, "shard", scatter_dimension=0, tiled=True)
+    d_tokens = d_first_in + d_tokens.astype(jnp.float32)
     block_kind = jax.ShapeDtypeStruct((packed_rows, own), bf16)
     like = [jax.ShapeDtypeStruct(each.shape, each.dtype) for each in (qkv_mom, out_mom)]
     grad_qkv, grad_wout, new_qkv_mom, new_out_mom, *blocks = run_kernel(
@@ -1018,7 +1049,6 @@
         [row_kind, row_kind, jax.ShapeDtypeStruct((packed_rows - depth, own), jnp.float32)],
         scalars=1,
         scratch=[pltpu.VMEM((depth, width), bf16)],
-        ties=[d_tokens],
     )(place, *send_parts(blocks, "shard"), gram_rows, swap(gram_rows, "shard", 1))
     grad_vec = grad_vec[:vec_rows, :vec_own]
     d_tokens = d_tokens.reshape(tokens.shape)
@@ -1032,23 +1062,26 @@
         [state_kind, state_kind],
         scalars=1,
         scratch=[pltpu.VMEM((width, width), bf16), pltpu.VMEM((width, width), jnp.float32)]
-        + [pltpu.VMEM((width, width), bf16)] * NS_STEPS,
+        + [pltpu.VMEM((width, width), bf16)] * (NS_STEPS - 1),
         far=(5,),
+        late=(5,),
     )(place, *pair_pieces, wide)
     block_kind = jax.ShapeDtypeStruct((depth, own), bf16)
     wide_kind = jax.ShapeDtypeStruct((depth, hidden), bf16)
-    *blocks, mine, far = run_kernel(
-        split_state, [block_kind] * shards + [wide_kind, wide_kind], scalars=1
+    kinds = [block_kind] * shards + [wide_kind]
+    kinds[shards // 2] = jax.ShapeDtypeStruct((depth, hidden + own), bf16)
+    *blocks, mine = run_kernel(
+        split_state, kinds, scalars=1
     )(place, kept, swap(sent, "dp", 1))
     qkv_new, out_new, ffn_new = run_kernel(
         new_weights,
         [jax.ShapeDtypeStruct(each.shape, each.dtype) for each in (qkv_w, out_w, ffn_w)],
         scalars=1,
         scratch=[pltpu.VMEM((shards, depth, own), jnp.float32)],
-        far=(7, 8, 9),
+        far=(6, 7, 8),
         far_out=(0, 1, 2),
     )(
-        place, *send_parts(blocks, "shard"), mine, swap(far, "shard", shards // 2), qkv_w, out_w, ffn_w
+        place, *send_parts(blocks, "shard"), mine, qkv_w, out_w, ffn_w
     )
 
     token_count = micro * rows * groups * shards

time: 299 us -> 296 us (0.990)
  Pallas kernels: 69 us -> 65.1 us
  starting transfers between devices: 61.4 us -> 58.4 us
  waiting for transfers between devices: 141 us -> 144 us
    ppermute x15 -> x14, waiting for transfers between devices: 48.2 us -> 29.3 us  [swap(): lax.ppermute(block, axis, [(i, i ^ bit) for i in range(lax.axis_size(axis...]
    ppermute x15 -> x12, waiting for transfers between devices: 28.3 us -> 41 us  [send_parts(): lax.ppermute(parts[step], axis, [(i, (i + step) % count) for i in range(c...]
    all_gather x1, waiting for transfers between devices: 0.02 us -> 8.33 us  [split_device(): wide = lax.all_gather(wide_rows, 'dp', axis=0, tiled=True)]
    pallas_call x17 -> x18, Pallas kernels: 69 us -> 65.1 us  [call(): pl.pallas_call(whole, out_shape=kinds, in_specs=[pl.BlockSpec(memory_spac...]
    ppermute x15 -> x12, starting transfers between devices: 22.4 us -> 19.5 us  [send_parts(): lax.ppermute(parts[step], axis, [(i, (i + step) % count) for i in range(c...]
    ppermute x15 -> x14, starting transfers between devices: 12.8 us -> 12.8 us  [swap(): lax.ppermute(block, axis, [(i, i ^ bit) for i in range(lax.axis_size(axis...]
  transfers between devices with their start and end apart: 46 -> 43, of which waited for: 27 -> 28; matrix products, arithmetic and copies ran while one was open for 2% -> 3% of each run, Pallas kernels for 10% -> 14%
where the time goes in v3:
time: 296 us; the launch traced here: 295 us
  waiting for transfers between devices  144 us (49%)
  Pallas kernels  65.1 us (22%)
  starting transfers between devices  58.4 us (20%)
  between operations  14.4 us (5%)
  local copies, waits for them, and re-layouts  7.91 us (3%)
  other arithmetic  5.23 us (2%)
    pallas_call x18, Pallas kernels, call(): pl.pallas_call(whole, out_shape=kinds, in_specs=[pl.BlockSpec(memory_spac...  65.1 us
    ppermute x12, waiting for transfers between devices, send_parts(): lax.ppermute(parts[step], axis, [(i, (i + step) % count) for i in range(c...  41 us
    ppermute x9, waiting for transfers between devices, pieces_of(): lax.ppermute(block, axis, [(i, (i + step) % count) for i in range(count)])  34.4 us
    ppermute x14, waiting for transfers between devices, swap(): lax.ppermute(block, axis, [(i, i ^ bit) for i in range(lax.axis_size(axis...  29.3 us
    ppermute x12, starting transfers between devices, send_parts(): lax.ppermute(parts[step], axis, [(i, (i + step) % count) for i in range(c...  19.5 us
    ppermute x9, starting transfers between devices, pieces_of(): lax.ppermute(block, axis, [(i, (i + step) % count) for i in range(count)])  18 us
    all_gather x1, waiting for transfers between devices, split_device(): out_b = lax.all_gather(out_part, 'dp', axis=0, tiled=True)  15.3 us
    ppermute x3, waiting for transfers between devices, gather_direct(): lax.ppermute(block, axis, [(i, (i + step) % count) for i in range(count)])  14 us
  transfers between devices with their start and end apart: 43, of which 28 were waited for; matrix products, arithmetic and copies ran while one was open for 3% of the time, Pallas kernels for 14%

profile of v3, /device:TPU:0, one launch (start us, length us, event | category | flops | bytes accessed | tf_op | source)
XLA Modules:
  0.0 295.3 jit_solution(5818422553709269856)
XLA Ops:
  10.9 4.1 %collective-permute-start.1 = (bf16[160,768]{1,0:T(8,128)(2,1)S(1)}, bf16[160,768]{1,0:T(8,128)(2,1)S(1)}, u32[]{:S(2)}, u32[]{:S(2)}) collective-permute-start(bf16[160,768]{1,0:T(8,128)(2,1)S(1)} %pad_maximum_fusion), channel_id=1, source_target_pairs={{0,2},{1,3},{2,0},{3,1},{4,6},{5,7},{6,4},{7,5},{8,10},{9,11},{10,... | collective-permute-start | bytes 737288 | tf_op jit(solution)/shard_map/ppermute | solution.py:386
  16.6 2.2 collective-permute-start.2
  19.1 9.5 %collective-permute-done = bf16[160,768]{1,0:T(8,128)(2,1)S(1)} collective-permute-done((bf16[160,768]{1,0:T(8,128)(2,1)S(1)}, bf16[160,768]{1,0:T(8,128)(2,1)S(1)}, u32[]{:S(2)}, u32[]{:S(2)}) %collective-permute-start) | collective-permute-done | bytes 245792 | tf_op jit(solution)/shard_map/ppermute | solution.py:386
  28.6 3.8 %collective-permute-done.1 = bf16[160,768]{1,0:T(8,128)(2,1)S(1)} collective-permute-done((bf16[160,768]{1,0:T(8,128)(2,1)S(1)}, bf16[160,768]{1,0:T(8,128)(2,1)S(1)}, u32[]{:S(2)}, u32[]{:S(2)}) %collective-permute-start.1) | collective-permute-done | bytes 245792 | tf_op jit(solution)/shard_map/ppermute | solution.py:386
  38.1 2.1 collective-permute-done.4
  45.0 1.8 all-gather.4.cloned.1.call-done.refs_2_.refs_8_.refs_6_.refs_1_
  46.7 4.8 %shard_map.218 = (bf16[512,576]{1,0:T(8,128)(2,1)}, bf16[256,384]{1,0:T(8,128)(2,1)S(1)}) custom-call(s32[3]{0:T(128)S(1)} %pad_add_fusion.refs_0_, bf16[512,768]{1,0:T(8,128)(2,1)} %bitcast.37, bf16[768,2176]{1,0:T(8,128)(2,1)} %all-gather.4.cloned.1.call-done.refs_2_.refs_8_.refs_6_.refs_1_, f32[1,576]{1,0:T(1,128)S(1)} %broadcast_in_dim.38.refs_3_, ...), custom_call_target="tpu_custom_call" | custom-call | tf_op jit(solution)/shard_map/pallas_call | solution.py:817
  51.6 3.4 %collective-permute-start.8 = (bf16[256,384]{1,0:T(8,128)(2,1)S(1)}, bf16[256,384]{1,0:T(8,128)(2,1)S(1)}, u32[]{:S(2)}, u32[]{:S(2)}) collective-permute-start(bf16[256,384]{1,0:T(8,128)(2,1)S(1)} %get-tuple-element.70.refs_1_.refs_5_), channel_id=1, source_target_pairs={{0,3},{1,0},{2,1},{3,2},{4,7},{5,4},{6,5},{7,6},{8,11},{9,8},{10,9... | collective-permute-start | bytes 589832 | tf_op jit(solution)/shard_map/ppermute | solution.py:394
  56.0 1.9 collective-permute-start.6
  58.0 15.3 %all-gather.6.cloned.1.call-done.refs_5_.refs_9_ = bf16[768,768]{1,0:T(8,128)(2,1)} async-done(((bf16[96,768]{1,0:T(8,128)(2,1)}), bf16[768,768]{1,0:T(8,128)(2,1)}) %all-gather.6.cloned.1.call-update) | async-done | bytes 1179664 | tf_op jit(solution)/shard_map/all_gather | solution.py:922
  73.3 6.2 %shard_map.219 = (bf16[512,768]{1,0:T(8,128)(2,1)S(1)}, bf16[512,768]{1,0:T(8,128)(2,1)S(1)}, f32[512,768]{1,0:T(8,128)S(1)}, f32[128,768]{1,0:T(8,128)S(1)}, f3...) custom-call(s32[3]{0:T(128)S(1)} %pad_add_fusion.refs_0_, ...), custom_call_target="tpu_custom_call" | custom-call | tf_op jit(solution)/shard_map/pallas_call | solution.py:817
  81.1 2.4 collective-permute-start.10
  84.9 4.3 %collective-permute-done.9.refs_2_ = bf16[128,768]{1,0:T(8,128)(2,1)S(1)} collective-permute-done((bf16[128,768]{1,0:T(8,128)(2,1)S(1)}, bf16[128,768]{1,0:T(8,128)(2,1)S(1)}, u32[]{:S(2)}, u32[]{:S(2)}) %collective-permute-start.9) | collective-permute-done | bytes 196640 | tf_op jit(solution)/shard_map/ppermute | solution.py:402
  89.3 7.8 %collective-permute-done.10.refs_3_ = bf16[128,768]{1,0:T(8,128)(2,1)S(1)} collective-permute-done((bf16[128,768]{1,0:T(8,128)(2,1)S(1)}, bf16[128,768]{1,0:T(8,128)(2,1)S(1)}, u32[]{:S(2)}, u32[]{:S(2)}) %collective-permute-start.10) | collective-permute-done | bytes 196640 | tf_op jit(solution)/shard_map/ppermute | solution.py:402
  97.1 3.1 %shard_map.220 = (bf16[128,768]{1,0:T(8,128)(2,1)}, bf16[128,768]{1,0:T(8,128)(2,1)S(1)}, f32[128,768]{1,0:T(8,128)}, f32[8,768]{1,0:T(8,128)}) custom-call(s32[3]{0:T(128)S(1)} %pad_add_fusion.refs_0_, f32[128,768]{1,0:T(8,128)S(1)} %get-tuple-element.71.refs_1_, bf16[128,768]{1,0:T(8,128)(2,1)S(1)} %collective-permute-done.9.refs_2_, ...), custom_call_target="tpu_custom_call" | custom-call | tf_op jit(solution)/shard_map/pallas_call | solution.py:817
  100.1 5.6 %collective-permute-start.14 = (bf16[128,768]{1,0:T(8,128)(2,1)S(1)}, bf16[128,768]{1,0:T(8,128)(2,1)S(1)}, u32[]{:S(2)}, u32[]{:S(2)}) collective-permute-start(bf16[128,768]{1,0:T(8,128)(2,1)S(1)} %get-tuple-element.77.refs_1_), channel_id=1, source_target_pairs={{0,3},{1,0},{2,1},{3,2},{4,7},{5,4},{6,5},{7,6},{8,11},{9,8},{10,9... | collective-permute-start | bytes 589832 | tf_op jit(solution)/shard_map/ppermute | solution.py:394
  106.4 4.8 %collective-permute-done.14.refs_4_ = bf16[128,768]{1,0:T(8,128)(2,1)S(1)} collective-permute-done((bf16[128,768]{1,0:T(8,128)(2,1)S(1)}, bf16[128,768]{1,0:T(8,128)(2,1)S(1)}, u32[]{:S(2)}, u32[]{:S(2)}) %collective-permute-start.14) | collective-permute-done | bytes 196640 | tf_op jit(solution)/shard_map/ppermute | solution.py:394
  111.2 12.6 %collective-permute-done.13.refs_3_ = bf16[128,768]{1,0:T(8,128)(2,1)S(1)} collective-permute-done((bf16[128,768]{1,0:T(8,128)(2,1)S(1)}, bf16[128,768]{1,0:T(8,128)(2,1)S(1)}, u32[]{:S(2)}, u32[]{:S(2)}) %collective-permute-start.13) | collective-permute-done | bytes 196640 | tf_op jit(solution)/shard_map/ppermute | solution.py:394
  123.8 4.9 %shard_map.221 = (bf16[512,768]{1,0:T(8,128)(2,1)S(1)}, bf16[512,768]{1,0:T(8,128)(2,1)S(1)}, f32[1,768]{1,0:T(1,128)}, f32[128,768]{1,0:T(8,128)}, bf16[128,768...) custom-call(s32[3]{0:T(128)S(1)} %pad_add_fusion.refs_0_, ...), custom_call_target="tpu_custom_call" | custom-call | tf_op jit(solution)/shard_map/pallas_call | solution.py:817
  128.7 2.9 shard_map.223
  133.6 2.8 collective-permute-start.17
  136.5 5.8 %collective-permute-done.15.refs_1_ = bf16[128,768]{1,0:T(8,128)(2,1)S(1)} collective-permute-done((bf16[128,768]{1,0:T(8,128)(2,1)S(1)}, bf16[128,768]{1,0:T(8,128)(2,1)S(1)}, u32[]{:S(2)}, u32[]{:S(2)}) %collective-permute-start.15) | collective-permute-done | bytes 196640 | tf_op jit(solution)/shard_map/ppermute | solution.py:402
  142.3 6.7 %collective-permute-done.16.refs_2_ = bf16[128,768]{1,0:T(8,128)(2,1)S(1)} collective-permute-done((bf16[128,768]{1,0:T(8,128)(2,1)S(1)}, bf16[128,768]{1,0:T(8,128)(2,1)S(1)}, u32[]{:S(2)}, u32[]{:S(2)}) %collective-permute-start.16) | collective-permute-done | bytes 196640 | tf_op jit(solution)/shard_map/ppermute | solution.py:402
  148.9 2.5 shard_map.222
  151.4 4.1 %collective-permute-start.20 = (bf16[128,768]{1,0:T(8,128)(2,1)}, bf16[128,768]{1,0:T(8,128)(2,1)S(1)}, u32[]{:S(2)}, u32[]{:S(2)}) collective-permute-start(bf16[128,768]{1,0:T(8,128)(2,1)} %get-tuple-element.85.refs_1_), channel_id=1, source_target_pairs={{0,3},{1,0},{2,1},{3,2},{4,7},{5,4},{6,5},{7,6},{8,11},{9,8},{10,9... | collective-permute-start | bytes 589832 | tf_op jit(solution)/shard_map/ppermute | solution.py:394
  156.8 4.5 %collective-permute-done.20.refs_5_.refs_4_ = bf16[128,768]{1,0:T(8,128)(2,1)S(1)} collective-permute-done((bf16[128,768]{1,0:T(8,128)(2,1)}, bf16[128,768]{1,0:T(8,128)(2,1)S(1)}, u32[]{:S(2)}, u32[]{:S(2)}) %collective-permute-start.20) | collective-permute-done | bytes 196640 | tf_op jit(solution)/shard_map/ppermute | solution.py:394
  161.3 12.5 %collective-permute-done.19.refs_4_.refs_3_ = bf16[128,768]{1,0:T(8,128)(2,1)S(1)} collective-permute-done((bf16[128,768]{1,0:T(8,128)(2,1)}, bf16[128,768]{1,0:T(8,128)(2,1)S(1)}, u32[]{:S(2)}, u32[]{:S(2)}) %collective-permute-start.19) | collective-permute-done | bytes 196640 | tf_op jit(solution)/shard_map/ppermute | solution.py:394
  173.8 2.9 shard_map.224
  177.4 12.0 %shard_map.225 = (f32[4,112,768]{2,1,0:T(8,128)}, bf16[4,112,768]{2,1,0:T(8,128)(2,1)S(1)}, bf16[512,576]{1,0:T(8,128)(2,1)}) custom-call(s32[3]{0:T(128)S(1)} %pad_add_fusion.refs_0_, bf16[128,768]{1,0:T(8,128)(2,1)} %get-tuple-element.85.refs_1_, bf16[128,768]{1,0:T(8,128)(2,1)} %copy-done.8, bf16[128,768]{1,0:T(8,128)(2,1)} %copy-done.7, ...), custom_call_target="tpu_custom_call" | custom-call | tf_op jit(solution)/shard_map/pallas_call | solution.py:817
  191.6 2.1 collective-permute-done.21.refs_2_
  193.8 2.1 shard_map.226
  195.8 3.2 %shard_map.227 = bf16[512,768]{1,0:T(8,128)(2,1)} custom-call(bf16[512,576]{1,0:T(8,128)(2,1)} %get-tuple-element.95.refs_0_, bf16[768,2176]{1,0:T(8,128)(2,1)} %all-gather.4.cloned.1.call-done.refs_2_.refs_8_.refs_6_.refs_1_, f32[112,768]{1,0:T(8,128)S(1)} %get-tuple-element.98.refs_2_.refs_1_), custom_call_target="tpu_custom_call" | custom-call | tf_op jit(solution)/shard_map/pallas_call | solution.py:817
  202.6 5.4 %collective-permute-done.22.refs_2_ = bf16[112,768]{1,0:T(8,128)(2,1)S(1)} collective-permute-done((bf16[112,768]{1,0:T(8,128)(2,1)S(1)}, bf16[112,768]{1,0:T(8,128)(2,1)S(1)}, u32[]{:S(2)}, u32[]{:S(2)}) %collective-permute-start.22) | collective-permute-done | bytes 172064 | tf_op jit(solution)/shard_map/ppermute | solution.py:408
  208.0 4.2 %collective-permute-done.24.refs_4_ = bf16[112,768]{1,0:T(8,128)(2,1)S(1)} collective-permute-done((bf16[112,768]{1,0:T(8,128)(2,1)S(1)}, bf16[112,768]{1,0:T(8,128)(2,1)S(1)}, u32[]{:S(2)}, u32[]{:S(2)}) %collective-permute-start.24) | collective-permute-done | bytes 172064 | tf_op jit(solution)/shard_map/ppermute | solution.py:408
  212.2 2.6 shard_map.228
  214.8 8.3 %all-gather.8.cloned.1.call-done.refs_1_.refs_5_ = bf16[768,1536]{1,0:T(8,128)(2,1)} async-done(((bf16[96,1536]{1,0:T(8,128)(2,1)}), bf16[768,1536]{1,0:T(8,128)(2,1)}) %all-gather.8.cloned.1.call-update) | async-done | bytes 2359312 | tf_op jit(solution)/shard_map/all_gather | solution.py:1023
  223.1 2.6 shard_map.230.refs_5_
  227.9 2.4 collective-permute-start.26
  230.3 2.4 collective-permute-start.27
  232.7 3.2 %collective-permute-done.25.refs_2_ = bf16[112,192]{1,0:T(8,128)(2,1)S(1)} collective-permute-done((bf16[112,192]{1,0:T(8,128)(2,1)S(1)}, bf16[112,192]{1,0:T(8,128)(2,1)S(1)}, u32[]{:S(2)}, u32[]{:S(2)}) %collective-permute-start.25) | collective-permute-done | bytes 43040 | tf_op jit(solution)/shard_map/ppermute | solution.py:402
  236.6 1.8 collective-permute-done.27.refs_4_
  242.0 2.4 collective-permute-start.32
  245.2 7.3 %collective-permute-done.33.refs_4_ = bf16[192,768]{1,0:T(8,128)(2,1)S(1)} collective-permute-done((bf16[192,768]{1,0:T(8,128)(2,1)S(1)}, bf16[192,768]{1,0:T(8,128)(2,1)S(1)}, u32[]{:S(2)}, u32[]{:S(2)}) %collective-permute-start.33) | collective-permute-done | bytes 294944 | tf_op jit(solution)/shard_map/ppermute | solution.py:408
  252.5 5.3 %collective-permute-done.32.refs_3_ = bf16[192,768]{1,0:T(8,128)(2,1)S(1)} collective-permute-done((bf16[192,768]{1,0:T(8,128)(2,1)S(1)}, bf16[192,768]{1,0:T(8,128)(2,1)S(1)}, u32[]{:S(2)}, u32[]{:S(2)}) %collective-permute-start.32) | collective-permute-done | bytes 294944 | tf_op jit(solution)/shard_map/ppermute | solution.py:408
  257.7 9.4 %shard_map.233 = (bf16[96,1536]{1,0:T(8,128)(2,1)S(1)}, bf16[96,1536]{1,0:T(8,128)(2,1)S(1)}) custom-call(s32[3]{0:T(128)S(1)} %pad_add_fusion.refs_0_, bf16[192,768]{1,0:T(8,128)(2,1)S(1)} %shard_map.232.refs_1_, bf16[192,768]{1,0:T(8,128)(2,1)S(1)} %collective-permute-done.31.refs_2_, bf16[192,768]{1,0:T(8,128)(2,1)S(1)} %collective-permute-done.32.refs_3_, ...), custom_call_target="tpu_custom_call" | custom-call | tf_op jit(solution)/shard_map/pallas_call | solution.py:817
  271.2 2.9 collective-permute-start.37
  276.5 9.4 %collective-permute-done.36.refs_3_ = bf16[96,960]{1,0:T(8,128)(2,1)S(1)} collective-permute-done((bf16[96,960]{1,0:T(8,128)(2,1)S(1)}, bf16[96,960]{1,0:T(8,128)(2,1)S(1)}, u32[]{:S(2)}, u32[]{:S(2)}) %collective-permute-start.36) | collective-permute-done | bytes 184352 | tf_op jit(solution)/shard_map/ppermute | solution.py:402
  285.9 2.8 shard_map.235
  (164 shorter events, 43.7 us)
Async XLA Ops:
  7.2 39.5 %all-gather.4.cloned.1.call-start = ((), (), s32[]{:S(2)}) async-start(), calls=%async_computation.2 | async-start | bytes 3760128 | tf_op jit(solution)/shard_map/all_gather | solution.py:904
  10.4 62.9 %all-gather.6.cloned.1.call-start = ((), (), s32[]{:S(2)}) async-start(), calls=%async_computation.3 | async-start | bytes 1327104 | tf_op jit(solution)/shard_map/all_gather | solution.py:922
  10.9 21.5 %collective-permute-start.1 = (bf16[160,768]{1,0:T(8,128)(2,1)S(1)}, bf16[160,768]{1,0:T(8,128)(2,1)S(1)}, u32[]{:S(2)}, u32[]{:S(2)}) collective-permute-start(bf16[160,768]{1,0:T(8,128)(2,1)S(1)} %pad_maximum_fusion), channel_id=1, source_target_pairs={{0,2},{1,3},{2,0},{3,1},{4,6},{5,7},{6,4},{7,5},{8,10},{9,11},{10,... | collective-permute-start | bytes 737288 | tf_op jit(solution)/shard_map/ppermute | solution.py:386
  15.0 13.5 %collective-permute-start = (bf16[160,768]{1,0:T(8,128)(2,1)S(1)}, bf16[160,768]{1,0:T(8,128)(2,1)S(1)}, u32[]{:S(2)}, u32[]{:S(2)}) collective-permute-start(bf16[160,768]{1,0:T(8,128)(2,1)S(1)} %pad_maximum_fusion), channel_id=1, source_target_pairs={{0,1},{1,2},{2,3},{3,0},{4,5},{5,6},{6,7},{7,4},{8,9},{9,10},{10,1... | collective-permute-start | bytes 737288 | tf_op jit(solution)/shard_map/ppermute | solution.py:386
  16.6 16.5 %collective-permute-start.2 = (bf16[160,768]{1,0:T(8,128)(2,1)S(1)}, bf16[160,768]{1,0:T(8,128)(2,1)S(1)}, u32[]{:S(2)}, u32[]{:S(2)}) collective-permute-start(bf16[160,768]{1,0:T(8,128)(2,1)S(1)} %pad_maximum_fusion), channel_id=1, source_target_pairs={{0,3},{1,0},{2,1},{3,2},{4,7},{5,4},{6,5},{7,6},{8,11},{9,8},{10,9... | collective-permute-start | bytes 737288 | tf_op jit(solution)/shard_map/ppermute | solution.py:386
  34.5 139.4 %reduce-scatter.3.cloned.1.call-start = ((), (), s32[]{:S(2)}) async-start(), calls=%async_computation.4 | async-start | bytes 2654208 | tf_op jit(solution)/shard_map/reduce_scatter | solution.py:985
  35.1 1.2 collective-permute-start.3
  36.3 3.9 %collective-permute-start.4 = (bf16[2,12,96]{2,1,0:T(8,128)(2,1)S(1)}, bf16[2,12,96]{2,1,0:T(8,128)(2,1)S(1)}, u32[]{:S(2)}, u32[]{:S(2)}) collective-permute-start(bf16[2,12,96]{2,1,0:T(8,128)(2,1)S(1)} %pad_maximum_fusion.2), channel_id=1, source_target_pairs={{0,8},{4,12},{8,0},{12,4},{16,24},{20,28},{24,16},{28,20},{1,9},{5... | collective-permute-start | bytes 13832 | tf_op jit(solution)/shard_map/ppermute | solution.py:408
  40.2 4.1 %collective-permute-start.5 = (bf16[4,12,96]{2,1,0:T(8,128)(2,1)S(1)}, bf16[4,12,96]{2,1,0:T(8,128)(2,1)S(1)}, u32[]{:S(2)}, u32[]{:S(2)}) collective-permute-start(bf16[4,12,96]{2,1,0:T(8,128)(2,1)S(1)} %pad_maximum_fusion.1), channel_id=1, source_target_pairs={{0,16},{4,20},{8,24},{12,28},{16,0},{20,4},{24,8},{28,12},{1,17},{... | collective-permute-start | bytes 27656 | tf_op jit(solution)/shard_map/ppermute | solution.py:408
  51.6 27.9 %copy-start.2 = (bf16[256,384]{1,0:T(8,128)(2,1)}, bf16[256,384]{1,0:T(8,128)(2,1)S(1)}, u32[]{:S(2)}) copy-start(bf16[256,384]{1,0:T(8,128)(2,1)S(1)} %get-tuple-element.70.refs_1_.refs_5_) | copy-start | bytes 589828
  51.6 21.7 %collective-permute-start.8 = (bf16[256,384]{1,0:T(8,128)(2,1)S(1)}, bf16[256,384]{1,0:T(8,128)(2,1)S(1)}, u32[]{:S(2)}, u32[]{:S(2)}) collective-permute-start(bf16[256,384]{1,0:T(8,128)(2,1)S(1)} %get-tuple-element.70.refs_1_.refs_5_), channel_id=1, source_target_pairs={{0,3},{1,0},{2,1},{3,2},{4,7},{5,4},{6,5},{7,6},{8,11},{9,8},{10,9... | collective-permute-start | bytes 589832 | tf_op jit(solution)/shard_map/ppermute | solution.py:394
  55.0 18.3 %collective-permute-start.7 = (bf16[256,384]{1,0:T(8,128)(2,1)S(1)}, bf16[256,384]{1,0:T(8,128)(2,1)S(1)}, u32[]{:S(2)}, u32[]{:S(2)}) collective-permute-start(bf16[256,384]{1,0:T(8,128)(2,1)S(1)} %get-tuple-element.70.refs_1_.refs_5_), channel_id=1, source_target_pairs={{0,2},{1,3},{2,0},{3,1},{4,6},{5,7},{6,4},{7,5},{8,10},{9,11},{10,... | collective-permute-start | bytes 589832 | tf_op jit(solution)/shard_map/ppermute | solution.py:394
  56.0 17.3 %collective-permute-start.6 = (bf16[256,384]{1,0:T(8,128)(2,1)S(1)}, bf16[256,384]{1,0:T(8,128)(2,1)S(1)}, u32[]{:S(2)}, u32[]{:S(2)}) collective-permute-start(bf16[256,384]{1,0:T(8,128)(2,1)S(1)} %get-tuple-element.70.refs_1_.refs_5_), channel_id=1, source_target_pairs={{0,1},{1,2},{2,3},{3,0},{4,5},{5,6},{6,7},{7,4},{8,9},{9,10},{10,1... | collective-permute-start | bytes 589832 | tf_op jit(solution)/shard_map/ppermute | solution.py:394
  79.6 49.1 %copy-start.1 = (f32[128,768]{1,0:T(8,128)}, f32[128,768]{1,0:T(8,128)S(1)}, u32[]{:S(2)}) copy-start(f32[128,768]{1,0:T(8,128)S(1)} %get-tuple-element.75.refs_5_) | copy-start | bytes 1179652
  79.6 9.7 %collective-permute-start.9 = (bf16[128,768]{1,0:T(8,128)(2,1)S(1)}, bf16[128,768]{1,0:T(8,128)(2,1)S(1)}, u32[]{:S(2)}, u32[]{:S(2)}) collective-permute-start(bf16[128,768]{1,0:T(8,128)(2,1)S(1)} %get-tuple-element.72), channel_id=1, source_target_pairs={{0,1},{1,2},{2,3},{3,0},{4,5},{5,6},{6,7},{7,4},{8,9},{9,10},{10,1... | collective-permute-start | bytes 589832 | tf_op jit(solution)/shard_map/ppermute | solution.py:402
  81.1 16.0 %collective-permute-start.10 = (bf16[128,768]{1,0:T(8,128)(2,1)S(1)}, bf16[128,768]{1,0:T(8,128)(2,1)S(1)}, u32[]{:S(2)}, u32[]{:S(2)}) collective-permute-start(bf16[128,768]{1,0:T(8,128)(2,1)S(1)} %get-tuple-element.73), channel_id=1, source_target_pairs={{0,2},{1,3},{2,0},{3,1},{4,6},{5,7},{6,4},{7,5},{8,10},{9,11},{10,... | collective-permute-start | bytes 589832 | tf_op jit(solution)/shard_map/ppermute | solution.py:402
  83.5 13.5 %collective-permute-start.11 = (bf16[128,768]{1,0:T(8,128)(2,1)S(1)}, bf16[128,768]{1,0:T(8,128)(2,1)S(1)}, u32[]{:S(2)}, u32[]{:S(2)}) collective-permute-start(bf16[128,768]{1,0:T(8,128)(2,1)S(1)} %get-tuple-element.74), channel_id=1, source_target_pairs={{0,3},{1,0},{2,1},{3,2},{4,7},{5,4},{6,5},{7,6},{8,11},{9,8},{10,9... | collective-permute-start | bytes 589832 | tf_op jit(solution)/shard_map/ppermute | solution.py:402
  100.1 11.0 %collective-permute-start.14 = (bf16[128,768]{1,0:T(8,128)(2,1)S(1)}, bf16[128,768]{1,0:T(8,128)(2,1)S(1)}, u32[]{:S(2)}, u32[]{:S(2)}) collective-permute-start(bf16[128,768]{1,0:T(8,128)(2,1)S(1)} %get-tuple-element.77.refs_1_), channel_id=1, source_target_pairs={{0,3},{1,0},{2,1},{3,2},{4,7},{5,4},{6,5},{7,6},{8,11},{9,8},{10,9... | collective-permute-start | bytes 589832 | tf_op jit(solution)/shard_map/ppermute | solution.py:394
  105.8 18.0 %collective-permute-start.13 = (bf16[128,768]{1,0:T(8,128)(2,1)S(1)}, bf16[128,768]{1,0:T(8,128)(2,1)S(1)}, u32[]{:S(2)}, u32[]{:S(2)}) collective-permute-start(bf16[128,768]{1,0:T(8,128)(2,1)S(1)} %get-tuple-element.77.refs_1_), channel_id=1, source_target_pairs={{0,2},{1,3},{2,0},{3,1},{4,6},{5,7},{6,4},{7,5},{8,10},{9,11},{10,... | collective-permute-start | bytes 589832 | tf_op jit(solution)/shard_map/ppermute | solution.py:394
  106.3 17.4 %collective-permute-start.12 = (bf16[128,768]{1,0:T(8,128)(2,1)S(1)}, bf16[128,768]{1,0:T(8,128)(2,1)S(1)}, u32[]{:S(2)}, u32[]{:S(2)}) collective-permute-start(bf16[128,768]{1,0:T(8,128)(2,1)S(1)} %get-tuple-element.77.refs_1_), channel_id=1, source_target_pairs={{0,1},{1,2},{2,3},{3,0},{4,5},{5,6},{6,7},{7,4},{8,9},{9,10},{10,1... | collective-permute-start | bytes 589832 | tf_op jit(solution)/shard_map/ppermute | solution.py:394
  131.6 45.7 %copy-start.9 = (f32[1,768]{1,0:T(1,128)S(1)}, f32[1,768]{1,0:T(1,128)}, u32[]{:S(2)}) copy-start(f32[1,768]{1,0:T(1,128)} %get-tuple-element.89.refs_16_) | copy-start | bytes 9220
  131.7 91.5 %all-gather.8.cloned.1.call-start = ((), (), s32[]{:S(2)}) async-start(), calls=%async_computation.6 | async-start | bytes 2654208 | tf_op jit(solution)/shard_map/all_gather | solution.py:1023
  132.5 9.7 %collective-permute-start.15 = (bf16[128,768]{1,0:T(8,128)(2,1)S(1)}, bf16[128,768]{1,0:T(8,128)(2,1)S(1)}, u32[]{:S(2)}, u32[]{:S(2)}) collective-permute-start(bf16[128,768]{1,0:T(8,128)(2,1)S(1)} %copy-done.17), channel_id=1, source_target_pairs={{0,1},{1,2},{2,3},{3,0},{4,5},{5,6},{6,7},{7,4},{8,9},{9,10},{10,1... | collective-permute-start | bytes 589832 | tf_op jit(solution)/shard_map/ppermute | solution.py:402
  132.6 16.3 %collective-permute-start.16 = (bf16[128,768]{1,0:T(8,128)(2,1)S(1)}, bf16[128,768]{1,0:T(8,128)(2,1)S(1)}, u32[]{:S(2)}, u32[]{:S(2)}) collective-permute-start(bf16[128,768]{1,0:T(8,128)(2,1)S(1)} %copy-done.16), channel_id=1, source_target_pairs={{0,2},{1,3},{2,0},{3,1},{4,6},{5,7},{6,4},{7,5},{8,10},{9,11},{10,... | collective-permute-start | bytes 589832 | tf_op jit(solution)/shard_map/ppermute | solution.py:402
  133.6 15.3 %collective-permute-start.17 = (bf16[128,768]{1,0:T(8,128)(2,1)S(1)}, bf16[128,768]{1,0:T(8,128)(2,1)S(1)}, u32[]{:S(2)}, u32[]{:S(2)}) collective-permute-start(bf16[128,768]{1,0:T(8,128)(2,1)S(1)} %copy-done.15), channel_id=1, source_target_pairs={{0,3},{1,0},{2,1},{3,2},{4,7},{5,4},{6,5},{7,6},{8,11},{9,8},{10,9... | collective-permute-start | bytes 589832 | tf_op jit(solution)/shard_map/ppermute | solution.py:402
  151.4 9.8 %collective-permute-start.20 = (bf16[128,768]{1,0:T(8,128)(2,1)}, bf16[128,768]{1,0:T(8,128)(2,1)S(1)}, u32[]{:S(2)}, u32[]{:S(2)}) collective-permute-start(bf16[128,768]{1,0:T(8,128)(2,1)} %get-tuple-element.85.refs_1_), channel_id=1, source_target_pairs={{0,3},{1,0},{2,1},{3,2},{4,7},{5,4},{6,5},{7,6},{8,11},{9,8},{10,9... | collective-permute-start | bytes 589832 | tf_op jit(solution)/shard_map/ppermute | solution.py:394
  155.6 18.2 %collective-permute-start.19 = (bf16[128,768]{1,0:T(8,128)(2,1)}, bf16[128,768]{1,0:T(8,128)(2,1)S(1)}, u32[]{:S(2)}, u32[]{:S(2)}) collective-permute-start(bf16[128,768]{1,0:T(8,128)(2,1)} %get-tuple-element.85.refs_1_), channel_id=1, source_target_pairs={{0,2},{1,3},{2,0},{3,1},{4,6},{5,7},{6,4},{7,5},{8,10},{9,11},{10,... | collective-permute-start | bytes 589832 | tf_op jit(solution)/shard_map/ppermute | solution.py:394
  156.8 17.0 %collective-permute-start.18 = (bf16[128,768]{1,0:T(8,128)(2,1)}, bf16[128,768]{1,0:T(8,128)(2,1)S(1)}, u32[]{:S(2)}, u32[]{:S(2)}) collective-permute-start(bf16[128,768]{1,0:T(8,128)(2,1)} %get-tuple-element.85.refs_1_), channel_id=1, source_target_pairs={{0,1},{1,2},{2,3},{3,0},{4,5},{5,6},{6,7},{7,4},{8,9},{9,10},{10,1... | collective-permute-start | bytes 589832 | tf_op jit(solution)/shard_map/ppermute | solution.py:394
  176.7 12.7 %collective-permute-start.28 = (bf16[96,768]{1,0:T(8,128)(2,1)S(1)}, bf16[96,768]{1,0:T(8,128)(2,1)S(1)}, u32[]{:S(2)}, u32[]{:S(2)}) collective-permute-start(bf16[96,768]{1,0:T(8,128)(2,1)S(1)} %get-tuple-element.94.refs_17_), channel_id=1, source_target_pairs={{0,2},{1,3},{2,0},{3,1},{4,6},{5,7},{6,4},{7,5},{8,10},{9,11},{10,... | collective-permute-start | bytes 442376 | tf_op jit(solution)/shard_map/ppermute | solution.py:408
  191.5 75.7 %reduce-scatter.5.cloned.1.call-start = ((), (), s32[]{:S(2)}) async-start(), calls=%async_computation.5 | async-start | bytes 983040 | tf_op jit(solution)/shard_map/reduce_scatter | solution.py:1031
  191.6 2.2 collective-permute-start.21
  199.0 8.9 %collective-permute-start.22 = (bf16[112,768]{1,0:T(8,128)(2,1)S(1)}, bf16[112,768]{1,0:T(8,128)(2,1)S(1)}, u32[]{:S(2)}, u32[]{:S(2)}) collective-permute-start(bf16[112,768]{1,0:T(8,128)(2,1)S(1)} %get-tuple-element.99), channel_id=1, source_target_pairs={{0,8},{4,12},{8,0},{12,4},{16,24},{20,28},{24,16},{28,20},{1,9},{5... | collective-permute-start | bytes 516104 | tf_op jit(solution)/shard_map/ppermute | solution.py:408
  200.4 7.5 %collective-permute-start.23 = (bf16[112,768]{1,0:T(8,128)(2,1)S(1)}, bf16[112,768]{1,0:T(8,128)(2,1)S(1)}, u32[]{:S(2)}, u32[]{:S(2)}) collective-permute-start(bf16[112,768]{1,0:T(8,128)(2,1)S(1)} %get-tuple-element.100), channel_id=1, source_target_pairs={{0,16},{4,20},{8,24},{12,28},{16,0},{20,4},{24,8},{28,12},{1,17},{... | collective-permute-start | bytes 516104 | tf_op jit(solution)/shard_map/ppermute | solution.py:408
  201.1 11.2 %collective-permute-start.24 = (bf16[112,768]{1,0:T(8,128)(2,1)S(1)}, bf16[112,768]{1,0:T(8,128)(2,1)S(1)}, u32[]{:S(2)}, u32[]{:S(2)}) collective-permute-start(bf16[112,768]{1,0:T(8,128)(2,1)S(1)} %get-tuple-element.101), channel_id=1, source_target_pairs={{0,24},{4,28},{8,16},{12,20},{16,8},{20,12},{24,0},{28,4},{1,25},{... | collective-permute-start | bytes 516104 | tf_op jit(solution)/shard_map/ppermute | solution.py:408
  225.8 41.4 %copy-start.11 = (f32[128,768]{1,0:T(8,128)S(1)}, f32[128,768]{1,0:T(8,128)}, u32[]{:S(2)}) copy-start(f32[128,768]{1,0:T(8,128)} %get-tuple-element.84) | copy-start | bytes 1179652
  225.8 12.7 %collective-permute-start.29 = (bf16[96,768]{1,0:T(8,128)(2,1)S(1)}, bf16[96,768]{1,0:T(8,128)(2,1)S(1)}, u32[]{:S(2)}, u32[]{:S(2)}) collective-permute-start(bf16[96,768]{1,0:T(8,128)(2,1)S(1)} %shard_map.230.refs_5_), channel_id=1, source_target_pairs={{0,1},{1,0},{2,3},{3,2},{4,5},{5,4},{6,7},{7,6},{8,9},{9,8},{10,11... | collective-permute-start | bytes 442376 | tf_op jit(solution)/shard_map/ppermute | solution.py:408
  227.3 8.6 %collective-permute-start.25 = (bf16[112,192]{1,0:T(8,128)(2,1)S(1)}, bf16[112,192]{1,0:T(8,128)(2,1)S(1)}, u32[]{:S(2)}, u32[]{:S(2)}) collective-permute-start(bf16[112,192]{1,0:T(8,128)(2,1)S(1)} %get-tuple-element.106.refs_3_), channel_id=1, source_target_pairs={{0,1},{1,2},{2,3},{3,0},{4,5},{5,6},{6,7},{7,4},{8,9},{9,10},{10,1... | collective-permute-start | bytes 129032 | tf_op jit(solution)/shard_map/ppermute | solution.py:402
  227.9 8.7 %collective-permute-start.26 = (bf16[112,192]{1,0:T(8,128)(2,1)S(1)}, bf16[112,192]{1,0:T(8,128)(2,1)S(1)}, u32[]{:S(2)}, u32[]{:S(2)}) collective-permute-start(bf16[112,192]{1,0:T(8,128)(2,1)S(1)} %get-tuple-element.107.refs_4_), channel_id=1, source_target_pairs={{0,2},{1,3},{2,0},{3,1},{4,6},{5,7},{6,4},{7,5},{8,10},{9,11},{10,... | collective-permute-start | bytes 129032 | tf_op jit(solution)/shard_map/ppermute | solution.py:402
  230.3 8.1 %collective-permute-start.27 = (bf16[112,192]{1,0:T(8,128)(2,1)S(1)}, bf16[112,192]{1,0:T(8,128)(2,1)S(1)}, u32[]{:S(2)}, u32[]{:S(2)}) collective-permute-start(bf16[112,192]{1,0:T(8,128)(2,1)S(1)} %get-tuple-element.108.refs_5_), channel_id=1, source_target_pairs={{0,3},{1,0},{2,1},{3,2},{4,7},{5,4},{6,5},{7,6},{8,11},{9,8},{10,9... | collective-permute-start | bytes 129032 | tf_op jit(solution)/shard_map/ppermute | solution.py:402
  239.6 1.4 collective-permute-start.30
  241.6 33.1 %copy-start.14 = (f32[12,24]{1,0:T(8,128)S(1)}, f32[12,24]{1,0:T(8,128)}, u32[]{:S(2)}) copy-start(f32[12,24]{1,0:T(8,128)} %param.21) | copy-start | bytes 3460
  241.6 10.9 %collective-permute-start.33 = (bf16[192,768]{1,0:T(8,128)(2,1)S(1)}, bf16[192,768]{1,0:T(8,128)(2,1)S(1)}, u32[]{:S(2)}, u32[]{:S(2)}) collective-permute-start(bf16[192,768]{1,0:T(8,128)(2,1)S(1)} %shard_map.232.refs_1_), channel_id=1, source_target_pairs={{0,24},{4,28},{8,16},{12,20},{16,8},{20,12},{24,0},{28,4},{1,25},{... | collective-permute-start | bytes 884744 | tf_op jit(solution)/shard_map/ppermute | solution.py:408
  242.0 15.8 %collective-permute-start.32 = (bf16[192,768]{1,0:T(8,128)(2,1)S(1)}, bf16[192,768]{1,0:T(8,128)(2,1)S(1)}, u32[]{:S(2)}, u32[]{:S(2)}) collective-permute-start(bf16[192,768]{1,0:T(8,128)(2,1)S(1)} %shard_map.232.refs_1_), channel_id=1, source_target_pairs={{0,16},{4,20},{8,24},{12,28},{16,0},{20,4},{24,8},{28,12},{1,17},{... | collective-permute-start | bytes 884744 | tf_op jit(solution)/shard_map/ppermute | solution.py:408
  244.4 13.4 %collective-permute-start.31 = (bf16[192,768]{1,0:T(8,128)(2,1)S(1)}, bf16[192,768]{1,0:T(8,128)(2,1)S(1)}, u32[]{:S(2)}, u32[]{:S(2)}) collective-permute-start(bf16[192,768]{1,0:T(8,128)(2,1)S(1)} %shard_map.232.refs_1_), channel_id=1, source_target_pairs={{0,8},{4,12},{8,0},{12,4},{16,24},{20,28},{24,16},{28,20},{1,9},{5... | collective-permute-start | bytes 884744 | tf_op jit(solution)/shard_map/ppermute | solution.py:408
  267.1 1.8 collective-permute-start.34
  269.8 6.8 %collective-permute-start.35 = (bf16[96,192]{1,0:T(8,128)(2,1)S(1)}, bf16[96,192]{1,0:T(8,128)(2,1)S(1)}, u32[]{:S(2)}, u32[]{:S(2)}) collective-permute-start(bf16[96,192]{1,0:T(8,128)(2,1)S(1)} %get-tuple-element.119), channel_id=1, source_target_pairs={{0,1},{1,2},{2,3},{3,0},{4,5},{5,6},{6,7},{7,4},{8,9},{9,10},{10,1... | collective-permute-start | bytes 110600 | tf_op jit(solution)/shard_map/ppermute | solution.py:402
  271.2 5.3 %collective-permute-start.37 = (bf16[96,192]{1,0:T(8,128)(2,1)S(1)}, bf16[96,192]{1,0:T(8,128)(2,1)S(1)}, u32[]{:S(2)}, u32[]{:S(2)}) collective-permute-start(bf16[96,192]{1,0:T(8,128)(2,1)S(1)} %get-tuple-element.121), channel_id=1, source_target_pairs={{0,3},{1,0},{2,1},{3,2},{4,7},{5,4},{6,5},{7,6},{8,11},{9,8},{10,9... | collective-permute-start | bytes 110600 | tf_op jit(solution)/shard_map/ppermute | solution.py:402
  274.2 11.8 %collective-permute-start.36 = (bf16[96,960]{1,0:T(8,128)(2,1)S(1)}, bf16[96,960]{1,0:T(8,128)(2,1)S(1)}, u32[]{:S(2)}, u32[]{:S(2)}) collective-permute-start(bf16[96,960]{1,0:T(8,128)(2,1)S(1)} %get-tuple-element.120), channel_id=1, source_target_pairs={{0,2},{1,3},{2,0},{3,1},{4,6},{5,7},{6,4},{7,5},{8,10},{9,11},{10,... | collective-permute-start | bytes 552968 | tf_op jit(solution)/shard_map/ppermute | solution.py:402
  (14 other events, 61.1 us)
Sparse Core Ops, SparseCore 0:
  10.5 36.1 all-gather.3
  49.2 24.0 all-gather.5
  131.8 40.2 reduce-scatter.2
  191.6 31.4 all-gather.7
  225.4 25.4 reduce-scatter.4

commit v4 on v3

--- a/solution.py
+++ b/solution.py
@@ -634,13 +634,12 @@
             mixed[:, at : at + HEAD] = part.astype(jnp.bfloat16)
 
 
-def attention_backward(waits, place, *refs):
-    pieces, mixed, refs = refs[:SPLIT], refs[SPLIT : 2 * SPLIT], refs[2 * SPLIT :]
-    out_weight, qkv, id_column, id_row, tokens, sums_one, sums_two, sums_up, *refs = refs
-    kept, sent, d_proj, d_attended, sums = refs
-    rows, width = tokens.shape
+def attention_backward(place, *refs):
+    pieces, refs = refs[:SPLIT], refs[SPLIT:]
+    out_weight, qkv, id_column, id_row, d_proj, d_columns, d_attended = refs
+    rows = qkv.shape[0]
     own = qkv.shape[1] // 3
-    column, core = place[0], place[1]
+    column = place[0]
     put_pieces(pieces, column, d_attended)
     out_rows = out_weight[pl.ds(pl.multiple_of(column * own, own), own), :]
     d_mixed = dot(d_attended[...], out_rows, ((1,), (1,))).astype(jnp.bfloat16)
@@ -658,13 +657,20 @@
             for part, value in enumerate((d_queries, d_keys, d_values)):
                 at = part * own + head * HEAD
                 d_proj[rows_at, at : at + HEAD] = value.astype(jnp.bfloat16)
+    for at in range(SPLIT):
+
+        @pl.when(column == at)
+        def _():
+            d_columns[...] = d_attended[:, at * own : (at + 1) * own]
+
+
+def square_gradients(place, *refs):
+    mixed, refs = refs[:SPLIT], refs[SPLIT:]
+    tokens, d_proj, d_columns, sums_one, sums_two, sums_up, kept, sent, sums = refs
+    rows, width = tokens.shape
+    own = d_columns.shape[1]
+    column, core = place[0], place[1]
     d_proj_all = d_proj[...]
-    d_columns = d_attended[:, :own]
-    for place_at in range(1, width // own):
-        other = d_attended[:, place_at * own : (place_at + 1) * own]
-        d_columns = jnp.where(column == place_at, other, d_columns)
-    for wait in waits:
-        wait()
     grad_proj = dot(tokens[...], d_proj_all, ((0,), (0,)))
     proj_sums = row_sums(d_proj_all.astype(jnp.float32))
     sums[...] = jnp.zeros_like(sums)
@@ -688,7 +694,7 @@
         pl.when(core == group % 2)(lambda: put(kept, jnp.float32))
         pl.when(core != group % 2)(lambda: put(sent, jnp.bfloat16))
     for step, piece in enumerate(mixed):
-        grad_out = dot(unpack_rows(piece, rows), d_columns, ((0,), (0,)))
+        grad_out = dot(unpack_rows(piece, rows), d_columns[...], ((0,), (0,)))
         source = source_of(column, step)
         for half in range(2):
             block = grad_out[half * depth : (half + 1) * depth]
@@ -1000,27 +1006,34 @@
     far_rows = swap(far_send, "shard", shards // 2)
 
     packed_rows = depth + 16
-    kept, sent, d_proj = run_kernel(
+    d_proj, d_columns = run_kernel(
         attention_backward,
+        [
+            jax.ShapeDtypeStruct((slots * rows, 3 * own), bf16),
+            jax.ShapeDtypeStruct((slots * rows, own), bf16),
+        ],
+        scalars=1,
+        scratch=[pltpu.VMEM((slots * rows, width), bf16)],
+        ties=[far_send],
+        far=(1, 2, 3, 4, 5, 6, 7),
+        far_out=(0, 1),
+    )(place, *d_attended_pieces, out_b, qkv, id_column, id_row)
+    (wide_rows,) = run_kernel(
+        join_wide, [jax.ShapeDtypeStruct((depth, 2 * hidden), bf16)], ties=[d_proj], far_out=(0,)
+    )(mine, far_rows)
+    wide = lax.all_gather(wide_rows, "dp", axis=0, tiled=True)
+    kept, sent = run_kernel(
+        square_gradients,
         [
             jax.ShapeDtypeStruct((groups // 2, packed_rows, width), jnp.float32),
             jax.ShapeDtypeStruct((groups // 2, packed_rows, width), bf16),
-            jax.ShapeDtypeStruct((slots * rows, 3 * own), bf16),
         ],
         scalars=1,
-        scratch=[pltpu.VMEM((slots * rows, width), bf16), pltpu.VMEM((16, width), jnp.float32)],
-        far=(1, 2, 3, 4, 9, 10, 11, 5, 6, 7, 8, 13, 14, 15),
-        far_out=(0, 2),
-        late=(5, 6, 7, 8, 13, 14, 15),
-        ties=[far_send],
-    )(
-        place, *d_attended_pieces, *mixed_pieces, out_b, qkv, id_column, id_row, tokens_b,
-        sums_one, sums_two, d_bias_up,
-    )
-    (wide_rows,) = run_kernel(
-        join_wide, [jax.ShapeDtypeStruct((depth, 2 * hidden), bf16)], ties=[kept], far_out=(0,)
-    )(mine, far_rows)
-    wide = lax.all_gather(wide_rows, "dp", axis=0, tiled=True)
+        scratch=[pltpu.VMEM((16, width), jnp.float32)],
+        ties=[wide_rows],
+        far=(1, 2, 3, 4, 5, 6, 7, 8, 9),
+        far_out=(0,),
+    )(place, *mixed_pieces, tokens_b, d_proj, d_columns, sums_one, sums_two, d_bias_up)
     block_kind = jax.ShapeDtypeStruct((packed_rows, width), bf16)
     total, *blocks = run_kernel(
         pair_sum, [jax.ShapeDtypeStruct((packed_rows, width), jnp.float32)] + [block_kind] * 3, scalars=1, far=(1,)
@@ -1040,7 +1053,8 @@
         far=(5, 6),
         far_out=(0, 1, 2, 3),
     )(place, total, *[swap(block, "dp", 2 * at + 2) for at, block in enumerate(blocks)], qkv_mom, out_mom)
-    (gram_rows,) = run_kernel(wide_gram, [jax.ShapeDtypeStruct((depth, width), bf16)], ties=blocks, far=(0, 1))(
+    square_pieces = send_parts(blocks, "shard")
+    (gram_rows,) = run_kernel(wide_gram, [jax.ShapeDtypeStruct((depth, width), bf16)], ties=square_pieces[1:], far=(0, 1))(
         wide_rows, wide
     )
     row_kind = jax.ShapeDtypeStruct((depth, width), bf16)
@@ -1049,7 +1063,7 @@
         [row_kind, row_kind, jax.ShapeDtypeStruct((packed_rows - depth, own), jnp.float32)],
         scalars=1,
         scratch=[pltpu.VMEM((depth, width), bf16)],
-    )(place, *send_parts(blocks, "shard"), gram_rows, swap(gram_rows, "shard", 1))
+    )(place, *square_pieces, gram_rows, swap(gram_rows, "shard", 1))
     grad_vec = grad_vec[:vec_rows, :vec_own]
     d_tokens = d_tokens.reshape(tokens.shape)
     (pair_rows,) = run_kernel(

time: 296 us -> 300 us (1.014)
    ppermute x14, waiting for transfers between devices: 29.3 us -> 40.9 us  [swap(): lax.ppermute(block, axis, [(i, i ^ bit) for i in range(lax.axis_size(axis...]
    all_gather x1, waiting for transfers between devices: 8.33 us -> 0.01 us  [split_device(): wide = lax.all_gather(wide_rows, 'dp', axis=0, tiled=True)]
    pallas_call x18 -> x19, Pallas kernels: 65.1 us -> 67 us  [call(): pl.pallas_call(whole, out_shape=kinds, in_specs=[pl.BlockSpec(memory_spac...]
  transfers between devices with their start and end apart: 43 -> 43, of which waited for: 28 -> 29; matrix products, arithmetic and copies ran while one was open for 3% -> 3% of each run, Pallas kernels for 14% -> 14%
where the time goes in v4:
time: 300 us; the launch traced here: 299 us
  waiting for transfers between devices  145 us (48%)
  Pallas kernels  67 us (22%)
  starting transfers between devices  59.2 us (20%)
  between operations  14.4 us (5%)
  local copies, waits for them, and re-layouts  8.68 us (3%)
  other arithmetic  5.23 us (2%)
    pallas_call x19, Pallas kernels, call(): pl.pallas_call(whole, out_shape=kinds, in_specs=[pl.BlockSpec(memory_spac...  67 us
    ppermute x14, waiting for transfers between devices, swap(): lax.ppermute(block, axis, [(i, i ^ bit) for i in range(lax.axis_size(axis...  40.9 us
    ppermute x12, waiting for transfers between devices, send_parts(): lax.ppermute(parts[step], axis, [(i, (i + step) % count) for i in range(c...  38.3 us
    ppermute x9, waiting for transfers between devices, pieces_of(): lax.ppermute(block, axis, [(i, (i + step) % count) for i in range(count)])  34.4 us
    ppermute x12, starting transfers between devices, send_parts(): lax.ppermute(parts[step], axis, [(i, (i + step) % count) for i in range(c...  18.6 us
    ppermute x9, starting transfers between devices, pieces_of(): lax.ppermute(block, axis, [(i, (i + step) % count) for i in range(count)])  18 us
    all_gather x1, waiting for transfers between devices, split_device(): out_b = lax.all_gather(out_part, 'dp', axis=0, tiled=True)  15.3 us
    ppermute x14, starting transfers between devices, swap(): lax.ppermute(block, axis, [(i, i ^ bit) for i in range(lax.axis_size(axis...  14.5 us
  transfers between devices with their start and end apart: 43, of which 29 were waited for; matrix products, arithmetic and copies ran while one was open for 3% of the time, Pallas kernels for 14%

profile of v4, /device:TPU:0, one launch (start us, length us, event | category | flops | bytes accessed | tf_op | source)
XLA Modules:
  0.0 299.3 jit_solution(18395207729854286153)
XLA Ops:
  10.9 4.1 %collective-permute-start.1 = (bf16[160,768]{1,0:T(8,128)(2,1)S(1)}, bf16[160,768]{1,0:T(8,128)(2,1)S(1)}, u32[]{:S(2)}, u32[]{:S(2)}) collective-permute-start(bf16[160,768]{1,0:T(8,128)(2,1)S(1)} %pad_maximum_fusion), channel_id=1, source_target_pairs={{0,2},{1,3},{2,0},{3,1},{4,6},{5,7},{6,4},{7,5},{8,10},{9,11},{10,... | collective-permute-start | bytes 737288 | tf_op jit(solution)/shard_map/ppermute | solution.py:386
  16.6 2.2 collective-permute-start.2
  19.1 9.5 %collective-permute-done = bf16[160,768]{1,0:T(8,128)(2,1)S(1)} collective-permute-done((bf16[160,768]{1,0:T(8,128)(2,1)S(1)}, bf16[160,768]{1,0:T(8,128)(2,1)S(1)}, u32[]{:S(2)}, u32[]{:S(2)}) %collective-permute-start) | collective-permute-done | bytes 245792 | tf_op jit(solution)/shard_map/ppermute | solution.py:386
  28.6 3.8 %collective-permute-done.1 = bf16[160,768]{1,0:T(8,128)(2,1)S(1)} collective-permute-done((bf16[160,768]{1,0:T(8,128)(2,1)S(1)}, bf16[160,768]{1,0:T(8,128)(2,1)S(1)}, u32[]{:S(2)}, u32[]{:S(2)}) %collective-permute-start.1) | collective-permute-done | bytes 245792 | tf_op jit(solution)/shard_map/ppermute | solution.py:386
  38.1 2.1 collective-permute-done.4
  46.7 4.8 %shard_map.218 = (bf16[512,576]{1,0:T(8,128)(2,1)}, bf16[256,384]{1,0:T(8,128)(2,1)S(1)}) custom-call(s32[3]{0:T(128)S(1)} %pad_add_fusion.refs_0_, bf16[512,768]{1,0:T(8,128)(2,1)} %bitcast.37, bf16[768,2176]{1,0:T(8,128)(2,1)} %all-gather.4.cloned.1.call-done.refs_2_.refs_8_.refs_6_.refs_1_, f32[1,576]{1,0:T(1,128)S(1)} %broadcast_in_dim.38.refs_3_, ...), custom_call_target="tpu_custom_call" | custom-call | tf_op jit(solution)/shard_map/pallas_call | solution.py:823
  51.6 3.4 %collective-permute-start.8 = (bf16[256,384]{1,0:T(8,128)(2,1)S(1)}, bf16[256,384]{1,0:T(8,128)(2,1)S(1)}, u32[]{:S(2)}, u32[]{:S(2)}) collective-permute-start(bf16[256,384]{1,0:T(8,128)(2,1)S(1)} %get-tuple-element.71.refs_1_), channel_id=1, source_target_pairs={{0,3},{1,0},{2,1},{3,2},{4,7},{5,4},{6,5},{7,6},{8,11},{9,8},{10,9... | collective-permute-start | bytes 589832 | tf_op jit(solution)/shard_map/ppermute | solution.py:394
  56.0 1.9 collective-permute-start.6
  58.0 15.3 %all-gather.6.cloned.1.call-done.refs_5_ = bf16[768,768]{1,0:T(8,128)(2,1)} async-done(((bf16[96,768]{1,0:T(8,128)(2,1)}), bf16[768,768]{1,0:T(8,128)(2,1)}) %all-gather.6.cloned.1.call-update) | async-done | bytes 1179664 | tf_op jit(solution)/shard_map/all_gather | solution.py:928
  73.3 6.2 %shard_map.219 = (bf16[512,768]{1,0:T(8,128)(2,1)S(1)}, bf16[512,768]{1,0:T(8,128)(2,1)S(1)}, f32[512,768]{1,0:T(8,128)S(1)}, f32[128,768]{1,0:T(8,128)S(1)}, f3...) custom-call(s32[3]{0:T(128)S(1)} %pad_add_fusion.refs_0_, ...), custom_call_target="tpu_custom_call" | custom-call | tf_op jit(solution)/shard_map/pallas_call | solution.py:823
  81.1 2.4 collective-permute-start.10
  84.9 4.3 %collective-permute-done.9.refs_2_ = bf16[128,768]{1,0:T(8,128)(2,1)S(1)} collective-permute-done((bf16[128,768]{1,0:T(8,128)(2,1)S(1)}, bf16[128,768]{1,0:T(8,128)(2,1)S(1)}, u32[]{:S(2)}, u32[]{:S(2)}) %collective-permute-start.9) | collective-permute-done | bytes 196640 | tf_op jit(solution)/shard_map/ppermute | solution.py:402
  89.3 7.8 %collective-permute-done.10.refs_3_ = bf16[128,768]{1,0:T(8,128)(2,1)S(1)} collective-permute-done((bf16[128,768]{1,0:T(8,128)(2,1)S(1)}, bf16[128,768]{1,0:T(8,128)(2,1)S(1)}, u32[]{:S(2)}, u32[]{:S(2)}) %collective-permute-start.10) | collective-permute-done | bytes 196640 | tf_op jit(solution)/shard_map/ppermute | solution.py:402
  97.1 3.1 %shard_map.220 = (bf16[128,768]{1,0:T(8,128)(2,1)}, bf16[128,768]{1,0:T(8,128)(2,1)S(1)}, f32[128,768]{1,0:T(8,128)}, f32[8,768]{1,0:T(8,128)}) custom-call(s32[3]{0:T(128)S(1)} %pad_add_fusion.refs_0_, f32[128,768]{1,0:T(8,128)S(1)} %get-tuple-element.72.refs_1_, bf16[128,768]{1,0:T(8,128)(2,1)S(1)} %collective-permute-done.9.refs_2_, ...), custom_call_target="tpu_custom_call" | custom-call | tf_op jit(solution)/shard_map/pallas_call | solution.py:823
  100.1 5.6 %collective-permute-start.14 = (bf16[128,768]{1,0:T(8,128)(2,1)S(1)}, bf16[128,768]{1,0:T(8,128)(2,1)S(1)}, u32[]{:S(2)}, u32[]{:S(2)}) collective-permute-start(bf16[128,768]{1,0:T(8,128)(2,1)S(1)} %get-tuple-element.78.refs_1_), channel_id=1, source_target_pairs={{0,3},{1,0},{2,1},{3,2},{4,7},{5,4},{6,5},{7,6},{8,11},{9,8},{10,9... | collective-permute-start | bytes 589832 | tf_op jit(solution)/shard_map/ppermute | solution.py:394
  106.4 4.8 %collective-permute-done.14.refs_4_ = bf16[128,768]{1,0:T(8,128)(2,1)S(1)} collective-permute-done((bf16[128,768]{1,0:T(8,128)(2,1)S(1)}, bf16[128,768]{1,0:T(8,128)(2,1)S(1)}, u32[]{:S(2)}, u32[]{:S(2)}) %collective-permute-start.14) | collective-permute-done | bytes 196640 | tf_op jit(solution)/shard_map/ppermute | solution.py:394
  111.2 12.6 %collective-permute-done.13.refs_3_ = bf16[128,768]{1,0:T(8,128)(2,1)S(1)} collective-permute-done((bf16[128,768]{1,0:T(8,128)(2,1)S(1)}, bf16[128,768]{1,0:T(8,128)(2,1)S(1)}, u32[]{:S(2)}, u32[]{:S(2)}) %collective-permute-start.13) | collective-permute-done | bytes 196640 | tf_op jit(solution)/shard_map/ppermute | solution.py:394
  123.8 4.9 %shard_map.221 = (bf16[512,768]{1,0:T(8,128)(2,1)S(1)}, bf16[512,768]{1,0:T(8,128)(2,1)S(1)}, f32[1,768]{1,0:T(1,128)}, f32[128,768]{1,0:T(8,128)}, bf16[128,768...) custom-call(s32[3]{0:T(128)S(1)} %pad_add_fusion.refs_0_, ...), custom_call_target="tpu_custom_call" | custom-call | tf_op jit(solution)/shard_map/pallas_call | solution.py:823
  128.7 2.9 shard_map.223
  133.6 2.8 collective-permute-start.17
  136.5 5.8 %collective-permute-done.15.refs_1_ = bf16[128,768]{1,0:T(8,128)(2,1)S(1)} collective-permute-done((bf16[128,768]{1,0:T(8,128)(2,1)S(1)}, bf16[128,768]{1,0:T(8,128)(2,1)S(1)}, u32[]{:S(2)}, u32[]{:S(2)}) %collective-permute-start.15) | collective-permute-done | bytes 196640 | tf_op jit(solution)/shard_map/ppermute | solution.py:402
  142.3 6.7 %collective-permute-done.16.refs_2_ = bf16[128,768]{1,0:T(8,128)(2,1)S(1)} collective-permute-done((bf16[128,768]{1,0:T(8,128)(2,1)S(1)}, bf16[128,768]{1,0:T(8,128)(2,1)S(1)}, u32[]{:S(2)}, u32[]{:S(2)}) %collective-permute-start.16) | collective-permute-done | bytes 196640 | tf_op jit(solution)/shard_map/ppermute | solution.py:402
  148.9 2.5 shard_map.222
  151.4 4.1 %collective-permute-start.20 = (bf16[128,768]{1,0:T(8,128)(2,1)}, bf16[128,768]{1,0:T(8,128)(2,1)S(1)}, u32[]{:S(2)}, u32[]{:S(2)}) collective-permute-start(bf16[128,768]{1,0:T(8,128)(2,1)} %get-tuple-element.86.refs_1_), channel_id=1, source_target_pairs={{0,3},{1,0},{2,1},{3,2},{4,7},{5,4},{6,5},{7,6},{8,11},{9,8},{10,9... | collective-permute-start | bytes 589832 | tf_op jit(solution)/shard_map/ppermute | solution.py:394
  156.8 4.5 %collective-permute-done.20.refs_5_.refs_4_ = bf16[128,768]{1,0:T(8,128)(2,1)S(1)} collective-permute-done((bf16[128,768]{1,0:T(8,128)(2,1)}, bf16[128,768]{1,0:T(8,128)(2,1)S(1)}, u32[]{:S(2)}, u32[]{:S(2)}) %collective-permute-start.20) | collective-permute-done | bytes 196640 | tf_op jit(solution)/shard_map/ppermute | solution.py:394
  161.3 12.5 %collective-permute-done.19.refs_4_.refs_3_ = bf16[128,768]{1,0:T(8,128)(2,1)S(1)} collective-permute-done((bf16[128,768]{1,0:T(8,128)(2,1)}, bf16[128,768]{1,0:T(8,128)(2,1)S(1)}, u32[]{:S(2)}, u32[]{:S(2)}) %collective-permute-start.19) | collective-permute-done | bytes 196640 | tf_op jit(solution)/shard_map/ppermute | solution.py:394
  173.8 2.9 shard_map.224
  177.4 7.1 %shard_map.225 = (bf16[512,576]{1,0:T(8,128)(2,1)}, bf16[512,192]{1,0:T(8,128)(2,1)}) custom-call(s32[3]{0:T(128)S(1)} %pad_add_fusion.refs_0_, bf16[128,768]{1,0:T(8,128)(2,1)} %get-tuple-element.86.refs_1_, bf16[128,768]{1,0:T(8,128)(2,1)} %copy-done.9, bf16[128,768]{1,0:T(8,128)(2,1)} %copy-done.8, bf16[128,768]{1,0:T(8,128)(2,1)} %copy-done.7, ...), custom_call_target="tpu_custom_call" | custom-call | tf_op jit(solution)/shard_map/pallas_call | solution.py:823
  188.2 6.8 %shard_map.227 = (f32[4,112,768]{2,1,0:T(8,128)}, bf16[4,112,768]{2,1,0:T(8,128)(2,1)S(1)}) custom-call(s32[3]{0:T(128)S(1)} %pad_add_fusion.refs_0_, bf16[256,384]{1,0:T(8,128)(2,1)} %copy-done.3, bf16[256,384]{1,0:T(8,128)(2,1)} %copy-done.6, bf16[256,384]{1,0:T(8,128)(2,1)} %copy-done.5, bf16[256,384]{1,0:T(8,128)(2,1)} %copy-done.4, ...), custom_call_target="tpu_custom_call" | custom-call | tf_op jit(solution)/shard_map/pallas_call | solution.py:823
  195.1 2.1 collective-permute-done.22.refs_2_
  197.2 2.1 shard_map.228
  199.3 3.1 %shard_map.229 = bf16[512,768]{1,0:T(8,128)(2,1)} custom-call(bf16[512,576]{1,0:T(8,128)(2,1)} %get-tuple-element.93.refs_2_.refs_6_.refs_0_, bf16[768,2176]{1,0:T(8,128)(2,1)} %all-gather.4.cloned.1.call-done.refs_2_.refs_8_.refs_6_.refs_1_, f32[112,768]{1,0:T(8,128)S(1)} %get-tuple-element.101.refs_2_.refs_1_), custom_call_target="tpu_custom_call" | custom-call | tf_op jit(solution)/shard_map/pallas_call | solution.py:823
  203.9 2.0 collective-permute-start.25
  206.0 5.8 %collective-permute-done.23.refs_2_ = bf16[112,768]{1,0:T(8,128)(2,1)S(1)} collective-permute-done((bf16[112,768]{1,0:T(8,128)(2,1)S(1)}, bf16[112,768]{1,0:T(8,128)(2,1)S(1)}, u32[]{:S(2)}, u32[]{:S(2)}) %collective-permute-start.23) | collective-permute-done | bytes 172064 | tf_op jit(solution)/shard_map/ppermute | solution.py:408
  211.7 4.8 %collective-permute-done.24.refs_3_ = bf16[112,768]{1,0:T(8,128)(2,1)S(1)} collective-permute-done((bf16[112,768]{1,0:T(8,128)(2,1)S(1)}, bf16[112,768]{1,0:T(8,128)(2,1)S(1)}, u32[]{:S(2)}, u32[]{:S(2)}) %collective-permute-start.24) | collective-permute-done | bytes 172064 | tf_op jit(solution)/shard_map/ppermute | solution.py:408
  216.5 2.0 collective-permute-done.25.refs_4_
  218.6 2.6 shard_map.230
  221.5 2.4 collective-permute-start.27
  225.0 2.2 collective-permute-done.26.refs_2_
  228.1 2.8 shard_map.231.refs_5_
  232.6 7.4 %collective-permute-done.29.refs_6_ = bf16[96,768]{1,0:T(8,128)(2,1)S(1)} collective-permute-done((bf16[96,768]{1,0:T(8,128)(2,1)S(1)}, bf16[96,768]{1,0:T(8,128)(2,1)S(1)}, u32[]{:S(2)}, u32[]{:S(2)}) %collective-permute-start.29) | collective-permute-done | bytes 147488 | tf_op jit(solution)/shard_map/ppermute | solution.py:408
  243.1 4.5 %collective-permute-start.33 = (bf16[192,768]{1,0:T(8,128)(2,1)S(1)}, bf16[192,768]{1,0:T(8,128)(2,1)S(1)}, u32[]{:S(2)}, u32[]{:S(2)}) collective-permute-start(bf16[192,768]{1,0:T(8,128)(2,1)S(1)} %shard_map.233.refs_1_), channel_id=1, source_target_pairs={{0,24},{4,28},{8,16},{12,20},{16,8},{20,12},{24,0},{28,4},{1,25},{... | collective-permute-start | bytes 884744 | tf_op jit(solution)/shard_map/ppermute | solution.py:408
  248.2 7.2 %collective-permute-done.33.refs_4_ = bf16[192,768]{1,0:T(8,128)(2,1)S(1)} collective-permute-done((bf16[192,768]{1,0:T(8,128)(2,1)S(1)}, bf16[192,768]{1,0:T(8,128)(2,1)S(1)}, u32[]{:S(2)}, u32[]{:S(2)}) %collective-permute-start.33) | collective-permute-done | bytes 294944 | tf_op jit(solution)/shard_map/ppermute | solution.py:408
  255.4 5.8 %collective-permute-done.32.refs_3_ = bf16[192,768]{1,0:T(8,128)(2,1)S(1)} collective-permute-done((bf16[192,768]{1,0:T(8,128)(2,1)S(1)}, bf16[192,768]{1,0:T(8,128)(2,1)S(1)}, u32[]{:S(2)}, u32[]{:S(2)}) %collective-permute-start.32) | collective-permute-done | bytes 294944 | tf_op jit(solution)/shard_map/ppermute | solution.py:408
  261.2 9.4 %shard_map.234 = (bf16[96,1536]{1,0:T(8,128)(2,1)S(1)}, bf16[96,1536]{1,0:T(8,128)(2,1)S(1)}) custom-call(s32[3]{0:T(128)S(1)} %pad_add_fusion.refs_0_, bf16[192,768]{1,0:T(8,128)(2,1)S(1)} %shard_map.233.refs_1_, bf16[192,768]{1,0:T(8,128)(2,1)S(1)} %collective-permute-done.31.refs_2_, bf16[192,768]{1,0:T(8,128)(2,1)S(1)} %collective-permute-done.32.refs_3_, ...), custom_call_target="tpu_custom_call" | custom-call | tf_op jit(solution)/shard_map/pallas_call | solution.py:823
  273.3 4.9 %collective-permute-start.37 = (bf16[96,192]{1,0:T(8,128)(2,1)S(1)}, bf16[96,192]{1,0:T(8,128)(2,1)S(1)}, u32[]{:S(2)}, u32[]{:S(2)}) collective-permute-start(bf16[96,192]{1,0:T(8,128)(2,1)S(1)} %get-tuple-element.123), channel_id=1, source_target_pairs={{0,3},{1,0},{2,1},{3,2},{4,7},{5,4},{6,5},{7,6},{8,11},{9,8},{10,9... | collective-permute-start | bytes 110600 | tf_op jit(solution)/shard_map/ppermute | solution.py:402
  280.6 9.4 %collective-permute-done.36.refs_3_ = bf16[96,960]{1,0:T(8,128)(2,1)S(1)} collective-permute-done((bf16[96,960]{1,0:T(8,128)(2,1)S(1)}, bf16[96,960]{1,0:T(8,128)(2,1)S(1)}, u32[]{:S(2)}, u32[]{:S(2)}) %collective-permute-start.36) | collective-permute-done | bytes 184352 | tf_op jit(solution)/shard_map/ppermute | solution.py:402
  290.0 2.8 shard_map.236
  (167 shorter events, 44.3 us)
Async XLA Ops:
  7.2 39.5 %all-gather.4.cloned.1.call-start = ((), (), s32[]{:S(2)}) async-start(), calls=%async_computation.2 | async-start | bytes 3760128 | tf_op jit(solution)/shard_map/all_gather | solution.py:910
  10.4 62.9 %all-gather.6.cloned.1.call-start = ((), (), s32[]{:S(2)}) async-start(), calls=%async_computation.3 | async-start | bytes 1327104 | tf_op jit(solution)/shard_map/all_gather | solution.py:928
  10.9 21.5 %collective-permute-start.1 = (bf16[160,768]{1,0:T(8,128)(2,1)S(1)}, bf16[160,768]{1,0:T(8,128)(2,1)S(1)}, u32[]{:S(2)}, u32[]{:S(2)}) collective-permute-start(bf16[160,768]{1,0:T(8,128)(2,1)S(1)} %pad_maximum_fusion), channel_id=1, source_target_pairs={{0,2},{1,3},{2,0},{3,1},{4,6},{5,7},{6,4},{7,5},{8,10},{9,11},{10,... | collective-permute-start | bytes 737288 | tf_op jit(solution)/shard_map/ppermute | solution.py:386
  15.0 13.5 %collective-permute-start = (bf16[160,768]{1,0:T(8,128)(2,1)S(1)}, bf16[160,768]{1,0:T(8,128)(2,1)S(1)}, u32[]{:S(2)}, u32[]{:S(2)}) collective-permute-start(bf16[160,768]{1,0:T(8,128)(2,1)S(1)} %pad_maximum_fusion), channel_id=1, source_target_pairs={{0,1},{1,2},{2,3},{3,0},{4,5},{5,6},{6,7},{7,4},{8,9},{9,10},{10,1... | collective-permute-start | bytes 737288 | tf_op jit(solution)/shard_map/ppermute | solution.py:386
  16.6 16.5 %collective-permute-start.2 = (bf16[160,768]{1,0:T(8,128)(2,1)S(1)}, bf16[160,768]{1,0:T(8,128)(2,1)S(1)}, u32[]{:S(2)}, u32[]{:S(2)}) collective-permute-start(bf16[160,768]{1,0:T(8,128)(2,1)S(1)} %pad_maximum_fusion), channel_id=1, source_target_pairs={{0,3},{1,0},{2,1},{3,2},{4,7},{5,4},{6,5},{7,6},{8,11},{9,8},{10,9... | collective-permute-start | bytes 737288 | tf_op jit(solution)/shard_map/ppermute | solution.py:386
  34.5 139.4 %reduce-scatter.3.cloned.1.call-start = ((), (), s32[]{:S(2)}) async-start(), calls=%async_computation.4 | async-start | bytes 2654208 | tf_op jit(solution)/shard_map/reduce_scatter | solution.py:991
  35.1 1.2 collective-permute-start.3
  36.3 3.9 %collective-permute-start.4 = (bf16[2,12,96]{2,1,0:T(8,128)(2,1)S(1)}, bf16[2,12,96]{2,1,0:T(8,128)(2,1)S(1)}, u32[]{:S(2)}, u32[]{:S(2)}) collective-permute-start(bf16[2,12,96]{2,1,0:T(8,128)(2,1)S(1)} %pad_maximum_fusion.2), channel_id=1, source_target_pairs={{0,8},{4,12},{8,0},{12,4},{16,24},{20,28},{24,16},{28,20},{1,9},{5... | collective-permute-start | bytes 13832 | tf_op jit(solution)/shard_map/ppermute | solution.py:408
  40.2 4.1 %collective-permute-start.5 = (bf16[4,12,96]{2,1,0:T(8,128)(2,1)S(1)}, bf16[4,12,96]{2,1,0:T(8,128)(2,1)S(1)}, u32[]{:S(2)}, u32[]{:S(2)}) collective-permute-start(bf16[4,12,96]{2,1,0:T(8,128)(2,1)S(1)} %pad_maximum_fusion.1), channel_id=1, source_target_pairs={{0,16},{4,20},{8,24},{12,28},{16,0},{20,4},{24,8},{28,12},{1,17},{... | collective-permute-start | bytes 27656 | tf_op jit(solution)/shard_map/ppermute | solution.py:408
  51.6 27.9 %copy-start.3 = (bf16[256,384]{1,0:T(8,128)(2,1)}, bf16[256,384]{1,0:T(8,128)(2,1)S(1)}, u32[]{:S(2)}) copy-start(bf16[256,384]{1,0:T(8,128)(2,1)S(1)} %get-tuple-element.71.refs_1_) | copy-start | bytes 589828
  51.6 21.7 %collective-permute-start.8 = (bf16[256,384]{1,0:T(8,128)(2,1)S(1)}, bf16[256,384]{1,0:T(8,128)(2,1)S(1)}, u32[]{:S(2)}, u32[]{:S(2)}) collective-permute-start(bf16[256,384]{1,0:T(8,128)(2,1)S(1)} %get-tuple-element.71.refs_1_), channel_id=1, source_target_pairs={{0,3},{1,0},{2,1},{3,2},{4,7},{5,4},{6,5},{7,6},{8,11},{9,8},{10,9... | collective-permute-start | bytes 589832 | tf_op jit(solution)/shard_map/ppermute | solution.py:394
  55.0 18.3 %collective-permute-start.7 = (bf16[256,384]{1,0:T(8,128)(2,1)S(1)}, bf16[256,384]{1,0:T(8,128)(2,1)S(1)}, u32[]{:S(2)}, u32[]{:S(2)}) collective-permute-start(bf16[256,384]{1,0:T(8,128)(2,1)S(1)} %get-tuple-element.71.refs_1_), channel_id=1, source_target_pairs={{0,2},{1,3},{2,0},{3,1},{4,6},{5,7},{6,4},{7,5},{8,10},{9,11},{10,... | collective-permute-start | bytes 589832 | tf_op jit(solution)/shard_map/ppermute | solution.py:394
  56.0 17.3 %collective-permute-start.6 = (bf16[256,384]{1,0:T(8,128)(2,1)S(1)}, bf16[256,384]{1,0:T(8,128)(2,1)S(1)}, u32[]{:S(2)}, u32[]{:S(2)}) collective-permute-start(bf16[256,384]{1,0:T(8,128)(2,1)S(1)} %get-tuple-element.71.refs_1_), channel_id=1, source_target_pairs={{0,1},{1,2},{2,3},{3,0},{4,5},{5,6},{6,7},{7,4},{8,9},{9,10},{10,1... | collective-permute-start | bytes 589832 | tf_op jit(solution)/shard_map/ppermute | solution.py:394
  79.6 49.1 %copy-start.2 = (f32[128,768]{1,0:T(8,128)}, f32[128,768]{1,0:T(8,128)S(1)}, u32[]{:S(2)}) copy-start(f32[128,768]{1,0:T(8,128)S(1)} %get-tuple-element.76.refs_5_) | copy-start | bytes 1179652
  79.6 9.7 %collective-permute-start.9 = (bf16[128,768]{1,0:T(8,128)(2,1)S(1)}, bf16[128,768]{1,0:T(8,128)(2,1)S(1)}, u32[]{:S(2)}, u32[]{:S(2)}) collective-permute-start(bf16[128,768]{1,0:T(8,128)(2,1)S(1)} %get-tuple-element.73), channel_id=1, source_target_pairs={{0,1},{1,2},{2,3},{3,0},{4,5},{5,6},{6,7},{7,4},{8,9},{9,10},{10,1... | collective-permute-start | bytes 589832 | tf_op jit(solution)/shard_map/ppermute | solution.py:402
  81.1 16.0 %collective-permute-start.10 = (bf16[128,768]{1,0:T(8,128)(2,1)S(1)}, bf16[128,768]{1,0:T(8,128)(2,1)S(1)}, u32[]{:S(2)}, u32[]{:S(2)}) collective-permute-start(bf16[128,768]{1,0:T(8,128)(2,1)S(1)} %get-tuple-element.74), channel_id=1, source_target_pairs={{0,2},{1,3},{2,0},{3,1},{4,6},{5,7},{6,4},{7,5},{8,10},{9,11},{10,... | collective-permute-start | bytes 589832 | tf_op jit(solution)/shard_map/ppermute | solution.py:402
  83.5 13.5 %collective-permute-start.11 = (bf16[128,768]{1,0:T(8,128)(2,1)S(1)}, bf16[128,768]{1,0:T(8,128)(2,1)S(1)}, u32[]{:S(2)}, u32[]{:S(2)}) collective-permute-start(bf16[128,768]{1,0:T(8,128)(2,1)S(1)} %get-tuple-element.75), channel_id=1, source_target_pairs={{0,3},{1,0},{2,1},{3,2},{4,7},{5,4},{6,5},{7,6},{8,11},{9,8},{10,9... | collective-permute-start | bytes 589832 | tf_op jit(solution)/shard_map/ppermute | solution.py:402
  100.1 11.0 %collective-permute-start.14 = (bf16[128,768]{1,0:T(8,128)(2,1)S(1)}, bf16[128,768]{1,0:T(8,128)(2,1)S(1)}, u32[]{:S(2)}, u32[]{:S(2)}) collective-permute-start(bf16[128,768]{1,0:T(8,128)(2,1)S(1)} %get-tuple-element.78.refs_1_), channel_id=1, source_target_pairs={{0,3},{1,0},{2,1},{3,2},{4,7},{5,4},{6,5},{7,6},{8,11},{9,8},{10,9... | collective-permute-start | bytes 589832 | tf_op jit(solution)/shard_map/ppermute | solution.py:394
  105.8 18.0 %collective-permute-start.13 = (bf16[128,768]{1,0:T(8,128)(2,1)S(1)}, bf16[128,768]{1,0:T(8,128)(2,1)S(1)}, u32[]{:S(2)}, u32[]{:S(2)}) collective-permute-start(bf16[128,768]{1,0:T(8,128)(2,1)S(1)} %get-tuple-element.78.refs_1_), channel_id=1, source_target_pairs={{0,2},{1,3},{2,0},{3,1},{4,6},{5,7},{6,4},{7,5},{8,10},{9,11},{10,... | collective-permute-start | bytes 589832 | tf_op jit(solution)/shard_map/ppermute | solution.py:394
  106.3 17.4 %collective-permute-start.12 = (bf16[128,768]{1,0:T(8,128)(2,1)S(1)}, bf16[128,768]{1,0:T(8,128)(2,1)S(1)}, u32[]{:S(2)}, u32[]{:S(2)}) collective-permute-start(bf16[128,768]{1,0:T(8,128)(2,1)S(1)} %get-tuple-element.78.refs_1_), channel_id=1, source_target_pairs={{0,1},{1,2},{2,3},{3,0},{4,5},{5,6},{6,7},{7,4},{8,9},{9,10},{10,1... | collective-permute-start | bytes 589832 | tf_op jit(solution)/shard_map/ppermute | solution.py:394
  131.6 96.5 %all-gather.8.cloned.1.call-start = ((), (), s32[]{:S(2)}) async-start(), calls=%async_computation.6 | async-start | bytes 2654208 | tf_op jit(solution)/shard_map/all_gather | solution.py:1024
  132.5 9.7 %collective-permute-start.15 = (bf16[128,768]{1,0:T(8,128)(2,1)S(1)}, bf16[128,768]{1,0:T(8,128)(2,1)S(1)}, u32[]{:S(2)}, u32[]{:S(2)}) collective-permute-start(bf16[128,768]{1,0:T(8,128)(2,1)S(1)} %copy-done.18), channel_id=1, source_target_pairs={{0,1},{1,2},{2,3},{3,0},{4,5},{5,6},{6,7},{7,4},{8,9},{9,10},{10,1... | collective-permute-start | bytes 589832 | tf_op jit(solution)/shard_map/ppermute | solution.py:402
  132.6 16.3 %collective-permute-start.16 = (bf16[128,768]{1,0:T(8,128)(2,1)S(1)}, bf16[128,768]{1,0:T(8,128)(2,1)S(1)}, u32[]{:S(2)}, u32[]{:S(2)}) collective-permute-start(bf16[128,768]{1,0:T(8,128)(2,1)S(1)} %copy-done.17), channel_id=1, source_target_pairs={{0,2},{1,3},{2,0},{3,1},{4,6},{5,7},{6,4},{7,5},{8,10},{9,11},{10,... | collective-permute-start | bytes 589832 | tf_op jit(solution)/shard_map/ppermute | solution.py:402
  133.6 15.3 %collective-permute-start.17 = (bf16[128,768]{1,0:T(8,128)(2,1)S(1)}, bf16[128,768]{1,0:T(8,128)(2,1)S(1)}, u32[]{:S(2)}, u32[]{:S(2)}) collective-permute-start(bf16[128,768]{1,0:T(8,128)(2,1)S(1)} %copy-done.16), channel_id=1, source_target_pairs={{0,3},{1,0},{2,1},{3,2},{4,7},{5,4},{6,5},{7,6},{8,11},{9,8},{10,9... | collective-permute-start | bytes 589832 | tf_op jit(solution)/shard_map/ppermute | solution.py:402
  151.4 9.8 %collective-permute-start.20 = (bf16[128,768]{1,0:T(8,128)(2,1)}, bf16[128,768]{1,0:T(8,128)(2,1)S(1)}, u32[]{:S(2)}, u32[]{:S(2)}) collective-permute-start(bf16[128,768]{1,0:T(8,128)(2,1)} %get-tuple-element.86.refs_1_), channel_id=1, source_target_pairs={{0,3},{1,0},{2,1},{3,2},{4,7},{5,4},{6,5},{7,6},{8,11},{9,8},{10,9... | collective-permute-start | bytes 589832 | tf_op jit(solution)/shard_map/ppermute | solution.py:394
  155.6 18.2 %collective-permute-start.19 = (bf16[128,768]{1,0:T(8,128)(2,1)}, bf16[128,768]{1,0:T(8,128)(2,1)S(1)}, u32[]{:S(2)}, u32[]{:S(2)}) collective-permute-start(bf16[128,768]{1,0:T(8,128)(2,1)} %get-tuple-element.86.refs_1_), channel_id=1, source_target_pairs={{0,2},{1,3},{2,0},{3,1},{4,6},{5,7},{6,4},{7,5},{8,10},{9,11},{10,... | collective-permute-start | bytes 589832 | tf_op jit(solution)/shard_map/ppermute | solution.py:394
  156.8 17.0 %collective-permute-start.18 = (bf16[128,768]{1,0:T(8,128)(2,1)}, bf16[128,768]{1,0:T(8,128)(2,1)S(1)}, u32[]{:S(2)}, u32[]{:S(2)}) collective-permute-start(bf16[128,768]{1,0:T(8,128)(2,1)} %get-tuple-element.86.refs_1_), channel_id=1, source_target_pairs={{0,1},{1,2},{2,3},{3,0},{4,5},{5,6},{6,7},{7,4},{8,9},{9,10},{10,1... | collective-permute-start | bytes 589832 | tf_op jit(solution)/shard_map/ppermute | solution.py:394
  161.3 16.1 %copy-start.7 = (bf16[128,768]{1,0:T(8,128)(2,1)}, bf16[128,768]{1,0:T(8,128)(2,1)S(1)}, u32[]{:S(2)}) copy-start(bf16[128,768]{1,0:T(8,128)(2,1)S(1)} %collective-permute-done.20.refs_5_.refs_4_) | copy-start | bytes 589828
  176.7 8.6 %collective-permute-start.21 = (bf16[96,768]{1,0:T(8,128)(2,1)S(1)}, bf16[96,768]{1,0:T(8,128)(2,1)S(1)}, u32[]{:S(2)}, u32[]{:S(2)}) collective-permute-start(bf16[96,768]{1,0:T(8,128)(2,1)S(1)} %get-tuple-element.92.refs_9_), channel_id=1, source_target_pairs={{0,2},{1,3},{2,0},{3,1},{4,6},{5,7},{6,4},{7,5},{8,10},{9,11},{10,... | collective-permute-start | bytes 442376 | tf_op jit(solution)/shard_map/ppermute | solution.py:408
  187.2 83.5 %reduce-scatter.5.cloned.1.call-start = ((), (), s32[]{:S(2)}) async-start(), calls=%async_computation.5 | async-start | bytes 983040 | tf_op jit(solution)/shard_map/reduce_scatter | solution.py:1044
  195.0 2.2 collective-permute-start.22
  202.4 9.3 %collective-permute-start.23 = (bf16[112,768]{1,0:T(8,128)(2,1)S(1)}, bf16[112,768]{1,0:T(8,128)(2,1)S(1)}, u32[]{:S(2)}, u32[]{:S(2)}) collective-permute-start(bf16[112,768]{1,0:T(8,128)(2,1)S(1)} %get-tuple-element.102), channel_id=1, source_target_pairs={{0,8},{4,12},{8,0},{12,4},{16,24},{20,28},{24,16},{28,20},{1,9},{5... | collective-permute-start | bytes 516104 | tf_op jit(solution)/shard_map/ppermute | solution.py:408
  203.9 12.6 %collective-permute-start.24 = (bf16[112,768]{1,0:T(8,128)(2,1)S(1)}, bf16[112,768]{1,0:T(8,128)(2,1)S(1)}, u32[]{:S(2)}, u32[]{:S(2)}) collective-permute-start(bf16[112,768]{1,0:T(8,128)(2,1)S(1)} %get-tuple-element.103), channel_id=1, source_target_pairs={{0,16},{4,20},{8,24},{12,28},{16,0},{20,4},{24,8},{28,12},{1,17},{... | collective-permute-start | bytes 516104 | tf_op jit(solution)/shard_map/ppermute | solution.py:408
  203.9 14.6 %collective-permute-start.25 = (bf16[112,768]{1,0:T(8,128)(2,1)S(1)}, bf16[112,768]{1,0:T(8,128)(2,1)S(1)}, u32[]{:S(2)}, u32[]{:S(2)}) collective-permute-start(bf16[112,768]{1,0:T(8,128)(2,1)S(1)} %get-tuple-element.104), channel_id=1, source_target_pairs={{0,24},{4,28},{8,16},{12,20},{16,8},{20,12},{24,0},{28,4},{1,25},{... | collective-permute-start | bytes 516104 | tf_op jit(solution)/shard_map/ppermute | solution.py:408
  221.1 6.1 %collective-permute-start.26 = (bf16[112,192]{1,0:T(8,128)(2,1)S(1)}, bf16[112,192]{1,0:T(8,128)(2,1)S(1)}, u32[]{:S(2)}, u32[]{:S(2)}) collective-permute-start(bf16[112,192]{1,0:T(8,128)(2,1)S(1)} %get-tuple-element.109), channel_id=1, source_target_pairs={{0,1},{1,2},{2,3},{3,0},{4,5},{5,6},{6,7},{7,4},{8,9},{9,10},{10,1... | collective-permute-start | bytes 129032 | tf_op jit(solution)/shard_map/ppermute | solution.py:402
  221.5 5.7 %collective-permute-start.27 = (bf16[112,192]{1,0:T(8,128)(2,1)S(1)}, bf16[112,192]{1,0:T(8,128)(2,1)S(1)}, u32[]{:S(2)}, u32[]{:S(2)}) collective-permute-start(bf16[112,192]{1,0:T(8,128)(2,1)S(1)} %get-tuple-element.110), channel_id=1, source_target_pairs={{0,2},{1,3},{2,0},{3,1},{4,6},{5,7},{6,4},{7,5},{8,10},{9,11},{10,... | collective-permute-start | bytes 129032 | tf_op jit(solution)/shard_map/ppermute | solution.py:402
  223.9 4.2 %collective-permute-start.28 = (bf16[112,192]{1,0:T(8,128)(2,1)S(1)}, bf16[112,192]{1,0:T(8,128)(2,1)S(1)}, u32[]{:S(2)}, u32[]{:S(2)}) collective-permute-start(bf16[112,192]{1,0:T(8,128)(2,1)S(1)} %get-tuple-element.111), channel_id=1, source_target_pairs={{0,3},{1,0},{2,1},{3,2},{4,7},{5,4},{6,5},{7,6},{8,11},{9,8},{10,9... | collective-permute-start | bytes 129032 | tf_op jit(solution)/shard_map/ppermute | solution.py:402
  230.9 39.8 %copy-start.12 = (f32[128,768]{1,0:T(8,128)S(1)}, f32[128,768]{1,0:T(8,128)}, u32[]{:S(2)}) copy-start(f32[128,768]{1,0:T(8,128)} %get-tuple-element.85) | copy-start | bytes 1179652
  230.9 9.0 %collective-permute-start.29 = (bf16[96,768]{1,0:T(8,128)(2,1)S(1)}, bf16[96,768]{1,0:T(8,128)(2,1)S(1)}, u32[]{:S(2)}, u32[]{:S(2)}) collective-permute-start(bf16[96,768]{1,0:T(8,128)(2,1)S(1)} %shard_map.231.refs_5_), channel_id=1, source_target_pairs={{0,1},{1,0},{2,3},{3,2},{4,5},{5,4},{6,7},{7,6},{8,9},{9,8},{10,11... | collective-permute-start | bytes 442376 | tf_op jit(solution)/shard_map/ppermute | solution.py:408
  241.1 1.4 collective-permute-start.30
  243.1 35.6 %copy-start.15 = (f32[12,24]{1,0:T(8,128)S(1)}, f32[12,24]{1,0:T(8,128)}, u32[]{:S(2)}) copy-start(f32[12,24]{1,0:T(8,128)} %param.21) | copy-start | bytes 3460
  243.1 12.3 %collective-permute-start.33 = (bf16[192,768]{1,0:T(8,128)(2,1)S(1)}, bf16[192,768]{1,0:T(8,128)(2,1)S(1)}, u32[]{:S(2)}, u32[]{:S(2)}) collective-permute-start(bf16[192,768]{1,0:T(8,128)(2,1)S(1)} %shard_map.233.refs_1_), channel_id=1, source_target_pairs={{0,24},{4,28},{8,16},{12,20},{16,8},{20,12},{24,0},{28,4},{1,25},{... | collective-permute-start | bytes 884744 | tf_op jit(solution)/shard_map/ppermute | solution.py:408
  247.6 13.6 %collective-permute-start.32 = (bf16[192,768]{1,0:T(8,128)(2,1)S(1)}, bf16[192,768]{1,0:T(8,128)(2,1)S(1)}, u32[]{:S(2)}, u32[]{:S(2)}) collective-permute-start(bf16[192,768]{1,0:T(8,128)(2,1)S(1)} %shard_map.233.refs_1_), channel_id=1, source_target_pairs={{0,16},{4,20},{8,24},{12,28},{16,0},{20,4},{24,8},{28,12},{1,17},{... | collective-permute-start | bytes 884744 | tf_op jit(solution)/shard_map/ppermute | solution.py:408
  247.6 13.6 %collective-permute-start.31 = (bf16[192,768]{1,0:T(8,128)(2,1)S(1)}, bf16[192,768]{1,0:T(8,128)(2,1)S(1)}, u32[]{:S(2)}, u32[]{:S(2)}) collective-permute-start(bf16[192,768]{1,0:T(8,128)(2,1)S(1)} %shard_map.233.refs_1_), channel_id=1, source_target_pairs={{0,8},{4,12},{8,0},{12,4},{16,24},{20,28},{24,16},{28,20},{1,9},{5... | collective-permute-start | bytes 884744 | tf_op jit(solution)/shard_map/ppermute | solution.py:408
  270.6 1.8 collective-permute-start.34
  273.3 7.3 %collective-permute-start.35 = (bf16[96,192]{1,0:T(8,128)(2,1)S(1)}, bf16[96,192]{1,0:T(8,128)(2,1)S(1)}, u32[]{:S(2)}, u32[]{:S(2)}) collective-permute-start(bf16[96,192]{1,0:T(8,128)(2,1)S(1)} %get-tuple-element.121), channel_id=1, source_target_pairs={{0,1},{1,2},{2,3},{3,0},{4,5},{5,6},{6,7},{7,4},{8,9},{9,10},{10,1... | collective-permute-start | bytes 110600 | tf_op jit(solution)/shard_map/ppermute | solution.py:402
  273.3 7.3 %collective-permute-start.37 = (bf16[96,192]{1,0:T(8,128)(2,1)S(1)}, bf16[96,192]{1,0:T(8,128)(2,1)S(1)}, u32[]{:S(2)}, u32[]{:S(2)}) collective-permute-start(bf16[96,192]{1,0:T(8,128)(2,1)S(1)} %get-tuple-element.123), channel_id=1, source_target_pairs={{0,3},{1,0},{2,1},{3,2},{4,7},{5,4},{6,5},{7,6},{8,11},{9,8},{10,9... | collective-permute-start | bytes 110600 | tf_op jit(solution)/shard_map/ppermute | solution.py:402
  278.2 11.8 %collective-permute-start.36 = (bf16[96,960]{1,0:T(8,128)(2,1)S(1)}, bf16[96,960]{1,0:T(8,128)(2,1)S(1)}, u32[]{:S(2)}, u32[]{:S(2)}) collective-permute-start(bf16[96,960]{1,0:T(8,128)(2,1)S(1)} %get-tuple-element.122), channel_id=1, source_target_pairs={{0,2},{1,3},{2,0},{3,1},{4,6},{5,7},{6,4},{7,5},{8,10},{9,11},{10,... | collective-permute-start | bytes 552968 | tf_op jit(solution)/shard_map/ppermute | solution.py:402
  (15 other events, 56.3 us)
Sparse Core Ops, SparseCore 0:
  10.5 36.1 all-gather.3
  49.2 24.0 all-gather.5
  131.8 40.2 reduce-scatter.2
  187.3 34.3 all-gather.7
  224.0 24.0 reduce-scatter.4

commit v5 on v3

--- a/solution.py
+++ b/solution.py
@@ -705,6 +705,10 @@
     part[...] = dot(d_proj[...], proj, ((1,), (1,))).astype(jnp.bfloat16)
 
 
+def add_rows(left, right, total):
+    total[...] = left[...] + right[...].astype(jnp.float32)
+
+
 def pair_sum(place, kept, other, total, *blocks):
     chip = place[2]
     total[...] = kept[chip] + other[chip].astype(jnp.float32)
@@ -1025,11 +1029,6 @@
     total, *blocks = run_kernel(
         pair_sum, [jax.ShapeDtypeStruct((packed_rows, width), jnp.float32)] + [block_kind] * 3, scalars=1, far=(1,)
     )(place, kept, swap(sent, "dp", 1))
-    (part,) = run_kernel(
-        token_part, [whole_b], ties=[total], far=(0, 1), far_out=(0,), lanes={1: proj_lanes}
-    )(d_proj, weights)
-    d_tokens = lax.psum_scatter(part, "shard", scatter_dimension=0, tiled=True)
-    d_tokens = d_first_in + d_tokens.astype(jnp.float32)
     block_kind = jax.ShapeDtypeStruct((packed_rows, own), bf16)
     like = [jax.ShapeDtypeStruct(each.shape, each.dtype) for each in (qkv_mom, out_mom)]
     grad_qkv, grad_wout, new_qkv_mom, new_out_mom, *blocks = run_kernel(
@@ -1040,7 +1039,8 @@
         far=(5, 6),
         far_out=(0, 1, 2, 3),
     )(place, total, *[swap(block, "dp", 2 * at + 2) for at, block in enumerate(blocks)], qkv_mom, out_mom)
-    (gram_rows,) = run_kernel(wide_gram, [jax.ShapeDtypeStruct((depth, width), bf16)], ties=blocks, far=(0, 1))(
+    square_pieces = send_parts(blocks, "shard")
+    (gram_rows,) = run_kernel(wide_gram, [jax.ShapeDtypeStruct((depth, width), bf16)], ties=square_pieces[1:], far=(0, 1))(
         wide_rows, wide
     )
     row_kind = jax.ShapeDtypeStruct((depth, width), bf16)
@@ -1049,9 +1049,12 @@
         [row_kind, row_kind, jax.ShapeDtypeStruct((packed_rows - depth, own), jnp.float32)],
         scalars=1,
         scratch=[pltpu.VMEM((depth, width), bf16)],
-    )(place, *send_parts(blocks, "shard"), gram_rows, swap(gram_rows, "shard", 1))
+    )(place, *square_pieces, gram_rows, swap(gram_rows, "shard", 1))
     grad_vec = grad_vec[:vec_rows, :vec_own]
-    d_tokens = d_tokens.reshape(tokens.shape)
+    (part,) = run_kernel(
+        token_part, [whole_b], ties=[other], far=(0, 1), far_out=(0,), lanes={1: proj_lanes}
+    )(d_proj, weights)
+    d_tokens = lax.psum_scatter(part, "shard", scatter_dimension=0, tiled=True)
     (pair_rows,) = run_kernel(
         join_pair, [jax.ShapeDtypeStruct((2 * depth, width), bf16)], scalars=1
     )(place, mine, swap(other, "dp", 1))
@@ -1073,6 +1076,11 @@
     *blocks, mine = run_kernel(
         split_state, kinds, scalars=1
     )(place, kept, swap(sent, "dp", 1))
+    state_pieces = send_parts(blocks, "shard")
+    (d_tokens,) = run_kernel(add_rows, [own_f], ties=[state_pieces[1]], far=(0, 1), far_out=(0,))(
+        d_first_in, d_tokens
+    )
+    d_tokens = d_tokens.reshape(tokens.shape)
     qkv_new, out_new, ffn_new = run_kernel(
         new_weights,
         [jax.ShapeDtypeStruct(each.shape, each.dtype) for each in (qkv_w, out_w, ffn_w)],
@@ -1081,7 +1089,7 @@
         far=(6, 7, 8),
         far_out=(0, 1, 2),
     )(
-        place, *send_parts(blocks, "shard"), mine, qkv_w, out_w, ffn_w
+        place, *state_pieces, mine, qkv_w, out_w, ffn_w
     )
 
     token_count = micro * rows * groups * shards

time: 296 us -> 294 us (level)
    ppermute x14, waiting for transfers between devices: 29.3 us -> 36.9 us  [swap(): lax.ppermute(block, axis, [(i, i ^ bit) for i in range(lax.axis_size(axis...]
    all_gather x1, waiting for transfers between devices: 8.33 us -> 3.39 us  [split_device(): wide = lax.all_gather(wide_rows, 'dp', axis=0, tiled=True)]
    ppermute x12, waiting for transfers between devices: 41 us -> 37 us  [send_parts(): lax.ppermute(parts[step], axis, [(i, (i + step) % count) for i in range(c...]
    pallas_call x18 -> x19, Pallas kernels: 65.1 us -> 66.9 us  [call(): pl.pallas_call(whole, out_shape=kinds, in_specs=[pl.BlockSpec(memory_spac...]
  transfers between devices with their start and end apart: 43 -> 43, of which waited for: 28 -> 29; matrix products, arithmetic and copies ran while one was open for 3% -> 2% of each run, Pallas kernels for 14% -> 13%
where the time goes in v5:
time: 294 us
  waiting for transfers between devices  143 us (49%)
  Pallas kernels  66.9 us (23%)
  starting transfers between devices  58 us (20%)
  between operations  14.4 us (5%)
  local copies, waits for them, and re-layouts  7.92 us (3%)
  other arithmetic  3.51 us (1%)
    pallas_call x19, Pallas kernels, call(): pl.pallas_call(whole, out_shape=kinds, in_specs=[pl.BlockSpec(memory_spac...  66.9 us
    ppermute x12, waiting for transfers between devices, send_parts(): lax.ppermute(parts[step], axis, [(i, (i + step) % count) for i in range(c...  37 us
    ppermute x14, waiting for transfers between devices, swap(): lax.ppermute(block, axis, [(i, i ^ bit) for i in range(lax.axis_size(axis...  36.9 us
    ppermute x9, waiting for transfers between devices, pieces_of(): lax.ppermute(block, axis, [(i, (i + step) % count) for i in range(count)])  34.4 us
    ppermute x12, starting transfers between devices, send_parts(): lax.ppermute(parts[step], axis, [(i, (i + step) % count) for i in range(c...  19.1 us
    ppermute x9, starting transfers between devices, pieces_of(): lax.ppermute(block, axis, [(i, (i + step) % count) for i in range(count)])  18 us
    all_gather x1, waiting for transfers between devices, split_device(): out_b = lax.all_gather(out_part, 'dp', axis=0, tiled=True)  15.3 us
    ppermute x3, waiting for transfers between devices, gather_direct(): lax.ppermute(block, axis, [(i, (i + step) % count) for i in range(count)])  14 us
  transfers between devices with their start and end apart: 43, of which 29 were waited for; matrix products, arithmetic and copies ran while one was open for 2% of the time, Pallas kernels for 13%

profile of v5, /device:TPU:0, one launch (start us, length us, event | category | flops | bytes accessed | tf_op | source)
XLA Modules:
  0.0 293.6 jit_solution(10871299028243666141)
XLA Ops:
  10.9 4.1 %collective-permute-start.1 = (bf16[160,768]{1,0:T(8,128)(2,1)S(1)}, bf16[160,768]{1,0:T(8,128)(2,1)S(1)}, u32[]{:S(2)}, u32[]{:S(2)}) collective-permute-start(bf16[160,768]{1,0:T(8,128)(2,1)S(1)} %pad_maximum_fusion), channel_id=1, source_target_pairs={{0,2},{1,3},{2,0},{3,1},{4,6},{5,7},{6,4},{7,5},{8,10},{9,11},{10,... | collective-permute-start | bytes 737288 | tf_op jit(solution)/shard_map/ppermute | solution.py:386
  16.6 2.2 collective-permute-start.2
  19.1 9.5 %collective-permute-done = bf16[160,768]{1,0:T(8,128)(2,1)S(1)} collective-permute-done((bf16[160,768]{1,0:T(8,128)(2,1)S(1)}, bf16[160,768]{1,0:T(8,128)(2,1)S(1)}, u32[]{:S(2)}, u32[]{:S(2)}) %collective-permute-start) | collective-permute-done | bytes 245792 | tf_op jit(solution)/shard_map/ppermute | solution.py:386
  28.6 3.8 %collective-permute-done.1 = bf16[160,768]{1,0:T(8,128)(2,1)S(1)} collective-permute-done((bf16[160,768]{1,0:T(8,128)(2,1)S(1)}, bf16[160,768]{1,0:T(8,128)(2,1)S(1)}, u32[]{:S(2)}, u32[]{:S(2)}) %collective-permute-start.1) | collective-permute-done | bytes 245792 | tf_op jit(solution)/shard_map/ppermute | solution.py:386
  36.3 1.6 collective-permute-start.4
  38.1 2.1 collective-permute-done.4
  40.2 1.6 collective-permute-start.5
  45.0 1.8 all-gather.4.cloned.1.call-done.refs_2_.refs_8_.refs_6_.refs_1_
  46.7 4.8 %shard_map.218 = (bf16[512,576]{1,0:T(8,128)(2,1)}, bf16[256,384]{1,0:T(8,128)(2,1)S(1)}) custom-call(s32[3]{0:T(128)S(1)} %pad_add_fusion.refs_0_, bf16[512,768]{1,0:T(8,128)(2,1)} %bitcast.37, bf16[768,2176]{1,0:T(8,128)(2,1)} %all-gather.4.cloned.1.call-done.refs_2_.refs_8_.refs_6_.refs_1_, f32[1,576]{1,0:T(1,128)S(1)} %broadcast_in_dim.38.refs_3_, ...), custom_call_target="tpu_custom_call" | custom-call | tf_op jit(solution)/shard_map/pallas_call | solution.py:821
  51.6 3.4 %collective-permute-start.8 = (bf16[256,384]{1,0:T(8,128)(2,1)S(1)}, bf16[256,384]{1,0:T(8,128)(2,1)S(1)}, u32[]{:S(2)}, u32[]{:S(2)}) collective-permute-start(bf16[256,384]{1,0:T(8,128)(2,1)S(1)} %get-tuple-element.70.refs_1_.refs_5_), channel_id=1, source_target_pairs={{0,3},{1,0},{2,1},{3,2},{4,7},{5,4},{6,5},{7,6},{8,11},{9,8},{10,9... | collective-permute-start | bytes 589832 | tf_op jit(solution)/shard_map/ppermute | solution.py:394
  56.0 1.9 collective-permute-start.6
  58.0 15.3 %all-gather.6.cloned.1.call-done.refs_5_.refs_9_ = bf16[768,768]{1,0:T(8,128)(2,1)} async-done(((bf16[96,768]{1,0:T(8,128)(2,1)}), bf16[768,768]{1,0:T(8,128)(2,1)}) %all-gather.6.cloned.1.call-update) | async-done | bytes 1179664 | tf_op jit(solution)/shard_map/all_gather | solution.py:926
  73.3 6.2 %shard_map.219 = (bf16[512,768]{1,0:T(8,128)(2,1)S(1)}, bf16[512,768]{1,0:T(8,128)(2,1)S(1)}, f32[512,768]{1,0:T(8,128)S(1)}, f32[128,768]{1,0:T(8,128)S(1)}, f3...) custom-call(s32[3]{0:T(128)S(1)} %pad_add_fusion.refs_0_, ...), custom_call_target="tpu_custom_call" | custom-call | tf_op jit(solution)/shard_map/pallas_call | solution.py:821
  81.1 2.4 collective-permute-start.10
  84.9 4.3 %collective-permute-done.9.refs_2_ = bf16[128,768]{1,0:T(8,128)(2,1)S(1)} collective-permute-done((bf16[128,768]{1,0:T(8,128)(2,1)S(1)}, bf16[128,768]{1,0:T(8,128)(2,1)S(1)}, u32[]{:S(2)}, u32[]{:S(2)}) %collective-permute-start.9) | collective-permute-done | bytes 196640 | tf_op jit(solution)/shard_map/ppermute | solution.py:402
  89.3 7.8 %collective-permute-done.10.refs_3_ = bf16[128,768]{1,0:T(8,128)(2,1)S(1)} collective-permute-done((bf16[128,768]{1,0:T(8,128)(2,1)S(1)}, bf16[128,768]{1,0:T(8,128)(2,1)S(1)}, u32[]{:S(2)}, u32[]{:S(2)}) %collective-permute-start.10) | collective-permute-done | bytes 196640 | tf_op jit(solution)/shard_map/ppermute | solution.py:402
  97.1 3.1 %shard_map.220 = (bf16[128,768]{1,0:T(8,128)(2,1)}, bf16[128,768]{1,0:T(8,128)(2,1)S(1)}, f32[128,768]{1,0:T(8,128)}, f32[8,768]{1,0:T(8,128)}) custom-call(s32[3]{0:T(128)S(1)} %pad_add_fusion.refs_0_, f32[128,768]{1,0:T(8,128)S(1)} %get-tuple-element.71.refs_1_, bf16[128,768]{1,0:T(8,128)(2,1)S(1)} %collective-permute-done.9.refs_2_, ...), custom_call_target="tpu_custom_call" | custom-call | tf_op jit(solution)/shard_map/pallas_call | solution.py:821
  100.1 5.6 %collective-permute-start.14 = (bf16[128,768]{1,0:T(8,128)(2,1)S(1)}, bf16[128,768]{1,0:T(8,128)(2,1)S(1)}, u32[]{:S(2)}, u32[]{:S(2)}) collective-permute-start(bf16[128,768]{1,0:T(8,128)(2,1)S(1)} %get-tuple-element.77.refs_1_), channel_id=1, source_target_pairs={{0,3},{1,0},{2,1},{3,2},{4,7},{5,4},{6,5},{7,6},{8,11},{9,8},{10,9... | collective-permute-start | bytes 589832 | tf_op jit(solution)/shard_map/ppermute | solution.py:394
  106.4 4.8 %collective-permute-done.14.refs_4_ = bf16[128,768]{1,0:T(8,128)(2,1)S(1)} collective-permute-done((bf16[128,768]{1,0:T(8,128)(2,1)S(1)}, bf16[128,768]{1,0:T(8,128)(2,1)S(1)}, u32[]{:S(2)}, u32[]{:S(2)}) %collective-permute-start.14) | collective-permute-done | bytes 196640 | tf_op jit(solution)/shard_map/ppermute | solution.py:394
  111.2 12.6 %collective-permute-done.13.refs_3_ = bf16[128,768]{1,0:T(8,128)(2,1)S(1)} collective-permute-done((bf16[128,768]{1,0:T(8,128)(2,1)S(1)}, bf16[128,768]{1,0:T(8,128)(2,1)S(1)}, u32[]{:S(2)}, u32[]{:S(2)}) %collective-permute-start.13) | collective-permute-done | bytes 196640 | tf_op jit(solution)/shard_map/ppermute | solution.py:394
  123.8 4.9 %shard_map.221 = (bf16[512,768]{1,0:T(8,128)(2,1)S(1)}, bf16[512,768]{1,0:T(8,128)(2,1)S(1)}, f32[1,768]{1,0:T(1,128)}, f32[128,768]{1,0:T(8,128)}, bf16[128,768...) custom-call(s32[3]{0:T(128)S(1)} %pad_add_fusion.refs_0_, ...), custom_call_target="tpu_custom_call" | custom-call | tf_op jit(solution)/shard_map/pallas_call | solution.py:821
  128.7 2.9 shard_map.223
  133.7 2.8 collective-permute-start.17
  136.5 5.8 %collective-permute-done.15.refs_1_ = bf16[128,768]{1,0:T(8,128)(2,1)S(1)} collective-permute-done((bf16[128,768]{1,0:T(8,128)(2,1)S(1)}, bf16[128,768]{1,0:T(8,128)(2,1)S(1)}, u32[]{:S(2)}, u32[]{:S(2)}) %collective-permute-start.15) | collective-permute-done | bytes 196640 | tf_op jit(solution)/shard_map/ppermute | solution.py:402
  142.3 6.7 %collective-permute-done.16.refs_2_ = bf16[128,768]{1,0:T(8,128)(2,1)S(1)} collective-permute-done((bf16[128,768]{1,0:T(8,128)(2,1)S(1)}, bf16[128,768]{1,0:T(8,128)(2,1)S(1)}, u32[]{:S(2)}, u32[]{:S(2)}) %collective-permute-start.16) | collective-permute-done | bytes 196640 | tf_op jit(solution)/shard_map/ppermute | solution.py:402
  148.9 2.5 shard_map.222
  151.4 4.1 %collective-permute-start.20 = (bf16[128,768]{1,0:T(8,128)(2,1)}, bf16[128,768]{1,0:T(8,128)(2,1)S(1)}, u32[]{:S(2)}, u32[]{:S(2)}) collective-permute-start(bf16[128,768]{1,0:T(8,128)(2,1)} %get-tuple-element.85.refs_1_), channel_id=1, source_target_pairs={{0,3},{1,0},{2,1},{3,2},{4,7},{5,4},{6,5},{7,6},{8,11},{9,8},{10,9... | collective-permute-start | bytes 589832 | tf_op jit(solution)/shard_map/ppermute | solution.py:394
  156.8 4.5 %collective-permute-done.20.refs_5_.refs_4_ = bf16[128,768]{1,0:T(8,128)(2,1)S(1)} collective-permute-done((bf16[128,768]{1,0:T(8,128)(2,1)}, bf16[128,768]{1,0:T(8,128)(2,1)S(1)}, u32[]{:S(2)}, u32[]{:S(2)}) %collective-permute-start.20) | collective-permute-done | bytes 196640 | tf_op jit(solution)/shard_map/ppermute | solution.py:394
  161.3 12.5 %collective-permute-done.19.refs_4_.refs_3_ = bf16[128,768]{1,0:T(8,128)(2,1)S(1)} collective-permute-done((bf16[128,768]{1,0:T(8,128)(2,1)}, bf16[128,768]{1,0:T(8,128)(2,1)S(1)}, u32[]{:S(2)}, u32[]{:S(2)}) %collective-permute-start.19) | collective-permute-done | bytes 196640 | tf_op jit(solution)/shard_map/ppermute | solution.py:394
  173.8 2.9 shard_map.224
  177.4 12.0 %shard_map.225 = (f32[4,112,768]{2,1,0:T(8,128)}, bf16[4,112,768]{2,1,0:T(8,128)(2,1)S(1)}, bf16[512,576]{1,0:T(8,128)(2,1)}) custom-call(s32[3]{0:T(128)S(1)} %pad_add_fusion.refs_0_, bf16[128,768]{1,0:T(8,128)(2,1)} %get-tuple-element.85.refs_1_, bf16[128,768]{1,0:T(8,128)(2,1)} %copy-done.8, bf16[128,768]{1,0:T(8,128)(2,1)} %copy-done.7, ...), custom_call_target="tpu_custom_call" | custom-call | tf_op jit(solution)/shard_map/pallas_call | solution.py:821
  191.7 2.1 collective-permute-done.21.refs_2_
  193.8 2.1 shard_map.226
  199.4 6.0 %collective-permute-done.22.refs_2_ = bf16[112,768]{1,0:T(8,128)(2,1)S(1)} collective-permute-done((bf16[112,768]{1,0:T(8,128)(2,1)S(1)}, bf16[112,768]{1,0:T(8,128)(2,1)S(1)}, u32[]{:S(2)}, u32[]{:S(2)}) %collective-permute-start.22) | collective-permute-done | bytes 172064 | tf_op jit(solution)/shard_map/ppermute | solution.py:408
  205.4 4.9 %collective-permute-done.23.refs_3_ = bf16[112,768]{1,0:T(8,128)(2,1)S(1)} collective-permute-done((bf16[112,768]{1,0:T(8,128)(2,1)S(1)}, bf16[112,768]{1,0:T(8,128)(2,1)S(1)}, u32[]{:S(2)}, u32[]{:S(2)}) %collective-permute-start.23) | collective-permute-done | bytes 172064 | tf_op jit(solution)/shard_map/ppermute | solution.py:408
  210.3 2.6 shard_map.227
  215.4 2.8 collective-permute-start.27
  220.7 3.4 %all-gather.8.cloned.1.call-done.refs_1_.refs_5_ = bf16[768,1536]{1,0:T(8,128)(2,1)} async-done(((bf16[96,1536]{1,0:T(8,128)(2,1)}), bf16[768,1536]{1,0:T(8,128)(2,1)}) %all-gather.8.cloned.1.call-update) | async-done | bytes 2359312 | tf_op jit(solution)/shard_map/all_gather | solution.py:1027
  224.1 2.6 shard_map.229.refs_5_
  228.2 4.5 %collective-permute-done.29.refs_6_ = bf16[96,768]{1,0:T(8,128)(2,1)S(1)} collective-permute-done((bf16[96,768]{1,0:T(8,128)(2,1)S(1)}, bf16[96,768]{1,0:T(8,128)(2,1)S(1)}, u32[]{:S(2)}, u32[]{:S(2)}) %collective-permute-start.29) | collective-permute-done | bytes 147488 | tf_op jit(solution)/shard_map/ppermute | solution.py:408
  233.9 3.1 %shard_map.231 = bf16[512,768]{1,0:T(8,128)(2,1)} custom-call(bf16[512,576]{1,0:T(8,128)(2,1)} %get-tuple-element.95.refs_0_, bf16[768,2176]{1,0:T(8,128)(2,1)} %all-gather.4.cloned.1.call-done.refs_2_.refs_8_.refs_6_.refs_1_, bf16[96,768]{1,0:T(8,128)(2,1)S(1)} %get-tuple-element.107.refs_2_), custom_call_target="tpu_custom_call" | custom-call | tf_op jit(solution)/shard_map/pallas_call | solution.py:821
  242.6 7.3 %collective-permute-done.33.refs_4_ = bf16[192,768]{1,0:T(8,128)(2,1)S(1)} collective-permute-done((bf16[192,768]{1,0:T(8,128)(2,1)S(1)}, bf16[192,768]{1,0:T(8,128)(2,1)S(1)}, u32[]{:S(2)}, u32[]{:S(2)}) %collective-permute-start.33) | collective-permute-done | bytes 294944 | tf_op jit(solution)/shard_map/ppermute | solution.py:408
  249.9 5.5 %collective-permute-done.32.refs_3_ = bf16[192,768]{1,0:T(8,128)(2,1)S(1)} collective-permute-done((bf16[192,768]{1,0:T(8,128)(2,1)S(1)}, bf16[192,768]{1,0:T(8,128)(2,1)S(1)}, u32[]{:S(2)}, u32[]{:S(2)}) %collective-permute-start.32) | collective-permute-done | bytes 294944 | tf_op jit(solution)/shard_map/ppermute | solution.py:408
  255.4 9.4 %shard_map.233 = (bf16[96,1536]{1,0:T(8,128)(2,1)S(1)}, bf16[96,1536]{1,0:T(8,128)(2,1)S(1)}) custom-call(s32[3]{0:T(128)S(1)} %pad_add_fusion.refs_0_, bf16[192,768]{1,0:T(8,128)(2,1)S(1)} %shard_map.232.refs_1_, bf16[192,768]{1,0:T(8,128)(2,1)S(1)} %collective-permute-done.31.refs_2_, bf16[192,768]{1,0:T(8,128)(2,1)S(1)} %collective-permute-done.32.refs_3_, ...), custom_call_target="tpu_custom_call" | custom-call | tf_op jit(solution)/shard_map/pallas_call | solution.py:821
  268.8 2.3 collective-permute-start.37
  273.5 8.9 %collective-permute-done.36.refs_3_ = bf16[96,960]{1,0:T(8,128)(2,1)S(1)} collective-permute-done((bf16[96,960]{1,0:T(8,128)(2,1)S(1)}, bf16[96,960]{1,0:T(8,128)(2,1)S(1)}, u32[]{:S(2)}, u32[]{:S(2)}) %collective-permute-start.36) | collective-permute-done | bytes 184352 | tf_op jit(solution)/shard_map/ppermute | solution.py:402
  282.4 2.8 shard_map.236
  285.2 1.8 shard_map.235
  (162 shorter events, 46.4 us)
Async XLA Ops:
  7.2 39.5 %all-gather.4.cloned.1.call-start = ((), (), s32[]{:S(2)}) async-start(), calls=%async_computation.2 | async-start | bytes 3760128 | tf_op jit(solution)/shard_map/all_gather | solution.py:908
  10.4 62.9 %all-gather.6.cloned.1.call-start = ((), (), s32[]{:S(2)}) async-start(), calls=%async_computation.3 | async-start | bytes 1327104 | tf_op jit(solution)/shard_map/all_gather | solution.py:926
  10.9 21.5 %collective-permute-start.1 = (bf16[160,768]{1,0:T(8,128)(2,1)S(1)}, bf16[160,768]{1,0:T(8,128)(2,1)S(1)}, u32[]{:S(2)}, u32[]{:S(2)}) collective-permute-start(bf16[160,768]{1,0:T(8,128)(2,1)S(1)} %pad_maximum_fusion), channel_id=1, source_target_pairs={{0,2},{1,3},{2,0},{3,1},{4,6},{5,7},{6,4},{7,5},{8,10},{9,11},{10,... | collective-permute-start | bytes 737288 | tf_op jit(solution)/shard_map/ppermute | solution.py:386
  15.0 13.5 %collective-permute-start = (bf16[160,768]{1,0:T(8,128)(2,1)S(1)}, bf16[160,768]{1,0:T(8,128)(2,1)S(1)}, u32[]{:S(2)}, u32[]{:S(2)}) collective-permute-start(bf16[160,768]{1,0:T(8,128)(2,1)S(1)} %pad_maximum_fusion), channel_id=1, source_target_pairs={{0,1},{1,2},{2,3},{3,0},{4,5},{5,6},{6,7},{7,4},{8,9},{9,10},{10,1... | collective-permute-start | bytes 737288 | tf_op jit(solution)/shard_map/ppermute | solution.py:386
  16.6 16.5 %collective-permute-start.2 = (bf16[160,768]{1,0:T(8,128)(2,1)S(1)}, bf16[160,768]{1,0:T(8,128)(2,1)S(1)}, u32[]{:S(2)}, u32[]{:S(2)}) collective-permute-start(bf16[160,768]{1,0:T(8,128)(2,1)S(1)} %pad_maximum_fusion), channel_id=1, source_target_pairs={{0,3},{1,0},{2,1},{3,2},{4,7},{5,4},{6,5},{7,6},{8,11},{9,8},{10,9... | collective-permute-start | bytes 737288 | tf_op jit(solution)/shard_map/ppermute | solution.py:386
  34.5 139.4 %reduce-scatter.3.cloned.1.call-start = ((), (), s32[]{:S(2)}) async-start(), calls=%async_computation.4 | async-start | bytes 2654208 | tf_op jit(solution)/shard_map/reduce_scatter | solution.py:989
  35.1 1.2 collective-permute-start.3
  36.3 3.9 %collective-permute-start.4 = (bf16[2,12,96]{2,1,0:T(8,128)(2,1)S(1)}, bf16[2,12,96]{2,1,0:T(8,128)(2,1)S(1)}, u32[]{:S(2)}, u32[]{:S(2)}) collective-permute-start(bf16[2,12,96]{2,1,0:T(8,128)(2,1)S(1)} %pad_maximum_fusion.2), channel_id=1, source_target_pairs={{0,8},{4,12},{8,0},{12,4},{16,24},{20,28},{24,16},{28,20},{1,9},{5... | collective-permute-start | bytes 13832 | tf_op jit(solution)/shard_map/ppermute | solution.py:408
  40.2 4.1 %collective-permute-start.5 = (bf16[4,12,96]{2,1,0:T(8,128)(2,1)S(1)}, bf16[4,12,96]{2,1,0:T(8,128)(2,1)S(1)}, u32[]{:S(2)}, u32[]{:S(2)}) collective-permute-start(bf16[4,12,96]{2,1,0:T(8,128)(2,1)S(1)} %pad_maximum_fusion.1), channel_id=1, source_target_pairs={{0,16},{4,20},{8,24},{12,28},{16,0},{20,4},{24,8},{28,12},{1,17},{... | collective-permute-start | bytes 27656 | tf_op jit(solution)/shard_map/ppermute | solution.py:408
  51.6 27.9 %copy-start.2 = (bf16[256,384]{1,0:T(8,128)(2,1)}, bf16[256,384]{1,0:T(8,128)(2,1)S(1)}, u32[]{:S(2)}) copy-start(bf16[256,384]{1,0:T(8,128)(2,1)S(1)} %get-tuple-element.70.refs_1_.refs_5_) | copy-start | bytes 589828
  51.6 21.7 %collective-permute-start.8 = (bf16[256,384]{1,0:T(8,128)(2,1)S(1)}, bf16[256,384]{1,0:T(8,128)(2,1)S(1)}, u32[]{:S(2)}, u32[]{:S(2)}) collective-permute-start(bf16[256,384]{1,0:T(8,128)(2,1)S(1)} %get-tuple-element.70.refs_1_.refs_5_), channel_id=1, source_target_pairs={{0,3},{1,0},{2,1},{3,2},{4,7},{5,4},{6,5},{7,6},{8,11},{9,8},{10,9... | collective-permute-start | bytes 589832 | tf_op jit(solution)/shard_map/ppermute | solution.py:394
  55.0 18.3 %collective-permute-start.7 = (bf16[256,384]{1,0:T(8,128)(2,1)S(1)}, bf16[256,384]{1,0:T(8,128)(2,1)S(1)}, u32[]{:S(2)}, u32[]{:S(2)}) collective-permute-start(bf16[256,384]{1,0:T(8,128)(2,1)S(1)} %get-tuple-element.70.refs_1_.refs_5_), channel_id=1, source_target_pairs={{0,2},{1,3},{2,0},{3,1},{4,6},{5,7},{6,4},{7,5},{8,10},{9,11},{10,... | collective-permute-start | bytes 589832 | tf_op jit(solution)/shard_map/ppermute | solution.py:394
  56.0 17.3 %collective-permute-start.6 = (bf16[256,384]{1,0:T(8,128)(2,1)S(1)}, bf16[256,384]{1,0:T(8,128)(2,1)S(1)}, u32[]{:S(2)}, u32[]{:S(2)}) collective-permute-start(bf16[256,384]{1,0:T(8,128)(2,1)S(1)} %get-tuple-element.70.refs_1_.refs_5_), channel_id=1, source_target_pairs={{0,1},{1,2},{2,3},{3,0},{4,5},{5,6},{6,7},{7,4},{8,9},{9,10},{10,1... | collective-permute-start | bytes 589832 | tf_op jit(solution)/shard_map/ppermute | solution.py:394
  79.6 49.1 %copy-start.1 = (f32[128,768]{1,0:T(8,128)}, f32[128,768]{1,0:T(8,128)S(1)}, u32[]{:S(2)}) copy-start(f32[128,768]{1,0:T(8,128)S(1)} %get-tuple-element.75.refs_5_) | copy-start | bytes 1179652
  79.6 9.7 %collective-permute-start.9 = (bf16[128,768]{1,0:T(8,128)(2,1)S(1)}, bf16[128,768]{1,0:T(8,128)(2,1)S(1)}, u32[]{:S(2)}, u32[]{:S(2)}) collective-permute-start(bf16[128,768]{1,0:T(8,128)(2,1)S(1)} %get-tuple-element.72), channel_id=1, source_target_pairs={{0,1},{1,2},{2,3},{3,0},{4,5},{5,6},{6,7},{7,4},{8,9},{9,10},{10,1... | collective-permute-start | bytes 589832 | tf_op jit(solution)/shard_map/ppermute | solution.py:402
  81.1 16.0 %collective-permute-start.10 = (bf16[128,768]{1,0:T(8,128)(2,1)S(1)}, bf16[128,768]{1,0:T(8,128)(2,1)S(1)}, u32[]{:S(2)}, u32[]{:S(2)}) collective-permute-start(bf16[128,768]{1,0:T(8,128)(2,1)S(1)} %get-tuple-element.73), channel_id=1, source_target_pairs={{0,2},{1,3},{2,0},{3,1},{4,6},{5,7},{6,4},{7,5},{8,10},{9,11},{10,... | collective-permute-start | bytes 589832 | tf_op jit(solution)/shard_map/ppermute | solution.py:402
  83.5 13.5 %collective-permute-start.11 = (bf16[128,768]{1,0:T(8,128)(2,1)S(1)}, bf16[128,768]{1,0:T(8,128)(2,1)S(1)}, u32[]{:S(2)}, u32[]{:S(2)}) collective-permute-start(bf16[128,768]{1,0:T(8,128)(2,1)S(1)} %get-tuple-element.74), channel_id=1, source_target_pairs={{0,3},{1,0},{2,1},{3,2},{4,7},{5,4},{6,5},{7,6},{8,11},{9,8},{10,9... | collective-permute-start | bytes 589832 | tf_op jit(solution)/shard_map/ppermute | solution.py:402
  100.1 11.0 %collective-permute-start.14 = (bf16[128,768]{1,0:T(8,128)(2,1)S(1)}, bf16[128,768]{1,0:T(8,128)(2,1)S(1)}, u32[]{:S(2)}, u32[]{:S(2)}) collective-permute-start(bf16[128,768]{1,0:T(8,128)(2,1)S(1)} %get-tuple-element.77.refs_1_), channel_id=1, source_target_pairs={{0,3},{1,0},{2,1},{3,2},{4,7},{5,4},{6,5},{7,6},{8,11},{9,8},{10,9... | collective-permute-start | bytes 589832 | tf_op jit(solution)/shard_map/ppermute | solution.py:394
  105.8 18.0 %collective-permute-start.13 = (bf16[128,768]{1,0:T(8,128)(2,1)S(1)}, bf16[128,768]{1,0:T(8,128)(2,1)S(1)}, u32[]{:S(2)}, u32[]{:S(2)}) collective-permute-start(bf16[128,768]{1,0:T(8,128)(2,1)S(1)} %get-tuple-element.77.refs_1_), channel_id=1, source_target_pairs={{0,2},{1,3},{2,0},{3,1},{4,6},{5,7},{6,4},{7,5},{8,10},{9,11},{10,... | collective-permute-start | bytes 589832 | tf_op jit(solution)/shard_map/ppermute | solution.py:394
  106.3 17.4 %collective-permute-start.12 = (bf16[128,768]{1,0:T(8,128)(2,1)S(1)}, bf16[128,768]{1,0:T(8,128)(2,1)S(1)}, u32[]{:S(2)}, u32[]{:S(2)}) collective-permute-start(bf16[128,768]{1,0:T(8,128)(2,1)S(1)} %get-tuple-element.77.refs_1_), channel_id=1, source_target_pairs={{0,1},{1,2},{2,3},{3,0},{4,5},{5,6},{6,7},{7,4},{8,9},{9,10},{10,1... | collective-permute-start | bytes 589832 | tf_op jit(solution)/shard_map/ppermute | solution.py:394
  131.6 45.7 %copy-start.9 = (f32[1,768]{1,0:T(1,128)S(1)}, f32[1,768]{1,0:T(1,128)}, u32[]{:S(2)}) copy-start(f32[1,768]{1,0:T(1,128)} %get-tuple-element.89.refs_16_) | copy-start | bytes 9220
  131.7 92.4 %all-gather.8.cloned.1.call-start = ((), (), s32[]{:S(2)}) async-start(), calls=%async_computation.5 | async-start | bytes 2654208 | tf_op jit(solution)/shard_map/all_gather | solution.py:1027
  132.5 9.7 %collective-permute-start.15 = (bf16[128,768]{1,0:T(8,128)(2,1)S(1)}, bf16[128,768]{1,0:T(8,128)(2,1)S(1)}, u32[]{:S(2)}, u32[]{:S(2)}) collective-permute-start(bf16[128,768]{1,0:T(8,128)(2,1)S(1)} %copy-done.16), channel_id=1, source_target_pairs={{0,1},{1,2},{2,3},{3,0},{4,5},{5,6},{6,7},{7,4},{8,9},{9,10},{10,1... | collective-permute-start | bytes 589832 | tf_op jit(solution)/shard_map/ppermute | solution.py:402
  132.6 16.3 %collective-permute-start.16 = (bf16[128,768]{1,0:T(8,128)(2,1)S(1)}, bf16[128,768]{1,0:T(8,128)(2,1)S(1)}, u32[]{:S(2)}, u32[]{:S(2)}) collective-permute-start(bf16[128,768]{1,0:T(8,128)(2,1)S(1)} %copy-done.15), channel_id=1, source_target_pairs={{0,2},{1,3},{2,0},{3,1},{4,6},{5,7},{6,4},{7,5},{8,10},{9,11},{10,... | collective-permute-start | bytes 589832 | tf_op jit(solution)/shard_map/ppermute | solution.py:402
  133.7 15.3 %collective-permute-start.17 = (bf16[128,768]{1,0:T(8,128)(2,1)S(1)}, bf16[128,768]{1,0:T(8,128)(2,1)S(1)}, u32[]{:S(2)}, u32[]{:S(2)}) collective-permute-start(bf16[128,768]{1,0:T(8,128)(2,1)S(1)} %copy-done.14), channel_id=1, source_target_pairs={{0,3},{1,0},{2,1},{3,2},{4,7},{5,4},{6,5},{7,6},{8,11},{9,8},{10,9... | collective-permute-start | bytes 589832 | tf_op jit(solution)/shard_map/ppermute | solution.py:402
  151.4 9.8 %collective-permute-start.20 = (bf16[128,768]{1,0:T(8,128)(2,1)}, bf16[128,768]{1,0:T(8,128)(2,1)S(1)}, u32[]{:S(2)}, u32[]{:S(2)}) collective-permute-start(bf16[128,768]{1,0:T(8,128)(2,1)} %get-tuple-element.85.refs_1_), channel_id=1, source_target_pairs={{0,3},{1,0},{2,1},{3,2},{4,7},{5,4},{6,5},{7,6},{8,11},{9,8},{10,9... | collective-permute-start | bytes 589832 | tf_op jit(solution)/shard_map/ppermute | solution.py:394
  155.6 18.2 %collective-permute-start.19 = (bf16[128,768]{1,0:T(8,128)(2,1)}, bf16[128,768]{1,0:T(8,128)(2,1)S(1)}, u32[]{:S(2)}, u32[]{:S(2)}) collective-permute-start(bf16[128,768]{1,0:T(8,128)(2,1)} %get-tuple-element.85.refs_1_), channel_id=1, source_target_pairs={{0,2},{1,3},{2,0},{3,1},{4,6},{5,7},{6,4},{7,5},{8,10},{9,11},{10,... | collective-permute-start | bytes 589832 | tf_op jit(solution)/shard_map/ppermute | solution.py:394
  156.8 17.0 %collective-permute-start.18 = (bf16[128,768]{1,0:T(8,128)(2,1)}, bf16[128,768]{1,0:T(8,128)(2,1)S(1)}, u32[]{:S(2)}, u32[]{:S(2)}) collective-permute-start(bf16[128,768]{1,0:T(8,128)(2,1)} %get-tuple-element.85.refs_1_), channel_id=1, source_target_pairs={{0,1},{1,2},{2,3},{3,0},{4,5},{5,6},{6,7},{7,4},{8,9},{9,10},{10,1... | collective-permute-start | bytes 589832 | tf_op jit(solution)/shard_map/ppermute | solution.py:394
  161.3 16.1 %copy-start.6 = (bf16[128,768]{1,0:T(8,128)(2,1)}, bf16[128,768]{1,0:T(8,128)(2,1)S(1)}, u32[]{:S(2)}) copy-start(bf16[128,768]{1,0:T(8,128)(2,1)S(1)} %collective-permute-done.20.refs_5_.refs_4_) | copy-start | bytes 589828
  176.7 12.7 %collective-permute-start.28 = (bf16[96,768]{1,0:T(8,128)(2,1)S(1)}, bf16[96,768]{1,0:T(8,128)(2,1)S(1)}, u32[]{:S(2)}, u32[]{:S(2)}) collective-permute-start(bf16[96,768]{1,0:T(8,128)(2,1)S(1)} %get-tuple-element.94.refs_17_), channel_id=1, source_target_pairs={{0,2},{1,3},{2,0},{3,1},{4,6},{5,7},{6,4},{7,5},{8,10},{9,11},{10,... | collective-permute-start | bytes 442376 | tf_op jit(solution)/shard_map/ppermute | solution.py:408
  191.5 93.7 %reduce-scatter.5.cloned.1.call-start = ((), (), s32[]{:S(2)}) async-start(), calls=%async_computation.6 | async-start | bytes 983040 | tf_op jit(solution)/shard_map/reduce_scatter | solution.py:1057
  191.6 2.2 collective-permute-start.21
  195.9 9.6 %collective-permute-start.22 = (bf16[112,768]{1,0:T(8,128)(2,1)S(1)}, bf16[112,768]{1,0:T(8,128)(2,1)S(1)}, u32[]{:S(2)}, u32[]{:S(2)}) collective-permute-start(bf16[112,768]{1,0:T(8,128)(2,1)S(1)} %get-tuple-element.99), channel_id=1, source_target_pairs={{0,8},{4,12},{8,0},{12,4},{16,24},{20,28},{24,16},{28,20},{1,9},{5... | collective-permute-start | bytes 516104 | tf_op jit(solution)/shard_map/ppermute | solution.py:408
  197.3 13.0 %collective-permute-start.23 = (bf16[112,768]{1,0:T(8,128)(2,1)S(1)}, bf16[112,768]{1,0:T(8,128)(2,1)S(1)}, u32[]{:S(2)}, u32[]{:S(2)}) collective-permute-start(bf16[112,768]{1,0:T(8,128)(2,1)S(1)} %get-tuple-element.100), channel_id=1, source_target_pairs={{0,16},{4,20},{8,24},{12,28},{16,0},{20,4},{24,8},{28,12},{1,17},{... | collective-permute-start | bytes 516104 | tf_op jit(solution)/shard_map/ppermute | solution.py:408
  197.9 12.4 %collective-permute-start.24 = (bf16[112,768]{1,0:T(8,128)(2,1)S(1)}, bf16[112,768]{1,0:T(8,128)(2,1)S(1)}, u32[]{:S(2)}, u32[]{:S(2)}) collective-permute-start(bf16[112,768]{1,0:T(8,128)(2,1)S(1)} %get-tuple-element.101), channel_id=1, source_target_pairs={{0,24},{4,28},{8,16},{12,20},{16,8},{20,12},{24,0},{28,4},{1,25},{... | collective-permute-start | bytes 516104 | tf_op jit(solution)/shard_map/ppermute | solution.py:408
  212.9 6.5 %collective-permute-start.25 = (bf16[112,192]{1,0:T(8,128)(2,1)S(1)}, bf16[112,192]{1,0:T(8,128)(2,1)S(1)}, u32[]{:S(2)}, u32[]{:S(2)}) collective-permute-start(bf16[112,192]{1,0:T(8,128)(2,1)S(1)} %get-tuple-element.103), channel_id=1, source_target_pairs={{0,1},{1,2},{2,3},{3,0},{4,5},{5,6},{6,7},{7,4},{8,9},{9,10},{10,1... | collective-permute-start | bytes 129032 | tf_op jit(solution)/shard_map/ppermute | solution.py:402
  214.4 6.2 %collective-permute-start.26 = (bf16[112,192]{1,0:T(8,128)(2,1)S(1)}, bf16[112,192]{1,0:T(8,128)(2,1)S(1)}, u32[]{:S(2)}, u32[]{:S(2)}) collective-permute-start(bf16[112,192]{1,0:T(8,128)(2,1)S(1)} %get-tuple-element.104), channel_id=1, source_target_pairs={{0,2},{1,3},{2,0},{3,1},{4,6},{5,7},{6,4},{7,5},{8,10},{9,11},{10,... | collective-permute-start | bytes 129032 | tf_op jit(solution)/shard_map/ppermute | solution.py:402
  215.4 5.3 %collective-permute-start.27 = (bf16[112,192]{1,0:T(8,128)(2,1)S(1)}, bf16[112,192]{1,0:T(8,128)(2,1)S(1)}, u32[]{:S(2)}, u32[]{:S(2)}) collective-permute-start(bf16[112,192]{1,0:T(8,128)(2,1)S(1)} %get-tuple-element.105), channel_id=1, source_target_pairs={{0,3},{1,0},{2,1},{3,2},{4,7},{5,4},{6,5},{7,6},{8,11},{9,8},{10,9... | collective-permute-start | bytes 129032 | tf_op jit(solution)/shard_map/ppermute | solution.py:402
  226.7 6.1 %collective-permute-start.29 = (bf16[96,768]{1,0:T(8,128)(2,1)S(1)}, bf16[96,768]{1,0:T(8,128)(2,1)S(1)}, u32[]{:S(2)}, u32[]{:S(2)}) collective-permute-start(bf16[96,768]{1,0:T(8,128)(2,1)S(1)} %shard_map.229.refs_5_), channel_id=1, source_target_pairs={{0,1},{1,0},{2,3},{3,2},{4,5},{5,4},{6,7},{7,6},{8,9},{9,8},{10,11... | collective-permute-start | bytes 442376 | tf_op jit(solution)/shard_map/ppermute | solution.py:408
  237.1 1.4 collective-permute-start.30
  238.5 33.2 %copy-start.13 = (f32[12,24]{1,0:T(8,128)S(1)}, f32[12,24]{1,0:T(8,128)}, u32[]{:S(2)}) copy-start(f32[12,24]{1,0:T(8,128)} %param.21) | copy-start | bytes 3460
  239.1 10.9 %collective-permute-start.33 = (bf16[192,768]{1,0:T(8,128)(2,1)S(1)}, bf16[192,768]{1,0:T(8,128)(2,1)S(1)}, u32[]{:S(2)}, u32[]{:S(2)}) collective-permute-start(bf16[192,768]{1,0:T(8,128)(2,1)S(1)} %shard_map.232.refs_1_), channel_id=1, source_target_pairs={{0,24},{4,28},{8,16},{12,20},{16,8},{20,12},{24,0},{28,4},{1,25},{... | collective-permute-start | bytes 884744 | tf_op jit(solution)/shard_map/ppermute | solution.py:408
  240.6 14.8 %collective-permute-start.32 = (bf16[192,768]{1,0:T(8,128)(2,1)S(1)}, bf16[192,768]{1,0:T(8,128)(2,1)S(1)}, u32[]{:S(2)}, u32[]{:S(2)}) collective-permute-start(bf16[192,768]{1,0:T(8,128)(2,1)S(1)} %shard_map.232.refs_1_), channel_id=1, source_target_pairs={{0,16},{4,20},{8,24},{12,28},{16,0},{20,4},{24,8},{28,12},{1,17},{... | collective-permute-start | bytes 884744 | tf_op jit(solution)/shard_map/ppermute | solution.py:408
  242.1 13.3 %collective-permute-start.31 = (bf16[192,768]{1,0:T(8,128)(2,1)S(1)}, bf16[192,768]{1,0:T(8,128)(2,1)S(1)}, u32[]{:S(2)}, u32[]{:S(2)}) collective-permute-start(bf16[192,768]{1,0:T(8,128)(2,1)S(1)} %shard_map.232.refs_1_), channel_id=1, source_target_pairs={{0,8},{4,12},{8,0},{12,4},{16,24},{20,28},{24,16},{28,20},{1,9},{5... | collective-permute-start | bytes 884744 | tf_op jit(solution)/shard_map/ppermute | solution.py:408
  264.8 1.6 collective-permute-start.34
  267.3 6.1 %collective-permute-start.35 = (bf16[96,192]{1,0:T(8,128)(2,1)S(1)}, bf16[96,192]{1,0:T(8,128)(2,1)S(1)}, u32[]{:S(2)}, u32[]{:S(2)}) collective-permute-start(bf16[96,192]{1,0:T(8,128)(2,1)S(1)} %get-tuple-element.111), channel_id=1, source_target_pairs={{0,1},{1,2},{2,3},{3,0},{4,5},{5,6},{6,7},{7,4},{8,9},{9,10},{10,1... | collective-permute-start | bytes 110600 | tf_op jit(solution)/shard_map/ppermute | solution.py:402
  268.8 4.6 %collective-permute-start.37 = (bf16[96,192]{1,0:T(8,128)(2,1)S(1)}, bf16[96,192]{1,0:T(8,128)(2,1)S(1)}, u32[]{:S(2)}, u32[]{:S(2)}) collective-permute-start(bf16[96,192]{1,0:T(8,128)(2,1)S(1)} %get-tuple-element.121), channel_id=1, source_target_pairs={{0,3},{1,0},{2,1},{3,2},{4,7},{5,4},{6,5},{7,6},{8,11},{9,8},{10,9... | collective-permute-start | bytes 110600 | tf_op jit(solution)/shard_map/ppermute | solution.py:402
  271.2 11.2 %collective-permute-start.36 = (bf16[96,960]{1,0:T(8,128)(2,1)S(1)}, bf16[96,960]{1,0:T(8,128)(2,1)S(1)}, u32[]{:S(2)}, u32[]{:S(2)}) collective-permute-start(bf16[96,960]{1,0:T(8,128)(2,1)S(1)} %get-tuple-element.120), channel_id=1, source_target_pairs={{0,2},{1,3},{2,0},{3,1},{4,6},{5,7},{6,4},{7,5},{8,10},{9,11},{10,... | collective-permute-start | bytes 552968 | tf_op jit(solution)/shard_map/ppermute | solution.py:402
  (13 other events, 45.0 us)
Sparse Core Ops, SparseCore 0:
  10.5 36.1 all-gather.3
  49.2 24.0 all-gather.5
  131.8 40.2 reduce-scatter.2
  191.7 32.3 all-gather.7
  237.2 23.2 reduce-scatter.4

commit v6 on v5

--- a/solution.py
+++ b/solution.py
@@ -1051,14 +1051,14 @@
         scratch=[pltpu.VMEM((depth, width), bf16)],
     )(place, *square_pieces, gram_rows, swap(gram_rows, "shard", 1))
     grad_vec = grad_vec[:vec_rows, :vec_own]
-    (part,) = run_kernel(
-        token_part, [whole_b], ties=[other], far=(0, 1), far_out=(0,), lanes={1: proj_lanes}
-    )(d_proj, weights)
-    d_tokens = lax.psum_scatter(part, "shard", scatter_dimension=0, tiled=True)
     (pair_rows,) = run_kernel(
         join_pair, [jax.ShapeDtypeStruct((2 * depth, width), bf16)], scalars=1
     )(place, mine, swap(other, "dp", 1))
     pair_pieces = [pair_rows] + [swap(pair_rows, "dp", bit) for bit in (2, 4, 6)]
+    (part,) = run_kernel(
+        token_part, [whole_b], ties=[pair_rows], far=(0, 1), far_out=(0,), lanes={1: proj_lanes}
+    )(d_proj, weights)
+    d_tokens = lax.psum_scatter(part, "shard", scatter_dimension=0, tiled=True)
     state_kind = jax.ShapeDtypeStruct((depth, 2 * hidden), bf16)
     kept, sent = run_kernel(
         newton_schulz,
@@ -1080,18 +1080,19 @@
     (d_tokens,) = run_kernel(add_rows, [own_f], ties=[state_pieces[1]], far=(0, 1), far_out=(0,))(
         d_first_in, d_tokens
     )
-    d_tokens = d_tokens.reshape(tokens.shape)
     qkv_new, out_new, ffn_new = run_kernel(
         new_weights,
         [jax.ShapeDtypeStruct(each.shape, each.dtype) for each in (qkv_w, out_w, ffn_w)],
         scalars=1,
         scratch=[pltpu.VMEM((shards, depth, own), jnp.float32)],
+        ties=[d_tokens],
         far=(6, 7, 8),
         far_out=(0, 1, 2),
     )(
         place, *state_pieces, mine, qkv_w, out_w, ffn_w
     )
 
+    d_tokens = d_tokens.reshape(tokens.shape)
     token_count = micro * rows * groups * shards
     new_vec_mom = momentum_decay * vec_mom + grad_vec
     vec_new = vecs - vec_rate * token_count ** (-0.5) * new_vec_mom

time: 294 us -> 293 us (level)
  transfers between devices with their start and end apart: 43 -> 43, of which waited for: 29 -> 29; matrix products, arithmetic and copies ran while one was open for 2% -> 2% of each run, Pallas kernels for 13% -> 12%
where the time goes in v6:
time: 293 us
  waiting for transfers between devices  141 us (48%)
  Pallas kernels  66.9 us (23%)
  starting transfers between devices  58 us (20%)
  between operations  14.4 us (5%)
  local copies, waits for them, and re-layouts  8.9 us (3%)
  other arithmetic  3.51 us (1%)
    pallas_call x19, Pallas kernels, call(): pl.pallas_call(whole, out_shape=kinds, in_specs=[pl.BlockSpec(memory_spac...  66.9 us
    ppermute x14, waiting for transfers between devices, swap(): lax.ppermute(block, axis, [(i, i ^ bit) for i in range(lax.axis_size(axis...  36.9 us
    ppermute x12, waiting for transfers between devices, send_parts(): lax.ppermute(parts[step], axis, [(i, (i + step) % count) for i in range(c...  35.1 us
    ppermute x9, waiting for transfers between devices, pieces_of(): lax.ppermute(block, axis, [(i, (i + step) % count) for i in range(count)])  34.4 us
    ppermute x12, starting transfers between devices, send_parts(): lax.ppermute(parts[step], axis, [(i, (i + step) % count) for i in range(c...  19.1 us
    ppermute x9, starting transfers between devices, pieces_of(): lax.ppermute(block, axis, [(i, (i + step) % count) for i in range(count)])  18 us
    all_gather x1, waiting for transfers between devices, split_device(): out_b = lax.all_gather(out_part, 'dp', axis=0, tiled=True)  15.3 us
    ppermute x3, waiting for transfers between devices, gather_direct(): lax.ppermute(block, axis, [(i, (i + step) % count) for i in range(count)])  14 us
  transfers between devices with their start and end apart: 43, of which 29 were waited for; matrix products, arithmetic and copies ran while one was open for 2% of the time, Pallas kernels for 12%

profile of v6, /device:TPU:0, one launch (start us, length us, event | category | flops | bytes accessed | tf_op | source)
XLA Modules:
  0.0 292.7 jit_solution(503435313646402436)
XLA Ops:
  10.9 4.1 %collective-permute-start.1 = (bf16[160,768]{1,0:T(8,128)(2,1)S(1)}, bf16[160,768]{1,0:T(8,128)(2,1)S(1)}, u32[]{:S(2)}, u32[]{:S(2)}) collective-permute-start(bf16[160,768]{1,0:T(8,128)(2,1)S(1)} %pad_maximum_fusion), channel_id=1, source_target_pairs={{0,2},{1,3},{2,0},{3,1},{4,6},{5,7},{6,4},{7,5},{8,10},{9,11},{10,... | collective-permute-start | bytes 737288 | tf_op jit(solution)/shard_map/ppermute | solution.py:386
  16.6 2.2 collective-permute-start.2
  19.1 9.5 %collective-permute-done = bf16[160,768]{1,0:T(8,128)(2,1)S(1)} collective-permute-done((bf16[160,768]{1,0:T(8,128)(2,1)S(1)}, bf16[160,768]{1,0:T(8,128)(2,1)S(1)}, u32[]{:S(2)}, u32[]{:S(2)}) %collective-permute-start) | collective-permute-done | bytes 245792 | tf_op jit(solution)/shard_map/ppermute | solution.py:386
  28.6 3.8 %collective-permute-done.1 = bf16[160,768]{1,0:T(8,128)(2,1)S(1)} collective-permute-done((bf16[160,768]{1,0:T(8,128)(2,1)S(1)}, bf16[160,768]{1,0:T(8,128)(2,1)S(1)}, u32[]{:S(2)}, u32[]{:S(2)}) %collective-permute-start.1) | collective-permute-done | bytes 245792 | tf_op jit(solution)/shard_map/ppermute | solution.py:386
  36.3 1.6 collective-permute-start.4
  38.1 2.1 collective-permute-done.4
  40.2 1.6 collective-permute-start.5
  45.0 1.8 all-gather.4.cloned.1.call-done.refs_2_.refs_8_.refs_6_.refs_1_
  46.7 4.8 %shard_map.218 = (bf16[512,576]{1,0:T(8,128)(2,1)}, bf16[256,384]{1,0:T(8,128)(2,1)S(1)}) custom-call(s32[3]{0:T(128)S(1)} %pad_add_fusion.refs_0_, bf16[512,768]{1,0:T(8,128)(2,1)} %bitcast.38, bf16[768,2176]{1,0:T(8,128)(2,1)} %all-gather.4.cloned.1.call-done.refs_2_.refs_8_.refs_6_.refs_1_, f32[1,576]{1,0:T(1,128)S(1)} %broadcast_in_dim.38.refs_3_, ...), custom_call_target="tpu_custom_call" | custom-call | tf_op jit(solution)/shard_map/pallas_call | solution.py:821
  51.6 3.4 %collective-permute-start.8 = (bf16[256,384]{1,0:T(8,128)(2,1)S(1)}, bf16[256,384]{1,0:T(8,128)(2,1)S(1)}, u32[]{:S(2)}, u32[]{:S(2)}) collective-permute-start(bf16[256,384]{1,0:T(8,128)(2,1)S(1)} %get-tuple-element.70.refs_1_.refs_5_), channel_id=1, source_target_pairs={{0,3},{1,0},{2,1},{3,2},{4,7},{5,4},{6,5},{7,6},{8,11},{9,8},{10,9... | collective-permute-start | bytes 589832 | tf_op jit(solution)/shard_map/ppermute | solution.py:394
  56.0 1.9 collective-permute-start.6
  58.0 15.3 %all-gather.6.cloned.1.call-done.refs_5_.refs_9_ = bf16[768,768]{1,0:T(8,128)(2,1)} async-done(((bf16[96,768]{1,0:T(8,128)(2,1)}), bf16[768,768]{1,0:T(8,128)(2,1)}) %all-gather.6.cloned.1.call-update) | async-done | bytes 1179664 | tf_op jit(solution)/shard_map/all_gather | solution.py:926
  73.3 6.2 %shard_map.219 = (bf16[512,768]{1,0:T(8,128)(2,1)S(1)}, bf16[512,768]{1,0:T(8,128)(2,1)S(1)}, f32[512,768]{1,0:T(8,128)S(1)}, f32[128,768]{1,0:T(8,128)S(1)}, f3...) custom-call(s32[3]{0:T(128)S(1)} %pad_add_fusion.refs_0_, ...), custom_call_target="tpu_custom_call" | custom-call | tf_op jit(solution)/shard_map/pallas_call | solution.py:821
  81.1 2.4 collective-permute-start.10
  84.9 4.3 %collective-permute-done.9.refs_2_ = bf16[128,768]{1,0:T(8,128)(2,1)S(1)} collective-permute-done((bf16[128,768]{1,0:T(8,128)(2,1)S(1)}, bf16[128,768]{1,0:T(8,128)(2,1)S(1)}, u32[]{:S(2)}, u32[]{:S(2)}) %collective-permute-start.9) | collective-permute-done | bytes 196640 | tf_op jit(solution)/shard_map/ppermute | solution.py:402
  89.3 7.8 %collective-permute-done.10.refs_3_ = bf16[128,768]{1,0:T(8,128)(2,1)S(1)} collective-permute-done((bf16[128,768]{1,0:T(8,128)(2,1)S(1)}, bf16[128,768]{1,0:T(8,128)(2,1)S(1)}, u32[]{:S(2)}, u32[]{:S(2)}) %collective-permute-start.10) | collective-permute-done | bytes 196640 | tf_op jit(solution)/shard_map/ppermute | solution.py:402
  97.1 3.1 %shard_map.220 = (bf16[128,768]{1,0:T(8,128)(2,1)}, bf16[128,768]{1,0:T(8,128)(2,1)S(1)}, f32[128,768]{1,0:T(8,128)}, f32[8,768]{1,0:T(8,128)}) custom-call(s32[3]{0:T(128)S(1)} %pad_add_fusion.refs_0_, f32[128,768]{1,0:T(8,128)S(1)} %get-tuple-element.71.refs_1_, bf16[128,768]{1,0:T(8,128)(2,1)S(1)} %collective-permute-done.9.refs_2_, ...), custom_call_target="tpu_custom_call" | custom-call | tf_op jit(solution)/shard_map/pallas_call | solution.py:821
  100.1 5.6 %collective-permute-start.14 = (bf16[128,768]{1,0:T(8,128)(2,1)S(1)}, bf16[128,768]{1,0:T(8,128)(2,1)S(1)}, u32[]{:S(2)}, u32[]{:S(2)}) collective-permute-start(bf16[128,768]{1,0:T(8,128)(2,1)S(1)} %get-tuple-element.77.refs_1_), channel_id=1, source_target_pairs={{0,3},{1,0},{2,1},{3,2},{4,7},{5,4},{6,5},{7,6},{8,11},{9,8},{10,9... | collective-permute-start | bytes 589832 | tf_op jit(solution)/shard_map/ppermute | solution.py:394
  106.4 4.8 %collective-permute-done.14.refs_4_ = bf16[128,768]{1,0:T(8,128)(2,1)S(1)} collective-permute-done((bf16[128,768]{1,0:T(8,128)(2,1)S(1)}, bf16[128,768]{1,0:T(8,128)(2,1)S(1)}, u32[]{:S(2)}, u32[]{:S(2)}) %collective-permute-start.14) | collective-permute-done | bytes 196640 | tf_op jit(solution)/shard_map/ppermute | solution.py:394
  111.2 12.6 %collective-permute-done.13.refs_3_ = bf16[128,768]{1,0:T(8,128)(2,1)S(1)} collective-permute-done((bf16[128,768]{1,0:T(8,128)(2,1)S(1)}, bf16[128,768]{1,0:T(8,128)(2,1)S(1)}, u32[]{:S(2)}, u32[]{:S(2)}) %collective-permute-start.13) | collective-permute-done | bytes 196640 | tf_op jit(solution)/shard_map/ppermute | solution.py:394
  123.8 4.9 %shard_map.221 = (bf16[512,768]{1,0:T(8,128)(2,1)S(1)}, bf16[512,768]{1,0:T(8,128)(2,1)S(1)}, f32[1,768]{1,0:T(1,128)}, f32[128,768]{1,0:T(8,128)}, bf16[128,768...) custom-call(s32[3]{0:T(128)S(1)} %pad_add_fusion.refs_0_, ...), custom_call_target="tpu_custom_call" | custom-call | tf_op jit(solution)/shard_map/pallas_call | solution.py:821
  128.7 2.9 shard_map.223
  133.6 2.8 collective-permute-start.17
  136.5 5.8 %collective-permute-done.15.refs_1_ = bf16[128,768]{1,0:T(8,128)(2,1)S(1)} collective-permute-done((bf16[128,768]{1,0:T(8,128)(2,1)S(1)}, bf16[128,768]{1,0:T(8,128)(2,1)S(1)}, u32[]{:S(2)}, u32[]{:S(2)}) %collective-permute-start.15) | collective-permute-done | bytes 196640 | tf_op jit(solution)/shard_map/ppermute | solution.py:402
  142.3 6.7 %collective-permute-done.16.refs_2_ = bf16[128,768]{1,0:T(8,128)(2,1)S(1)} collective-permute-done((bf16[128,768]{1,0:T(8,128)(2,1)S(1)}, bf16[128,768]{1,0:T(8,128)(2,1)S(1)}, u32[]{:S(2)}, u32[]{:S(2)}) %collective-permute-start.16) | collective-permute-done | bytes 196640 | tf_op jit(solution)/shard_map/ppermute | solution.py:402
  148.9 2.5 shard_map.222
  151.4 4.1 %collective-permute-start.20 = (bf16[128,768]{1,0:T(8,128)(2,1)}, bf16[128,768]{1,0:T(8,128)(2,1)S(1)}, u32[]{:S(2)}, u32[]{:S(2)}) collective-permute-start(bf16[128,768]{1,0:T(8,128)(2,1)} %get-tuple-element.85.refs_1_), channel_id=1, source_target_pairs={{0,3},{1,0},{2,1},{3,2},{4,7},{5,4},{6,5},{7,6},{8,11},{9,8},{10,9... | collective-permute-start | bytes 589832 | tf_op jit(solution)/shard_map/ppermute | solution.py:394
  156.8 4.5 %collective-permute-done.20.refs_5_.refs_4_ = bf16[128,768]{1,0:T(8,128)(2,1)S(1)} collective-permute-done((bf16[128,768]{1,0:T(8,128)(2,1)}, bf16[128,768]{1,0:T(8,128)(2,1)S(1)}, u32[]{:S(2)}, u32[]{:S(2)}) %collective-permute-start.20) | collective-permute-done | bytes 196640 | tf_op jit(solution)/shard_map/ppermute | solution.py:394
  161.3 12.5 %collective-permute-done.19.refs_4_.refs_3_ = bf16[128,768]{1,0:T(8,128)(2,1)S(1)} collective-permute-done((bf16[128,768]{1,0:T(8,128)(2,1)}, bf16[128,768]{1,0:T(8,128)(2,1)S(1)}, u32[]{:S(2)}, u32[]{:S(2)}) %collective-permute-start.19) | collective-permute-done | bytes 196640 | tf_op jit(solution)/shard_map/ppermute | solution.py:394
  173.8 2.9 shard_map.224
  177.4 12.0 %shard_map.225 = (f32[4,112,768]{2,1,0:T(8,128)}, bf16[4,112,768]{2,1,0:T(8,128)(2,1)S(1)}, bf16[512,576]{1,0:T(8,128)(2,1)}) custom-call(s32[3]{0:T(128)S(1)} %pad_add_fusion.refs_0_, bf16[128,768]{1,0:T(8,128)(2,1)} %get-tuple-element.85.refs_1_, bf16[128,768]{1,0:T(8,128)(2,1)} %copy-done.9, bf16[128,768]{1,0:T(8,128)(2,1)} %copy-done.8, ...), custom_call_target="tpu_custom_call" | custom-call | tf_op jit(solution)/shard_map/pallas_call | solution.py:821
  191.6 2.1 collective-permute-done.21.refs_2_
  193.8 2.1 shard_map.226
  199.4 6.0 %collective-permute-done.22.refs_2_ = bf16[112,768]{1,0:T(8,128)(2,1)S(1)} collective-permute-done((bf16[112,768]{1,0:T(8,128)(2,1)S(1)}, bf16[112,768]{1,0:T(8,128)(2,1)S(1)}, u32[]{:S(2)}, u32[]{:S(2)}) %collective-permute-start.22) | collective-permute-done | bytes 172064 | tf_op jit(solution)/shard_map/ppermute | solution.py:408
  205.4 4.9 %collective-permute-done.23.refs_3_ = bf16[112,768]{1,0:T(8,128)(2,1)S(1)} collective-permute-done((bf16[112,768]{1,0:T(8,128)(2,1)S(1)}, bf16[112,768]{1,0:T(8,128)(2,1)S(1)}, u32[]{:S(2)}, u32[]{:S(2)}) %collective-permute-start.23) | collective-permute-done | bytes 172064 | tf_op jit(solution)/shard_map/ppermute | solution.py:408
  210.3 2.6 shard_map.227
  215.4 2.8 collective-permute-start.27
  220.6 3.4 %all-gather.8.cloned.1.call-done.refs_1_.refs_5_ = bf16[768,1536]{1,0:T(8,128)(2,1)} async-done(((bf16[96,1536]{1,0:T(8,128)(2,1)}), bf16[768,1536]{1,0:T(8,128)(2,1)}) %all-gather.8.cloned.1.call-update) | async-done | bytes 2359312 | tf_op jit(solution)/shard_map/all_gather | solution.py:1027
  224.0 2.6 shard_map.229.refs_5_
  228.2 4.5 %collective-permute-done.29.refs_6_ = bf16[96,768]{1,0:T(8,128)(2,1)S(1)} collective-permute-done((bf16[96,768]{1,0:T(8,128)(2,1)S(1)}, bf16[96,768]{1,0:T(8,128)(2,1)S(1)}, u32[]{:S(2)}, u32[]{:S(2)}) %collective-permute-start.29) | collective-permute-done | bytes 147488 | tf_op jit(solution)/shard_map/ppermute | solution.py:408
  235.9 3.1 %shard_map.232 = bf16[512,768]{1,0:T(8,128)(2,1)} custom-call(bf16[512,576]{1,0:T(8,128)(2,1)} %get-tuple-element.95.refs_0_, bf16[768,2176]{1,0:T(8,128)(2,1)} %all-gather.4.cloned.1.call-done.refs_2_.refs_8_.refs_6_.refs_1_, bf16[192,768]{1,0:T(8,128)(2,1)S(1)} %shard_map.231.refs_2_.refs_1_), custom_call_target="tpu_custom_call" | custom-call | tf_op jit(solution)/shard_map/pallas_call | solution.py:821
  242.6 7.3 %collective-permute-done.33.refs_4_ = bf16[192,768]{1,0:T(8,128)(2,1)S(1)} collective-permute-done((bf16[192,768]{1,0:T(8,128)(2,1)S(1)}, bf16[192,768]{1,0:T(8,128)(2,1)S(1)}, u32[]{:S(2)}, u32[]{:S(2)}) %collective-permute-start.33) | collective-permute-done | bytes 294944 | tf_op jit(solution)/shard_map/ppermute | solution.py:408
  249.9 5.5 %collective-permute-done.32.refs_3_ = bf16[192,768]{1,0:T(8,128)(2,1)S(1)} collective-permute-done((bf16[192,768]{1,0:T(8,128)(2,1)S(1)}, bf16[192,768]{1,0:T(8,128)(2,1)S(1)}, u32[]{:S(2)}, u32[]{:S(2)}) %collective-permute-start.32) | collective-permute-done | bytes 294944 | tf_op jit(solution)/shard_map/ppermute | solution.py:408
  255.4 9.4 %shard_map.233 = (bf16[96,1536]{1,0:T(8,128)(2,1)S(1)}, bf16[96,1536]{1,0:T(8,128)(2,1)S(1)}) custom-call(s32[3]{0:T(128)S(1)} %pad_add_fusion.refs_0_, bf16[192,768]{1,0:T(8,128)(2,1)S(1)} %shard_map.231.refs_2_.refs_1_, bf16[192,768]{1,0:T(8,128)(2,1)S(1)} %collective-permute-done.31.refs_2_, bf16[192,768]{1,0:T(8,128)(2,1)S(1)} %collective-permute-done.32.refs_3_, ...), custom_call_target="tpu_custom_call" | custom-call | tf_op jit(solution)/shard_map/pallas_call | solution.py:821
  268.8 2.3 collective-permute-start.37
  273.4 1.8 shard_map.235.refs_9_
  275.3 7.1 %collective-permute-done.36.refs_3_ = bf16[96,960]{1,0:T(8,128)(2,1)S(1)} collective-permute-done((bf16[96,960]{1,0:T(8,128)(2,1)S(1)}, bf16[96,960]{1,0:T(8,128)(2,1)S(1)}, u32[]{:S(2)}, u32[]{:S(2)}) %collective-permute-start.36) | collective-permute-done | bytes 184352 | tf_op jit(solution)/shard_map/ppermute | solution.py:402
  283.4 2.8 shard_map.236
  (164 shorter events, 47.3 us)
Async XLA Ops:
  7.2 39.5 %all-gather.4.cloned.1.call-start = ((), (), s32[]{:S(2)}) async-start(), calls=%async_computation.2 | async-start | bytes 3760128 | tf_op jit(solution)/shard_map/all_gather | solution.py:908
  10.4 62.9 %all-gather.6.cloned.1.call-start = ((), (), s32[]{:S(2)}) async-start(), calls=%async_computation.3 | async-start | bytes 1327104 | tf_op jit(solution)/shard_map/all_gather | solution.py:926
  10.9 21.5 %collective-permute-start.1 = (bf16[160,768]{1,0:T(8,128)(2,1)S(1)}, bf16[160,768]{1,0:T(8,128)(2,1)S(1)}, u32[]{:S(2)}, u32[]{:S(2)}) collective-permute-start(bf16[160,768]{1,0:T(8,128)(2,1)S(1)} %pad_maximum_fusion), channel_id=1, source_target_pairs={{0,2},{1,3},{2,0},{3,1},{4,6},{5,7},{6,4},{7,5},{8,10},{9,11},{10,... | collective-permute-start | bytes 737288 | tf_op jit(solution)/shard_map/ppermute | solution.py:386
  15.0 13.5 %collective-permute-start = (bf16[160,768]{1,0:T(8,128)(2,1)S(1)}, bf16[160,768]{1,0:T(8,128)(2,1)S(1)}, u32[]{:S(2)}, u32[]{:S(2)}) collective-permute-start(bf16[160,768]{1,0:T(8,128)(2,1)S(1)} %pad_maximum_fusion), channel_id=1, source_target_pairs={{0,1},{1,2},{2,3},{3,0},{4,5},{5,6},{6,7},{7,4},{8,9},{9,10},{10,1... | collective-permute-start | bytes 737288 | tf_op jit(solution)/shard_map/ppermute | solution.py:386
  16.6 16.5 %collective-permute-start.2 = (bf16[160,768]{1,0:T(8,128)(2,1)S(1)}, bf16[160,768]{1,0:T(8,128)(2,1)S(1)}, u32[]{:S(2)}, u32[]{:S(2)}) collective-permute-start(bf16[160,768]{1,0:T(8,128)(2,1)S(1)} %pad_maximum_fusion), channel_id=1, source_target_pairs={{0,3},{1,0},{2,1},{3,2},{4,7},{5,4},{6,5},{7,6},{8,11},{9,8},{10,9... | collective-permute-start | bytes 737288 | tf_op jit(solution)/shard_map/ppermute | solution.py:386
  34.5 139.4 %reduce-scatter.3.cloned.1.call-start = ((), (), s32[]{:S(2)}) async-start(), calls=%async_computation.4 | async-start | bytes 2654208 | tf_op jit(solution)/shard_map/reduce_scatter | solution.py:989
  35.1 1.2 collective-permute-start.3
  36.3 3.9 %collective-permute-start.4 = (bf16[2,12,96]{2,1,0:T(8,128)(2,1)S(1)}, bf16[2,12,96]{2,1,0:T(8,128)(2,1)S(1)}, u32[]{:S(2)}, u32[]{:S(2)}) collective-permute-start(bf16[2,12,96]{2,1,0:T(8,128)(2,1)S(1)} %pad_maximum_fusion.2), channel_id=1, source_target_pairs={{0,8},{4,12},{8,0},{12,4},{16,24},{20,28},{24,16},{28,20},{1,9},{5... | collective-permute-start | bytes 13832 | tf_op jit(solution)/shard_map/ppermute | solution.py:408
  40.2 4.1 %collective-permute-start.5 = (bf16[4,12,96]{2,1,0:T(8,128)(2,1)S(1)}, bf16[4,12,96]{2,1,0:T(8,128)(2,1)S(1)}, u32[]{:S(2)}, u32[]{:S(2)}) collective-permute-start(bf16[4,12,96]{2,1,0:T(8,128)(2,1)S(1)} %pad_maximum_fusion.1), channel_id=1, source_target_pairs={{0,16},{4,20},{8,24},{12,28},{16,0},{20,4},{24,8},{28,12},{1,17},{... | collective-permute-start | bytes 27656 | tf_op jit(solution)/shard_map/ppermute | solution.py:408
  51.6 27.9 %copy-start.3 = (bf16[256,384]{1,0:T(8,128)(2,1)}, bf16[256,384]{1,0:T(8,128)(2,1)S(1)}, u32[]{:S(2)}) copy-start(bf16[256,384]{1,0:T(8,128)(2,1)S(1)} %get-tuple-element.70.refs_1_.refs_5_) | copy-start | bytes 589828
  51.6 21.7 %collective-permute-start.8 = (bf16[256,384]{1,0:T(8,128)(2,1)S(1)}, bf16[256,384]{1,0:T(8,128)(2,1)S(1)}, u32[]{:S(2)}, u32[]{:S(2)}) collective-permute-start(bf16[256,384]{1,0:T(8,128)(2,1)S(1)} %get-tuple-element.70.refs_1_.refs_5_), channel_id=1, source_target_pairs={{0,3},{1,0},{2,1},{3,2},{4,7},{5,4},{6,5},{7,6},{8,11},{9,8},{10,9... | collective-permute-start | bytes 589832 | tf_op jit(solution)/shard_map/ppermute | solution.py:394
  55.0 18.3 %collective-permute-start.7 = (bf16[256,384]{1,0:T(8,128)(2,1)S(1)}, bf16[256,384]{1,0:T(8,128)(2,1)S(1)}, u32[]{:S(2)}, u32[]{:S(2)}) collective-permute-start(bf16[256,384]{1,0:T(8,128)(2,1)S(1)} %get-tuple-element.70.refs_1_.refs_5_), channel_id=1, source_target_pairs={{0,2},{1,3},{2,0},{3,1},{4,6},{5,7},{6,4},{7,5},{8,10},{9,11},{10,... | collective-permute-start | bytes 589832 | tf_op jit(solution)/shard_map/ppermute | solution.py:394
  56.0 17.3 %collective-permute-start.6 = (bf16[256,384]{1,0:T(8,128)(2,1)S(1)}, bf16[256,384]{1,0:T(8,128)(2,1)S(1)}, u32[]{:S(2)}, u32[]{:S(2)}) collective-permute-start(bf16[256,384]{1,0:T(8,128)(2,1)S(1)} %get-tuple-element.70.refs_1_.refs_5_), channel_id=1, source_target_pairs={{0,1},{1,2},{2,3},{3,0},{4,5},{5,6},{6,7},{7,4},{8,9},{9,10},{10,1... | collective-permute-start | bytes 589832 | tf_op jit(solution)/shard_map/ppermute | solution.py:394
  79.6 49.1 %copy-start.1 = (f32[128,768]{1,0:T(8,128)}, f32[128,768]{1,0:T(8,128)S(1)}, u32[]{:S(2)}) copy-start(f32[128,768]{1,0:T(8,128)S(1)} %get-tuple-element.75.refs_5_) | copy-start | bytes 1179652
  79.6 9.7 %collective-permute-start.9 = (bf16[128,768]{1,0:T(8,128)(2,1)S(1)}, bf16[128,768]{1,0:T(8,128)(2,1)S(1)}, u32[]{:S(2)}, u32[]{:S(2)}) collective-permute-start(bf16[128,768]{1,0:T(8,128)(2,1)S(1)} %get-tuple-element.72), channel_id=1, source_target_pairs={{0,1},{1,2},{2,3},{3,0},{4,5},{5,6},{6,7},{7,4},{8,9},{9,10},{10,1... | collective-permute-start | bytes 589832 | tf_op jit(solution)/shard_map/ppermute | solution.py:402
  81.1 16.0 %collective-permute-start.10 = (bf16[128,768]{1,0:T(8,128)(2,1)S(1)}, bf16[128,768]{1,0:T(8,128)(2,1)S(1)}, u32[]{:S(2)}, u32[]{:S(2)}) collective-permute-start(bf16[128,768]{1,0:T(8,128)(2,1)S(1)} %get-tuple-element.73), channel_id=1, source_target_pairs={{0,2},{1,3},{2,0},{3,1},{4,6},{5,7},{6,4},{7,5},{8,10},{9,11},{10,... | collective-permute-start | bytes 589832 | tf_op jit(solution)/shard_map/ppermute | solution.py:402
  83.5 13.5 %collective-permute-start.11 = (bf16[128,768]{1,0:T(8,128)(2,1)S(1)}, bf16[128,768]{1,0:T(8,128)(2,1)S(1)}, u32[]{:S(2)}, u32[]{:S(2)}) collective-permute-start(bf16[128,768]{1,0:T(8,128)(2,1)S(1)} %get-tuple-element.74), channel_id=1, source_target_pairs={{0,3},{1,0},{2,1},{3,2},{4,7},{5,4},{6,5},{7,6},{8,11},{9,8},{10,9... | collective-permute-start | bytes 589832 | tf_op jit(solution)/shard_map/ppermute | solution.py:402
  100.1 11.0 %collective-permute-start.14 = (bf16[128,768]{1,0:T(8,128)(2,1)S(1)}, bf16[128,768]{1,0:T(8,128)(2,1)S(1)}, u32[]{:S(2)}, u32[]{:S(2)}) collective-permute-start(bf16[128,768]{1,0:T(8,128)(2,1)S(1)} %get-tuple-element.77.refs_1_), channel_id=1, source_target_pairs={{0,3},{1,0},{2,1},{3,2},{4,7},{5,4},{6,5},{7,6},{8,11},{9,8},{10,9... | collective-permute-start | bytes 589832 | tf_op jit(solution)/shard_map/ppermute | solution.py:394
  105.8 18.0 %collective-permute-start.13 = (bf16[128,768]{1,0:T(8,128)(2,1)S(1)}, bf16[128,768]{1,0:T(8,128)(2,1)S(1)}, u32[]{:S(2)}, u32[]{:S(2)}) collective-permute-start(bf16[128,768]{1,0:T(8,128)(2,1)S(1)} %get-tuple-element.77.refs_1_), channel_id=1, source_target_pairs={{0,2},{1,3},{2,0},{3,1},{4,6},{5,7},{6,4},{7,5},{8,10},{9,11},{10,... | collective-permute-start | bytes 589832 | tf_op jit(solution)/shard_map/ppermute | solution.py:394
  106.3 17.4 %collective-permute-start.12 = (bf16[128,768]{1,0:T(8,128)(2,1)S(1)}, bf16[128,768]{1,0:T(8,128)(2,1)S(1)}, u32[]{:S(2)}, u32[]{:S(2)}) collective-permute-start(bf16[128,768]{1,0:T(8,128)(2,1)S(1)} %get-tuple-element.77.refs_1_), channel_id=1, source_target_pairs={{0,1},{1,2},{2,3},{3,0},{4,5},{5,6},{6,7},{7,4},{8,9},{9,10},{10,1... | collective-permute-start | bytes 589832 | tf_op jit(solution)/shard_map/ppermute | solution.py:394
  131.6 45.7 %copy-start.10 = (f32[1,768]{1,0:T(1,128)S(1)}, f32[1,768]{1,0:T(1,128)}, u32[]{:S(2)}) copy-start(f32[1,768]{1,0:T(1,128)} %get-tuple-element.89.refs_16_) | copy-start | bytes 9220
  131.7 92.4 %all-gather.8.cloned.1.call-start = ((), (), s32[]{:S(2)}) async-start(), calls=%async_computation.5 | async-start | bytes 2654208 | tf_op jit(solution)/shard_map/all_gather | solution.py:1027
  132.5 9.7 %collective-permute-start.15 = (bf16[128,768]{1,0:T(8,128)(2,1)S(1)}, bf16[128,768]{1,0:T(8,128)(2,1)S(1)}, u32[]{:S(2)}, u32[]{:S(2)}) collective-permute-start(bf16[128,768]{1,0:T(8,128)(2,1)S(1)} %copy-done.17), channel_id=1, source_target_pairs={{0,1},{1,2},{2,3},{3,0},{4,5},{5,6},{6,7},{7,4},{8,9},{9,10},{10,1... | collective-permute-start | bytes 589832 | tf_op jit(solution)/shard_map/ppermute | solution.py:402
  132.6 16.3 %collective-permute-start.16 = (bf16[128,768]{1,0:T(8,128)(2,1)S(1)}, bf16[128,768]{1,0:T(8,128)(2,1)S(1)}, u32[]{:S(2)}, u32[]{:S(2)}) collective-permute-start(bf16[128,768]{1,0:T(8,128)(2,1)S(1)} %copy-done.16), channel_id=1, source_target_pairs={{0,2},{1,3},{2,0},{3,1},{4,6},{5,7},{6,4},{7,5},{8,10},{9,11},{10,... | collective-permute-start | bytes 589832 | tf_op jit(solution)/shard_map/ppermute | solution.py:402
  133.6 15.3 %collective-permute-start.17 = (bf16[128,768]{1,0:T(8,128)(2,1)S(1)}, bf16[128,768]{1,0:T(8,128)(2,1)S(1)}, u32[]{:S(2)}, u32[]{:S(2)}) collective-permute-start(bf16[128,768]{1,0:T(8,128)(2,1)S(1)} %copy-done.15), channel_id=1, source_target_pairs={{0,3},{1,0},{2,1},{3,2},{4,7},{5,4},{6,5},{7,6},{8,11},{9,8},{10,9... | collective-permute-start | bytes 589832 | tf_op jit(solution)/shard_map/ppermute | solution.py:402
  151.4 9.8 %collective-permute-start.20 = (bf16[128,768]{1,0:T(8,128)(2,1)}, bf16[128,768]{1,0:T(8,128)(2,1)S(1)}, u32[]{:S(2)}, u32[]{:S(2)}) collective-permute-start(bf16[128,768]{1,0:T(8,128)(2,1)} %get-tuple-element.85.refs_1_), channel_id=1, source_target_pairs={{0,3},{1,0},{2,1},{3,2},{4,7},{5,4},{6,5},{7,6},{8,11},{9,8},{10,9... | collective-permute-start | bytes 589832 | tf_op jit(solution)/shard_map/ppermute | solution.py:394
  155.6 18.2 %collective-permute-start.19 = (bf16[128,768]{1,0:T(8,128)(2,1)}, bf16[128,768]{1,0:T(8,128)(2,1)S(1)}, u32[]{:S(2)}, u32[]{:S(2)}) collective-permute-start(bf16[128,768]{1,0:T(8,128)(2,1)} %get-tuple-element.85.refs_1_), channel_id=1, source_target_pairs={{0,2},{1,3},{2,0},{3,1},{4,6},{5,7},{6,4},{7,5},{8,10},{9,11},{10,... | collective-permute-start | bytes 589832 | tf_op jit(solution)/shard_map/ppermute | solution.py:394
  156.8 17.0 %collective-permute-start.18 = (bf16[128,768]{1,0:T(8,128)(2,1)}, bf16[128,768]{1,0:T(8,128)(2,1)S(1)}, u32[]{:S(2)}, u32[]{:S(2)}) collective-permute-start(bf16[128,768]{1,0:T(8,128)(2,1)} %get-tuple-element.85.refs_1_), channel_id=1, source_target_pairs={{0,1},{1,2},{2,3},{3,0},{4,5},{5,6},{6,7},{7,4},{8,9},{9,10},{10,1... | collective-permute-start | bytes 589832 | tf_op jit(solution)/shard_map/ppermute | solution.py:394
  161.3 16.1 %copy-start.7 = (bf16[128,768]{1,0:T(8,128)(2,1)}, bf16[128,768]{1,0:T(8,128)(2,1)S(1)}, u32[]{:S(2)}) copy-start(bf16[128,768]{1,0:T(8,128)(2,1)S(1)} %collective-permute-done.20.refs_5_.refs_4_) | copy-start | bytes 589828
  176.7 12.7 %collective-permute-start.28 = (bf16[96,768]{1,0:T(8,128)(2,1)S(1)}, bf16[96,768]{1,0:T(8,128)(2,1)S(1)}, u32[]{:S(2)}, u32[]{:S(2)}) collective-permute-start(bf16[96,768]{1,0:T(8,128)(2,1)S(1)} %get-tuple-element.94.refs_17_), channel_id=1, source_target_pairs={{0,2},{1,3},{2,0},{3,1},{4,6},{5,7},{6,4},{7,5},{8,10},{9,11},{10,... | collective-permute-start | bytes 442376 | tf_op jit(solution)/shard_map/ppermute | solution.py:408
  191.5 81.9 %reduce-scatter.5.cloned.1.call-start = ((), (), s32[]{:S(2)}) async-start(), calls=%async_computation.6 | async-start | bytes 983040 | tf_op jit(solution)/shard_map/reduce_scatter | solution.py:1061
  191.6 2.2 collective-permute-start.21
  195.8 9.6 %collective-permute-start.22 = (bf16[112,768]{1,0:T(8,128)(2,1)S(1)}, bf16[112,768]{1,0:T(8,128)(2,1)S(1)}, u32[]{:S(2)}, u32[]{:S(2)}) collective-permute-start(bf16[112,768]{1,0:T(8,128)(2,1)S(1)} %get-tuple-element.99), channel_id=1, source_target_pairs={{0,8},{4,12},{8,0},{12,4},{16,24},{20,28},{24,16},{28,20},{1,9},{5... | collective-permute-start | bytes 516104 | tf_op jit(solution)/shard_map/ppermute | solution.py:408
  197.3 13.0 %collective-permute-start.23 = (bf16[112,768]{1,0:T(8,128)(2,1)S(1)}, bf16[112,768]{1,0:T(8,128)(2,1)S(1)}, u32[]{:S(2)}, u32[]{:S(2)}) collective-permute-start(bf16[112,768]{1,0:T(8,128)(2,1)S(1)} %get-tuple-element.100), channel_id=1, source_target_pairs={{0,16},{4,20},{8,24},{12,28},{16,0},{20,4},{24,8},{28,12},{1,17},{... | collective-permute-start | bytes 516104 | tf_op jit(solution)/shard_map/ppermute | solution.py:408
  197.9 12.4 %collective-permute-start.24 = (bf16[112,768]{1,0:T(8,128)(2,1)S(1)}, bf16[112,768]{1,0:T(8,128)(2,1)S(1)}, u32[]{:S(2)}, u32[]{:S(2)}) collective-permute-start(bf16[112,768]{1,0:T(8,128)(2,1)S(1)} %get-tuple-element.101), channel_id=1, source_target_pairs={{0,24},{4,28},{8,16},{12,20},{16,8},{20,12},{24,0},{28,4},{1,25},{... | collective-permute-start | bytes 516104 | tf_op jit(solution)/shard_map/ppermute | solution.py:408
  212.9 6.5 %collective-permute-start.25 = (bf16[112,192]{1,0:T(8,128)(2,1)S(1)}, bf16[112,192]{1,0:T(8,128)(2,1)S(1)}, u32[]{:S(2)}, u32[]{:S(2)}) collective-permute-start(bf16[112,192]{1,0:T(8,128)(2,1)S(1)} %get-tuple-element.103), channel_id=1, source_target_pairs={{0,1},{1,2},{2,3},{3,0},{4,5},{5,6},{6,7},{7,4},{8,9},{9,10},{10,1... | collective-permute-start | bytes 129032 | tf_op jit(solution)/shard_map/ppermute | solution.py:402
  214.4 6.2 %collective-permute-start.26 = (bf16[112,192]{1,0:T(8,128)(2,1)S(1)}, bf16[112,192]{1,0:T(8,128)(2,1)S(1)}, u32[]{:S(2)}, u32[]{:S(2)}) collective-permute-start(bf16[112,192]{1,0:T(8,128)(2,1)S(1)} %get-tuple-element.104), channel_id=1, source_target_pairs={{0,2},{1,3},{2,0},{3,1},{4,6},{5,7},{6,4},{7,5},{8,10},{9,11},{10,... | collective-permute-start | bytes 129032 | tf_op jit(solution)/shard_map/ppermute | solution.py:402
  215.4 5.3 %collective-permute-start.27 = (bf16[112,192]{1,0:T(8,128)(2,1)S(1)}, bf16[112,192]{1,0:T(8,128)(2,1)S(1)}, u32[]{:S(2)}, u32[]{:S(2)}) collective-permute-start(bf16[112,192]{1,0:T(8,128)(2,1)S(1)} %get-tuple-element.105), channel_id=1, source_target_pairs={{0,3},{1,0},{2,1},{3,2},{4,7},{5,4},{6,5},{7,6},{8,11},{9,8},{10,9... | collective-permute-start | bytes 129032 | tf_op jit(solution)/shard_map/ppermute | solution.py:402
  226.7 6.1 %collective-permute-start.29 = (bf16[96,768]{1,0:T(8,128)(2,1)S(1)}, bf16[96,768]{1,0:T(8,128)(2,1)S(1)}, u32[]{:S(2)}, u32[]{:S(2)}) collective-permute-start(bf16[96,768]{1,0:T(8,128)(2,1)S(1)} %shard_map.229.refs_5_), channel_id=1, source_target_pairs={{0,1},{1,0},{2,3},{3,2},{4,5},{5,4},{6,7},{7,6},{8,9},{9,8},{10,11... | collective-permute-start | bytes 442376 | tf_op jit(solution)/shard_map/ppermute | solution.py:408
  233.9 1.4 collective-permute-start.30
  239.0 32.7 %copy-start.14 = (f32[12,24]{1,0:T(8,128)S(1)}, f32[12,24]{1,0:T(8,128)}, u32[]{:S(2)}) copy-start(f32[12,24]{1,0:T(8,128)} %param.21) | copy-start | bytes 3460
  239.1 10.9 %collective-permute-start.33 = (bf16[192,768]{1,0:T(8,128)(2,1)S(1)}, bf16[192,768]{1,0:T(8,128)(2,1)S(1)}, u32[]{:S(2)}, u32[]{:S(2)}) collective-permute-start(bf16[192,768]{1,0:T(8,128)(2,1)S(1)} %shard_map.231.refs_2_.refs_1_), channel_id=1, source_target_pairs={{0,24},{4,28},{8,16},{12,20},{16,8},{20,12},{24,0},{28,4},{1,25},{... | collective-permute-start | bytes 884744 | tf_op jit(solution)/shard_map/ppermute | solution.py:408
  240.6 14.8 %collective-permute-start.32 = (bf16[192,768]{1,0:T(8,128)(2,1)S(1)}, bf16[192,768]{1,0:T(8,128)(2,1)S(1)}, u32[]{:S(2)}, u32[]{:S(2)}) collective-permute-start(bf16[192,768]{1,0:T(8,128)(2,1)S(1)} %shard_map.231.refs_2_.refs_1_), channel_id=1, source_target_pairs={{0,16},{4,20},{8,24},{12,28},{16,0},{20,4},{24,8},{28,12},{1,17},{... | collective-permute-start | bytes 884744 | tf_op jit(solution)/shard_map/ppermute | solution.py:408
  242.1 13.3 %collective-permute-start.31 = (bf16[192,768]{1,0:T(8,128)(2,1)S(1)}, bf16[192,768]{1,0:T(8,128)(2,1)S(1)}, u32[]{:S(2)}, u32[]{:S(2)}) collective-permute-start(bf16[192,768]{1,0:T(8,128)(2,1)S(1)} %shard_map.231.refs_2_.refs_1_), channel_id=1, source_target_pairs={{0,8},{4,12},{8,0},{12,4},{16,24},{20,28},{24,16},{28,20},{1,9},{5... | collective-permute-start | bytes 884744 | tf_op jit(solution)/shard_map/ppermute | solution.py:408
  264.8 1.6 collective-permute-start.34
  267.3 6.1 %collective-permute-start.35 = (bf16[96,192]{1,0:T(8,128)(2,1)S(1)}, bf16[96,192]{1,0:T(8,128)(2,1)S(1)}, u32[]{:S(2)}, u32[]{:S(2)}) collective-permute-start(bf16[96,192]{1,0:T(8,128)(2,1)S(1)} %get-tuple-element.111), channel_id=1, source_target_pairs={{0,1},{1,2},{2,3},{3,0},{4,5},{5,6},{6,7},{7,4},{8,9},{9,10},{10,1... | collective-permute-start | bytes 110600 | tf_op jit(solution)/shard_map/ppermute | solution.py:402
  268.8 6.5 %collective-permute-start.37 = (bf16[96,192]{1,0:T(8,128)(2,1)S(1)}, bf16[96,192]{1,0:T(8,128)(2,1)S(1)}, u32[]{:S(2)}, u32[]{:S(2)}) collective-permute-start(bf16[96,192]{1,0:T(8,128)(2,1)S(1)} %get-tuple-element.121), channel_id=1, source_target_pairs={{0,3},{1,0},{2,1},{3,2},{4,7},{5,4},{6,5},{7,6},{8,11},{9,8},{10,9... | collective-permute-start | bytes 110600 | tf_op jit(solution)/shard_map/ppermute | solution.py:402
  271.1 11.2 %collective-permute-start.36 = (bf16[96,960]{1,0:T(8,128)(2,1)S(1)}, bf16[96,960]{1,0:T(8,128)(2,1)S(1)}, u32[]{:S(2)}, u32[]{:S(2)}) collective-permute-start(bf16[96,960]{1,0:T(8,128)(2,1)S(1)} %get-tuple-element.120), channel_id=1, source_target_pairs={{0,2},{1,3},{2,0},{3,1},{4,6},{5,7},{6,4},{7,5},{8,10},{9,11},{10,... | collective-permute-start | bytes 552968 | tf_op jit(solution)/shard_map/ppermute | solution.py:402
  (14 other events, 46.0 us)
Sparse Core Ops, SparseCore 0:
  10.5 36.1 all-gather.3
  49.2 24.0 all-gather.5
  131.8 40.2 reduce-scatter.2
  191.6 32.3 all-gather.7
  239.2 23.2 reduce-scatter.4

commit v7 on v6

--- a/solution.py
+++ b/solution.py
@@ -705,7 +705,18 @@
     part[...] = dot(d_proj[...], proj, ((1,), (1,))).astype(jnp.bfloat16)
 
 
-def add_rows(left, right, total):
+def pack_weights(ffn, qkv, packed):
+    hidden, own = ffn.shape[2], qkv.shape[2]
+    packed[:, 2 * hidden :] = jnp.zeros_like(packed[:, 2 * hidden :])
+    for part in range(2):
+        packed[:, part * hidden : (part + 1) * hidden] = ffn[part].astype(jnp.bfloat16)
+    for part in range(3):
+        at = 2 * hidden + part * own
+        packed[:, at : at + own] = qkv[part].astype(jnp.bfloat16)
+
+
+def add_rows(left, right, total, flag):
+    flag[...] = jnp.zeros_like(flag)
     total[...] = left[...] + right[...].astype(jnp.float32)
 
 
@@ -902,9 +913,8 @@
     hidden = ffn_w.shape[2]
     bf16 = jnp.bfloat16
 
-    packed = jnp.concatenate(
-        [ffn_w[0], ffn_w[1], qkv_w[0], qkv_w[1], qkv_w[2], jnp.zeros((ffn_w.shape[1], PAD))], axis=1
-    ).astype(bf16)
+    packed_kind = jax.ShapeDtypeStruct((ffn_w.shape[1], 2 * hidden + 3 * own + PAD), bf16)
+    (packed,) = run_kernel(pack_weights, [packed_kind], far=(0, 1), far_out=(0,))(ffn_w, qkv_w)
     weights = lax.all_gather(packed, "dp", axis=0, tiled=True)
 
     flat = tokens.reshape(micro * rows, width)
@@ -1077,7 +1087,8 @@
         split_state, kinds, scalars=1
     )(place, kept, swap(sent, "dp", 1))
     state_pieces = send_parts(blocks, "shard")
-    (d_tokens,) = run_kernel(add_rows, [own_f], ties=[state_pieces[1]], far=(0, 1), far_out=(0,))(
+    flag_kind = jax.ShapeDtypeStruct((8, 128), jnp.float32)
+    d_tokens, flag = run_kernel(add_rows, [own_f, flag_kind], ties=[state_pieces[1]], far=(0, 1), far_out=(0,))(
         d_first_in, d_tokens
     )
     qkv_new, out_new, ffn_new = run_kernel(
@@ -1085,7 +1096,7 @@
         [jax.ShapeDtypeStruct(each.shape, each.dtype) for each in (qkv_w, out_w, ffn_w)],
         scalars=1,
         scratch=[pltpu.VMEM((shards, depth, own), jnp.float32)],
-        ties=[d_tokens],
+        ties=[flag],
         far=(6, 7, 8),
         far_out=(0, 1, 2),
     )(

time: 293 us -> 292 us (level)
  waiting for transfers between devices: 141 us -> 138 us
    pallas_call x19 -> x20, Pallas kernels: 66.9 us -> 68.9 us  [call(): pl.pallas_call(whole, out_shape=kinds, in_specs=[pl.BlockSpec(memory_spac...]
  transfers between devices with their start and end apart: 43 -> 43, of which waited for: 29 -> 29; matrix products, arithmetic and copies ran while one was open for 2% -> 3% of each run, Pallas kernels for 12% -> 12%
where the time goes in v7:
time: 292 us
  waiting for transfers between devices  138 us (47%)
  Pallas kernels  68.9 us (24%)
  starting transfers between devices  59.3 us (20%)
  between operations  14.3 us (5%)
  local copies, waits for them, and re-layouts  7.01 us (2%)
  other arithmetic  4.55 us (2%)
    pallas_call x20, Pallas kernels, call(): pl.pallas_call(whole, out_shape=kinds, in_specs=[pl.BlockSpec(memory_spac...  68.9 us
    ppermute x14, waiting for transfers between devices, swap(): lax.ppermute(block, axis, [(i, i ^ bit) for i in range(lax.axis_size(axis...  36.5 us
    ppermute x9, waiting for transfers between devices, pieces_of(): lax.ppermute(block, axis, [(i, (i + step) % count) for i in range(count)])  35.1 us
    ppermute x12, waiting for transfers between devices, send_parts(): lax.ppermute(parts[step], axis, [(i, (i + step) % count) for i in range(c...  35.1 us
    ppermute x9, starting transfers between devices, pieces_of(): lax.ppermute(block, axis, [(i, (i + step) % count) for i in range(count)])  20 us
    ppermute x12, starting transfers between devices, send_parts(): lax.ppermute(parts[step], axis, [(i, (i + step) % count) for i in range(c...  18.3 us
    ppermute x3, waiting for transfers between devices, gather_direct(): lax.ppermute(block, axis, [(i, (i + step) % count) for i in range(count)])  14 us
    all_gather x1, waiting for transfers between devices, split_device(): out_b = lax.all_gather(out_part, 'dp', axis=0, tiled=True)  13.4 us
  transfers between devices with their start and end apart: 43, of which 29 were waited for; matrix products, arithmetic and copies ran while one was open for 3% of the time, Pallas kernels for 12%

profile of v7, /device:TPU:0, one launch (start us, length us, event | category | flops | bytes accessed | tf_op | source)
XLA Modules:
  0.0 291.8 jit_solution(13903878364635632164)
XLA Ops:
  7.2 2.0 shard_map.218
  13.0 4.1 %collective-permute-start.1 = (bf16[160,768]{1,0:T(8,128)(2,1)S(1)}, bf16[160,768]{1,0:T(8,128)(2,1)S(1)}, u32[]{:S(2)}, u32[]{:S(2)}) collective-permute-start(bf16[160,768]{1,0:T(8,128)(2,1)S(1)} %pad_maximum_fusion), channel_id=1, source_target_pairs={{0,2},{1,3},{2,0},{3,1},{4,6},{5,7},{6,4},{7,5},{8,10},{9,11},{10,... | collective-permute-start | bytes 737288 | tf_op jit(solution)/shard_map/ppermute | solution.py:386
  18.7 2.2 collective-permute-start.2
  21.1 9.5 %collective-permute-done = bf16[160,768]{1,0:T(8,128)(2,1)S(1)} collective-permute-done((bf16[160,768]{1,0:T(8,128)(2,1)S(1)}, bf16[160,768]{1,0:T(8,128)(2,1)S(1)}, u32[]{:S(2)}, u32[]{:S(2)}) %collective-permute-start) | collective-permute-done | bytes 245792 | tf_op jit(solution)/shard_map/ppermute | solution.py:386
  30.7 3.8 %collective-permute-done.1 = bf16[160,768]{1,0:T(8,128)(2,1)S(1)} collective-permute-done((bf16[160,768]{1,0:T(8,128)(2,1)S(1)}, bf16[160,768]{1,0:T(8,128)(2,1)S(1)}, u32[]{:S(2)}, u32[]{:S(2)}) %collective-permute-start.1) | collective-permute-done | bytes 245792 | tf_op jit(solution)/shard_map/ppermute | solution.py:386
  40.2 2.1 collective-permute-done.4
  42.3 1.6 collective-permute-start.5
  46.7 4.8 %shard_map.219 = (bf16[512,576]{1,0:T(8,128)(2,1)}, bf16[256,384]{1,0:T(8,128)(2,1)S(1)}) custom-call(s32[3]{0:T(128)S(1)} %pad_add_fusion.refs_0_, bf16[512,768]{1,0:T(8,128)(2,1)} %bitcast.27, bf16[768,2176]{1,0:T(8,128)(2,1)} %all-gather.4.cloned.1.call-done.refs_2_.refs_8_.refs_6_.refs_1_, f32[1,576]{1,0:T(1,128)S(1)} %broadcast_in_dim.34.refs_3_, ...), custom_call_target="tpu_custom_call" | custom-call | tf_op jit(solution)/shard_map/pallas_call | solution.py:832
  51.6 3.4 %collective-permute-start.8 = (bf16[256,384]{1,0:T(8,128)(2,1)S(1)}, bf16[256,384]{1,0:T(8,128)(2,1)S(1)}, u32[]{:S(2)}, u32[]{:S(2)}) collective-permute-start(bf16[256,384]{1,0:T(8,128)(2,1)S(1)} %get-tuple-element.72.refs_1_.refs_5_), channel_id=1, source_target_pairs={{0,3},{1,0},{2,1},{3,2},{4,7},{5,4},{6,5},{7,6},{8,11},{9,8},{10,9... | collective-permute-start | bytes 589832 | tf_op jit(solution)/shard_map/ppermute | solution.py:394
  55.0 3.0 %collective-permute-start.7 = (bf16[256,384]{1,0:T(8,128)(2,1)S(1)}, bf16[256,384]{1,0:T(8,128)(2,1)S(1)}, u32[]{:S(2)}, u32[]{:S(2)}) collective-permute-start(bf16[256,384]{1,0:T(8,128)(2,1)S(1)} %get-tuple-element.72.refs_1_.refs_5_), channel_id=1, source_target_pairs={{0,2},{1,3},{2,0},{3,1},{4,6},{5,7},{6,4},{7,5},{8,10},{9,11},{10,... | collective-permute-start | bytes 589832 | tf_op jit(solution)/shard_map/ppermute | solution.py:394
  58.0 1.9 collective-permute-start.6
  59.9 13.4 %all-gather.6.cloned.1.call-done.refs_5_.refs_9_ = bf16[768,768]{1,0:T(8,128)(2,1)} async-done(((bf16[96,768]{1,0:T(8,128)(2,1)}), bf16[768,768]{1,0:T(8,128)(2,1)}) %all-gather.6.cloned.1.call-update) | async-done | bytes 1179664 | tf_op jit(solution)/shard_map/all_gather | solution.py:936
  74.1 6.2 %shard_map.220 = (bf16[512,768]{1,0:T(8,128)(2,1)S(1)}, bf16[512,768]{1,0:T(8,128)(2,1)S(1)}, f32[512,768]{1,0:T(8,128)S(1)}, f32[128,768]{1,0:T(8,128)S(1)}, f3...) custom-call(s32[3]{0:T(128)S(1)} %pad_add_fusion.refs_0_, ...), custom_call_target="tpu_custom_call" | custom-call | tf_op jit(solution)/shard_map/pallas_call | solution.py:832
  81.1 2.4 collective-permute-start.10
  85.0 5.1 %collective-permute-done.9.refs_2_ = bf16[128,768]{1,0:T(8,128)(2,1)S(1)} collective-permute-done((bf16[128,768]{1,0:T(8,128)(2,1)S(1)}, bf16[128,768]{1,0:T(8,128)(2,1)S(1)}, u32[]{:S(2)}, u32[]{:S(2)}) %collective-permute-start.9) | collective-permute-done | bytes 196640 | tf_op jit(solution)/shard_map/ppermute | solution.py:402
  90.1 6.9 %collective-permute-done.10.refs_3_ = bf16[128,768]{1,0:T(8,128)(2,1)S(1)} collective-permute-done((bf16[128,768]{1,0:T(8,128)(2,1)S(1)}, bf16[128,768]{1,0:T(8,128)(2,1)S(1)}, u32[]{:S(2)}, u32[]{:S(2)}) %collective-permute-start.10) | collective-permute-done | bytes 196640 | tf_op jit(solution)/shard_map/ppermute | solution.py:402
  97.1 3.1 %shard_map.221 = (bf16[128,768]{1,0:T(8,128)(2,1)}, bf16[128,768]{1,0:T(8,128)(2,1)S(1)}, f32[128,768]{1,0:T(8,128)}, f32[8,768]{1,0:T(8,128)}) custom-call(s32[3]{0:T(128)S(1)} %pad_add_fusion.refs_0_, f32[128,768]{1,0:T(8,128)S(1)} %get-tuple-element.73.refs_1_, bf16[128,768]{1,0:T(8,128)(2,1)S(1)} %collective-permute-done.9.refs_2_, ...), custom_call_target="tpu_custom_call" | custom-call | tf_op jit(solution)/shard_map/pallas_call | solution.py:832
  100.1 5.7 %collective-permute-start.14 = (bf16[128,768]{1,0:T(8,128)(2,1)S(1)}, bf16[128,768]{1,0:T(8,128)(2,1)S(1)}, u32[]{:S(2)}, u32[]{:S(2)}) collective-permute-start(bf16[128,768]{1,0:T(8,128)(2,1)S(1)} %get-tuple-element.79.refs_1_), channel_id=1, source_target_pairs={{0,3},{1,0},{2,1},{3,2},{4,7},{5,4},{6,5},{7,6},{8,11},{9,8},{10,9... | collective-permute-start | bytes 589832 | tf_op jit(solution)/shard_map/ppermute | solution.py:394
  106.4 4.8 %collective-permute-done.14.refs_4_ = bf16[128,768]{1,0:T(8,128)(2,1)S(1)} collective-permute-done((bf16[128,768]{1,0:T(8,128)(2,1)S(1)}, bf16[128,768]{1,0:T(8,128)(2,1)S(1)}, u32[]{:S(2)}, u32[]{:S(2)}) %collective-permute-start.14) | collective-permute-done | bytes 196640 | tf_op jit(solution)/shard_map/ppermute | solution.py:394
  111.2 12.6 %collective-permute-done.13.refs_3_ = bf16[128,768]{1,0:T(8,128)(2,1)S(1)} collective-permute-done((bf16[128,768]{1,0:T(8,128)(2,1)S(1)}, bf16[128,768]{1,0:T(8,128)(2,1)S(1)}, u32[]{:S(2)}, u32[]{:S(2)}) %collective-permute-start.13) | collective-permute-done | bytes 196640 | tf_op jit(solution)/shard_map/ppermute | solution.py:394
  123.8 4.9 %shard_map.222 = (bf16[512,768]{1,0:T(8,128)(2,1)S(1)}, bf16[512,768]{1,0:T(8,128)(2,1)S(1)}, f32[1,768]{1,0:T(1,128)}, f32[128,768]{1,0:T(8,128)}, bf16[128,768...) custom-call(s32[3]{0:T(128)S(1)} %pad_add_fusion.refs_0_, ...), custom_call_target="tpu_custom_call" | custom-call | tf_op jit(solution)/shard_map/pallas_call | solution.py:832
  128.7 2.9 shard_map.224
  133.7 2.8 collective-permute-start.17
  136.5 5.7 %collective-permute-done.15.refs_1_ = bf16[128,768]{1,0:T(8,128)(2,1)S(1)} collective-permute-done((bf16[128,768]{1,0:T(8,128)(2,1)S(1)}, bf16[128,768]{1,0:T(8,128)(2,1)S(1)}, u32[]{:S(2)}, u32[]{:S(2)}) %collective-permute-start.15) | collective-permute-done | bytes 196640 | tf_op jit(solution)/shard_map/ppermute | solution.py:402
  142.2 6.7 %collective-permute-done.16.refs_2_ = bf16[128,768]{1,0:T(8,128)(2,1)S(1)} collective-permute-done((bf16[128,768]{1,0:T(8,128)(2,1)S(1)}, bf16[128,768]{1,0:T(8,128)(2,1)S(1)}, u32[]{:S(2)}, u32[]{:S(2)}) %collective-permute-start.16) | collective-permute-done | bytes 196640 | tf_op jit(solution)/shard_map/ppermute | solution.py:402
  148.9 2.5 shard_map.223
  151.4 4.2 %collective-permute-start.20 = (bf16[128,768]{1,0:T(8,128)(2,1)}, bf16[128,768]{1,0:T(8,128)(2,1)S(1)}, u32[]{:S(2)}, u32[]{:S(2)}) collective-permute-start(bf16[128,768]{1,0:T(8,128)(2,1)} %get-tuple-element.87.refs_1_), channel_id=1, source_target_pairs={{0,3},{1,0},{2,1},{3,2},{4,7},{5,4},{6,5},{7,6},{8,11},{9,8},{10,9... | collective-permute-start | bytes 589832 | tf_op jit(solution)/shard_map/ppermute | solution.py:394
  156.8 4.5 %collective-permute-done.20.refs_5_.refs_4_ = bf16[128,768]{1,0:T(8,128)(2,1)S(1)} collective-permute-done((bf16[128,768]{1,0:T(8,128)(2,1)}, bf16[128,768]{1,0:T(8,128)(2,1)S(1)}, u32[]{:S(2)}, u32[]{:S(2)}) %collective-permute-start.20) | collective-permute-done | bytes 196640 | tf_op jit(solution)/shard_map/ppermute | solution.py:394
  161.3 12.5 %collective-permute-done.19.refs_4_.refs_3_ = bf16[128,768]{1,0:T(8,128)(2,1)S(1)} collective-permute-done((bf16[128,768]{1,0:T(8,128)(2,1)}, bf16[128,768]{1,0:T(8,128)(2,1)S(1)}, u32[]{:S(2)}, u32[]{:S(2)}) %collective-permute-start.19) | collective-permute-done | bytes 196640 | tf_op jit(solution)/shard_map/ppermute | solution.py:394
  173.8 2.9 shard_map.225
  177.4 12.0 %shard_map.226 = (f32[4,112,768]{2,1,0:T(8,128)}, bf16[4,112,768]{2,1,0:T(8,128)(2,1)S(1)}, bf16[512,576]{1,0:T(8,128)(2,1)}) custom-call(s32[3]{0:T(128)S(1)} %pad_add_fusion.refs_0_, bf16[128,768]{1,0:T(8,128)(2,1)} %get-tuple-element.87.refs_1_, bf16[128,768]{1,0:T(8,128)(2,1)} %copy-done.8, bf16[128,768]{1,0:T(8,128)(2,1)} %copy-done.7, ...), custom_call_target="tpu_custom_call" | custom-call | tf_op jit(solution)/shard_map/pallas_call | solution.py:832
  191.7 2.1 collective-permute-done.21.refs_2_
  193.8 2.1 shard_map.227
  199.5 6.1 %collective-permute-done.22.refs_2_ = bf16[112,768]{1,0:T(8,128)(2,1)S(1)} collective-permute-done((bf16[112,768]{1,0:T(8,128)(2,1)S(1)}, bf16[112,768]{1,0:T(8,128)(2,1)S(1)}, u32[]{:S(2)}, u32[]{:S(2)}) %collective-permute-start.22) | collective-permute-done | bytes 172064 | tf_op jit(solution)/shard_map/ppermute | solution.py:408
  205.5 4.8 %collective-permute-done.23.refs_3_ = bf16[112,768]{1,0:T(8,128)(2,1)S(1)} collective-permute-done((bf16[112,768]{1,0:T(8,128)(2,1)S(1)}, bf16[112,768]{1,0:T(8,128)(2,1)S(1)}, u32[]{:S(2)}, u32[]{:S(2)}) %collective-permute-start.23) | collective-permute-done | bytes 172064 | tf_op jit(solution)/shard_map/ppermute | solution.py:408
  210.3 2.6 shard_map.228
  215.4 2.8 collective-permute-start.27
  220.7 3.4 %all-gather.8.cloned.1.call-done.refs_1_.refs_5_ = bf16[768,1536]{1,0:T(8,128)(2,1)} async-done(((bf16[96,1536]{1,0:T(8,128)(2,1)}), bf16[768,1536]{1,0:T(8,128)(2,1)}) %all-gather.8.cloned.1.call-update) | async-done | bytes 2359312 | tf_op jit(solution)/shard_map/all_gather | solution.py:1037
  224.1 2.6 shard_map.230.refs_5_
  228.3 4.5 %collective-permute-done.29.refs_6_ = bf16[96,768]{1,0:T(8,128)(2,1)S(1)} collective-permute-done((bf16[96,768]{1,0:T(8,128)(2,1)S(1)}, bf16[96,768]{1,0:T(8,128)(2,1)S(1)}, u32[]{:S(2)}, u32[]{:S(2)}) %collective-permute-start.29) | collective-permute-done | bytes 147488 | tf_op jit(solution)/shard_map/ppermute | solution.py:408
  235.7 3.1 %shard_map.233 = bf16[512,768]{1,0:T(8,128)(2,1)} custom-call(bf16[512,576]{1,0:T(8,128)(2,1)} %get-tuple-element.97.refs_0_, bf16[768,2176]{1,0:T(8,128)(2,1)} %all-gather.4.cloned.1.call-done.refs_2_.refs_8_.refs_6_.refs_1_, bf16[192,768]{1,0:T(8,128)(2,1)S(1)} %shard_map.232.refs_2_.refs_1_), custom_call_target="tpu_custom_call" | custom-call | tf_op jit(solution)/shard_map/pallas_call | solution.py:832
  242.4 7.3 %collective-permute-done.33.refs_4_ = bf16[192,768]{1,0:T(8,128)(2,1)S(1)} collective-permute-done((bf16[192,768]{1,0:T(8,128)(2,1)S(1)}, bf16[192,768]{1,0:T(8,128)(2,1)S(1)}, u32[]{:S(2)}, u32[]{:S(2)}) %collective-permute-start.33) | collective-permute-done | bytes 294944 | tf_op jit(solution)/shard_map/ppermute | solution.py:408
  249.7 5.5 %collective-permute-done.32.refs_3_ = bf16[192,768]{1,0:T(8,128)(2,1)S(1)} collective-permute-done((bf16[192,768]{1,0:T(8,128)(2,1)S(1)}, bf16[192,768]{1,0:T(8,128)(2,1)S(1)}, u32[]{:S(2)}, u32[]{:S(2)}) %collective-permute-start.32) | collective-permute-done | bytes 294944 | tf_op jit(solution)/shard_map/ppermute | solution.py:408
  255.2 9.6 %shard_map.234 = (bf16[96,1536]{1,0:T(8,128)(2,1)S(1)}, bf16[96,1536]{1,0:T(8,128)(2,1)S(1)}) custom-call(s32[3]{0:T(128)S(1)} %pad_add_fusion.refs_0_, bf16[192,768]{1,0:T(8,128)(2,1)S(1)} %shard_map.232.refs_2_.refs_1_, bf16[192,768]{1,0:T(8,128)(2,1)S(1)} %collective-permute-done.31.refs_2_, bf16[192,768]{1,0:T(8,128)(2,1)S(1)} %collective-permute-done.32.refs_3_, ...), custom_call_target="tpu_custom_call" | custom-call | tf_op jit(solution)/shard_map/pallas_call | solution.py:832
  268.8 2.3 collective-permute-start.37
  273.4 1.8 shard_map.236
  275.3 7.1 %collective-permute-done.36.refs_3_ = bf16[96,960]{1,0:T(8,128)(2,1)S(1)} collective-permute-done((bf16[96,960]{1,0:T(8,128)(2,1)S(1)}, bf16[96,960]{1,0:T(8,128)(2,1)S(1)}, u32[]{:S(2)}, u32[]{:S(2)}) %collective-permute-start.36) | collective-permute-done | bytes 184352 | tf_op jit(solution)/shard_map/ppermute | solution.py:402
  282.4 2.8 shard_map.237
  (153 shorter events, 46.5 us)
Async XLA Ops:
  7.2 39.5 %all-gather.4.cloned.1.call-start = ((), (), s32[]{:S(2)}) async-start(), calls=%async_computation.2 | async-start | bytes 3760128 | tf_op jit(solution)/shard_map/all_gather | solution.py:918
  9.3 64.0 %all-gather.6.cloned.1.call-start = ((), (), s32[]{:S(2)}) async-start(), calls=%async_computation.3 | async-start | bytes 1327104 | tf_op jit(solution)/shard_map/all_gather | solution.py:936
  13.0 21.5 %collective-permute-start.1 = (bf16[160,768]{1,0:T(8,128)(2,1)S(1)}, bf16[160,768]{1,0:T(8,128)(2,1)S(1)}, u32[]{:S(2)}, u32[]{:S(2)}) collective-permute-start(bf16[160,768]{1,0:T(8,128)(2,1)S(1)} %pad_maximum_fusion), channel_id=1, source_target_pairs={{0,2},{1,3},{2,0},{3,1},{4,6},{5,7},{6,4},{7,5},{8,10},{9,11},{10,... | collective-permute-start | bytes 737288 | tf_op jit(solution)/shard_map/ppermute | solution.py:386
  17.1 13.5 %collective-permute-start = (bf16[160,768]{1,0:T(8,128)(2,1)S(1)}, bf16[160,768]{1,0:T(8,128)(2,1)S(1)}, u32[]{:S(2)}, u32[]{:S(2)}) collective-permute-start(bf16[160,768]{1,0:T(8,128)(2,1)S(1)} %pad_maximum_fusion), channel_id=1, source_target_pairs={{0,1},{1,2},{2,3},{3,0},{4,5},{5,6},{6,7},{7,4},{8,9},{9,10},{10,1... | collective-permute-start | bytes 737288 | tf_op jit(solution)/shard_map/ppermute | solution.py:386
  18.7 16.5 %collective-permute-start.2 = (bf16[160,768]{1,0:T(8,128)(2,1)S(1)}, bf16[160,768]{1,0:T(8,128)(2,1)S(1)}, u32[]{:S(2)}, u32[]{:S(2)}) collective-permute-start(bf16[160,768]{1,0:T(8,128)(2,1)S(1)} %pad_maximum_fusion), channel_id=1, source_target_pairs={{0,3},{1,0},{2,1},{3,2},{4,7},{5,4},{6,5},{7,6},{8,11},{9,8},{10,9... | collective-permute-start | bytes 737288 | tf_op jit(solution)/shard_map/ppermute | solution.py:386
  36.5 137.3 %reduce-scatter.3.cloned.1.call-start = ((), (), s32[]{:S(2)}) async-start(), calls=%async_computation.4 | async-start | bytes 2654208 | tf_op jit(solution)/shard_map/reduce_scatter | solution.py:999
  37.2 1.2 collective-permute-start.3
  38.4 3.9 %collective-permute-start.4 = (bf16[2,12,96]{2,1,0:T(8,128)(2,1)S(1)}, bf16[2,12,96]{2,1,0:T(8,128)(2,1)S(1)}, u32[]{:S(2)}, u32[]{:S(2)}) collective-permute-start(bf16[2,12,96]{2,1,0:T(8,128)(2,1)S(1)} %pad_maximum_fusion.2), channel_id=1, source_target_pairs={{0,8},{4,12},{8,0},{12,4},{16,24},{20,28},{24,16},{28,20},{1,9},{5... | collective-permute-start | bytes 13832 | tf_op jit(solution)/shard_map/ppermute | solution.py:408
  42.3 3.8 %collective-permute-start.5 = (bf16[4,12,96]{2,1,0:T(8,128)(2,1)S(1)}, bf16[4,12,96]{2,1,0:T(8,128)(2,1)S(1)}, u32[]{:S(2)}, u32[]{:S(2)}) collective-permute-start(bf16[4,12,96]{2,1,0:T(8,128)(2,1)S(1)} %pad_maximum_fusion.1), channel_id=1, source_target_pairs={{0,16},{4,20},{8,24},{12,28},{16,0},{20,4},{24,8},{28,12},{1,17},{... | collective-permute-start | bytes 27656 | tf_op jit(solution)/shard_map/ppermute | solution.py:408
  51.6 28.7 %copy-start.2 = (bf16[256,384]{1,0:T(8,128)(2,1)}, bf16[256,384]{1,0:T(8,128)(2,1)S(1)}, u32[]{:S(2)}) copy-start(bf16[256,384]{1,0:T(8,128)(2,1)S(1)} %get-tuple-element.72.refs_1_.refs_5_) | copy-start | bytes 589828
  51.6 21.8 %collective-permute-start.8 = (bf16[256,384]{1,0:T(8,128)(2,1)S(1)}, bf16[256,384]{1,0:T(8,128)(2,1)S(1)}, u32[]{:S(2)}, u32[]{:S(2)}) collective-permute-start(bf16[256,384]{1,0:T(8,128)(2,1)S(1)} %get-tuple-element.72.refs_1_.refs_5_), channel_id=1, source_target_pairs={{0,3},{1,0},{2,1},{3,2},{4,7},{5,4},{6,5},{7,6},{8,11},{9,8},{10,9... | collective-permute-start | bytes 589832 | tf_op jit(solution)/shard_map/ppermute | solution.py:394
  55.0 19.1 %collective-permute-start.7 = (bf16[256,384]{1,0:T(8,128)(2,1)S(1)}, bf16[256,384]{1,0:T(8,128)(2,1)S(1)}, u32[]{:S(2)}, u32[]{:S(2)}) collective-permute-start(bf16[256,384]{1,0:T(8,128)(2,1)S(1)} %get-tuple-element.72.refs_1_.refs_5_), channel_id=1, source_target_pairs={{0,2},{1,3},{2,0},{3,1},{4,6},{5,7},{6,4},{7,5},{8,10},{9,11},{10,... | collective-permute-start | bytes 589832 | tf_op jit(solution)/shard_map/ppermute | solution.py:394
  58.0 16.2 %collective-permute-start.6 = (bf16[256,384]{1,0:T(8,128)(2,1)S(1)}, bf16[256,384]{1,0:T(8,128)(2,1)S(1)}, u32[]{:S(2)}, u32[]{:S(2)}) collective-permute-start(bf16[256,384]{1,0:T(8,128)(2,1)S(1)} %get-tuple-element.72.refs_1_.refs_5_), channel_id=1, source_target_pairs={{0,1},{1,2},{2,3},{3,0},{4,5},{5,6},{6,7},{7,4},{8,9},{9,10},{10,1... | collective-permute-start | bytes 589832 | tf_op jit(solution)/shard_map/ppermute | solution.py:394
  80.3 48.3 %copy-start.1 = (f32[128,768]{1,0:T(8,128)}, f32[128,768]{1,0:T(8,128)S(1)}, u32[]{:S(2)}) copy-start(f32[128,768]{1,0:T(8,128)S(1)} %get-tuple-element.77.refs_5_) | copy-start | bytes 1179652
  80.4 9.8 %collective-permute-start.9 = (bf16[128,768]{1,0:T(8,128)(2,1)S(1)}, bf16[128,768]{1,0:T(8,128)(2,1)S(1)}, u32[]{:S(2)}, u32[]{:S(2)}) collective-permute-start(bf16[128,768]{1,0:T(8,128)(2,1)S(1)} %get-tuple-element.74), channel_id=1, source_target_pairs={{0,1},{1,2},{2,3},{3,0},{4,5},{5,6},{6,7},{7,4},{8,9},{9,10},{10,1... | collective-permute-start | bytes 589832 | tf_op jit(solution)/shard_map/ppermute | solution.py:402
  81.1 15.9 %collective-permute-start.10 = (bf16[128,768]{1,0:T(8,128)(2,1)S(1)}, bf16[128,768]{1,0:T(8,128)(2,1)S(1)}, u32[]{:S(2)}, u32[]{:S(2)}) collective-permute-start(bf16[128,768]{1,0:T(8,128)(2,1)S(1)} %get-tuple-element.75), channel_id=1, source_target_pairs={{0,2},{1,3},{2,0},{3,1},{4,6},{5,7},{6,4},{7,5},{8,10},{9,11},{10,... | collective-permute-start | bytes 589832 | tf_op jit(solution)/shard_map/ppermute | solution.py:402
  83.6 13.5 %collective-permute-start.11 = (bf16[128,768]{1,0:T(8,128)(2,1)S(1)}, bf16[128,768]{1,0:T(8,128)(2,1)S(1)}, u32[]{:S(2)}, u32[]{:S(2)}) collective-permute-start(bf16[128,768]{1,0:T(8,128)(2,1)S(1)} %get-tuple-element.76), channel_id=1, source_target_pairs={{0,3},{1,0},{2,1},{3,2},{4,7},{5,4},{6,5},{7,6},{8,11},{9,8},{10,9... | collective-permute-start | bytes 589832 | tf_op jit(solution)/shard_map/ppermute | solution.py:402
  100.1 11.1 %collective-permute-start.14 = (bf16[128,768]{1,0:T(8,128)(2,1)S(1)}, bf16[128,768]{1,0:T(8,128)(2,1)S(1)}, u32[]{:S(2)}, u32[]{:S(2)}) collective-permute-start(bf16[128,768]{1,0:T(8,128)(2,1)S(1)} %get-tuple-element.79.refs_1_), channel_id=1, source_target_pairs={{0,3},{1,0},{2,1},{3,2},{4,7},{5,4},{6,5},{7,6},{8,11},{9,8},{10,9... | collective-permute-start | bytes 589832 | tf_op jit(solution)/shard_map/ppermute | solution.py:394
  105.8 18.0 %collective-permute-start.13 = (bf16[128,768]{1,0:T(8,128)(2,1)S(1)}, bf16[128,768]{1,0:T(8,128)(2,1)S(1)}, u32[]{:S(2)}, u32[]{:S(2)}) collective-permute-start(bf16[128,768]{1,0:T(8,128)(2,1)S(1)} %get-tuple-element.79.refs_1_), channel_id=1, source_target_pairs={{0,2},{1,3},{2,0},{3,1},{4,6},{5,7},{6,4},{7,5},{8,10},{9,11},{10,... | collective-permute-start | bytes 589832 | tf_op jit(solution)/shard_map/ppermute | solution.py:394
  106.3 17.4 %collective-permute-start.12 = (bf16[128,768]{1,0:T(8,128)(2,1)S(1)}, bf16[128,768]{1,0:T(8,128)(2,1)S(1)}, u32[]{:S(2)}, u32[]{:S(2)}) collective-permute-start(bf16[128,768]{1,0:T(8,128)(2,1)S(1)} %get-tuple-element.79.refs_1_), channel_id=1, source_target_pairs={{0,1},{1,2},{2,3},{3,0},{4,5},{5,6},{6,7},{7,4},{8,9},{9,10},{10,1... | collective-permute-start | bytes 589832 | tf_op jit(solution)/shard_map/ppermute | solution.py:394
  131.6 45.8 %copy-start.9 = (f32[1,768]{1,0:T(1,128)S(1)}, f32[1,768]{1,0:T(1,128)}, u32[]{:S(2)}) copy-start(f32[1,768]{1,0:T(1,128)} %get-tuple-element.91.refs_16_) | copy-start | bytes 9220
  131.7 92.4 %all-gather.8.cloned.1.call-start = ((), (), s32[]{:S(2)}) async-start(), calls=%async_computation.5 | async-start | bytes 2654208 | tf_op jit(solution)/shard_map/all_gather | solution.py:1037
  132.5 9.7 %collective-permute-start.15 = (bf16[128,768]{1,0:T(8,128)(2,1)S(1)}, bf16[128,768]{1,0:T(8,128)(2,1)S(1)}, u32[]{:S(2)}, u32[]{:S(2)}) collective-permute-start(bf16[128,768]{1,0:T(8,128)(2,1)S(1)} %copy-done.15), channel_id=1, source_target_pairs={{0,1},{1,2},{2,3},{3,0},{4,5},{5,6},{6,7},{7,4},{8,9},{9,10},{10,1... | collective-permute-start | bytes 589832 | tf_op jit(solution)/shard_map/ppermute | solution.py:402
  132.6 16.3 %collective-permute-start.16 = (bf16[128,768]{1,0:T(8,128)(2,1)S(1)}, bf16[128,768]{1,0:T(8,128)(2,1)S(1)}, u32[]{:S(2)}, u32[]{:S(2)}) collective-permute-start(bf16[128,768]{1,0:T(8,128)(2,1)S(1)} %copy-done.14), channel_id=1, source_target_pairs={{0,2},{1,3},{2,0},{3,1},{4,6},{5,7},{6,4},{7,5},{8,10},{9,11},{10,... | collective-permute-start | bytes 589832 | tf_op jit(solution)/shard_map/ppermute | solution.py:402
  133.7 15.2 %collective-permute-start.17 = (bf16[128,768]{1,0:T(8,128)(2,1)S(1)}, bf16[128,768]{1,0:T(8,128)(2,1)S(1)}, u32[]{:S(2)}, u32[]{:S(2)}) collective-permute-start(bf16[128,768]{1,0:T(8,128)(2,1)S(1)} %copy-done.13), channel_id=1, source_target_pairs={{0,3},{1,0},{2,1},{3,2},{4,7},{5,4},{6,5},{7,6},{8,11},{9,8},{10,9... | collective-permute-start | bytes 589832 | tf_op jit(solution)/shard_map/ppermute | solution.py:402
  151.4 9.9 %collective-permute-start.20 = (bf16[128,768]{1,0:T(8,128)(2,1)}, bf16[128,768]{1,0:T(8,128)(2,1)S(1)}, u32[]{:S(2)}, u32[]{:S(2)}) collective-permute-start(bf16[128,768]{1,0:T(8,128)(2,1)} %get-tuple-element.87.refs_1_), channel_id=1, source_target_pairs={{0,3},{1,0},{2,1},{3,2},{4,7},{5,4},{6,5},{7,6},{8,11},{9,8},{10,9... | collective-permute-start | bytes 589832 | tf_op jit(solution)/shard_map/ppermute | solution.py:394
  155.6 18.1 %collective-permute-start.19 = (bf16[128,768]{1,0:T(8,128)(2,1)}, bf16[128,768]{1,0:T(8,128)(2,1)S(1)}, u32[]{:S(2)}, u32[]{:S(2)}) collective-permute-start(bf16[128,768]{1,0:T(8,128)(2,1)} %get-tuple-element.87.refs_1_), channel_id=1, source_target_pairs={{0,2},{1,3},{2,0},{3,1},{4,6},{5,7},{6,4},{7,5},{8,10},{9,11},{10,... | collective-permute-start | bytes 589832 | tf_op jit(solution)/shard_map/ppermute | solution.py:394
  156.8 17.0 %collective-permute-start.18 = (bf16[128,768]{1,0:T(8,128)(2,1)}, bf16[128,768]{1,0:T(8,128)(2,1)S(1)}, u32[]{:S(2)}, u32[]{:S(2)}) collective-permute-start(bf16[128,768]{1,0:T(8,128)(2,1)} %get-tuple-element.87.refs_1_), channel_id=1, source_target_pairs={{0,1},{1,2},{2,3},{3,0},{4,5},{5,6},{6,7},{7,4},{8,9},{9,10},{10,1... | collective-permute-start | bytes 589832 | tf_op jit(solution)/shard_map/ppermute | solution.py:394
  176.7 12.8 %collective-permute-start.28 = (bf16[96,768]{1,0:T(8,128)(2,1)S(1)}, bf16[96,768]{1,0:T(8,128)(2,1)S(1)}, u32[]{:S(2)}, u32[]{:S(2)}) collective-permute-start(bf16[96,768]{1,0:T(8,128)(2,1)S(1)} %get-tuple-element.96.refs_17_), channel_id=1, source_target_pairs={{0,2},{1,3},{2,0},{3,1},{4,6},{5,7},{6,4},{7,5},{8,10},{9,11},{10,... | collective-permute-start | bytes 442376 | tf_op jit(solution)/shard_map/ppermute | solution.py:408
  191.6 81.8 %reduce-scatter.5.cloned.1.call-start = ((), (), s32[]{:S(2)}) async-start(), calls=%async_computation.6 | async-start | bytes 983040 | tf_op jit(solution)/shard_map/reduce_scatter | solution.py:1071
  191.6 2.2 collective-permute-start.21
  195.9 9.6 %collective-permute-start.22 = (bf16[112,768]{1,0:T(8,128)(2,1)S(1)}, bf16[112,768]{1,0:T(8,128)(2,1)S(1)}, u32[]{:S(2)}, u32[]{:S(2)}) collective-permute-start(bf16[112,768]{1,0:T(8,128)(2,1)S(1)} %get-tuple-element.101), channel_id=1, source_target_pairs={{0,8},{4,12},{8,0},{12,4},{16,24},{20,28},{24,16},{28,20},{1,9},{5... | collective-permute-start | bytes 516104 | tf_op jit(solution)/shard_map/ppermute | solution.py:408
  197.4 13.0 %collective-permute-start.23 = (bf16[112,768]{1,0:T(8,128)(2,1)S(1)}, bf16[112,768]{1,0:T(8,128)(2,1)S(1)}, u32[]{:S(2)}, u32[]{:S(2)}) collective-permute-start(bf16[112,768]{1,0:T(8,128)(2,1)S(1)} %get-tuple-element.102), channel_id=1, source_target_pairs={{0,16},{4,20},{8,24},{12,28},{16,0},{20,4},{24,8},{28,12},{1,17},{... | collective-permute-start | bytes 516104 | tf_op jit(solution)/shard_map/ppermute | solution.py:408
  198.0 12.4 %collective-permute-start.24 = (bf16[112,768]{1,0:T(8,128)(2,1)S(1)}, bf16[112,768]{1,0:T(8,128)(2,1)S(1)}, u32[]{:S(2)}, u32[]{:S(2)}) collective-permute-start(bf16[112,768]{1,0:T(8,128)(2,1)S(1)} %get-tuple-element.103), channel_id=1, source_target_pairs={{0,24},{4,28},{8,16},{12,20},{16,8},{20,12},{24,0},{28,4},{1,25},{... | collective-permute-start | bytes 516104 | tf_op jit(solution)/shard_map/ppermute | solution.py:408
  212.9 6.5 %collective-permute-start.25 = (bf16[112,192]{1,0:T(8,128)(2,1)S(1)}, bf16[112,192]{1,0:T(8,128)(2,1)S(1)}, u32[]{:S(2)}, u32[]{:S(2)}) collective-permute-start(bf16[112,192]{1,0:T(8,128)(2,1)S(1)} %get-tuple-element.105), channel_id=1, source_target_pairs={{0,1},{1,2},{2,3},{3,0},{4,5},{5,6},{6,7},{7,4},{8,9},{9,10},{10,1... | collective-permute-start | bytes 129032 | tf_op jit(solution)/shard_map/ppermute | solution.py:402
  214.5 6.2 %collective-permute-start.26 = (bf16[112,192]{1,0:T(8,128)(2,1)S(1)}, bf16[112,192]{1,0:T(8,128)(2,1)S(1)}, u32[]{:S(2)}, u32[]{:S(2)}) collective-permute-start(bf16[112,192]{1,0:T(8,128)(2,1)S(1)} %get-tuple-element.106), channel_id=1, source_target_pairs={{0,2},{1,3},{2,0},{3,1},{4,6},{5,7},{6,4},{7,5},{8,10},{9,11},{10,... | collective-permute-start | bytes 129032 | tf_op jit(solution)/shard_map/ppermute | solution.py:402
  215.4 5.3 %collective-permute-start.27 = (bf16[112,192]{1,0:T(8,128)(2,1)S(1)}, bf16[112,192]{1,0:T(8,128)(2,1)S(1)}, u32[]{:S(2)}, u32[]{:S(2)}) collective-permute-start(bf16[112,192]{1,0:T(8,128)(2,1)S(1)} %get-tuple-element.107), channel_id=1, source_target_pairs={{0,3},{1,0},{2,1},{3,2},{4,7},{5,4},{6,5},{7,6},{8,11},{9,8},{10,9... | collective-permute-start | bytes 129032 | tf_op jit(solution)/shard_map/ppermute | solution.py:402
  226.7 6.1 %collective-permute-start.29 = (bf16[96,768]{1,0:T(8,128)(2,1)S(1)}, bf16[96,768]{1,0:T(8,128)(2,1)S(1)}, u32[]{:S(2)}, u32[]{:S(2)}) collective-permute-start(bf16[96,768]{1,0:T(8,128)(2,1)S(1)} %shard_map.230.refs_5_), channel_id=1, source_target_pairs={{0,1},{1,0},{2,3},{3,2},{4,5},{5,4},{6,7},{7,6},{8,9},{9,8},{10,11... | collective-permute-start | bytes 442376 | tf_op jit(solution)/shard_map/ppermute | solution.py:408
  233.7 1.4 collective-permute-start.30
  238.8 32.9 %copy-start.11 = (f32[12,24]{1,0:T(8,128)S(1)}, f32[12,24]{1,0:T(8,128)}, u32[]{:S(2)}) copy-start(f32[12,24]{1,0:T(8,128)} %param.17) | copy-start | bytes 3460
  238.8 32.9 %copy-start.12 = (f32[12,24]{1,0:T(8,128)S(1)}, f32[12,24]{1,0:T(8,128)}, u32[]{:S(2)}) copy-start(f32[12,24]{1,0:T(8,128)} %param.21) | copy-start | bytes 3460
  238.9 10.9 %collective-permute-start.33 = (bf16[192,768]{1,0:T(8,128)(2,1)S(1)}, bf16[192,768]{1,0:T(8,128)(2,1)S(1)}, u32[]{:S(2)}, u32[]{:S(2)}) collective-permute-start(bf16[192,768]{1,0:T(8,128)(2,1)S(1)} %shard_map.232.refs_2_.refs_1_), channel_id=1, source_target_pairs={{0,24},{4,28},{8,16},{12,20},{16,8},{20,12},{24,0},{28,4},{1,25},{... | collective-permute-start | bytes 884744 | tf_op jit(solution)/shard_map/ppermute | solution.py:408
  240.4 14.8 %collective-permute-start.32 = (bf16[192,768]{1,0:T(8,128)(2,1)S(1)}, bf16[192,768]{1,0:T(8,128)(2,1)S(1)}, u32[]{:S(2)}, u32[]{:S(2)}) collective-permute-start(bf16[192,768]{1,0:T(8,128)(2,1)S(1)} %shard_map.232.refs_2_.refs_1_), channel_id=1, source_target_pairs={{0,16},{4,20},{8,24},{12,28},{16,0},{20,4},{24,8},{28,12},{1,17},{... | collective-permute-start | bytes 884744 | tf_op jit(solution)/shard_map/ppermute | solution.py:408
  241.9 13.3 %collective-permute-start.31 = (bf16[192,768]{1,0:T(8,128)(2,1)S(1)}, bf16[192,768]{1,0:T(8,128)(2,1)S(1)}, u32[]{:S(2)}, u32[]{:S(2)}) collective-permute-start(bf16[192,768]{1,0:T(8,128)(2,1)S(1)} %shard_map.232.refs_2_.refs_1_), channel_id=1, source_target_pairs={{0,8},{4,12},{8,0},{12,4},{16,24},{20,28},{24,16},{28,20},{1,9},{5... | collective-permute-start | bytes 884744 | tf_op jit(solution)/shard_map/ppermute | solution.py:408
  264.8 1.6 collective-permute-start.34
  267.3 6.1 %collective-permute-start.35 = (bf16[96,192]{1,0:T(8,128)(2,1)S(1)}, bf16[96,192]{1,0:T(8,128)(2,1)S(1)}, u32[]{:S(2)}, u32[]{:S(2)}) collective-permute-start(bf16[96,192]{1,0:T(8,128)(2,1)S(1)} %get-tuple-element.113), channel_id=1, source_target_pairs={{0,1},{1,2},{2,3},{3,0},{4,5},{5,6},{6,7},{7,4},{8,9},{9,10},{10,1... | collective-permute-start | bytes 110600 | tf_op jit(solution)/shard_map/ppermute | solution.py:402
  268.8 6.4 %collective-permute-start.37 = (bf16[96,192]{1,0:T(8,128)(2,1)S(1)}, bf16[96,192]{1,0:T(8,128)(2,1)S(1)}, u32[]{:S(2)}, u32[]{:S(2)}) collective-permute-start(bf16[96,192]{1,0:T(8,128)(2,1)S(1)} %get-tuple-element.124), channel_id=1, source_target_pairs={{0,3},{1,0},{2,1},{3,2},{4,7},{5,4},{6,5},{7,6},{8,11},{9,8},{10,9... | collective-permute-start | bytes 110600 | tf_op jit(solution)/shard_map/ppermute | solution.py:402
  271.2 11.2 %collective-permute-start.36 = (bf16[96,960]{1,0:T(8,128)(2,1)S(1)}, bf16[96,960]{1,0:T(8,128)(2,1)S(1)}, u32[]{:S(2)}, u32[]{:S(2)}) collective-permute-start(bf16[96,960]{1,0:T(8,128)(2,1)S(1)} %get-tuple-element.123), channel_id=1, source_target_pairs={{0,2},{1,3},{2,0},{3,1},{4,6},{5,7},{6,4},{7,5},{8,10},{9,11},{10,... | collective-permute-start | bytes 552968 | tf_op jit(solution)/shard_map/ppermute | solution.py:402
  (11 other events, 62.0 us)
Sparse Core Ops, SparseCore 0:
  10.5 36.0 all-gather.3
  49.0 24.2 all-gather.5
  131.8 40.2 reduce-scatter.2
  191.7 32.3 all-gather.7
  239.0 23.2 reduce-scatter.4
